TPU v7x, 32 devices: a whole 2x2x4 slice. The times are simulated.
32 devices in a mesh: tok: 2 (over core), row: 4 (over y, x), col: 4 (over z).
Axes of the slice: x: 2, y: 2, z: 4, core: 2. Of those that a mesh axis runs over, the one named last changes fastest.
Arguments:
- layer_in: bfloat16 [9216, 2048], P(('tok', 'row'), 'col'), may hold values from -6 to 6
- cotangent: bfloat16 [9216, 2048], P(('tok', 'row'), 'col'), may hold values from -6 to 6
- qkv_weight: bfloat16 [3, 2048, 2048], P(None, 'col', 'row'), may hold values from -0.125 to 0.125
- out_weight: bfloat16 [2048, 2048], P('row', 'col'), may hold values from -0.125 to 0.125
- ffn_weight: bfloat16 [2, 2048, 8192], P(None, 'col', 'row'), may hold values from -0.125 to 0.125
- down_weight: bfloat16 [8192, 2048], P('row', 'col'), may hold values from -0.0625 to 0.0625
- qk_gain: bfloat16 [2, 2048], P(None, 'row'), may hold values from 0.5 to 1.5
- post_gain: bfloat16 [2, 2048], P(None, 'col'), may hold values from 0.5 to 1.5
- qkv_lower: bfloat16 [3, 8, 2048, 16], P(None, None, 'col'), may hold values from -0.125 to 0.125
- qkv_raise: bfloat16 [3, 8, 16, 2048], P(None, None, None, 'row'), may hold values from -0.25 to 0.25
- out_lower: bfloat16 [8, 2048, 16], P(None, 'row'), may hold values from -0.125 to 0.125
- out_raise: bfloat16 [8, 16, 2048], P(None, None, 'col'), may hold values from -0.25 to 0.25
- ffn_lower: bfloat16 [2, 8, 2048, 16], P(None, None, 'col'), may hold values from -0.125 to 0.125
- ffn_raise: bfloat16 [2, 8, 16, 8192], P(None, None, None, 'row'), may hold values from -0.25 to 0.25
- down_lower: bfloat16 [8, 8192, 16], P(None, 'row'), may hold values from -0.0625 to 0.0625
- down_raise: bfloat16 [8, 16, 2048], P(None, None, 'col'), may hold values from -0.25 to 0.25
- adapter_ids: int32 [8, 7], replicated, may hold values from 0 to 7
- prompt_len: int32 [8], replicated, may hold values from 256 to 1024, as said below
Outputs:
- layer_out: float32 [9216, 2048], P(('tok', 'row'), 'col')
- grad_in: float32 [9216, 2048], P(('tok', 'row'), 'col')
- qkv_lower_grad: float32 [3, 8, 2048, 16], P(None, None, 'col')
- qkv_raise_grad: float32 [3, 8, 16, 2048], P(None, None, None, 'row')
- out_lower_grad: float32 [8, 2048, 16], P(None, 'row')
- out_raise_grad: float32 [8, 16, 2048], P(None, None, 'col')
- ffn_lower_grad: float32 [2, 8, 2048, 16], P(None, None, 'col')
- ffn_raise_grad: float32 [2, 8, 16, 8192], P(None, None, None, 'row')
- down_lower_grad: float32 [8, 8192, 16], P(None, 'row')
- down_raise_grad: float32 [8, 16, 2048], P(None, None, 'col')
Inputs may be any that keep to these rules, and one draw needn't show every extreme that they name: Group g's prompt holds prompt_len[g] real tokens at its start, the other slots of its 1024 are padding; in every draw some group's prompt is full. adapter_ids[g, p] is the adapter of projection p (q, k, v, out, gate, up, down) for group g.
All inputs are finite; a program needn't handle non-finite values.
Results may differ from a plain program's by a relative error of at most 0.018.
Values may be sent and summed in bfloat16 or wider, within the bound.
A program may use at most 320 MiB of HBM per device.

v0:
```python
import math

import jax
import jax.numpy as jnp
from jax import lax
from jax.sharding import PartitionSpec as P

D = 2048
HEAD_DIM = 128
RANK = 16
ADAPTERS = 8
PROMPT = 1024
CONT_LEN = 128
SLAB = 1152


adapter_scale = 2.0
norm_eps = 1e-06
rope_base = 500000.0
very_low = -1e30
full_precision = lax.Precision.HIGHEST


def rows_gather(values):
    return lax.all_gather(values, "row", axis=0, tiled=True)


def cols_scatter(values):
    return (
        lax.psum_scatter(values[0], "col", scatter_dimension=0, tiled=True),
        lax.psum_scatter(values[1], "col", scatter_dimension=0, tiled=True),
    )


def cols_gather(values):
    return lax.all_gather(values, "col", axis=0, tiled=True)


def rows_scatter(values):
    return (
        lax.psum_scatter(values[0], "row", scatter_dimension=0, tiled=True),
        lax.psum_scatter(values[1], "row", scatter_dimension=0, tiled=True),
    )


def col_total(values):
    return lax.psum(values, "col")


def row_total(values):
    return lax.psum((values[0], values[1]), "row")


def choose_rows(adapters, chosen_ids):
    onehot = (
        chosen_ids[:, None] == jnp.arange(adapters.shape[0], dtype=jnp.int32)[None, :]
    ).astype(adapters.dtype)
    return jnp.tensordot(onehot, adapters, axes=1)


def place_grad(chosen_id, number, gradient):
    onehot = (jnp.arange(number, dtype=jnp.int32) == chosen_id).astype(jnp.float32)
    return onehot.reshape((number,) + (1,) * gradient.ndim) * gradient[None]


def token_places(length):
    slot_ids = jnp.arange(SLAB, dtype=jnp.int32)
    return jnp.where(slot_ids < PROMPT, slot_ids, length + (slot_ids - PROMPT) % CONT_LEN)


def rotation(places, head_size):
    half_dim = head_size // 2
    frequency = jnp.exp(
        -(2.0 * jnp.arange(half_dim, dtype=jnp.float32) / head_size) * math.log(rope_base)
    )
    angles = places.astype(jnp.float32)[:, None] * frequency[None, :]
    return (jnp.cos(angles)[:, None, :], jnp.sin(angles)[:, None, :])


def rotate(values, cosine, sine, direction):
    half_dim = values.shape[-1] // 2
    front_half = values[..., :half_dim]
    back_half = values[..., half_dim:]
    return jnp.concatenate(
        [
            front_half * cosine - direction * back_half * sine,
            back_half * cosine + direction * front_half * sine,
        ],
        axis=-1,
    )


def key_mask(query_ids, key_ids, length):
    cont_start = jnp.where(
        query_ids >= PROMPT, PROMPT + (query_ids - PROMPT) // CONT_LEN * CONT_LEN, SLAB
    )
    causal = key_ids[None, :] <= query_ids[:, None]
    return causal & ((key_ids[None, :] < length) | (key_ids[None, :] >= cont_start[:, None]))


def grid_forward_in(local_rows, weights, lowers, raisers, slab_ids, own_ids, slab_count):
    gathered = rows_gather(local_rows)
    total_rows = gathered.shape[0]
    num_proj = weights.shape[0]
    output_width = weights.shape[2]
    rank_dim = lowers.shape[-1]
    dense_part = jnp.einsum(
        "td,pdo->tpo", gathered, weights, preferred_element_type=jnp.float32
    ).reshape(total_rows, num_proj * output_width)
    blocks = gathered.reshape(slab_count, total_rows // slab_count, gathered.shape[1])
    lowered = []
    for projection_index in range(num_proj):
        picked = choose_rows(lowers[projection_index], slab_ids[:, projection_index])
        lowered.append(
            jnp.einsum("std,sdr->str", blocks, picked, preferred_element_type=jnp.float32).reshape(
                total_rows, rank_dim
            )
        )
    total_output, adapter_update = cols_scatter((dense_part, jnp.concatenate(lowered, axis=1)))
    outputs = []
    for projection_index in range(num_proj):
        expanded_rows = choose_rows(
            raisers[projection_index], own_ids[projection_index : projection_index + 1]
        )[0].astype(jnp.float32)
        adapter_extra = jnp.dot(
            adapter_update[:, projection_index * rank_dim : (projection_index + 1) * rank_dim],
            expanded_rows,
            precision=full_precision,
        )
        outputs.append(
            total_output[:, projection_index * output_width : (projection_index + 1) * output_width]
            + adapter_scale * adapter_extra
        )
    return (outputs, adapter_update)


def grid_forward_out(
    local_slab, dense_weight, down_factor, up_factor, slab_ids, own_id, slab_count
):
    gathered = cols_gather(local_slab)
    total_rows = gathered.shape[0]
    dense_part = jnp.dot(gathered, dense_weight, preferred_element_type=jnp.float32)
    blocks = gathered.reshape(slab_count, total_rows // slab_count, gathered.shape[1])
    picked = choose_rows(down_factor, slab_ids)
    lowered = jnp.einsum(
        "std,sdr->str", blocks, picked, preferred_element_type=jnp.float32
    ).reshape(total_rows, down_factor.shape[-1])
    total_output, adapter_update = rows_scatter((dense_part, lowered))
    expanded_rows = choose_rows(up_factor, own_id[None])[0].astype(jnp.float32)
    return (
        total_output
        + adapter_scale * jnp.dot(adapter_update, expanded_rows, precision=full_precision),
        adapter_update,
    )


def grid_backward_in(grad_slab, weights, lowers, raisers, slab_ids, slab_count):
    gathered = cols_gather(grad_slab)
    total_rows = gathered.shape[0]
    num_proj, in_width, output_width = weights.shape
    rank_dim = lowers.shape[-1]
    pieces = gathered.reshape(total_rows, num_proj, output_width)
    back_dense = jnp.einsum("tpo,pdo->td", pieces, weights, preferred_element_type=jnp.float32)
    lowered = []
    for projection_index in range(num_proj):
        grad_blocks = pieces[:, projection_index, :].reshape(
            slab_count, total_rows // slab_count, output_width
        )
        expanded_rows = choose_rows(raisers[projection_index], slab_ids[:, projection_index])
        reduced_gradient = adapter_scale * jnp.einsum(
            "sto,sro->str", grad_blocks, expanded_rows, preferred_element_type=jnp.float32
        )
        picked = choose_rows(lowers[projection_index], slab_ids[:, projection_index]).astype(
            jnp.float32
        )
        back_dense = back_dense + jnp.einsum(
            "str,sdr->std", reduced_gradient, picked, precision=full_precision
        ).reshape(total_rows, in_width)
        lowered.append(reduced_gradient.reshape(total_rows, rank_dim))
    return rows_scatter((back_dense, jnp.concatenate(lowered, axis=1)))


def grid_backward_out(grad_rows, dense_weight, down_factor, up_factor, slab_ids, slab_count):
    gathered = rows_gather(grad_rows)
    total_rows = gathered.shape[0]
    in_width = dense_weight.shape[0]
    back_dense = jnp.einsum("to,io->ti", gathered, dense_weight, preferred_element_type=jnp.float32)
    grad_blocks = gathered.reshape(slab_count, total_rows // slab_count, gathered.shape[1])
    expanded_rows = choose_rows(up_factor, slab_ids)
    reduced_gradient = adapter_scale * jnp.einsum(
        "sto,sro->str", grad_blocks, expanded_rows, preferred_element_type=jnp.float32
    )
    picked = choose_rows(down_factor, slab_ids).astype(jnp.float32)
    back_dense = back_dense + jnp.einsum(
        "str,sir->sti", reduced_gradient, picked, precision=full_precision
    ).reshape(total_rows, in_width)
    return cols_scatter((back_dense, reduced_gradient.reshape(total_rows, down_factor.shape[-1])))


def norm_forward(values, gain):
    inverse = lax.rsqrt(col_total(jnp.sum(values * values, axis=1)) / D + norm_eps)
    return (values * inverse[:, None] * gain.astype(jnp.float32), inverse)


def norm_backward(values, inverse, gain, grad_out):
    weighted = grad_out * gain.astype(jnp.float32)
    inner = col_total(jnp.sum(values * weighted, axis=1)) / D
    return inverse[:, None] * weighted - values * (inverse**3 * inner)[:, None]


def attend_forward(queries, keys_low, values_low, length, block_len):
    slab_len = queries.shape[0]
    score_scale = 1.0 / math.sqrt(queries.shape[2])
    key_ids = jnp.arange(slab_len, dtype=jnp.int32)

    def one_block(block_start):
        q_block = lax.dynamic_slice_in_dim(queries, block_start, block_len, 0)
        query_ids = block_start + jnp.arange(block_len, dtype=jnp.int32)
        scores = (
            jnp.einsum("qhd,khd->hqk", q_block, keys_low, preferred_element_type=jnp.float32)
            * score_scale
        )
        scores = jnp.where(key_mask(query_ids, key_ids, length)[None], scores, very_low)
        row_top = jnp.max(scores, axis=2, keepdims=True)
        shifted = jnp.exp(scores - row_top)
        row_sum = jnp.sum(shifted, axis=2, keepdims=True)
        attn_probs = (shifted / row_sum).astype(jnp.bfloat16)
        attended = jnp.einsum(
            "hqk,khd->qhd", attn_probs, values_low, preferred_element_type=jnp.float32
        )
        return (attended, (row_top + jnp.log(row_sum))[:, :, 0])

    block_starts = jnp.arange(slab_len // block_len, dtype=jnp.int32) * block_len
    attended, log_sums = lax.map(one_block, block_starts)
    return (attended.reshape(queries.shape), log_sums)


def attend_backward(queries, keys_low, values_low, grad_out, log_sums, length, block_len):
    slab_len = queries.shape[0]
    score_scale = 1.0 / math.sqrt(queries.shape[2])
    key_ids = jnp.arange(slab_len, dtype=jnp.int32)

    def one_block(carry, input_rows):
        grad_keys, grad_values = carry
        block_start, block_sums = input_rows
        q_block = lax.dynamic_slice_in_dim(queries, block_start, block_len, 0)
        g_block = lax.dynamic_slice_in_dim(grad_out, block_start, block_len, 0)
        query_ids = block_start + jnp.arange(block_len, dtype=jnp.int32)
        scores = (
            jnp.einsum("qhd,khd->hqk", q_block, keys_low, preferred_element_type=jnp.float32)
            * score_scale
        )
        scores = jnp.where(key_mask(query_ids, key_ids, length)[None], scores, very_low)
        attn_probs = jnp.exp(scores - block_sums[:, :, None])
        probs_low = attn_probs.astype(jnp.bfloat16)
        grad_values = grad_values + jnp.einsum(
            "hqk,qhd->khd", probs_low, g_block, preferred_element_type=jnp.float32
        )
        grad_probs = jnp.einsum(
            "qhd,khd->hqk", g_block, values_low, preferred_element_type=jnp.float32
        )
        row_inner = jnp.sum(attn_probs * grad_probs, axis=2, keepdims=True)
        grad_scores = (attn_probs * (grad_probs - row_inner)).astype(jnp.bfloat16)
        grad_query = (
            jnp.einsum("hqk,khd->qhd", grad_scores, keys_low, preferred_element_type=jnp.float32)
            * score_scale
        )
        grad_keys = (
            grad_keys
            + jnp.einsum("hqk,qhd->khd", grad_scores, q_block, preferred_element_type=jnp.float32)
            * score_scale
        )
        return ((grad_keys, grad_values), grad_query)

    block_starts = jnp.arange(slab_len // block_len, dtype=jnp.int32) * block_len
    zeros_init = jnp.zeros(queries.shape, jnp.float32)
    (grad_keys, grad_values), grad_queries = lax.scan(
        one_block, (zeros_init, zeros_init), (block_starts, log_sums)
    )
    return (grad_queries.reshape(queries.shape), grad_keys, grad_values)


def on_device(
    layer_in,
    cotangent,
    qkv_weight,
    out_weight,
    ffn_weight,
    down_weight,
    qk_gain,
    post_gain,
    qkv_lower,
    qkv_raise,
    out_lower,
    out_raise,
    ffn_lower,
    ffn_raise,
    down_lower,
    down_raise,
    adapter_ids,
    prompt_len,
):
    row_count = lax.axis_size("row")
    col_count = lax.axis_size("col")
    per_slab = row_count // col_count
    group_base = lax.axis_index("tok") * col_count
    col_group = group_base + lax.axis_index("col")
    row_group = group_base + lax.axis_index("row") // per_slab
    slab_ids = lax.dynamic_slice_in_dim(adapter_ids, group_base, col_count, 0)
    col_ids = lax.dynamic_index_in_dim(adapter_ids, col_group, 0, keepdims=False)
    row_ids = lax.dynamic_index_in_dim(adapter_ids, row_group, 0, keepdims=False)
    length = lax.dynamic_index_in_dim(prompt_len, col_group, 0, keepdims=False)
    block_len = math.gcd(SLAB, 512)
    qkv_outs, qkv_lowrank = grid_forward_in(
        layer_in, qkv_weight, qkv_lower, qkv_raise, slab_ids[:, 0:3], col_ids[0:3], col_count
    )
    q_lin, k_lin, v_lin = qkv_outs
    norm_sums = row_total((jnp.sum(q_lin * q_lin, axis=1), jnp.sum(k_lin * k_lin, axis=1)))
    q_inverse = lax.rsqrt(norm_sums[0] / D + norm_eps)
    k_inverse = lax.rsqrt(norm_sums[1] / D + norm_eps)
    gains = qk_gain.astype(jnp.float32)
    local_heads = q_lin.shape[1] // HEAD_DIM
    cosine, sine = rotation(token_places(length), HEAD_DIM)
    q_low = rotate(
        (q_lin * q_inverse[:, None] * gains[0]).reshape(SLAB, local_heads, HEAD_DIM),
        cosine,
        sine,
        1.0,
    ).astype(jnp.bfloat16)
    k_low = rotate(
        (k_lin * k_inverse[:, None] * gains[1]).reshape(SLAB, local_heads, HEAD_DIM),
        cosine,
        sine,
        1.0,
    ).astype(jnp.bfloat16)
    v_low = v_lin.reshape(SLAB, local_heads, HEAD_DIM).astype(jnp.bfloat16)
    attended, log_sums = attend_forward(q_low, k_low, v_low, length, block_len)
    attn_low = attended.reshape(SLAB, -1).astype(jnp.bfloat16)
    attn_lin, output_adapter_rank = grid_forward_out(
        attn_low, out_weight, out_lower, out_raise, slab_ids[:, 3], row_ids[3], col_count
    )
    attn_norm, attn_inverse = norm_forward(attn_lin, post_gain[0])
    hidden = layer_in.astype(jnp.float32) + attn_norm
    hidden_low = hidden.astype(jnp.bfloat16)
    ffn_outs, ffn_lowrank = grid_forward_in(
        hidden_low, ffn_weight, ffn_lower, ffn_raise, slab_ids[:, 4:6], col_ids[4:6], col_count
    )
    gate_lin, up_lin = ffn_outs
    gate_sig = jax.nn.sigmoid(gate_lin)
    gate_act = gate_lin * gate_sig
    act_low = (gate_act * up_lin).astype(jnp.bfloat16)
    mlp_lin, down_adapter_rank = grid_forward_out(
        act_low, down_weight, down_lower, down_raise, slab_ids[:, 6], row_ids[6], col_count
    )
    mlp_norm, mlp_inverse = norm_forward(mlp_lin, post_gain[1])
    layer_out = hidden + mlp_norm
    grad_out = cotangent.astype(jnp.float32)
    feedforward_gradient = norm_backward(mlp_lin, mlp_inverse, post_gain[1], grad_out).astype(
        jnp.bfloat16
    )
    down_raise_grad = place_grad(
        row_ids[6],
        ADAPTERS,
        adapter_scale
        * jnp.dot(
            down_adapter_rank.T, feedforward_gradient.astype(jnp.float32), precision=full_precision
        ),
    )
    grad_act, down_low_grad = grid_backward_out(
        feedforward_gradient, down_weight, down_lower, down_raise, slab_ids[:, 6], col_count
    )
    down_lower_grad = place_grad(
        col_ids[6],
        ADAPTERS,
        jnp.dot(act_low.astype(jnp.float32).T, down_low_grad, precision=full_precision),
    )
    grad_gate = (grad_act * up_lin * gate_sig * (1.0 + gate_lin * (1.0 - gate_sig))).astype(
        jnp.bfloat16
    )
    grad_up = (grad_act * gate_act).astype(jnp.bfloat16)
    ffn_raise_grad = jnp.stack(
        [
            place_grad(
                col_ids[4],
                ADAPTERS,
                adapter_scale
                * jnp.dot(
                    ffn_lowrank[:, 0:RANK].T,
                    grad_gate.astype(jnp.float32),
                    precision=full_precision,
                ),
            ),
            place_grad(
                col_ids[5],
                ADAPTERS,
                adapter_scale
                * jnp.dot(
                    ffn_lowrank[:, RANK : 2 * RANK].T,
                    grad_up.astype(jnp.float32),
                    precision=full_precision,
                ),
            ),
        ]
    )
    grad_ffn_in, ffn_low_grad = grid_backward_in(
        jnp.concatenate([grad_gate, grad_up], axis=1),
        ffn_weight,
        ffn_lower,
        ffn_raise,
        slab_ids[:, 4:6],
        col_count,
    )
    hidden_wide = hidden_low.astype(jnp.float32)
    ffn_lower_grad = jnp.stack(
        [
            place_grad(
                row_ids[4],
                ADAPTERS,
                jnp.dot(hidden_wide.T, ffn_low_grad[:, 0:RANK], precision=full_precision),
            ),
            place_grad(
                row_ids[5],
                ADAPTERS,
                jnp.dot(hidden_wide.T, ffn_low_grad[:, RANK : 2 * RANK], precision=full_precision),
            ),
        ]
    )
    grad_hidden = grad_out + grad_ffn_in
    attention_gradient = norm_backward(attn_lin, attn_inverse, post_gain[0], grad_hidden).astype(
        jnp.bfloat16
    )
    out_raise_grad = place_grad(
        row_ids[3],
        ADAPTERS,
        adapter_scale
        * jnp.dot(
            output_adapter_rank.T, attention_gradient.astype(jnp.float32), precision=full_precision
        ),
    )
    grad_heads, out_low_grad = grid_backward_out(
        attention_gradient, out_weight, out_lower, out_raise, slab_ids[:, 3], col_count
    )
    out_lower_grad = place_grad(
        col_ids[3],
        ADAPTERS,
        jnp.dot(attn_low.astype(jnp.float32).T, out_low_grad, precision=full_precision),
    )
    grad_heads_low = grad_heads.astype(jnp.bfloat16).reshape(SLAB, local_heads, HEAD_DIM)
    grad_q_rot, grad_k_rot, grad_v_all = attend_backward(
        q_low, k_low, v_low, grad_heads_low, log_sums, length, block_len
    )
    weighted_q = rotate(grad_q_rot, cosine, sine, -1.0).reshape(SLAB, -1) * gains[0]
    weighted_k = rotate(grad_k_rot, cosine, sine, -1.0).reshape(SLAB, -1) * gains[1]
    inner_sums = row_total(
        (jnp.sum(q_lin * weighted_q, axis=1), jnp.sum(k_lin * weighted_k, axis=1))
    )
    grad_q_lin = (
        q_inverse[:, None] * weighted_q - q_lin * (q_inverse**3 * inner_sums[0] / D)[:, None]
    ).astype(jnp.bfloat16)
    grad_k_lin = (
        k_inverse[:, None] * weighted_k - k_lin * (k_inverse**3 * inner_sums[1] / D)[:, None]
    ).astype(jnp.bfloat16)
    grad_v_lin = grad_v_all.reshape(SLAB, -1).astype(jnp.bfloat16)
    grad_lins = [grad_q_lin, grad_k_lin, grad_v_lin]
    qkv_raise_grad = jnp.stack(
        [
            place_grad(
                col_ids[projection_index],
                ADAPTERS,
                adapter_scale
                * jnp.dot(
                    qkv_lowrank[:, projection_index * RANK : (projection_index + 1) * RANK].T,
                    grad_lins[projection_index].astype(jnp.float32),
                    precision=full_precision,
                ),
            )
            for projection_index in range(3)
        ]
    )
    grad_qkv_in, qkv_low_grad = grid_backward_in(
        jnp.concatenate(grad_lins, axis=1),
        qkv_weight,
        qkv_lower,
        qkv_raise,
        slab_ids[:, 0:3],
        col_count,
    )
    input_wide = layer_in.astype(jnp.float32)
    qkv_lower_grad = jnp.stack(
        [
            place_grad(
                row_ids[projection_index],
                ADAPTERS,
                jnp.dot(
                    input_wide.T,
                    qkv_low_grad[:, projection_index * RANK : (projection_index + 1) * RANK],
                    precision=full_precision,
                ),
            )
            for projection_index in range(3)
        ]
    )
    grad_in = grad_hidden + grad_qkv_in
    row_sums = (
        lax.psum(qkv_lower_grad.astype(jnp.bfloat16), ("tok", "row")).astype(jnp.float32),
        lax.psum(out_raise_grad.astype(jnp.bfloat16), ("tok", "row")).astype(jnp.float32),
        lax.psum(ffn_lower_grad.astype(jnp.bfloat16), ("tok", "row")).astype(jnp.float32),
        lax.psum(down_raise_grad.astype(jnp.bfloat16), ("tok", "row")).astype(jnp.float32),
    )
    col_sums = (
        lax.psum(qkv_raise_grad.astype(jnp.bfloat16), ("tok", "col")).astype(jnp.float32),
        lax.psum(out_lower_grad.astype(jnp.bfloat16), ("tok", "col")).astype(jnp.float32),
        lax.psum(ffn_raise_grad.astype(jnp.bfloat16), ("tok", "col")).astype(jnp.float32),
        lax.psum(down_lower_grad.astype(jnp.bfloat16), ("tok", "col")).astype(jnp.float32),
    )
    return (
        layer_out,
        grad_in,
        row_sums[0],
        col_sums[0],
        col_sums[1],
        row_sums[1],
        row_sums[2],
        col_sums[2],
        col_sums[3],
        row_sums[3],
    )


def solution(mesh):
    return jax.shard_map(
        on_device,
        mesh=mesh,
        in_specs=(
            P(("tok", "row"), "col"),
            P(("tok", "row"), "col"),
            P(None, "col", "row"),
            P("row", "col"),
            P(None, "col", "row"),
            P("row", "col"),
            P(None, "row"),
            P(None, "col"),
            P(None, None, "col", None),
            P(None, None, None, "row"),
            P(None, "row", None),
            P(None, None, "col"),
            P(None, None, "col", None),
            P(None, None, None, "row"),
            P(None, "row", None),
            P(None, None, "col"),
            P(),
            P(),
        ),
        out_specs=(
            P(("tok", "row"), "col"),
            P(("tok", "row"), "col"),
            P(None, None, "col", None),
            P(None, None, None, "row"),
            P(None, "row", None),
            P(None, None, "col"),
            P(None, None, "col", None),
            P(None, None, None, "row"),
            P(None, "row", None),
            P(None, None, "col"),
        ),
        check_vma=False,
    )
```

profile of v0, /device:TPU:0, one launch (start us, length us, event | category | flops | bytes accessed | tf_op | source)
XLA Modules:
  0.0 5517.8 jit_solution(902086497108582859)
XLA Ops:
  11.3 58.4 %all-gather.9.cloned.1.call-done = bf16[4608,512]{1,0:T(8,128)(2,1)} async-done(((bf16[1152,512]{1,0:T(8,128)(2,1)}), bf16[4608,512]{1,0:T(8,128)(2,1)}) %all-gather.9.cloned.1.call-update) | async-done | bytes 4718608 | tf_op jit(solution)/shard_map/all_gather | solution.py:25
  77.4 15.4 fusion.39
  103.7 464.6 %reduce-scatter.17.cloned.1.call-done = f32[1152,1536]{0,1:T(8,128)} async-done(((f32[4608,1536]{0,1:T(8,128)}), f32[1152,1536]{0,1:T(8,128)}) %reduce-scatter.17.cloned.1.call-update) | async-done | bytes 7077904 | tf_op jit(solution)/shard_map/reduce_scatter | solution.py:30
  577.1 17.1 all-reduce.2
  627.3 85.0 %while.34 = (s32[]{:T(128)}, bf16[9,128,4,128]{3,1,2,0:T(8,128)(2,1)}, f32[9,4,128]{2,1,0:T(4,128)}, s32[9]{0:T(128)S(1)}, s32[]{:T(128)}, /*index=5*/bf16[1152,...) while((s32[]{:T(128)}, ...), condition=%wide.region_9.10_spmd.clone.clone, body=%wide.region_6.9_spmd.clone.clone.sunk | while | flops 307301632 | bytes 10147239 | solution.py:234
  717.5 89.4 %all-gather.11.cloned.1.call-done = bf16[4608,512]{1,0:T(8,128)(2,1)} async-done(((bf16[1152,512]{1,0:T(8,128)(2,1)}), bf16[4608,512]{1,0:T(8,128)(2,1)}) %all-gather.11.cloned.1.call-update) | async-done | bytes 4718608 | tf_op jit(solution)/shard_map/all_gather | solution.py:36
  833.7 98.3 %reduce-scatter.21.cloned.1.call-done = f32[1152,512]{0,1:T(8,128)} async-done(((f32[4608,512]{0,1:T(8,128)}), f32[1152,512]{0,1:T(8,128)}) %reduce-scatter.21.cloned.1.call-update) | async-done | bytes 2359312 | tf_op jit(solution)/shard_map/reduce_scatter | solution.py:41
  952.6 53.9 all-gather.13.cloned.1.call-done
  1019.3 32.1 fusion.37
  1051.5 73.1 %copy.109 = f32[4608,4096]{1,0:T(8,128)} copy(f32[4608,4096]{0,1:T(8,128)} %bitcast.40) | data formatting | bytes 150994944 | tf_op jit(solution)/shard_map/reshape | solution.py:109
  1129.0 1225.9 %reduce-scatter.25.cloned.1.call-done = f32[1152,4096]{1,0:T(8,128)} async-done(((f32[4608,4096]{1,0:T(8,128)}), f32[1152,4096]{1,0:T(8,128)}) %reduce-scatter.25.cloned.1.call-update) | async-done | bytes 18874384 | tf_op jit(solution)/shard_map/reduce_scatter | solution.py:30
  2378.6 322.4 %all-gather.15.cloned.1.call-done = bf16[4608,2048]{1,0:T(8,128)(2,1)} async-done(((bf16[1152,2048]{1,0:T(8,128)(2,1)}), bf16[4608,2048]{1,0:T(8,128)(2,1)}) %all-gather.15.cloned.1.call-update) | async-done | bytes 18874384 | tf_op jit(solution)/shard_map/all_gather | solution.py:36
  2710.9 16.2 fusion.238
  2733.3 98.0 %reduce-scatter.29.cloned.1.call-done = f32[1152,512]{0,1:T(8,128)} async-done(((f32[4608,512]{0,1:T(8,128)}), f32[1152,512]{0,1:T(8,128)}) %reduce-scatter.29.cloned.1.call-update) | async-done | bytes 2359312 | tf_op jit(solution)/shard_map/reduce_scatter | solution.py:41
  2836.0 19.3 all-reduce
  2861.4 52.9 all-gather.17.cloned.1.call-done
  2925.4 19.2 fusion.66
  2944.6 27.2 bitcast_add_fusion
  2971.9 619.3 %reduce-scatter.33.cloned.1.call-done = f32[1152,2048]{1,0:T(8,128)} async-done(((f32[4608,2048]{1,0:T(8,128)}), f32[1152,2048]{1,0:T(8,128)}) %reduce-scatter.33.cloned.1.call-update) | async-done | bytes 9437200 | tf_op jit(solution)/shard_map/reduce_scatter | solution.py:30
  3612.5 630.7 %all-gather.19.cloned.1.call-done = bf16[4608,4096]{1,0:T(8,128)(2,1)} async-done(((bf16[1152,4096]{1,0:T(8,128)(2,1)}), bf16[4608,4096]{1,0:T(8,128)(2,1)}) %all-gather.19.cloned.1.call-update) | async-done | bytes 37748752 | tf_op jit(solution)/shard_map/all_gather | solution.py:36
  4243.2 25.3 copy.370
  4268.5 26.0 fusion.228
  4344.3 31.3 fusion.35
  4375.7 93.7 %reduce-scatter.35.cloned.1.call-done = f32[1152,512]{0,1:T(8,128)} async-done(((f32[4608,512]{0,1:T(8,128)}), f32[1152,512]{0,1:T(8,128)}) %reduce-scatter.35.cloned.1.call-update) | async-done | bytes 2359312 | tf_op jit(solution)/shard_map/reduce_scatter | solution.py:41
  4492.3 53.3 all-gather.21.cloned.1.call-done
  4569.3 157.9 %reduce-scatter.37.cloned.1.call-done = f32[1152,512]{1,0:T(8,128)} async-done(((f32[4608,512]{1,0:T(8,128)}), f32[1152,512]{1,0:T(8,128)}) %reduce-scatter.37.cloned.1.call-update) | async-done | bytes 2359312 | tf_op jit(solution)/shard_map/reduce_scatter | solution.py:30
  4730.7 176.3 %while.35 = (s32[]{:T(128)}, f32[1152,4,128]{0,2,1:T(8,128)}, f32[1152,4,128]{0,2,1:T(8,128)}, f32[9,128,4,128]{3,1,0,2:T(8,128)}, s32[9]{0:T(128)S(1)}, /*index...) while((s32[]{:T(128)}, f32[1152,4,128]{0,2,1:T(8,128)}, ...), condition=%wide.region_29.30_spmd.clone.clone, body=%wide.region_27.29_spmd.clone.clone.sunk | while | flops 763890944 | bytes 37796904 | solution.py:277
  4930.9 16.3 all-reduce.1
  5002.3 201.0 %all-gather.23.cloned.1.call-done = bf16[4608,1536]{0,1:T(8,128)(2,1)} async-done(((bf16[1152,1536]{0,1:T(8,128)(2,1)}), bf16[4608,1536]{0,1:T(8,128)(2,1)}) %all-gather.23.cloned.1.call-update) | async-done | bytes 14155792 | tf_op jit(solution)/shard_map/all_gather | solution.py:36
  5313.6 21.3 fusion.34
  5350.4 55.6 %all-reduce.10.cloned.1.call-done = (bf16[3,8,512,16]{2,3,1,0:T(8,128)(2,1)}, bf16[8,16,512]{2,1,0:T(8,128)(2,1)}, bf16[2,8,512,16]{2,3,1,0:T(8,128)(2,1)}, bf16[8,16,512]{2,1,0:T(8,128)(2,1)}) async-done(((bf16[3,8,512,16]{2,3,1,0:T(8,128)(2,1)}, bf16[8,16,512]{2,1,0:T(8,128)(2,1)}, bf16[2,8,512,16]{2,3,1,0:T(8,128)(2,1)}, bf16[8,16,512]{2,1,0:T(8,128)(2,1)}), (bf16[3,8,512,16]{2,3,1,0:T(8,128)(2,1)}, ...) | async-done | bytes 917520 | tf_op jit(solution)/shard_map/psum | solution.py:505
  5412.1 91.4 %reduce-scatter.39.cloned.1.call-done = f32[1152,512]{0,1:T(8,128)} async-done(((f32[4608,512]{0,1:T(8,128)}), f32[1152,512]{0,1:T(8,128)}) %reduce-scatter.39.cloned.1.call-update) | async-done | bytes 2359312 | tf_op jit(solution)/shard_map/reduce_scatter | solution.py:41
  (760 shorter events, 760.9 us)
Async XLA Ops:
  7.2 2703.7 %copy-start = (bf16[2048,512]{1,0:T(8,128)(2,1)S(1)}, bf16[2048,512]{1,0:T(8,128)(2,1)}, u32[]{:S(2)}) copy-start(bf16[2048,512]{1,0:T(8,128)(2,1)} %param.27) | copy-start | bytes 6291460
  7.2 62.5 %all-gather.9.cloned.1.call-start = ((), (), s32[]{:S(2)}) async-start(), calls=%async_computation.16 | async-start | bytes 5898240 | tf_op jit(solution)/shard_map/all_gather | solution.py:25
  7.9 95.8 %reduce-scatter.19.cloned.1.call-start = ((), (), s32[]{:S(2)}) async-start(), calls=%async_computation.18 | async-start | bytes 1105920 | tf_op jit(solution)/shard_map/reduce_scatter | solution.py:31
  77.3 490.9 %reduce-scatter.17.cloned.1.call-start = ((), (), s32[]{:S(2)}) async-start(), calls=%async_computation.17 | async-start | bytes 35389440 | tf_op jit(solution)/shard_map/reduce_scatter | solution.py:30
  92.8 714.1 %all-gather.11.cloned.1.call-start = ((), (), s32[]{:S(2)}) async-start(), calls=%async_computation.19 | async-start | bytes 5898240 | tf_op jit(solution)/shard_map/all_gather | solution.py:36
  96.6 498.3 %copy-start.105 = (f32[1,512]{1,0:T(1,128)}, f32[1,512]{1,0:T(1,128)S(1)}, u32[]{:S(2)}) copy-start(f32[1,512]{1,0:T(1,128)S(1)} %get-tuple-element.576) | copy-start | bytes 6148
  96.6 507.6 %copy-start.103 = (f32[1,512]{1,0:T(1,128)}, f32[1,512]{1,0:T(1,128)S(1)}, u32[]{:S(2)}) copy-start(f32[1,512]{1,0:T(1,128)S(1)} %get-tuple-element.575) | copy-start | bytes 6148
  103.7 516.2 %copy-start.34 = (f32[1152,64]{1,0:T(8,128)}, f32[1152,64]{1,0:T(8,128)S(1)}, u32[]{:S(2)}) copy-start(f32[1152,64]{1,0:T(8,128)S(1)} %get-tuple-element.568) | copy-start | bytes 884740
  103.7 469.1 %copy-start.64 = (f32[1152,48]{0,1:T(8,128)S(1)}, f32[1152,48]{0,1:T(8,128)}, u32[]{:S(2)}) copy-start(f32[1152,48]{0,1:T(8,128)} %reduce-scatter.19.cloned.1.call-done) | copy-start | bytes 663556
  717.2 116.5 %reduce-scatter.23.cloned.1.call-start = ((), (), s32[]{:S(2)}) async-start(), calls=%async_computation.21 | async-start | bytes 368640 | tf_op jit(solution)/shard_map/reduce_scatter | solution.py:42
  811.4 120.6 %reduce-scatter.21.cloned.1.call-start = ((), (), s32[]{:S(2)}) async-start(), calls=%async_computation.20 | async-start | bytes 11796480 | tf_op jit(solution)/shard_map/reduce_scatter | solution.py:41
  819.0 187.5 %all-gather.13.cloned.1.call-start = ((), (), s32[]{:S(2)}) async-start(), calls=%async_computation.22 | async-start | bytes 5898240 | tf_op jit(solution)/shard_map/all_gather | solution.py:25
  952.1 177.0 %reduce-scatter.27.cloned.1.call-start = ((), (), s32[]{:S(2)}) async-start(), calls=%async_computation.24 | async-start | bytes 737280 | tf_op jit(solution)/shard_map/reduce_scatter | solution.py:31
  1019.3 1335.6 %reduce-scatter.25.cloned.1.call-start = ((), (), s32[]{:S(2)}) async-start(), calls=%async_computation.23 | async-start | bytes 94371840 | tf_op jit(solution)/shard_map/reduce_scatter | solution.py:30
  1124.6 1576.3 %all-gather.15.cloned.1.call-start = ((), (), s32[]{:S(2)}) async-start(), calls=%async_computation.25 | async-start | bytes 23592960 | tf_op jit(solution)/shard_map/all_gather | solution.py:36
  1129.0 1232.8 %copy-start.82 = (f32[1152,32]{0,1:T(8,128)S(1)}, f32[1152,32]{0,1:T(8,128)}, u32[]{:S(2)}) copy-start(f32[1152,32]{0,1:T(8,128)} %reduce-scatter.27.cloned.1.call-done) | copy-start | bytes 442372
  2377.1 356.2 %reduce-scatter.31.cloned.1.call-start = ((), (), s32[]{:S(2)}) async-start(), calls=%async_computation.27 | async-start | bytes 368640 | tf_op jit(solution)/shard_map/reduce_scatter | solution.py:42
  2710.6 120.7 %reduce-scatter.29.cloned.1.call-start = ((), (), s32[]{:S(2)}) async-start(), calls=%async_computation.26 | async-start | bytes 11796480 | tf_op jit(solution)/shard_map/reduce_scatter | solution.py:41
  2727.1 187.2 %all-gather.17.cloned.1.call-start = ((), (), s32[]{:S(2)}) async-start(), calls=%async_computation.28 | async-start | bytes 5898240 | tf_op jit(solution)/shard_map/all_gather | solution.py:25
  2859.8 731.3 %reduce-scatter.33.cloned.1.call-start = ((), (), s32[]{:S(2)}) async-start(), calls=%async_computation.29 | async-start | bytes 47185920 | tf_op jit(solution)/shard_map/reduce_scatter | solution.py:30
  2971.8 1271.4 %all-gather.19.cloned.1.call-start = ((), (), s32[]{:S(2)}) async-start(), calls=%async_computation.30 | async-start | bytes 47185920 | tf_op jit(solution)/shard_map/all_gather | solution.py:36
  3610.5 858.8 %reduce-scatter.35.cloned.1.call-start = ((), (), s32[]{:S(2)}) async-start(), calls=%async_computation.31 | async-start | bytes 11796480 | tf_op jit(solution)/shard_map/reduce_scatter | solution.py:41
  4375.6 169.9 %all-gather.21.cloned.1.call-start = ((), (), s32[]{:S(2)}) async-start(), calls=%async_computation.32 | async-start | bytes 5898240 | tf_op jit(solution)/shard_map/all_gather | solution.py:25
  4491.1 236.1 %reduce-scatter.37.cloned.1.call-start = ((), (), s32[]{:S(2)}) async-start(), calls=%async_computation.33 | async-start | bytes 11796480 | tf_op jit(solution)/shard_map/reduce_scatter | solution.py:30
  4565.7 411.3 %reduce-scatter.47.cloned.1.call-start = ((), (), s32[]{:S(2)}) async-start(), calls=%async_computation.39 | async-start | bytes 368640 | tf_op jit(solution)/shard_map/reduce_scatter | solution.py:31
  4567.4 424.9 %reduce-scatter.45.cloned.1.call-start = ((), (), s32[]{:S(2)}) async-start(), calls=%async_computation.38 | async-start | bytes 737280 | tf_op jit(solution)/shard_map/reduce_scatter | solution.py:42
  4568.4 431.8 %reduce-scatter.43.cloned.1.call-start = ((), (), s32[]{:S(2)}) async-start(), calls=%async_computation.37 | async-start | bytes 368640 | tf_op jit(solution)/shard_map/reduce_scatter | solution.py:31
  4569.3 634.0 %all-gather.23.cloned.1.call-start = ((), (), s32[]{:S(2)}) async-start(), calls=%async_computation.34 | async-start | bytes 17694720 | tf_op jit(solution)/shard_map/all_gather | solution.py:36
  4960.1 347.8 %reduce-scatter.41.cloned.1.call-start = ((), (), s32[]{:S(2)}) async-start(), calls=%async_computation.36 | async-start | bytes 1105920 | tf_op jit(solution)/shard_map/reduce_scatter | solution.py:42
  5250.4 94.3 %all-reduce.8.cloned.1.call-start = ((), (), s32[]{:S(2)}) async-start(), calls=%async_computation.40 | async-start | bytes 4194304 | tf_op jit(solution)/shard_map/psum | solution.py:511
  5260.1 145.8 %all-reduce.10.cloned.1.call-start = ((), (), s32[]{:S(2)}) async-start(), calls=%async_computation.41 | async-start | bytes 1835008 | tf_op jit(solution)/shard_map/psum | solution.py:505
  5313.6 190.0 %reduce-scatter.39.cloned.1.call-start = ((), (), s32[]{:S(2)}) async-start(), calls=%async_computation.35 | async-start | bytes 11796480 | tf_op jit(solution)/shard_map/reduce_scatter | solution.py:41
  (152 other events, 2262.1 us)
Sparse Core Ops, SparseCore 0:
  9.9 59.8 all-gather.8
  77.5 24.5 reduce-scatter.18
  104.5 463.7 reduce-scatter.16
  717.3 89.5 all-gather.10
  811.5 22.1 reduce-scatter.22
  836.9 94.9 reduce-scatter.20
  952.2 54.2 all-gather.12
  1019.4 21.9 reduce-scatter.26
  1124.8 1230.0 reduce-scatter.24
  2377.2 323.6 all-gather.14
  2710.7 22.5 reduce-scatter.30
  2736.2 94.9 reduce-scatter.28
  2860.0 54.3 all-gather.16
  2971.9 619.1 reduce-scatter.32
  3610.6 632.5 all-gather.18
  4375.7 93.5 reduce-scatter.34
  4491.2 54.2 all-gather.20
  4565.8 161.2 reduce-scatter.36
  4730.1 20.6 reduce-scatter.46
  4754.4 23.3 reduce-scatter.44
  4780.1 19.8 reduce-scatter.42
  4960.3 242.9 all-gather.22
  5250.5 25.1 reduce-scatter.40
  5279.5 65.1 all-reduce.7
  5349.8 56.1 all-reduce.9
  5409.2 94.2 reduce-scatter.38
where the time goes:
time: 5530 us; the launch traced here: 5520 us
  waiting for transfers between devices  4390 us (79%)
  matrix products  515 us (9%)
  local copies, waits for them, and re-layouts  316 us (6%)
  other arithmetic  170 us (3%)
  blocking collectives  77.1 us (1%)
    reduce_scatter x4, waiting for transfers between devices, cols_scatter(): lax.psum_scatter(values[0], 'col', scatter_dimension=0, tiled=True)  2470 us
    all_gather x4, waiting for transfers between devices, cols_gather(): return lax.all_gather(values, 'col', axis=0, tiled=True)  1240 us
    reduce_scatter x4, waiting for transfers between devices, rows_scatter(): lax.psum_scatter(values[0], 'row', scatter_dimension=0, tiled=True)  381 us
    all_gather x4, waiting for transfers between devices, rows_gather(): return lax.all_gather(values, 'row', axis=0, tiled=True)  218 us
  transfers between devices with their start and end apart: 26, of which 20 were waited for; matrix products, arithmetic and copies ran while one was open for 9% of the time, Pallas kernels for 0%

commit v1 on v0

v1 whole, which is shorter than its diff:
```python
import math

import jax
import jax.numpy as jnp
from jax import lax
from jax.sharding import PartitionSpec as P

D = 2048
HEAD_DIM = 128
RANK = 16
ADAPTERS = 8
PROMPT = 1024
CONT_LEN = 128
SLAB = 1152

adapter_scale = 2.0
norm_eps = 1e-06
rope_base = 500000.0
very_low = -1e30
bf16 = jnp.bfloat16
f32 = jnp.float32


def dot(left, right):
    return jnp.dot(left, right, preferred_element_type=f32)


def dot_nt(left, right):
    return lax.dot_general(left, right, (((1,), (1,)), ((), ())), preferred_element_type=f32)


def dot_tn(left, right):
    return lax.dot_general(left, right, (((0,), (0,)), ((), ())), preferred_element_type=f32)


def gather_weight(local):
    half = local.shape[0] // lax.axis_size("tok")
    part = lax.dynamic_slice_in_dim(local, lax.axis_index("tok") * half, half, 0)
    return lax.all_gather(part, ("col", "tok"), axis=0, tiled=True)


def to_tokens(values):
    rows, cols = lax.axis_size("row"), lax.axis_size("col")
    width = values.shape[1]
    mixed = lax.all_to_all(values, "row", 0, 0, tiled=True)
    mixed = lax.all_to_all(mixed, "col", 0, 0, tiled=True)
    return mixed.reshape(cols, SLAB // rows, width).transpose(1, 0, 2).reshape(SLAB // rows, -1)


def from_tokens(values):
    rows, cols = lax.axis_size("row"), lax.axis_size("col")
    count = values.shape[0]
    mixed = values.reshape(count, cols, -1).transpose(1, 0, 2).reshape(cols * count, -1)
    mixed = lax.all_to_all(mixed, "col", 0, 0, tiled=True)
    return lax.all_to_all(mixed, "row", 0, 0, tiled=True)


def reorder(values, outer, inner):
    if outer == 1 or inner == 1:
        return values
    rest = values.shape[0] // (outer * inner)
    shape = (outer, inner, rest) + values.shape[1:]
    return values.reshape(shape).swapaxes(0, 1).reshape(values.shape)


def gather_tokens(values):
    rows, per_slab = lax.axis_size("row"), lax.axis_size("row") // lax.axis_size("col")
    return reorder(lax.all_gather(values, "row", axis=0, tiled=True), rows, per_slab)


def scatter_tokens(values):
    rows, per_slab = lax.axis_size("row"), lax.axis_size("row") // lax.axis_size("col")
    values = reorder(values.astype(bf16), per_slab, rows)
    return lax.psum_scatter(values, "row", scatter_dimension=0, tiled=True).astype(f32)


def token_places(length):
    slot_ids = jnp.arange(SLAB, dtype=jnp.int32)
    return jnp.where(slot_ids < PROMPT, slot_ids, length + (slot_ids - PROMPT) % CONT_LEN)


def rotation(places, head_size):
    half_dim = head_size // 2
    frequency = jnp.exp(
        -(2.0 * jnp.arange(half_dim, dtype=f32) / head_size) * math.log(rope_base)
    )
    angles = places.astype(f32)[:, None] * frequency[None, :]
    return (jnp.cos(angles)[:, None, :], jnp.sin(angles)[:, None, :])


def rotate(values, cosine, sine, direction):
    half_dim = values.shape[-1] // 2
    front_half = values[..., :half_dim]
    back_half = values[..., half_dim:]
    return jnp.concatenate(
        [
            front_half * cosine - direction * back_half * sine,
            back_half * cosine + direction * front_half * sine,
        ],
        axis=-1,
    )


def key_mask(query_ids, key_ids, length):
    cont_start = jnp.where(
        query_ids >= PROMPT, PROMPT + (query_ids - PROMPT) // CONT_LEN * CONT_LEN, SLAB
    )
    causal = key_ids[None, :] <= query_ids[:, None]
    return causal & ((key_ids[None, :] < length) | (key_ids[None, :] >= cont_start[:, None]))


def norm_forward(values, gain):
    inverse = lax.rsqrt(jnp.mean(values * values, axis=1, keepdims=True) + norm_eps)
    return (values * inverse * gain.astype(f32), inverse)


def norm_backward(values, inverse, gain, grad_out):
    weighted = grad_out * gain.astype(f32)
    inner = jnp.mean(values * weighted, axis=1, keepdims=True)
    return inverse * weighted - values * (inverse**3 * inner)


def attend_forward(queries, keys_low, values_low, length, block_len):
    slab_len = queries.shape[0]
    score_scale = 1.0 / math.sqrt(queries.shape[2])
    key_ids = jnp.arange(slab_len, dtype=jnp.int32)

    def one_block(block_start):
        q_block = lax.dynamic_slice_in_dim(queries, block_start, block_len, 0)
        query_ids = block_start + jnp.arange(block_len, dtype=jnp.int32)
        scores = (
            jnp.einsum("qhd,khd->hqk", q_block, keys_low, preferred_element_type=f32)
            * score_scale
        )
        scores = jnp.where(key_mask(query_ids, key_ids, length)[None], scores, very_low)
        row_top = jnp.max(scores, axis=2, keepdims=True)
        shifted = jnp.exp(scores - row_top)
        row_sum = jnp.sum(shifted, axis=2, keepdims=True)
        attn_probs = (shifted / row_sum).astype(bf16)
        attended = jnp.einsum("hqk,khd->qhd", attn_probs, values_low, preferred_element_type=f32)
        return (attended, (row_top + jnp.log(row_sum))[:, :, 0])

    block_starts = jnp.arange(slab_len // block_len, dtype=jnp.int32) * block_len
    attended, log_sums = lax.map(one_block, block_starts)
    return (attended.reshape(queries.shape), log_sums)


def attend_backward(queries, keys_low, values_low, grad_out, log_sums, length, block_len):
    slab_len = queries.shape[0]
    score_scale = 1.0 / math.sqrt(queries.shape[2])
    key_ids = jnp.arange(slab_len, dtype=jnp.int32)

    def one_block(carry, input_rows):
        grad_keys, grad_values = carry
        block_start, block_sums = input_rows
        q_block = lax.dynamic_slice_in_dim(queries, block_start, block_len, 0)
        g_block = lax.dynamic_slice_in_dim(grad_out, block_start, block_len, 0)
        query_ids = block_start + jnp.arange(block_len, dtype=jnp.int32)
        scores = (
            jnp.einsum("qhd,khd->hqk", q_block, keys_low, preferred_element_type=f32)
            * score_scale
        )
        scores = jnp.where(key_mask(query_ids, key_ids, length)[None], scores, very_low)
        attn_probs = jnp.exp(scores - block_sums[:, :, None])
        probs_low = attn_probs.astype(bf16)
        grad_values = grad_values + jnp.einsum(
            "hqk,qhd->khd", probs_low, g_block, preferred_element_type=f32
        )
        grad_probs = jnp.einsum("qhd,khd->hqk", g_block, values_low, preferred_element_type=f32)
        row_inner = jnp.sum(attn_probs * grad_probs, axis=2, keepdims=True)
        grad_scores = (attn_probs * (grad_probs - row_inner)).astype(bf16)
        grad_query = (
            jnp.einsum("hqk,khd->qhd", grad_scores, keys_low, preferred_element_type=f32)
            * score_scale
        )
        grad_keys = (
            grad_keys
            + jnp.einsum("hqk,qhd->khd", grad_scores, q_block, preferred_element_type=f32)
            * score_scale
        )
        return ((grad_keys, grad_values), grad_query)

    block_starts = jnp.arange(slab_len // block_len, dtype=jnp.int32) * block_len
    zeros_init = jnp.zeros(queries.shape, f32)
    (grad_keys, grad_values), grad_queries = lax.scan(
        one_block, (zeros_init, zeros_init), (block_starts, log_sums)
    )
    return (grad_queries.reshape(queries.shape), grad_keys, grad_values)


def pick(adapters, ids):
    onehot = (ids[:, None] == jnp.arange(adapters.shape[0], dtype=jnp.int32)).astype(adapters.dtype)
    return jnp.tensordot(onehot, adapters, axes=1)


def place(ids, gradients):
    onehot = (jnp.arange(ADAPTERS, dtype=jnp.int32)[:, None] == ids[None, :]).astype(f32)
    total = 0.0
    for index in range(gradients.shape[0]):
        weight = onehot[:, index].reshape((ADAPTERS,) + (1,) * (gradients.ndim - 1))
        total = total + weight * gradients[index][None].astype(f32)
    return total


def block_diagonal(factors):
    count = len(factors)
    lines = []
    for index, factor in enumerate(factors):
        blank = jnp.zeros_like(factor)
        lines.append(
            jnp.concatenate([factor if k == index else blank for k in range(count)], axis=1)
        )
    return jnp.concatenate(lines, axis=0)


def on_device(
    layer_in,
    cotangent,
    qkv_weight,
    out_weight,
    ffn_weight,
    down_weight,
    qk_gain,
    post_gain,
    qkv_lower,
    qkv_raise,
    out_lower,
    out_raise,
    ffn_lower,
    ffn_raise,
    down_lower,
    down_raise,
    adapter_ids,
    prompt_len,
):
    col_count = lax.axis_size("col")
    group_base = lax.axis_index("tok") * col_count
    group = group_base + lax.axis_index("col")
    slab_ids = lax.dynamic_slice_in_dim(adapter_ids, group_base, col_count, 0)
    own_ids = lax.dynamic_index_in_dim(adapter_ids, group, 0, keepdims=False)
    length = lax.dynamic_index_in_dim(prompt_len, group, 0, keepdims=False)
    block_len = math.gcd(SLAB, 512)
    width = layer_in.shape[1]
    head_width = qkv_weight.shape[2]
    ff_width = ffn_weight.shape[2]

    x_own = to_tokens(layer_in)
    qkv_full = gather_weight(qkv_weight.transpose(1, 0, 2).reshape(width, -1))
    out_full = gather_weight(out_weight.T)
    ffn_full = gather_weight(ffn_weight.transpose(1, 0, 2).reshape(width, -1))
    down_full = gather_weight(down_weight.T)

    pieces = jnp.stack(
        [pick(qkv_lower[p].swapaxes(1, 2), slab_ids[:, p]) for p in range(3)]
        + [pick(out_raise, slab_ids[:, 3])]
        + [pick(ffn_lower[p].swapaxes(1, 2), slab_ids[:, 4 + p]) for p in range(2)]
        + [pick(down_raise, slab_ids[:, 6])],
        axis=1,
    )
    factors = lax.all_to_all(pieces, "col", 0, 0, tiled=True)
    factors = factors.transpose(1, 2, 0, 3).reshape(7, RANK, D)
    qkv_a, out_b, ffn_a, down_b = (
        factors[0:3].reshape(3 * RANK, D),
        factors[3],
        factors[4:6].reshape(2 * RANK, D),
        factors[6],
    )
    qkv_b = block_diagonal([pick(qkv_raise[p], own_ids[p : p + 1])[0] for p in range(3)])
    out_a = pick(out_lower, own_ids[3:4])[0]
    ffn_b = block_diagonal([pick(ffn_raise[p], own_ids[4 + p : 5 + p])[0] for p in range(2)])
    down_a = pick(down_lower, own_ids[6:7])[0]

    gains = post_gain.astype(bf16)
    gains = lax.all_gather(gains, "col", axis=1, tiled=True)

    x_all = gather_tokens(x_own)
    qkv_low = (adapter_scale * dot_nt(x_all, qkv_a)).astype(bf16)
    qkv_lin = dot(x_all, qkv_full) + dot(qkv_low, qkv_b)
    q_lin = qkv_lin[:, :head_width]
    k_lin = qkv_lin[:, head_width : 2 * head_width]
    v_lin = qkv_lin[:, 2 * head_width :]
    sums = lax.psum(
        jnp.stack([jnp.sum(q_lin * q_lin, axis=1), jnp.sum(k_lin * k_lin, axis=1)]), "row"
    )
    inverses = lax.rsqrt(sums / D + norm_eps)
    q_inverse, k_inverse = inverses[0], inverses[1]
    head_gain = qk_gain.astype(f32)
    local_heads = head_width // HEAD_DIM
    cosine, sine = rotation(token_places(length), HEAD_DIM)
    heads = (SLAB, local_heads, HEAD_DIM)
    q_low = rotate(
        (q_lin * q_inverse[:, None] * head_gain[0]).reshape(heads), cosine, sine, 1.0
    ).astype(bf16)
    k_low = rotate(
        (k_lin * k_inverse[:, None] * head_gain[1]).reshape(heads), cosine, sine, 1.0
    ).astype(bf16)
    v_low = v_lin.reshape(heads).astype(bf16)
    attended, log_sums = attend_forward(q_low, k_low, v_low, length, block_len)
    attn_low = attended.reshape(SLAB, -1).astype(bf16)

    out_low = (adapter_scale * dot(attn_low, out_a)).astype(bf16)
    attn_lin = scatter_tokens(dot_nt(attn_low, out_full) + dot(out_low, out_b))
    attn_norm, attn_inverse = norm_forward(attn_lin, gains[0])
    hidden = x_own.astype(f32) + attn_norm
    h_all = gather_tokens(hidden.astype(bf16))

    ffn_low = (adapter_scale * dot_nt(h_all, ffn_a)).astype(bf16)
    ffn_lin = dot(h_all, ffn_full) + dot(ffn_low, ffn_b)
    gate_lin = ffn_lin[:, :ff_width]
    up_lin = ffn_lin[:, ff_width:]
    gate_sig = jax.nn.sigmoid(gate_lin)
    gate_act = gate_lin * gate_sig
    act_low = (gate_act * up_lin).astype(bf16)
    down_low = (adapter_scale * dot(act_low, down_a)).astype(bf16)
    mlp_lin = scatter_tokens(dot_nt(act_low, down_full) + dot(down_low, down_b))
    mlp_norm, mlp_inverse = norm_forward(mlp_lin, gains[1])
    layer_out = from_tokens((hidden + mlp_norm).astype(bf16)).astype(f32)

    grad_out = to_tokens(cotangent).astype(f32)
    dm_all = gather_tokens(norm_backward(mlp_lin, mlp_inverse, gains[1], grad_out).astype(bf16))
    down_raise_part = dot_tn(down_low, dm_all)
    down_dlow = (adapter_scale * dot_nt(dm_all, down_b)).astype(bf16)
    grad_act = dot(dm_all, down_full) + dot_nt(down_dlow, down_a)
    down_lower_part = dot_tn(act_low, down_dlow)
    grad_gate = (grad_act * up_lin * gate_sig * (1.0 + gate_lin * (1.0 - gate_sig))).astype(bf16)
    grad_up = (grad_act * gate_act).astype(bf16)
    grad_ffn = jnp.concatenate([grad_gate, grad_up], axis=1)
    ffn_dlow = (adapter_scale * dot_nt(grad_ffn, ffn_b)).astype(bf16)
    ffn_raise_part = dot_tn(ffn_low, grad_ffn)
    ffn_lower_part = dot_tn(ffn_dlow, h_all)
    grad_hidden = grad_out + scatter_tokens(dot_nt(grad_ffn, ffn_full) + dot(ffn_dlow, ffn_a))

    da_all = gather_tokens(
        norm_backward(attn_lin, attn_inverse, gains[0], grad_hidden).astype(bf16)
    )
    out_raise_part = dot_tn(out_low, da_all)
    out_dlow = (adapter_scale * dot_nt(da_all, out_b)).astype(bf16)
    grad_heads = (dot(da_all, out_full) + dot_nt(out_dlow, out_a)).astype(bf16)
    out_lower_part = dot_tn(attn_low, out_dlow)
    grad_q_rot, grad_k_rot, grad_v_all = attend_backward(
        q_low, k_low, v_low, grad_heads.reshape(heads), log_sums, length, block_len
    )
    weighted_q = rotate(grad_q_rot, cosine, sine, -1.0).reshape(SLAB, -1) * head_gain[0]
    weighted_k = rotate(grad_k_rot, cosine, sine, -1.0).reshape(SLAB, -1) * head_gain[1]
    inner = lax.psum(
        jnp.stack([jnp.sum(q_lin * weighted_q, axis=1), jnp.sum(k_lin * weighted_k, axis=1)]),
        "row",
    )
    factor = inverses**3 * inner / D
    grad_qkv = jnp.concatenate(
        [
            (q_inverse[:, None] * weighted_q - q_lin * factor[0][:, None]).astype(bf16),
            (k_inverse[:, None] * weighted_k - k_lin * factor[1][:, None]).astype(bf16),
            grad_v_all.reshape(SLAB, -1).astype(bf16),
        ],
        axis=1,
    )
    qkv_dlow = (adapter_scale * dot_nt(grad_qkv, qkv_b)).astype(bf16)
    qkv_raise_part = dot_tn(qkv_low, grad_qkv)
    qkv_lower_part = dot_tn(qkv_dlow, x_all)
    grad_x = grad_hidden + scatter_tokens(dot_nt(grad_qkv, qkv_full) + dot(qkv_dlow, qkv_a))
    grad_in = from_tokens(grad_x.astype(bf16)).astype(f32)

    parts = jnp.concatenate(
        [
            qkv_lower_part.reshape(3, RANK, D),
            out_raise_part[None],
            ffn_lower_part.reshape(2, RANK, D),
            down_raise_part[None],
        ]
    )
    parts = parts.astype(bf16).reshape(7, RANK, col_count, width).transpose(2, 0, 1, 3)
    parts = lax.all_to_all(parts, "col", 0, 0, tiled=True)
    placed = [place(slab_ids[:, p], parts[:, p]) for p in range(7)]
    col_split = lax.psum(jnp.stack(placed).astype(bf16), ("tok", "row")).astype(f32)
    own = jnp.concatenate(
        [
            qkv_raise_part[p * RANK : (p + 1) * RANK, p * head_width : (p + 1) * head_width]
            for p in range(3)
        ]
        + [out_lower_part.T]
        + [
            ffn_raise_part[p * RANK : (p + 1) * RANK, p * ff_width : (p + 1) * ff_width]
            for p in range(2)
        ]
        + [down_lower_part.T],
        axis=1,
    ).astype(bf16)
    every = lax.all_gather(own, ("tok", "col"), axis=0)
    starts = [0, 1, 2, 3, 4]
    starts = [s * head_width for s in starts] + [
        4 * head_width + (k + 1) * ff_width for k in range(3)
    ]
    row_split = [
        place(adapter_ids[:, p], every[:, :, starts[p] : starts[p + 1]]) for p in range(7)
    ]
    return (
        layer_out,
        grad_in,
        col_split[0:3].swapaxes(2, 3),
        jnp.stack(row_split[0:3]),
        row_split[3].swapaxes(1, 2),
        col_split[3],
        col_split[4:6].swapaxes(2, 3),
        jnp.stack(row_split[4:6]),
        row_split[6].swapaxes(1, 2),
        col_split[6],
    )


def solution(mesh):
    return jax.shard_map(
        on_device,
        mesh=mesh,
        in_specs=(
            P(("tok", "row"), "col"),
            P(("tok", "row"), "col"),
            P(None, "col", "row"),
            P("row", "col"),
            P(None, "col", "row"),
            P("row", "col"),
            P(None, "row"),
            P(None, "col"),
            P(None, None, "col", None),
            P(None, None, None, "row"),
            P(None, "row", None),
            P(None, None, "col"),
            P(None, None, "col", None),
            P(None, None, None, "row"),
            P(None, "row", None),
            P(None, None, "col"),
            P(),
            P(),
        ),
        out_specs=(
            P(("tok", "row"), "col"),
            P(("tok", "row"), "col"),
            P(None, None, "col", None),
            P(None, None, None, "row"),
            P(None, "row", None),
            P(None, None, "col"),
            P(None, None, "col", None),
            P(None, None, None, "row"),
            P(None, "row", None),
            P(None, None, "col"),
        ),
        check_vma=False,
    )
```

time: 5530 us -> 1510 us (0.27)
  waiting for transfers between devices: 4390 us -> 641 us
  local copies, waits for them, and re-layouts: 316 us -> 115 us
  matrix products: 515 us -> 367 us
  blocking collectives: 77.1 us -> 147 us
    reduce_scatter x16 -> x4, waiting for transfers between devices: 2860 us -> 151 us  [scatter_tokens(): lax.psum_scatter(values, 'row', scatter_dimension=0, tiled=True).astype(f32)]
    all_gather x8 -> x9, waiting for transfers between devices: 1460 us -> 411 us  [the longest x4 237 us: gather_weight(): return lax.all_gather(part, ('col', 'tok'), axis=0, tiled=True)]
    reshape x25 -> x3, local copies, waits for them, and re-layouts: 173 us -> 3.39 us  [the longest x2 2.23 us: from_tokens(): values.reshape(count, cols, -1).transpose(1, 0, 2).reshape(cols * count, -1)]
    dot_general x116 -> x91, matrix products: 481 us -> 332 us  [the longest x12 96.5 us: dot(): return jnp.dot(left, right, preferred_element_type=f32)]
    all_to_all x0 -> x4, blocking collectives: none -> 115 us  [the longest x2 62.5 us: to_tokens(): mixed = lax.all_to_all(mixed, 'col', 0, 0, tiled=True)]
    all_to_all x0 -> x6, waiting for transfers between devices: none -> 78.9 us  [the longest x2 47 us: from_tokens(): mixed = lax.all_to_all(mixed, 'col', 0, 0, tiled=True)]
    psum x2 -> x1, waiting for transfers between devices: 61.8 us -> 0.01 us  [on_device(): lax.psum(jnp.stack(placed).astype(bf16), ('tok', 'row')).astype(f32)]
    psum x5 -> x2, blocking collectives: 77.1 us -> 19.9 us  [the longest x1 10.4 us: on_device(): lax.psum(jnp.stack([jnp.sum(q_lin * q_lin, axis=1), jnp.sum(k_lin * k_lin...]
  transfers between devices with their start and end apart: 26 -> 20, of which waited for: 20 -> 17; matrix products, arithmetic and copies ran while one was open for 9% -> 20% of each run, Pallas kernels for 0% -> 0%
where the time goes in v1:
time: 1510 us; the launch traced here: 1490 us
  waiting for transfers between devices  641 us (42%)
  matrix products  367 us (24%)
  blocking collectives  147 us (10%)
  other arithmetic  145 us (10%)
  local copies, waits for them, and re-layouts  115 us (8%)
  loops' own time  35.5 us (2%)
  starting transfers between devices  25.5 us (2%)
  between operations  17.4 us (1%)
    all_gather x4, waiting for transfers between devices, gather_weight(): return lax.all_gather(part, ('col', 'tok'), axis=0, tiled=True)  237 us
    all_gather x4, waiting for transfers between devices, gather_tokens(): lax.all_gather(values, 'row', axis=0, tiled=True)  161 us
    reduce_scatter x4, waiting for transfers between devices, scatter_tokens(): lax.psum_scatter(values, 'row', scatter_dimension=0, tiled=True).astype(f32)  151 us
    dot_general x12, matrix products, dot(): return jnp.dot(left, right, preferred_element_type=f32)  96.5 us
    dot_general x12, matrix products, dot_nt(): lax.dot_general(left, right, (((1,), (1,)), ((), ())), preferred_element_...  85.2 us
    all_to_all x2, blocking collectives, to_tokens(): mixed = lax.all_to_all(mixed, 'col', 0, 0, tiled=True)  62.5 us
    all_to_all x2, blocking collectives, to_tokens(): mixed = lax.all_to_all(values, 'row', 0, 0, tiled=True)  52.7 us
    all_to_all x2, waiting for transfers between devices, from_tokens(): mixed = lax.all_to_all(mixed, 'col', 0, 0, tiled=True)  47 us
  transfers between devices with their start and end apart: 20, of which 17 were waited for; matrix products, arithmetic and copies ran while one was open for 20% of the time, Pallas kernels for 0%

profile of v1, /device:TPU:0, one launch (start us, length us, event | category | flops | bytes accessed | tf_op | source)
XLA Modules:
  0.0 1493.6 jit_solution(16801253681901686207)
XLA Ops:
  7.2 20.8 %all_to_all.64 = bf16[4,288,512]{2,1,0:T(8,128)(2,1)S(1)} all-to-all(bf16[4,288,512]{2,1,0:T(8,128)(2,1)} %bitcast.1036), channel_id=1, replica_groups=mesh['tok'=2,'row'=4,'col'=4] {'row'}, dimensions={0} | all-to-all | bytes 2359296 | tf_op jit(solution)/shard_map/all_to_all | solution.py:45
  28.1 31.8 %all_to_all.65 = bf16[4,288,512]{2,1,0:T(8,128)(2,1)S(1)} all-to-all(bf16[4,288,512]{2,1,0:T(8,128)(2,1)S(1)} %all_to_all.64), channel_id=1, replica_groups=mesh['tok'=2,'row'=4,'col'=4] {'col'}, dimensions={0} | all-to-all | bytes 2359296 | tf_op jit(solution)/shard_map/all_to_all | solution.py:46
  88.2 28.0 %all-gather.12.cloned.1.call-done = bf16[1152,2048]{1,0:T(8,128)(2,1)} async-done(((bf16[288,2048]{1,0:T(8,128)(2,1)}), bf16[1152,2048]{1,0:T(8,128)(2,1)}) %all-gather.12.cloned.1.call-update) | async-done | bytes 4718608 | tf_op jit(solution)/shard_map/all_gather | solution.py:68
  120.7 62.9 %all-gather.10.cloned.1.call-done = bf16[2048,1536]{0,1:T(8,128)(2,1)} async-done(((bf16[256,1536]{0,1:T(8,128)(2,1)}), bf16[2048,1536]{0,1:T(8,128)(2,1)}) %all-gather.10.cloned.1.call-update) | async-done | bytes 6291472 | tf_op jit(solution)/shard_map/all_gather | solution.py:39
  183.6 11.9 convolution_bitcast_fusion.1
  205.2 10.4 psum.21
  246.1 91.3 %while.34 = (s32[]{:T(128)}, bf16[9,128,4,128]{3,1,2,0:T(8,128)(2,1)}, f32[9,4,128]{2,1,0:T(4,128)}, s32[9]{0:T(128)}, s32[]{:T(128)}, /*index=5*/bf16[1152,4,12...) while((s32[]{:T(128)}, ...), condition=%wide.region_6.7_spmd.clone.clone, body=%wide.region_3.6_spmd.clone.clone.sunk | while | flops 307301632 | bytes 10147239 | solution.py:144
  350.4 11.9 all_gather.34
  362.3 41.1 %reduce-scatter.5.cloned.1.call-done = bf16[288,2048]{1,0:T(8,128)(2,1)} async-done(((bf16[1152,2048]{1,0:T(8,128)(2,1)}), bf16[288,2048]{1,0:T(8,128)(2,1)}) %reduce-scatter.5.cloned.1.call-update) | async-done | bytes 1179664 | tf_op jit(solution)/shard_map/reduce_scatter | solution.py:74
  424.9 40.3 %all-gather.16.cloned.1.call-done = bf16[1152,2048]{1,0:T(8,128)(2,1)} async-done(((bf16[288,2048]{1,0:T(8,128)(2,1)}), bf16[1152,2048]{1,0:T(8,128)(2,1)}) %all-gather.16.cloned.1.call-update) | async-done | bytes 4718608 | tf_op jit(solution)/shard_map/all_gather | solution.py:68
  469.7 16.6 %fusion.124 = f32[1152,4096]{1,0:T(8,128)} fusion(bf16[1152,32]{0,1:T(8,128)(2,1)S(1)} %fusion.57, bf16[16,2048]{1,0:T(8,128)(2,1)S(1)} %get-tuple-element.780, bf16[16,2048]{1,0:T(8,128)(2,1)S(1)} %get-tuple-element.781), kind=kOutput, calls=%fused_computation.266 | convolution fusion | flops 303038464 | bytes 19079168 | tf_op jit(solution)/shard_map/dot_general | solution.py:25
  486.3 132.8 %all-gather.18.cloned.1.call-done = bf16[2048,4096]{0,1:T(8,128)(2,1)} async-done(((bf16[256,4096]{0,1:T(8,128)(2,1)}), bf16[2048,4096]{0,1:T(8,128)(2,1)}) %all-gather.18.cloned.1.call-update) | async-done | bytes 16777232 | tf_op jit(solution)/shard_map/all_gather | solution.py:39
  619.1 27.9 %convolution_add_fusion = f32[1152,4096]{1,0:T(8,128)} fusion(f32[1152,4096]{1,0:T(8,128)} %fusion.124, bf16[1152,2048]{1,0:T(8,128)(2,1)} %all-gather.16.cloned.1.call-done, bf16[2048,4096]{0,1:T(8,128)(2,1)} %all-gather.18.cloned.1.call-done), kind=kOutput, calls=%fused_computation.60 | convolution fusion | flops 19332071424 | bytes 59244544 | tf_op jit(solution)/shard_map/dot_general | solution.py:25
  647.0 10.1 multiply_convert_fusion.3
  660.8 41.1 %all-gather.20.cloned.1.call-done = bf16[2048,2048]{0,1:T(8,128)(2,1)} async-done(((bf16[256,2048]{0,1:T(8,128)(2,1)}), bf16[2048,2048]{0,1:T(8,128)(2,1)}) %all-gather.20.cloned.1.call-update) | async-done | bytes 8388624 | tf_op jit(solution)/shard_map/all_gather | solution.py:39
  701.9 13.8 fusion.289
  720.6 31.9 %all_to_all.66 = bf16[4,288,512]{2,1,0:T(8,128)(2,1)S(1)} all-to-all(bf16[4,288,512]{2,1,0:T(8,128)(2,1)S(1)} %bitcast.1037), channel_id=1, replica_groups=mesh['tok'=2,'row'=4,'col'=4] {'row'}, dimensions={0} | all-to-all | bytes 2359296 | tf_op jit(solution)/shard_map/all_to_all | solution.py:45
  752.5 30.7 %all_to_all.67 = bf16[4,288,512]{2,1,0:T(8,128)(2,1)S(1)} all-to-all(bf16[4,288,512]{2,1,0:T(8,128)(2,1)S(1)} %all_to_all.66), channel_id=1, replica_groups=mesh['tok'=2,'row'=4,'col'=4] {'col'}, dimensions={0} | all-to-all | bytes 2359296 | tf_op jit(solution)/shard_map/all_to_all | solution.py:46
  788.8 57.2 %all-gather.22.cloned.1.call-done = bf16[1152,2048]{1,0:T(8,128)(2,1)} async-done(((bf16[288,2048]{1,0:T(8,128)(2,1)}), bf16[1152,2048]{1,0:T(8,128)(2,1)}) %all-gather.22.cloned.1.call-update) | async-done | bytes 4718608 | tf_op jit(solution)/shard_map/all_gather | solution.py:68
  846.0 17.0 %fusion.290 = f32[1152,2048]{1,0:T(8,128)} fusion(bf16[1152,2048]{1,0:T(8,128)(2,1)} %all-gather.22.cloned.1.call-done, bf16[2048,2048]{0,1:T(8,128)(2,1)} %all-gather.20.cloned.1.call-done), kind=kOutput, calls=%fused_computation.670 | convolution fusion | flops 9663676416 | bytes 22544384 | tf_op jit(solution)/shard_map/dot_general | solution.py:25
  864.3 11.1 multiply_convert_fusion.2
  883.3 26.8 %fusion.37 = bf16[1152,2048]{1,0:T(8,128)(2,1)} fusion(f32[1152,2048]{1,0:T(8,128)S(1)} %fusion.291, bf16[2048,4096]{0,1:T(8,128)(2,1)} %all-gather.18.cloned.1.call-done, bf16[1152,2048]{1,0:T(8,128)(2,1)} %copy-done.193, bf16[1152,2048]{1,0:T(8,128)(2,1)} %copy-done.192), kind=kOutput, calls=%fused_computation.77 | convolution fusion | flops 19350945792 | bytes 40370176 | tf_op jit(solution)/shard_map/dot_general | solution.py:29
  910.2 57.2 %reduce-scatter.9.cloned.1.call-done = bf16[288,2048]{1,0:T(8,128)(2,1)} async-done(((bf16[1152,2048]{1,0:T(8,128)(2,1)}), bf16[288,2048]{1,0:T(8,128)(2,1)}) %reduce-scatter.9.cloned.1.call-update) | async-done | bytes 1179664 | tf_op jit(solution)/shard_map/reduce_scatter | solution.py:74
  994.2 36.0 %all-gather.24.cloned.1.call-done = bf16[1152,2048]{1,0:T(8,128)(2,1)} async-done(((bf16[288,2048]{1,0:T(8,128)(2,1)}), bf16[1152,2048]{1,0:T(8,128)(2,1)}) %all-gather.24.cloned.1.call-update) | async-done | bytes 4718608 | tf_op jit(solution)/shard_map/all_gather | solution.py:68
  1038.5 178.5 %while.35 = (s32[]{:T(128)}, f32[1152,4,128]{0,2,1:T(8,128)}, f32[1152,4,128]{0,2,1:T(8,128)}, f32[9,128,4,128]{3,1,0,2:T(8,128)}, s32[9]{0:T(128)}, /*index=5*/...) while((s32[]{:T(128)}, f32[1152,4,128]{0,2,1:T(8,128)}, ...), condition=%wide.region_16.17_spmd.clone.clone, body=%wide.region_14.16_spmd.clone.clone.sunk | while | flops 763890944 | bytes 36486132 | solution.py:185
  1270.3 10.8 all-to-all-done.9
  1287.5 10.3 fusion.280
  1310.5 23.3 %all-to-all-done.3 = bf16[4,288,512]{2,1,0:T(8,128)(2,1)} async-done(((bf16[4,288,512]{2,1,0:T(8,128)(2,1)}), bf16[4,288,512]{2,1,0:T(8,128)(2,1)}, u32[]{:S(2)}, u32[]{:S(2)}) %all-to-all-start.3) | async-done | bytes 1179680 | tf_op jit(solution)/shard_map/all_to_all | solution.py:54
  1340.0 11.9 all-to-all-done.4
  1357.8 13.1 all-gather.26.cloned.1.call-done
  1379.2 51.2 %reduce-scatter.11.cloned.1.call-done = bf16[288,2048]{1,0:T(8,128)(2,1)} async-done(((bf16[1152,2048]{1,0:T(8,128)(2,1)}), bf16[288,2048]{1,0:T(8,128)(2,1)}) %reduce-scatter.11.cloned.1.call-update) | async-done | bytes 1179664 | tf_op jit(solution)/shard_map/reduce_scatter | solution.py:74
  1443.0 23.8 %all-to-all-done.7 = bf16[4,288,512]{2,1,0:T(8,128)(2,1)} async-done(((bf16[4,288,512]{2,1,0:T(8,128)(2,1)}), bf16[4,288,512]{2,1,0:T(8,128)(2,1)}, u32[]{:S(2)}, u32[]{:S(2)}) %all-to-all-start.7) | async-done | bytes 1179680 | tf_op jit(solution)/shard_map/all_to_all | solution.py:54
  (815 shorter events, 527.0 us)
Async XLA Ops:
  7.2 410.5 %copy-start = (bf16[2048,512]{1,0:T(8,128)(2,1)S(1)}, bf16[2048,512]{1,0:T(8,128)(2,1)}, u32[]{:S(2)}) copy-start(bf16[2048,512]{1,0:T(8,128)(2,1)} %param.27) | copy-start | bytes 6291460
  7.2 109.0 %all-gather.12.cloned.1.call-start = ((), (), s32[]{:S(2)}) async-start(), calls=%async_computation.15 | async-start | bytes 5898240 | tf_op jit(solution)/shard_map/all_gather | solution.py:68
  61.0 122.5 %all-gather.10.cloned.1.call-start = ((), (), s32[]{:S(2)}) async-start(), calls=%async_computation.14 | async-start | bytes 7077888 | tf_op jit(solution)/shard_map/all_gather | solution.py:39
  69.1 16.2 %all-to-all-start.2 = ((bf16[4,7,16,512]{3,2,1,0:T(8,128)(2,1)}), bf16[4,7,16,512]{3,2,1,0:T(8,128)(2,1)}, u32[]{:S(2)}, u32[]{:S(2)}) async-start(bf16[4,7,16,512]{3,2,1,0:T(8,128)(2,1)} %copy.123), calls=%async_computation.2 | async-start | bytes 917504 | tf_op jit(solution)/shard_map/all_to_all | solution.py:260
  73.2 268.3 %all-gather.14.cloned.1.call-start = ((), (), s32[]{:S(2)}) async-start(), calls=%async_computation.16 | async-start | bytes 2359296 | tf_op jit(solution)/shard_map/all_gather | solution.py:39
  74.0 329.4 %reduce-scatter.5.cloned.1.call-start = ((), (), s32[]{:S(2)}) async-start(), calls=%async_computation.17 | async-start | bytes 5898240 | tf_op jit(solution)/shard_map/reduce_scatter | solution.py:74
  80.0 115.5 %copy-start.100 = (bf16[1,16,512]{2,1,0:T(8,128)(2,1)}, bf16[1,16,512]{2,1,0:T(8,128)(2,1)S(1)}, u32[]{:S(2)}) copy-start(bf16[1,16,512]{2,1,0:T(8,128)(2,1)S(1)} %copy.245) | copy-start | bytes 49156
  85.3 153.4 %copy-start.19 = (f32[1152,64]{1,0:T(8,128)}, f32[1152,64]{1,0:T(8,128)S(1)}, u32[]{:S(2)}) copy-start(f32[1152,64]{1,0:T(8,128)S(1)} %get-tuple-element.674) | copy-start | bytes 884740
  88.2 257.9 %copy-start.38 = (bf16[2,8,4,512]{3,1,2,0:T(8,128)(2,1)}, bf16[2,8,4,512]{3,1,2,0:T(8,128)(2,1)S(1)}, u32[]{:S(2)}) copy-start(bf16[2,8,4,512]{3,1,2,0:T(8,128)(2,1)S(1)} %copy.193) | copy-start | bytes 196612
  349.7 55.3 %copy-start.10 = (bf16[4,36,8,512]{3,2,0,1:T(8,128)(2,1)S(1)}, bf16[4,36,8,512]{3,2,0,1:T(8,128)(2,1)}, u32[]{:S(2)}) copy-start(bf16[4,36,8,512]{3,2,0,1:T(8,128)(2,1)} %copy.189) | copy-start | bytes 3538948
  349.7 115.5 %all-gather.16.cloned.1.call-start = ((), (), s32[]{:S(2)}) async-start(), calls=%async_computation.18 | async-start | bytes 5898240 | tf_op jit(solution)/shard_map/all_gather | solution.py:68
  408.0 211.1 %all-gather.18.cloned.1.call-start = ((), (), s32[]{:S(2)}) async-start(), calls=%async_computation.19 | async-start | bytes 18874368 | tf_op jit(solution)/shard_map/all_gather | solution.py:39
  417.6 284.3 %all-gather.20.cloned.1.call-start = ((), (), s32[]{:S(2)}) async-start(), calls=%async_computation.20 | async-start | bytes 9437184 | tf_op jit(solution)/shard_map/all_gather | solution.py:39
  418.8 366.5 %reduce-scatter.7.cloned.1.call-start = ((), (), s32[]{:S(2)}) async-start(), calls=%async_computation.21 | async-start | bytes 5898240 | tf_op jit(solution)/shard_map/reduce_scatter | solution.py:74
  660.8 55.0 %copy-start.40 = (bf16[1152,16]{0,1:T(8,128)(2,1)}, bf16[1152,16]{0,1:T(8,128)(2,1)S(1)}, u32[]{:S(2)}) copy-start(bf16[1152,16]{0,1:T(8,128)(2,1)S(1)} %fusion.61) | copy-start | bytes 110596
  719.4 126.6 %all-gather.22.cloned.1.call-start = ((), (), s32[]{:S(2)}) async-start(), calls=%async_computation.22 | async-start | bytes 5898240 | tf_op jit(solution)/shard_map/all_gather | solution.py:68
  783.8 186.0 %copy-start.5 = (f32[4,36,8,512]{3,2,0,1:T(8,128)}, f32[4,36,8,512]{3,2,0,1:T(8,128)S(1)}, u32[]{:S(2)}) copy-start(f32[4,36,8,512]{3,2,0,1:T(8,128)S(1)} %copy.190) | copy-start | bytes 7077892
  788.7 178.6 %reduce-scatter.9.cloned.1.call-start = ((), (), s32[]{:S(2)}) async-start(), calls=%async_computation.23 | async-start | bytes 5898240 | tf_op jit(solution)/shard_map/reduce_scatter | solution.py:74
  910.1 57.3 %copy-start.75 = (f32[1,2048]{1,0:T(1,128)S(1)}, f32[1,2048]{1,0:T(1,128)}, u32[]{:S(2)}) copy-start(f32[1,2048]{1,0:T(1,128)} %copy-done.74) | copy-start | bytes 24580
  910.1 59.6 %copy-start.11 = (bf16[4,36,8,512]{3,2,0,1:T(8,128)(2,1)S(1)}, bf16[4,36,8,512]{3,2,0,1:T(8,128)(2,1)}, u32[]{:S(2)}) copy-start(bf16[4,36,8,512]{3,2,0,1:T(8,128)(2,1)} %copy.189) | copy-start | bytes 3538948
  910.1 120.1 %all-gather.24.cloned.1.call-start = ((), (), s32[]{:S(2)}) async-start(), calls=%async_computation.24 | async-start | bytes 5898240 | tf_op jit(solution)/shard_map/all_gather | solution.py:68
  988.0 46.0 %copy-start.188 = (bf16[2048,512]{0,1:T(8,128)(2,1)S(1)}, bf16[2048,512]{0,1:T(8,128)(2,1)}, u32[]{:S(2)}) copy-start(bf16[2048,512]{0,1:T(8,128)(2,1)} %all-gather.14.cloned.1.call-done) | copy-start | bytes 6291460
  1265.4 15.7 %all-to-all-start.9 = ((bf16[4,7,16,512]{3,2,1,0:T(8,128)(2,1)}), bf16[4,7,16,512]{3,2,1,0:T(8,128)(2,1)S(1)}, u32[]{:S(2)}, u32[]{:S(2)}) async-start(bf16[4,7,16,512]{3,2,1,0:T(8,128)(2,1)} %maximum_bitcast_fusion), calls=%async_computation.13 | async-start | bytes 917504 | tf_op jit(solution)/shard_map/all_to_all | solution.py:373
  1270.0 83.8 %all-reduce.6.cloned.1.call-start = ((), (), s32[]{:S(2)}) async-start(), calls=%async_computation.26 | async-start | bytes 1835008 | tf_op jit(solution)/shard_map/psum | solution.py:375
  1283.4 87.5 %all-gather.26.cloned.1.call-start = ((), (), s32[]{:S(2)}) async-start(), calls=%async_computation.27 | async-start | bytes 2359296 | tf_op jit(solution)/shard_map/all_gather | solution.py:389
  1287.5 142.9 %reduce-scatter.11.cloned.1.call-start = ((), (), s32[]{:S(2)}) async-start(), calls=%async_computation.25 | async-start | bytes 5898240 | tf_op jit(solution)/shard_map/reduce_scatter | solution.py:74
  1303.8 30.0 %all-to-all-start.3 = ((bf16[4,288,512]{2,1,0:T(8,128)(2,1)}), bf16[4,288,512]{2,1,0:T(8,128)(2,1)}, u32[]{:S(2)}, u32[]{:S(2)}) async-start(bf16[4,288,512]{2,1,0:T(8,128)(2,1)} %bitcast.975), calls=%async_computation.5 | async-start | bytes 2359296 | tf_op jit(solution)/shard_map/all_to_all | solution.py:54
  1333.8 18.1 %all-to-all-start.4 = ((bf16[4,288,512]{2,1,0:T(8,128)(2,1)}), bf16[4,288,512]{2,1,0:T(8,128)(2,1)S(1)}, u32[]{:S(2)}, u32[]{:S(2)}) async-start(bf16[4,288,512]{2,1,0:T(8,128)(2,1)} %all-to-all-done.3), calls=%async_computation.6 | async-start | bytes 2359296 | tf_op jit(solution)/shard_map/all_to_all | solution.py:55
  1356.9 73.5 %copy-start.6 = (f32[4,36,8,512]{3,2,0,1:T(8,128)S(1)}, f32[4,36,8,512]{3,2,0,1:T(8,128)}, u32[]{:S(2)}) copy-start(f32[4,36,8,512]{3,2,0,1:T(8,128)} %copy-done.5) | copy-start | bytes 7077892
  1356.9 73.5 %copy-start.14 = (bf16[288,2048]{1,0:T(8,128)(2,1)S(1)}, bf16[288,2048]{1,0:T(8,128)(2,1)}, u32[]{:S(2)}) copy-start(bf16[288,2048]{1,0:T(8,128)(2,1)} %reduce-scatter.9.cloned.1.call-done) | copy-start | bytes 3538948
  1433.6 33.2 %all-to-all-start.7 = ((bf16[4,288,512]{2,1,0:T(8,128)(2,1)}), bf16[4,288,512]{2,1,0:T(8,128)(2,1)}, u32[]{:S(2)}, u32[]{:S(2)}) async-start(bf16[4,288,512]{2,1,0:T(8,128)(2,1)} %bitcast.973), calls=%async_computation.11 | async-start | bytes 2359296 | tf_op jit(solution)/shard_map/all_to_all | solution.py:54
  1466.8 18.0 %all-to-all-start.8 = ((bf16[4,288,512]{2,1,0:T(8,128)(2,1)}), bf16[4,288,512]{2,1,0:T(8,128)(2,1)S(1)}, u32[]{:S(2)}, u32[]{:S(2)}) async-start(bf16[4,288,512]{2,1,0:T(8,128)(2,1)} %all-to-all-done.7), calls=%async_computation.12 | async-start | bytes 2359296 | tf_op jit(solution)/shard_map/all_to_all | solution.py:55
  (192 other events, 1269.4 us)
Sparse Core Ops, SparseCore 0:
  61.2 54.9 all-gather.11
  118.4 65.1 all-gather.9
  185.7 29.0 all-gather.13
  349.9 53.5 reduce-scatter.4
  408.1 57.0 all-gather.15
  467.2 151.8 all-gather.17
  621.2 80.6 all-gather.19
  719.5 65.7 reduce-scatter.6
  788.9 57.0 all-gather.21
  910.2 57.0 reduce-scatter.8
  973.1 57.0 all-gather.23
  1283.5 53.9 all-reduce.5
  1339.7 31.1 all-gather.25
  1373.8 56.5 reduce-scatter.10

commit v2 on v1

v2 whole, which is shorter than its diff:
```python
import functools
import math

import jax
import jax.numpy as jnp
from jax import lax
from jax.experimental import pallas as pl
from jax.experimental.pallas import tpu as pltpu
from jax.sharding import PartitionSpec as P

D = 2048
HEAD_DIM = 128
RANK = 16
ADAPTERS = 8
PROMPT = 1024
CONT_LEN = 128
SLAB = 1152

adapter_scale = 2.0
norm_eps = 1e-06
rope_base = 500000.0
very_low = -1e30
bf16 = jnp.bfloat16
f32 = jnp.float32
log2_scale = math.log2(math.e) / math.sqrt(HEAD_DIM)
score_scale = 1.0 / math.sqrt(HEAD_DIM)
BLOCK = 384
TILE = 512
MESH = pl.DeviceIdType.MESH


def mm(left, right):
    return jnp.dot(left, right, preferred_element_type=f32)

def mm_nt(left, right):
    return lax.dot_general(left, right, (((1,), (1,)), ((), ())), preferred_element_type=f32)

def greet(near):
    barrier = pltpu.get_barrier_semaphore()
    for other in near:
        pl.semaphore_signal(barrier, inc=1, device_id={"row": other}, device_id_type=MESH)
    pl.semaphore_wait(barrier, len(near))

def send(source, target, sems, index, other):
    copy = pltpu.make_async_remote_copy(
        src_ref=source, dst_ref=target, send_sem=sems[0].at[index], recv_sem=sems[1].at[index],
        device_id={"row": other}, device_id_type=MESH)
    return copy

def gather_matmul_kernel(finish, start, x_ref, w_hbm, f1_ref, f2_ref, *refs, extra_in, extra_out):
    ins = refs[:extra_in]
    all_ref, low_ref = refs[extra_in], refs[extra_in + 1]
    outs = refs[extra_in + 2 : extra_in + 2 + extra_out]
    w_ref, w_sem, send_sem, recv_sem = refs[extra_in + 2 + extra_out :]
    me = lax.axis_index("row")
    xn, yn, dg = me ^ 1, me ^ 2, me ^ 3
    count = x_ref.shape[0]
    half = count // 2
    n = w_ref.shape[1]
    load = pltpu.make_async_copy(w_hbm.at[:, pl.ds(start, w_ref.shape[1])], w_ref, w_sem)
    load.start()
    greet((xn, yn))
    sems = (send_sem, recv_sem)
    top, low = pl.ds(0, half), pl.ds(half, half)
    sends = [
        send(x_ref.at[top], all_ref.at[me, top], sems, 0, xn),
        send(x_ref.at[low], all_ref.at[me, low], sems, 1, yn),
        send(x_ref.at[low], all_ref.at[me, low], sems, 2, xn),
        send(x_ref.at[top], all_ref.at[me, top], sems, 3, yn),
    ]
    for copy in sends:
        copy.start()
    def arrive(owner, part, index):
        send(all_ref.at[owner, part], all_ref.at[owner, part], sems, index, xn).wait_recv()
    all_ref[me] = x_ref[...]
    load.wait()

    def work(owner):
        rows = all_ref[owner]
        lowered = (adapter_scale * mm_nt(rows, f1_ref[...])).astype(bf16)
        low_ref[owner] = lowered
        finish(all_ref, lowered, w_ref, f2_ref, owner, ins, outs)
    arrive(xn, top, 0)
    pass_y = send(all_ref.at[xn, top], all_ref.at[xn, top], sems, 4, yn)
    pass_y.start()
    arrive(yn, low, 1)
    pass_x = send(all_ref.at[yn, low], all_ref.at[yn, low], sems, 5, xn)
    pass_x.start()
    work(me)
    arrive(xn, low, 2)
    work(xn)
    arrive(yn, top, 3)
    work(yn)
    arrive(dg, top, 4)
    arrive(dg, low, 5)
    work(dg)
    for copy in sends + [pass_y, pass_x]:
        copy.wait_send()

def each_tile(width, step, body):
    @pl.loop(0, width // step)
    def _(tile):
        body(pl.ds(pl.multiple_of(tile * step, step), step), tile)


def tile_product(all_ref, lowered, w_ref, f2_ref, owner, cols):
    return mm(all_ref[owner], w_ref[:, cols]) + mm(lowered, f2_ref[:, cols])


def finish_qkv(all_ref, lowered, w_ref, f2_ref, owner, ins, outs):
    width = w_ref.shape[1] // 3
    for index in range(3):
        cols = slice(index * width, (index + 1) * width)
        value = tile_product(all_ref, lowered, w_ref, f2_ref, owner, cols)
        outs[0][owner, :, cols] = value
        if index < 2:
            outs[1][owner, :, index : index + 1] = jnp.sum(value * value, axis=1, keepdims=True)


def finish_plain(all_ref, lowered, w_ref, f2_ref, owner, ins, outs):
    def body(cols, _):
        value = tile_product(all_ref, lowered, w_ref, f2_ref, owner, cols)
        outs[0][owner, :, cols] = value.astype(bf16)

    each_tile(w_ref.shape[1], TILE, body)


def gated(gate, up):
    return gate * jax.nn.sigmoid(gate) * up


def gated_back(grad, gate, up):
    sig = jax.nn.sigmoid(gate)
    act = gate * sig
    return (grad * up * (sig + act * (1.0 - sig)), grad * act)


def finish_ffn(all_ref, lowered, w_ref, f2_ref, owner, ins, outs):
    width = w_ref.shape[1] // 2

    def body(cols, tile):
        shifted = pl.ds(pl.multiple_of(width + tile * TILE, TILE), TILE)
        gate = tile_product(all_ref, lowered, w_ref, f2_ref, owner, cols)
        up = tile_product(all_ref, lowered, w_ref, f2_ref, owner, shifted)
        outs[0][owner, :, cols] = gate.astype(bf16)
        outs[1][owner, :, cols] = up.astype(bf16)
        outs[2][owner, :, cols] = gated(gate, up).astype(bf16)

    each_tile(width, TILE, body)


def finish_gated_back(all_ref, lowered, w_ref, f2_ref, owner, ins, outs):
    width = w_ref.shape[1]

    def body(cols, tile):
        shifted = pl.ds(pl.multiple_of(width + tile * TILE, TILE), TILE)
        grad = tile_product(all_ref, lowered, w_ref, f2_ref, owner, cols)
        gate, up = ins[0][owner, :, cols].astype(f32), ins[1][owner, :, cols].astype(f32)
        grad_gate, grad_up = gated_back(grad, gate, up)
        outs[0][owner, :, cols] = grad_gate.astype(bf16)
        outs[0][owner, :, shifted] = grad_up.astype(bf16)

    each_tile(width, TILE, body)


def gather_matmul(x, w, start, f1, f2, finish, extra, out_shapes, collective_id, name):
    count, depth = x.shape
    n = f2.shape[1]
    vmem = pl.BlockSpec(memory_space=pltpu.VMEM)
    outs = [jax.ShapeDtypeStruct((4, count, depth), bf16), jax.ShapeDtypeStruct((4, count, f1.shape[0]), bf16)] + out_shapes
    return pl.pallas_call(
        functools.partial(gather_matmul_kernel, finish, start, extra_in=len(extra), extra_out=len(out_shapes)),
        in_specs=[vmem, pl.BlockSpec(memory_space=pl.ANY)] + [vmem] * (2 + len(extra)),
        out_specs=[vmem] * len(outs), out_shape=outs,
        scratch_shapes=[pltpu.VMEM((depth, n), bf16), pltpu.SemaphoreType.DMA, pltpu.SemaphoreType.DMA((6,)), pltpu.SemaphoreType.DMA((6,))],
        compiler_params=pltpu.CompilerParams(collective_id=collective_id, has_side_effects=True, vmem_limit_bytes=60 << 20),
        cost_estimate=pl.CostEstimate(flops=8*count*depth*n, bytes_accessed=2*depth*n, transcendentals=0),
        name=name,
    )(x, w, f1, f2, *extra)

def matmul_scatter_kernel(start, y_ref, w_hbm, f1_ref, f2_ref, o_ref, low_ref, w_ref, out_buf, relay_buf, final_buf, w_sem, send_sem, recv_sem):
    me = lax.axis_index("row")
    xn, yn, dg = me ^ 1, me ^ 2, me ^ 3
    count = y_ref.shape[1]
    half = count // 2
    load = pltpu.make_async_copy(w_hbm.at[:, pl.ds(start, w_ref.shape[1])], w_ref, w_sem)
    load.start()
    greet((xn, yn))
    sems = (send_sem, recv_sem)
    top, low = slice(0, half), slice(half, count)
    tiles = w_ref.shape[0] // TILE
    load.wait()
    def partial(owner, store):
        lowered = (adapter_scale * mm_nt(y_ref[owner], f1_ref[...])).astype(bf16)
        low_ref[owner] = lowered
        @pl.loop(0, tiles)
        def _(tile):
            cols = pl.ds(pl.multiple_of(tile * TILE, TILE), TILE)
            store(cols, mm_nt(y_ref[owner], w_ref[cols, :]) + mm(lowered, f2_ref[:, cols]))
    def keep(slot):
        def store(cols, value):
            out_buf[slot, :, cols] = value.astype(bf16)
        return store
    partial(dg, keep(0))
    first = [
        send(out_buf.at[0, top], relay_buf.at[0], sems, 0, xn),
        send(out_buf.at[0, low], relay_buf.at[1], sems, 1, yn),
    ]
    for copy in first:
        copy.start()
    partial(xn, keep(1))
    x_top = send(out_buf.at[1, top], final_buf.at[0, top], sems, 2, xn)
    x_top.start()
    partial(yn, keep(2))
    y_low = send(out_buf.at[2, low], final_buf.at[1, low], sems, 3, yn)
    y_low.start()
    first[0].wait_recv()
    out_buf[2, top] = (out_buf[2, top].astype(f32) + relay_buf[0].astype(f32)).astype(bf16)
    y_top = send(out_buf.at[2, top], final_buf.at[1, top], sems, 4, yn)
    y_top.start()
    first[1].wait_recv()
    out_buf[1, low] = (out_buf[1, low].astype(f32) + relay_buf[1].astype(f32)).astype(bf16)
    x_low = send(out_buf.at[1, low], final_buf.at[0, low], sems, 5, xn)
    x_low.start()
    def own(cols, value):
        o_ref[:, cols] = value
    partial(me, own)
    for copy in (x_top, y_low, y_top, x_low):
        copy.wait_recv()
    o_ref[...] += final_buf[0].astype(f32) + final_buf[1].astype(f32)
    for copy in first + [x_top, y_low, y_top, x_low]:
        copy.wait_send()

def matmul_scatter(y, w, start, f1, f2, collective_id, name):
    _, count, depth = y.shape
    n = w.shape[0]
    vmem = pl.BlockSpec(memory_space=pltpu.VMEM)
    return pl.pallas_call(
        functools.partial(matmul_scatter_kernel, start),
        in_specs=[vmem, pl.BlockSpec(memory_space=pl.ANY), vmem, vmem],
        out_specs=[vmem, vmem],
        out_shape=[jax.ShapeDtypeStruct((count, n), f32), jax.ShapeDtypeStruct((4, count, f1.shape[0]), bf16)],
        scratch_shapes=[pltpu.VMEM((n, depth), bf16), pltpu.VMEM((3, count, n), bf16), pltpu.VMEM((2, count // 2, n), bf16), pltpu.VMEM((2, count, n), bf16),
                        pltpu.SemaphoreType.DMA, pltpu.SemaphoreType.DMA((6,)), pltpu.SemaphoreType.DMA((6,))],
        compiler_params=pltpu.CompilerParams(collective_id=collective_id, has_side_effects=True, vmem_limit_bytes=60 << 20),
        cost_estimate=pl.CostEstimate(flops=8*count*depth*n, bytes_accessed=2*depth*n, transcendentals=0),
        name=name,
    )(y, w, f1, f2)


def score_blocks(k_ref, q_block, bias_ref, start, stop):
    parts = []
    if start:
        parts.append(mm_nt(k_ref[0:start], q_block) + bias_ref[0:start])
    own = mm_nt(k_ref[start:stop], q_block) + bias_ref[start:stop]
    keys = lax.broadcasted_iota(jnp.int32, own.shape, 0)
    queries = lax.broadcasted_iota(jnp.int32, own.shape, 1)
    parts.append(jnp.where(keys <= queries, own, very_low))
    return parts

def attend_kernel(q_ref, k_ref, v_ref, inv_ref, gain_ref, cos_ref, sin_ref, bias_ref,
                  ql_ref, kl_ref, vl_ref, o_ref, lse_ref):
    for source, target, index in ((q_ref, ql_ref, 0), (k_ref, kl_ref, 1)):
        normed = source[...] * inv_ref[:, index:index+1] * gain_ref[index:index+1, :]
        target[...] = (normed * cos_ref[...] + pltpu.roll(normed, HEAD_DIM // 2, 1) * sin_ref[...]).astype(bf16)
    values = v_ref[...].astype(bf16)
    vl_ref[...] = values
    values_t = v_ref[...].T.astype(bf16)
    for start in range(0, SLAB, BLOCK):
        stop = start + BLOCK
        parts = score_blocks(kl_ref, ql_ref[start:stop], bias_ref, start, stop)
        top = functools.reduce(jnp.maximum, [jnp.max(p, axis=0, keepdims=True) for p in parts]) * log2_scale
        total, out, at = 0.0, 0.0, 0
        for part in parts:
            shifted = jnp.exp2(part * log2_scale - top)
            total = total + jnp.sum(shifted, axis=0, keepdims=True)
            out = out + mm(values_t[:, at:at+part.shape[0]], shifted.astype(bf16))
            at += part.shape[0]
        o_ref[start:stop] = (out / total).T.astype(bf16)
        lse_ref[0, :, start:stop] = top + jnp.log2(total)

def attend_back_kernel(ql_ref, kl_ref, vl_ref, o_ref, do_ref, lse_ref, q_ref, k_ref, gain_ref, cos_ref, sin_ref, bias_ref,
                       wq_ref, wk_ref, dv_ref, sum_ref, dk_sum, dv_sum):
    keys_t = kl_ref[...].astype(f32).T.astype(bf16)
    delta_all = jnp.sum((do_ref[...].astype(f32) * o_ref[...].astype(f32)).T, axis=0, keepdims=True)
    dk_sum[...] = jnp.zeros_like(dk_sum)
    dv_sum[...] = jnp.zeros_like(dv_sum)
    def unrotate(values):
        return values * cos_ref[...] - pltpu.roll(values, HEAD_DIM // 2, 1) * sin_ref[...]
    dq_parts = []
    for start in range(0, SLAB, BLOCK):
        stop = start + BLOCK
        queries, grads = ql_ref[start:stop], do_ref[start:stop]
        parts = score_blocks(kl_ref, queries, bias_ref, start, stop)
        lse, delta = lse_ref[0, :, start:stop], delta_all[:, start:stop]
        at, dq = 0, 0.0
        for part in parts:
            span = slice(at, at + part.shape[0])
            probs = jnp.exp2(part * log2_scale - lse)
            dv_sum[span] += mm(probs.astype(bf16), grads)
            dscore = (probs * (mm_nt(vl_ref[span], grads) - delta)).astype(bf16)
            dk_sum[span] += mm(dscore, queries)
            dq = dq + mm(keys_t[:, span], dscore)
            at += part.shape[0]
        dq_parts.append(dq.T)
    dq_all = jnp.concatenate(dq_parts, axis=0) * score_scale
    dv_ref[...] = dv_sum[...].astype(bf16)
    lanes = lax.broadcasted_iota(jnp.int32, (1, 2), 1)
    wq = unrotate(dq_all) * gain_ref[0:1, :]
    wk = unrotate(dk_sum[...] * score_scale) * gain_ref[1:2, :]
    wq_ref[...] = wq.astype(wq_ref.dtype)
    wk_ref[...] = wk.astype(wk_ref.dtype)
    sq = jnp.sum(wq * q_ref[...], axis=1, keepdims=True)
    sk = jnp.sum(wk * k_ref[...], axis=1, keepdims=True)
    both = jnp.where(lanes == 0, sq, sk)
    @pl.when(pl.program_id(0) == 0)
    def _():
        sum_ref[...] = both
    @pl.when(pl.program_id(0) != 0)
    def _():
        sum_ref[...] += both

def attend_specs(heads):
    col = lambda base: pl.BlockSpec((SLAB, HEAD_DIM), lambda h: (0, base * heads + h))
    whole = lambda shape: pl.BlockSpec(shape, lambda h: (0,) * len(shape))
    return col, whole

def attend(qkv_lin, inverses, gains, cosine, sine, bias):
    heads = qkv_lin.shape[1] // (3 * HEAD_DIM)
    col, whole = attend_specs(heads)
    low = jax.ShapeDtypeStruct((SLAB, heads * HEAD_DIM), bf16)
    return pl.pallas_call(
        attend_kernel, grid=(heads,),
        in_specs=[col(0), col(1), col(2), whole((SLAB, 2)), pl.BlockSpec((2, HEAD_DIM), lambda h: (0, h)),
                  whole((SLAB, HEAD_DIM)), whole((SLAB, HEAD_DIM)), whole((SLAB, 1))],
        out_specs=[col(0)] * 4 + [pl.BlockSpec((1, 1, SLAB), lambda h: (h, 0, 0))],
        out_shape=[low] * 4 + [jax.ShapeDtypeStruct((heads, 1, SLAB), f32)],
        compiler_params=pltpu.CompilerParams(vmem_limit_bytes=48 << 20),
        cost_estimate=pl.CostEstimate(flops=heads*4*SLAB*SLAB*HEAD_DIM, bytes_accessed=heads*SLAB*HEAD_DIM*20, transcendentals=heads*SLAB*SLAB),
        name="attend",
    )(qkv_lin, qkv_lin, qkv_lin, inverses, gains, cosine, sine, bias)

def attend_back(ql, kl, vl, o, do, lse, qkv_lin, gains, cosine, sine, bias):
    heads = ql.shape[1] // HEAD_DIM
    col, whole = attend_specs(heads)
    wide = jax.ShapeDtypeStruct(ql.shape, f32)
    return pl.pallas_call(
        attend_back_kernel, grid=(heads,),
        in_specs=[col(0)] * 5 + [pl.BlockSpec((1, 1, SLAB), lambda h: (h, 0, 0)), col(0), col(1), pl.BlockSpec((2, HEAD_DIM), lambda h: (0, h)),
                  whole((SLAB, HEAD_DIM)), whole((SLAB, HEAD_DIM)), whole((SLAB, 1))],
        out_specs=[col(0)] * 3 + [whole((SLAB, 2))],
        out_shape=[wide, wide, jax.ShapeDtypeStruct(ql.shape, bf16), jax.ShapeDtypeStruct((SLAB, 2), f32)],
        scratch_shapes=[pltpu.VMEM((SLAB, HEAD_DIM), f32)] * 2,
        compiler_params=pltpu.CompilerParams(vmem_limit_bytes=48 << 20),
        cost_estimate=pl.CostEstimate(flops=heads*10*SLAB*SLAB*HEAD_DIM, bytes_accessed=heads*SLAB*HEAD_DIM*30, transcendentals=heads*SLAB*SLAB),
        name="attend_back",
    )(ql, kl, vl, o, do, lse, qkv_lin, qkv_lin, gains, cosine, sine, bias)


def dot(left, right):
    return jnp.dot(left, right, preferred_element_type=f32)


def dot_nt(left, right):
    return lax.dot_general(left, right, (((1,), (1,)), ((), ())), preferred_element_type=f32)


def dot_tn(left, right):
    return lax.dot_general(left, right, (((0,), (0,)), ((), ())), preferred_element_type=f32)


def gather_weight(local):
    half = local.shape[0] // lax.axis_size("tok")
    part = lax.dynamic_slice_in_dim(local, lax.axis_index("tok") * half, half, 0)
    return lax.all_gather(part, ("col", "tok"), axis=0, tiled=True)


def to_tokens(values):
    rows, cols = lax.axis_size("row"), lax.axis_size("col")
    width = values.shape[1]
    mixed = lax.all_to_all(values, "row", 0, 0, tiled=True)
    mixed = lax.all_to_all(mixed, "col", 0, 0, tiled=True)
    return mixed.reshape(cols, SLAB // rows, width).transpose(1, 0, 2).reshape(SLAB // rows, -1)


def from_tokens(values):
    rows, cols = lax.axis_size("row"), lax.axis_size("col")
    count = values.shape[0]
    mixed = values.reshape(count, cols, -1).transpose(1, 0, 2).reshape(cols * count, -1)
    mixed = lax.all_to_all(mixed, "col", 0, 0, tiled=True)
    return lax.all_to_all(mixed, "row", 0, 0, tiled=True)


def reorder(values, outer, inner):
    if outer == 1 or inner == 1:
        return values
    rest = values.shape[0] // (outer * inner)
    shape = (outer, inner, rest) + values.shape[1:]
    return values.reshape(shape).swapaxes(0, 1).reshape(values.shape)


def gather_tokens(values):
    rows, per_slab = lax.axis_size("row"), lax.axis_size("row") // lax.axis_size("col")
    return reorder(lax.all_gather(values, "row", axis=0, tiled=True), rows, per_slab)


def scatter_tokens(values):
    rows, per_slab = lax.axis_size("row"), lax.axis_size("row") // lax.axis_size("col")
    values = reorder(values.astype(bf16), per_slab, rows)
    return lax.psum_scatter(values, "row", scatter_dimension=0, tiled=True).astype(f32)


def token_places(length):
    slot_ids = jnp.arange(SLAB, dtype=jnp.int32)
    return jnp.where(slot_ids < PROMPT, slot_ids, length + (slot_ids - PROMPT) % CONT_LEN)


def rotation(places, head_size):
    half_dim = head_size // 2
    frequency = jnp.exp(
        -(2.0 * jnp.arange(half_dim, dtype=f32) / head_size) * math.log(rope_base)
    )
    angles = places.astype(f32)[:, None] * frequency[None, :]
    return (jnp.cos(angles), jnp.sin(angles))


def norm_forward(values, gain):
    inverse = lax.rsqrt(jnp.mean(values * values, axis=1, keepdims=True) + norm_eps)
    return (values * inverse * gain.astype(f32), inverse)


def norm_backward(values, inverse, gain, grad_out):
    weighted = grad_out * gain.astype(f32)
    inner = jnp.mean(values * weighted, axis=1, keepdims=True)
    return inverse * weighted - values * (inverse**3 * inner)


def pick(adapters, ids):
    onehot = (ids[:, None] == jnp.arange(adapters.shape[0], dtype=jnp.int32)).astype(adapters.dtype)
    return jnp.tensordot(onehot, adapters, axes=1)


def place(ids, gradients):
    onehot = (jnp.arange(ADAPTERS, dtype=jnp.int32)[:, None] == ids[None, :]).astype(f32)
    total = 0.0
    for index in range(gradients.shape[0]):
        weight = onehot[:, index].reshape((ADAPTERS,) + (1,) * (gradients.ndim - 1))
        total = total + weight * gradients[index][None].astype(f32)
    return total


def block_diagonal(factors):
    count = len(factors)
    lines = []
    for index, factor in enumerate(factors):
        blank = jnp.zeros_like(factor)
        lines.append(
            jnp.concatenate([factor if k == index else blank for k in range(count)], axis=1)
        )
    return jnp.concatenate(lines, axis=0)


def fast():
    return lax.axis_size("row") == 4


def flat(values):
    return values.reshape((SLAB,) + values.shape[2:])


def enter(x, w, start, f1, f2, finish, extra, outs, collective_id, name):
    if fast():
        shapes = [jax.ShapeDtypeStruct((4, x.shape[0]) + shape, kind) for shape, kind in outs]
        extra = [value.reshape((4, -1) + value.shape[1:]) for value in extra]
        results = gather_matmul(
            x, w, start, f1, f2, finish, extra, shapes, collective_id, name
        )
        return [flat(value) for value in results]
    everything = gather_tokens(x)
    lowered = (adapter_scale * dot_nt(everything, f1)).astype(bf16)
    value = dot(everything, w[:, start : start + f2.shape[1]]) + dot(lowered, f2)
    width = outs[0][0][0]
    if finish is finish_qkv:
        width = width // 3
        parts = [value[:, k * width : (k + 1) * width] for k in range(2)]
        results = [value, jnp.stack([jnp.sum(part * part, axis=1) for part in parts], axis=1)]
    elif finish is finish_ffn:
        gate, up = value[:, :width], value[:, width:]
        results = [gate, up, gated(gate, up)]
    elif finish is finish_gated_back:
        gate, up = extra[0].astype(f32), extra[1].astype(f32)
        results = [jnp.concatenate(gated_back(value, gate, up), axis=1)]
    else:
        results = [value]
    return [everything, lowered] + [r.astype(kind) for r, (_, kind) in zip(results, outs)]


def leave(y, w, start, f1, f2, collective_id, name):
    if fast():
        total, lowered = matmul_scatter(
            y.reshape(4, -1, y.shape[1]), w, start, f1, f2, collective_id, name
        )
        return total, flat(lowered)
    lowered = (adapter_scale * dot_nt(y, f1)).astype(bf16)
    value = dot_nt(y, w[:, start : start + y.shape[1]]) + dot(lowered, f2)
    return scatter_tokens(value), lowered


def on_device(
    layer_in,
    cotangent,
    qkv_weight,
    out_weight,
    ffn_weight,
    down_weight,
    qk_gain,
    post_gain,
    qkv_lower,
    qkv_raise,
    out_lower,
    out_raise,
    ffn_lower,
    ffn_raise,
    down_lower,
    down_raise,
    adapter_ids,
    prompt_len,
):
    col_count = lax.axis_size("col")
    group_base = lax.axis_index("tok") * col_count
    group = group_base + lax.axis_index("col")
    slab_ids = lax.dynamic_slice_in_dim(adapter_ids, group_base, col_count, 0)
    own_ids = lax.dynamic_index_in_dim(adapter_ids, group, 0, keepdims=False)
    length = lax.dynamic_index_in_dim(prompt_len, group, 0, keepdims=False)
    width = layer_in.shape[1]
    head_width = qkv_weight.shape[2]
    ff_width = ffn_weight.shape[2]

    local = jnp.concatenate([qkv_weight.transpose(1, 0, 2).reshape(width, -1), out_weight.T], axis=1)
    attn_full = gather_weight(local)
    ffn_full = gather_weight(ffn_weight.transpose(1, 0, 2).reshape(width, -1))
    down_full = gather_weight(down_weight.T)
    x_own = to_tokens(layer_in)

    pieces = jnp.stack(
        [pick(qkv_lower[p].swapaxes(1, 2), slab_ids[:, p]) for p in range(3)]
        + [pick(out_raise, slab_ids[:, 3])]
        + [pick(ffn_lower[p].swapaxes(1, 2), slab_ids[:, 4 + p]) for p in range(2)]
        + [pick(down_raise, slab_ids[:, 6])],
        axis=1,
    )
    factors = lax.all_to_all(pieces, "col", 0, 0, tiled=True)
    factors = factors.transpose(1, 2, 0, 3).reshape(7, RANK, D)
    qkv_a, out_b, ffn_a, down_b = (
        factors[0:3].reshape(3 * RANK, D),
        factors[3],
        factors[4:6].reshape(2 * RANK, D),
        factors[6],
    )
    qkv_b = block_diagonal([pick(qkv_raise[p], own_ids[p : p + 1])[0] for p in range(3)])
    out_a = pick(out_lower, own_ids[3:4])[0].T
    ffn_b = block_diagonal([pick(ffn_raise[p], own_ids[4 + p : 5 + p])[0] for p in range(2)])
    down_a = pick(down_lower, own_ids[6:7])[0].T
    gains = lax.all_gather(post_gain, "col", axis=1, tiled=True)
    qkv_width = 3 * head_width

    cosine, sine = rotation(token_places(length), HEAD_DIM)
    cosine = jnp.concatenate([cosine, cosine], axis=1)
    sine = jnp.concatenate([-sine, sine], axis=1)
    slots = jnp.arange(SLAB, dtype=jnp.int32)
    bias = jnp.where((slots < length) | (slots >= PROMPT), 0.0, very_low)[:, None].astype(f32)
    head_gain = qk_gain.astype(f32)

    x_all, qkv_low, qkv_lin, squares = enter(
        x_own, attn_full, 0, qkv_a, qkv_b, finish_qkv, [],
        [((qkv_width,), f32), ((2,), f32)], 1, "enter_qkv",
    )
    inverses = lax.rsqrt(lax.psum(squares, "row") / D + norm_eps)
    q_low, k_low, v_low, attn_low, log_sums = attend(
        qkv_lin, inverses, head_gain, cosine, sine, bias
    )
    attn_lin, out_low = leave(attn_low, attn_full, qkv_width, out_a, out_b, 2, "leave_out")
    attn_norm, attn_inverse = norm_forward(attn_lin, gains[0])
    hidden = x_own.astype(f32) + attn_norm
    h_all, ffn_low, gate_lin, up_lin, act_low = enter(
        hidden.astype(bf16), ffn_full, 0, ffn_a, ffn_b, finish_ffn, [],
        [((ff_width,), bf16)] * 3, 3, "enter_ffn",
    )
    mlp_lin, down_low = leave(act_low, down_full, 0, down_a, down_b, 4, "leave_down")
    mlp_norm, mlp_inverse = norm_forward(mlp_lin, gains[1])
    layer_out = from_tokens((hidden + mlp_norm).astype(bf16)).astype(f32)

    grad_out = to_tokens(cotangent).astype(f32)
    grad_mlp = norm_backward(mlp_lin, mlp_inverse, gains[1], grad_out).astype(bf16)
    dm_all, down_dlow, grad_ffn = enter(
        grad_mlp, down_full, 0, down_b, down_a, finish_gated_back, [gate_lin, up_lin],
        [((2 * ff_width,), bf16)], 5, "back_down",
    )
    grad_ffn_in, ffn_dlow = leave(grad_ffn, ffn_full, 0, ffn_b, ffn_a, 6, "back_ffn")
    grad_hidden = grad_out + grad_ffn_in
    grad_attn = norm_backward(attn_lin, attn_inverse, gains[0], grad_hidden).astype(bf16)
    da_all, out_dlow, grad_heads = enter(
        grad_attn, attn_full, qkv_width, out_b, out_a, finish_plain, [],
        [((head_width,), bf16)], 7, "back_out",
    )
    weighted_q, weighted_k, grad_v, inner = attend_back(
        q_low, k_low, v_low, attn_low, grad_heads, log_sums, qkv_lin, head_gain, cosine, sine, bias
    )
    factor = inverses**3 * lax.psum(inner, "row") / D
    q_lin, k_lin = qkv_lin[:, :head_width], qkv_lin[:, head_width : 2 * head_width]
    grad_qkv = jnp.concatenate(
        [
            (inverses[:, 0:1] * weighted_q - q_lin * factor[:, 0:1]).astype(bf16),
            (inverses[:, 1:2] * weighted_k - k_lin * factor[:, 1:2]).astype(bf16),
            grad_v,
        ],
        axis=1,
    )
    grad_qkv_in, qkv_dlow = leave(grad_qkv, attn_full, 0, qkv_b, qkv_a, 8, "back_qkv")
    grad_in = from_tokens((grad_hidden + grad_qkv_in).astype(bf16)).astype(f32)

    down_raise_part = dot_tn(down_low, dm_all)
    down_lower_part = dot_tn(act_low, down_dlow)
    ffn_raise_part = dot_tn(ffn_low, grad_ffn)
    ffn_lower_part = dot_tn(ffn_dlow, h_all)
    out_raise_part = dot_tn(out_low, da_all)
    out_lower_part = dot_tn(attn_low, out_dlow)
    qkv_raise_part = dot_tn(qkv_low, grad_qkv)
    qkv_lower_part = dot_tn(qkv_dlow, x_all)

    parts = jnp.concatenate(
        [
            qkv_lower_part.reshape(3, RANK, D),
            out_raise_part[None],
            ffn_lower_part.reshape(2, RANK, D),
            down_raise_part[None],
        ]
    )
    parts = parts.astype(bf16).reshape(7, RANK, col_count, width).transpose(2, 0, 1, 3)
    parts = lax.all_to_all(parts, "col", 0, 0, tiled=True)
    placed = [place(slab_ids[:, p], parts[:, p]) for p in range(7)]
    col_split = lax.psum(jnp.stack(placed).astype(bf16), ("tok", "row")).astype(f32)
    own = jnp.concatenate(
        [
            qkv_raise_part[p * RANK : (p + 1) * RANK, p * head_width : (p + 1) * head_width]
            for p in range(3)
        ]
        + [out_lower_part.T]
        + [
            ffn_raise_part[p * RANK : (p + 1) * RANK, p * ff_width : (p + 1) * ff_width]
            for p in range(2)
        ]
        + [down_lower_part.T],
        axis=1,
    ).astype(bf16)
    every = lax.all_gather(own, ("tok", "col"), axis=0)
    starts = [0, 1, 2, 3, 4]
    starts = [s * head_width for s in starts] + [
        4 * head_width + (k + 1) * ff_width for k in range(3)
    ]
    row_split = [
        place(adapter_ids[:, p], every[:, :, starts[p] : starts[p + 1]]) for p in range(7)
    ]
    return (
        layer_out,
        grad_in,
        col_split[0:3].swapaxes(2, 3),
        jnp.stack(row_split[0:3]),
        row_split[3].swapaxes(1, 2),
        col_split[3],
        col_split[4:6].swapaxes(2, 3),
        jnp.stack(row_split[4:6]),
        row_split[6].swapaxes(1, 2),
        col_split[6],
    )


def solution(mesh):
    return jax.shard_map(
        on_device,
        mesh=mesh,
        in_specs=(
            P(("tok", "row"), "col"),
            P(("tok", "row"), "col"),
            P(None, "col", "row"),
            P("row", "col"),
            P(None, "col", "row"),
            P("row", "col"),
            P(None, "row"),
            P(None, "col"),
            P(None, None, "col", None),
            P(None, None, None, "row"),
            P(None, "row", None),
            P(None, None, "col"),
            P(None, None, "col", None),
            P(None, None, None, "row"),
            P(None, "row", None),
            P(None, None, "col"),
            P(),
            P(),
        ),
        out_specs=(
            P(("tok", "row"), "col"),
            P(("tok", "row"), "col"),
            P(None, None, "col", None),
            P(None, None, None, "row"),
            P(None, "row", None),
            P(None, None, "col"),
            P(None, None, "col", None),
            P(None, None, None, "row"),
            P(None, "row", None),
            P(None, None, "col"),
        ),
        check_vma=False,
    )
```

time: 1510 us -> 870 us (0.58)
  waiting for transfers between devices: 641 us -> 161 us
  Pallas kernels: 0 us -> 382 us
  matrix products: 367 us -> 39.6 us
  other arithmetic: 145 us -> 52.8 us
  blocking collectives: 147 us -> 91.7 us
  local copies, waits for them, and re-layouts: 115 us -> 71.9 us
  loops' own time: 35.5 us -> 0 us
  starting transfers between devices: 25.5 us -> 44.4 us
    pallas_call x0 -> x10, Pallas kernels: none -> 382 us  [the longest x4 181 us: gather_matmul(): pl.pallas_call(functools.partial(gather_matmul_kernel, finish, start, ext...]
    dot_general x87 -> x0, matrix products: 337 us -> none  [the longest x12 96.5 us: dot(): return jnp.dot(left, right, preferred_element_type=f32)]
    all_gather x4 -> x3, waiting for transfers between devices: 237 us -> 0.02 us  [gather_weight(): return lax.all_gather(part, ('col', 'tok'), axis=0, tiled=True)]
    all_gather x4 -> x0, waiting for transfers between devices: 161 us -> none  [gather_tokens(): lax.all_gather(values, 'row', axis=0, tiled=True)]
    reduce_scatter x4 -> x0, waiting for transfers between devices: 151 us -> none  [scatter_tokens(): lax.psum_scatter(values, 'row', scatter_dimension=0, tiled=True).astype(f32)]
    all_to_all x4 -> x0, blocking collectives: 115 us -> none  [the longest x2 62.5 us: to_tokens(): mixed = lax.all_to_all(mixed, 'col', 0, 0, tiled=True)]
    all_to_all x0 -> x4, waiting for transfers between devices: none -> 80.2 us  [the longest x2 54.4 us: to_tokens(): mixed = lax.all_to_all(mixed, 'col', 0, 0, tiled=True)]
    another operation x2 -> x0, loops' own time: 35.5 us -> none  [the longest x1 17.7 us: attend_backward(): lax.scan(one_block, (zeros_init, zeros_init), (block_starts, log_sums))]
  transfers between devices with their start and end apart: 20 -> 15, of which waited for: 17 -> 9; matrix products, arithmetic and copies ran while one was open for 20% -> 10% of each run, Pallas kernels for 0% -> 16%
where the time goes in v2:
time: 870 us; the launch traced here: 859 us
  Pallas kernels  382 us (44%)
  waiting for transfers between devices  161 us (19%)
  blocking collectives  91.7 us (11%)
  local copies, waits for them, and re-layouts  71.9 us (8%)
  other arithmetic  52.8 us (6%)
  starting transfers between devices  44.4 us (5%)
  matrix products  39.6 us (5%)
  between operations  16.1 us (2%)
    pallas_call x4, Pallas kernels, gather_matmul(): pl.pallas_call(functools.partial(gather_matmul_kernel, finish, start, ext...  181 us
    pallas_call x4, Pallas kernels, matmul_scatter(): pl.pallas_call(functools.partial(matmul_scatter_kernel, start), in_specs=...  170 us
    all_to_all x2, waiting for transfers between devices, to_tokens(): mixed = lax.all_to_all(mixed, 'col', 0, 0, tiled=True)  54.4 us
    all_gather x1, blocking collectives, on_device(): gains = lax.all_gather(post_gain, 'col', axis=1, tiled=True)  40.5 us
    all_to_all x2, waiting for transfers between devices, from_tokens(): mixed = lax.all_to_all(mixed, 'col', 0, 0, tiled=True)  39.5 us
    all_to_all x2, waiting for transfers between devices, to_tokens(): mixed = lax.all_to_all(values, 'row', 0, 0, tiled=True)  25.9 us
    psum x1, blocking collectives, on_device(): factor = inverses ** 3 * lax.psum(inner, 'row') / D  25.7 us
    psum x1, blocking collectives, on_device(): inverses = lax.rsqrt(lax.psum(squares, 'row') / D + norm_eps)  25.5 us
  transfers between devices with their start and end apart: 15, of which 9 were waited for; matrix products, arithmetic and copies ran while one was open for 10% of the time, Pallas kernels for 16%

profile of v2, /device:TPU:0, one launch (start us, length us, event | category | flops | bytes accessed | tf_op | source)
XLA Modules:
  0.0 859.5 jit_solution(18252982861451129025)
XLA Ops:
  24.8 6.3 all-to-all-start.2
  38.9 6.2 fusion.25
  47.2 7.8 copy.122
  56.3 4.4 all-to-all-start
  63.7 12.1 %all-to-all-done = bf16[4,288,512]{2,1,0:T(8,128)(2,1)} async-done(((bf16[4,288,512]{2,1,0:T(8,128)(2,1)}), bf16[4,288,512]{2,1,0:T(8,128)(2,1)}, u32[]{:S(2)}, u32[]{:S(2)}) %all-to-all-start) | async-done | bytes 1179680 | tf_op jit(solution)/shard_map/all_to_all | solution.py:381
  80.1 13.7 %all-to-all-done.5 = bf16[4,288,512]{2,1,0:T(8,128)(2,1)S(1)} async-done(((bf16[4,288,512]{2,1,0:T(8,128)(2,1)}), bf16[4,288,512]{2,1,0:T(8,128)(2,1)S(1)}, u32[]{:S(2)}, u32[]{:S(2)}) %all-to-all-start.5) | async-done | bytes 1179680 | tf_op jit(solution)/shard_map/all_to_all | solution.py:381
  93.9 4.9 all-to-all-start.1
  98.7 40.5 %all_gather.17 = bf16[2,2048]{1,0:T(2,128)(2,1)} all-gather(bf16[2,512]{1,0:T(2,128)(2,1)S(1)} %copy-done.86), channel_id=1, replica_groups=mesh['tok'=2,'row'=4,'col'=4] {'col'}, dimensions={1}, use_global_device_ids=true | all-gather | bytes 10240 | tf_op jit(solution)/shard_map/all_gather | solution.py:564
  159.9 54.4 %all-to-all-done.6 = bf16[4,288,512]{2,1,0:T(8,128)(2,1)S(1)} async-done(((bf16[4,288,512]{2,1,0:T(8,128)(2,1)}), bf16[4,288,512]{2,1,0:T(8,128)(2,1)S(1)}, u32[]{:S(2)}, u32[]{:S(2)}) %all-to-all-start.6) | async-done | bytes 1179680 | tf_op jit(solution)/shard_map/all_to_all | solution.py:382
  216.3 43.7 %enter_qkv.1 = (bf16[4,288,2048]{2,1,0:T(8,128)(2,1)}, bf16[4,288,48]{2,1,0:T(8,128)(2,1)}, f32[4,288,1536]{2,1,0:T(8,128)}, f32[4,288,2]{2,1,0:T(8,128)}) custom-call(bf16[288,2048]{1,0:T(8,128)(2,1)} %bitcast.932, bf16[2048,2048]{1,0:T(8,128)(2,1)} %all-gather.5.cloned.1.call-done.w_hbm, bf16[48,2048]{1,0:T(8,128)(2,1)} %bitcast.961, ...), custom_call_target="tpu_custom_call" | custom-call | flops 7247757312 | bytes 6291456 | tf_op jit(solution)/shard_map/enter_qkv/pallas_call | solution.py:171
  260.1 6.9 copy.99
  267.0 25.5 %psum.21 = f32[1152,2]{1,0:T(8,128)S(1)} all-reduce(f32[1152,2]{1,0:T(8,128)S(1)} %bitcast.952), channel_id=1, replica_groups=mesh['tok'=2,'row'=4,'col'=4] {'row'}, use_global_device_ids=true, to_apply=%region_0.1 | all-reduce | flops 2304 | bytes 18432 | tf_op jit(solution)/shard_map/psum | solution.py:578
  293.7 13.3 %attend.1 = (bf16[1152,512]{1,0:T(8,128)(2,1)S(1)}, bf16[1152,512]{1,0:T(8,128)(2,1)S(1)}, bf16[1152,512]{1,0:T(8,128)(2,1)S(1)}, bf16[1152,512]{1,0:T(8,128)(2,1)}, f32[4,1,1152]{2,1,0:T(1,128)S(1)}) custom-call(f32[1152,1536]{1,0:T(8,128)} %bitcast.921, f32[1152,1536]{1,0:T(8,128)} %bitcast.922, f32[1152,1536]{1,0:T(8,128)} %bitcast.923, ...), custom_call_target="tpu_custom_call" | custom-call | flops 2717908992 | bytes 11796480 | tf_op jit(solution)/shard_map/attend/pallas_call | solution.py:332
  309.1 35.5 %leave_out.1 = (f32[288,2048]{1,0:T(8,128)}, bf16[4,288,16]{2,1,0:T(8,128)(2,1)}) custom-call(bf16[4,288,512]{2,1,0:T(8,128)(2,1)} %bitcast.937, bf16[2048,2048]{1,0:T(8,128)(2,1)} %all-gather.5.cloned.1.call-done.w_hbm, bf16[16,512]{1,0:T(8,128)(2,1)} %bitcast.963, bf16[16,2048]{1,0:T(8,128)(2,1)} %bitcast.950), custom_call_target="tpu_custom_call" | custom-call | flops 2415919104 | bytes 2097152 | tf_op jit(solution)/shard_map/leave_out/pallas_call | solution.py:238
  349.7 49.0 %enter_ffn.1 = (bf16[4,288,2048]{2,1,0:T(8,128)(2,1)}, bf16[4,288,32]{2,1,0:T(8,128)(2,1)}, bf16[4,288,2048]{2,1,0:T(8,128)(2,1)}, bf16[4,288,2048]{2,1,0:T(8,128)(2,1)}, bf16[4,288,2048]{2,1,0:T(8,128)(2,1)}) custom-call(bf16[288,2048]{1,0:T(8,128)(2,1)} %fusion.10.x_ref, bf16[2048,4096]{1,0:T(8,128)(2,1)} %all-gather.7.cloned.1.call-done.w_hbm, ...), custom_call_target="tpu_custom_call" | custom-call | flops 19327352832 | bytes 16777216 | tf_op jit(solution)/shard_map/enter_ffn/pallas_call | solution.py:171
  398.8 43.2 %leave_down.1 = (f32[288,2048]{1,0:T(8,128)}, bf16[4,288,16]{2,1,0:T(8,128)(2,1)}) custom-call(bf16[4,288,2048]{2,1,0:T(8,128)(2,1)} %get-tuple-element.46.y_ref, bf16[2048,2048]{1,0:T(8,128)(2,1)} %all-gather.9.cloned.1.call-done.w_hbm, bf16[16,2048]{1,0:T(8,128)(2,1)} %bitcast.974, bf16[16,2048]{1,0:T(8,128)(2,1)} %bitcast.976), custom_call_target="tpu_custom_call" | custom-call | flops 9663676416 | bytes 8388608 | tf_op jit(solution)/shard_map/leave_down/pallas_call | solution.py:238
  447.2 47.7 %back_down.1 = (bf16[4,288,2048]{2,1,0:T(8,128)(2,1)}, bf16[4,288,16]{2,1,0:T(8,128)(2,1)}, bf16[4,288,4096]{2,1,0:T(8,128)(2,1)}) custom-call(bf16[288,2048]{1,0:T(8,128)(2,1)} %subtract_convert_fusion.1.x_ref, bf16[2048,2048]{1,0:T(8,128)(2,1)} %all-gather.9.cloned.1.call-done.w_hbm, bf16[16,2048]{1,0:T(8,128)(2,1)} %bitcast.977, ...), custom_call_target="tpu_custom_call" | custom-call | flops 9663676416 | bytes 8388608 | tf_op jit(solution)/shard_map/back_down/pallas_call | solution.py:171
  494.9 6.2 fusion
  501.0 53.0 %back_ffn.1 = (f32[288,2048]{1,0:T(8,128)}, bf16[4,288,32]{2,1,0:T(8,128)(2,1)}) custom-call(bf16[4,288,4096]{2,1,0:T(8,128)(2,1)} %get-tuple-element.50.y_ref, bf16[2048,4096]{1,0:T(8,128)(2,1)} %all-gather.7.cloned.1.call-done.w_hbm, bf16[32,4096]{1,0:T(8,128)(2,1)} %fusion.35.f2_ref.f1_ref, bf16[32,2048]{1,0:T(8,128)(2,1)} %bitcast.966), custom_call_target="tpu_custom_call" | custom-call | flops 19327352832 | bytes 16777216 | tf_op jit(solution)/shard_map/back_ffn/pallas_call | solution.py:238
  566.8 6.9 copy.102
  573.7 40.1 %back_out.1 = (bf16[4,288,2048]{2,1,0:T(8,128)(2,1)}, bf16[4,288,16]{2,1,0:T(8,128)(2,1)}, bf16[4,288,512]{2,1,0:T(8,128)(2,1)}) custom-call(bf16[288,2048]{1,0:T(8,128)(2,1)} %get-tuple-element.98.x_ref, bf16[2048,2048]{1,0:T(8,128)(2,1)} %all-gather.5.cloned.1.call-done.w_hbm, bf16[16,2048]{1,0:T(8,128)(2,1)} %bitcast.951, bf16[16,512]{1,0:T(8,128)(2,1)} %bitcast.964), custom_call_target="tpu_custom_call" | custom-call | flops 2415919104 | bytes 2097152 | tf_op jit(solution)/shard_map/back_out/pallas_call | solution.py:171
  620.9 17.3 %attend_back.1 = (f32[1152,512]{1,0:T(8,128)}, f32[1152,512]{1,0:T(8,128)}, bf16[1152,512]{1,0:T(8,128)(2,1)S(1)}, f32[1152,2]{1,0:T(8,128)S(1)}) custom-call(bf16[1152,512]{1,0:T(8,128)(2,1)S(1)} %copy-done.3, bf16[1152,512]{1,0:T(8,128)(2,1)S(1)} %copy-done.5, bf16[1152,512]{1,0:T(8,128)(2,1)} %copy-done.6, bf16[1152,512]{1,0:T(8,128)(2,1)} %get-tuple-element.44.o_ref, ...), custom_call_target="tpu_custom_call" | custom-call | flops 6794772480 | bytes 17694720 | tf_op jit(solution)/shard_map/attend_back/pallas_call | solution.py:347
  638.2 25.7 %psum.22 = f32[1152,2]{1,0:T(8,128)S(1)} all-reduce(f32[1152,2]{1,0:T(8,128)S(1)} %get-tuple-element.58), channel_id=1, replica_groups=mesh['tok'=2,'row'=4,'col'=4] {'row'}, use_global_device_ids=true, to_apply=%region_5.6 | all-reduce | flops 2304 | bytes 18432 | tf_op jit(solution)/shard_map/psum | solution.py:609
  671.6 38.8 %back_qkv.1 = (f32[288,2048]{1,0:T(8,128)}, bf16[4,288,48]{2,1,0:T(8,128)(2,1)}) custom-call(bf16[4,288,1536]{2,1,0:T(8,128)(2,1)} %bitcast.931, bf16[2048,2048]{1,0:T(8,128)(2,1)} %all-gather.5.cloned.1.call-done.w_hbm, bf16[48,1536]{1,0:T(8,128)(2,1)} %fusion.37.f2_ref.f1_ref, bf16[48,2048]{1,0:T(8,128)(2,1)} %bitcast.962), custom_call_target="tpu_custom_call" | custom-call | flops 7247757312 | bytes 6291456 | tf_op jit(solution)/shard_map/back_qkv/pallas_call | solution.py:238
  726.3 13.6 %all-to-all-done.9 = bf16[4,7,16,512]{3,2,1,0:T(8,128)(2,1)S(1)} async-done(((bf16[4,7,16,512]{3,2,1,0:T(8,128)(2,1)}), bf16[4,7,16,512]{3,2,1,0:T(8,128)(2,1)S(1)}, u32[]{:S(2)}, u32[]{:S(2)}) %all-to-all-start.9) | async-done | bytes 458784 | tf_op jit(solution)/shard_map/all_to_all | solution.py:640
  740.0 6.1 all-to-all-start.3
  748.5 26.4 %all-to-all-done.3 = bf16[4,288,512]{2,1,0:T(8,128)(2,1)} async-done(((bf16[4,288,512]{2,1,0:T(8,128)(2,1)}), bf16[4,288,512]{2,1,0:T(8,128)(2,1)}, u32[]{:S(2)}, u32[]{:S(2)}) %all-to-all-start.3) | async-done | bytes 1179680 | tf_op jit(solution)/shard_map/all_to_all | solution.py:390
  782.6 13.1 %all-to-all-done.7 = bf16[4,288,512]{2,1,0:T(8,128)(2,1)S(1)} async-done(((bf16[4,288,512]{2,1,0:T(8,128)(2,1)}), bf16[4,288,512]{2,1,0:T(8,128)(2,1)S(1)}, u32[]{:S(2)}, u32[]{:S(2)}) %all-to-all-start.7) | async-done | bytes 1179680 | tf_op jit(solution)/shard_map/all_to_all | solution.py:390
  799.3 9.6 %all-reduce.6.cloned.1.call-done = bf16[7,8,16,512]{3,2,1,0:T(8,128)(2,1)} async-done(((bf16[7,8,16,512]{3,2,1,0:T(8,128)(2,1)}), bf16[7,8,16,512]{3,2,1,0:T(8,128)(2,1)}) %all-reduce.6.cloned.1.call-update) | async-done | bytes 917520 | tf_op jit(solution)/shard_map/psum | solution.py:642
  811.2 4.6 all-to-all-start.8
  819.3 9.9 %all-to-all-done.8 = bf16[4,288,512]{2,1,0:T(8,128)(2,1)} async-done(((bf16[4,288,512]{2,1,0:T(8,128)(2,1)}), bf16[4,288,512]{2,1,0:T(8,128)(2,1)}, u32[]{:S(2)}, u32[]{:S(2)}) %all-to-all-start.8) | async-done | bytes 1179680 | tf_op jit(solution)/shard_map/all_to_all | solution.py:391
  832.2 8.6 all-gather.11.cloned.1.call-done
  (371 shorter events, 148.5 us)
Async XLA Ops:
  7.2 209.1 %all-gather.5.cloned.1.call-start = ((), (), s32[]{:S(2)}) async-start(), calls=%async_computation.10 | async-start | bytes 9437184 | tf_op jit(solution)/shard_map/all_gather | solution.py:375
  16.1 333.7 %all-gather.7.cloned.1.call-start = ((), (), s32[]{:S(2)}) async-start(), calls=%async_computation.11 | async-start | bytes 18874368 | tf_op jit(solution)/shard_map/all_gather | solution.py:375
  20.1 378.6 %all-gather.9.cloned.1.call-start = ((), (), s32[]{:S(2)}) async-start(), calls=%async_computation.12 | async-start | bytes 9437184 | tf_op jit(solution)/shard_map/all_gather | solution.py:375
  24.8 31.5 %all-to-all-start.2 = ((bf16[4,7,16,512]{3,2,1,0:T(8,128)(2,1)}), bf16[4,7,16,512]{3,2,1,0:T(8,128)(2,1)S(1)}, u32[]{:S(2)}, u32[]{:S(2)}) async-start(bf16[4,7,16,512]{3,2,1,0:T(8,128)(2,1)} %copy.88), calls=%async_computation.2 | async-start | bytes 917504 | tf_op jit(solution)/shard_map/all_to_all | solution.py:552
  56.3 23.7 %copy-start.26 = (bf16[2,8,16,2048]{3,2,1,0:T(8,128)(2,1)S(1)}, bf16[2,8,16,2048]{3,2,1,0:T(8,128)(2,1)}, u32[]{:S(2)}) copy-start(bf16[2,8,16,2048]{3,2,1,0:T(8,128)(2,1)} %param.31) | copy-start | bytes 3145732
  56.3 19.5 %all-to-all-start = ((bf16[4,288,512]{2,1,0:T(8,128)(2,1)}), bf16[4,288,512]{2,1,0:T(8,128)(2,1)}, u32[]{:S(2)}, u32[]{:S(2)}) async-start(bf16[4,288,512]{2,1,0:T(8,128)(2,1)} %bitcast), calls=%async_computation | async-start | bytes 2359296 | tf_op jit(solution)/shard_map/all_to_all | solution.py:381
  75.9 18.0 %all-to-all-start.5 = ((bf16[4,288,512]{2,1,0:T(8,128)(2,1)}), bf16[4,288,512]{2,1,0:T(8,128)(2,1)S(1)}, u32[]{:S(2)}, u32[]{:S(2)}) async-start(bf16[4,288,512]{2,1,0:T(8,128)(2,1)} %bitcast.73), calls=%async_computation.5 | async-start | bytes 2359296 | tf_op jit(solution)/shard_map/all_to_all | solution.py:381
  80.1 64.1 %copy-start.97 = (f32[64]{0:T(128)S(1)}, f32[64]{0:T(128)}, u32[]{:S(2)}) copy-start(f32[64]{0:T(128)} %multiply_exponential_fusion) | copy-start | bytes 772
  93.9 52.5 %copy-start.21 = (bf16[4,288,512]{2,1,0:T(8,128)(2,1)}, bf16[4,288,512]{2,1,0:T(8,128)(2,1)S(1)}, u32[]{:S(2)}) copy-start(bf16[4,288,512]{2,1,0:T(8,128)(2,1)S(1)} %all-to-all-done.5) | copy-start | bytes 3538948
  93.9 52.9 %all-to-all-start.1 = ((bf16[4,288,512]{2,1,0:T(8,128)(2,1)}), bf16[4,288,512]{2,1,0:T(8,128)(2,1)}, u32[]{:S(2)}, u32[]{:S(2)}) async-start(bf16[4,288,512]{2,1,0:T(8,128)(2,1)} %all-to-all-done), calls=%async_computation.1 | async-start | bytes 2359296 | tf_op jit(solution)/shard_map/all_to_all | solution.py:382
  146.8 67.5 %all-to-all-start.6 = ((bf16[4,288,512]{2,1,0:T(8,128)(2,1)}), bf16[4,288,512]{2,1,0:T(8,128)(2,1)S(1)}, u32[]{:S(2)}, u32[]{:S(2)}) async-start(bf16[4,288,512]{2,1,0:T(8,128)(2,1)} %copy-done.21), calls=%async_computation.6 | async-start | bytes 2359296 | tf_op jit(solution)/shard_map/all_to_all | solution.py:382
  309.1 35.5 %copy-start.2 = (bf16[1152,512]{1,0:T(8,128)(2,1)}, bf16[1152,512]{1,0:T(8,128)(2,1)S(1)}, u32[]{:S(2)}) copy-start(bf16[1152,512]{1,0:T(8,128)(2,1)S(1)} %get-tuple-element.52.ql_ref) | copy-start | bytes 3538948
  309.1 35.5 %copy-start.7 = (f32[4,1,1152]{2,1,0:T(1,128)}, f32[4,1,1152]{2,1,0:T(1,128)S(1)}, u32[]{:S(2)}) copy-start(f32[4,1,1152]{2,1,0:T(1,128)S(1)} %get-tuple-element.56.lse_ref) | copy-start | bytes 55300
  447.2 47.7 %copy-start.37 = (bf16[4,288,32]{2,1,0:T(8,128)(2,1)S(1)}, bf16[4,288,32]{2,1,0:T(8,128)(2,1)}, u32[]{:S(2)}) copy-start(bf16[4,288,32]{2,1,0:T(8,128)(2,1)} %get-tuple-element.72) | copy-start | bytes 221188
  573.7 40.2 %copy-start.28 = (bf16[4,288,16]{2,1,0:T(8,128)(2,1)S(1)}, bf16[4,288,16]{2,1,0:T(8,128)(2,1)}, u32[]{:S(2)}) copy-start(bf16[4,288,16]{2,1,0:T(8,128)(2,1)} %get-tuple-element.64) | copy-start | bytes 110596
  638.2 27.7 %copy-start.49 = (f32[1152]{0:T(1024)S(1)}, f32[1152]{0:T(1024)}, u32[]{:S(2)}) copy-start(f32[1152]{0:T(1024)} %get-tuple-element.76) | copy-start | bytes 13828
  638.2 27.7 %copy-start.50 = (f32[1152]{0:T(1024)S(1)}, f32[1152]{0:T(1024)}, u32[]{:S(2)}) copy-start(f32[1152]{0:T(1024)} %get-tuple-element.77) | copy-start | bytes 13828
  671.6 38.8 %copy-start.15 = (f32[288,2048]{1,0:T(8,128)S(1)}, f32[288,2048]{1,0:T(8,128)}, u32[]{:S(2)}) copy-start(f32[288,2048]{1,0:T(8,128)} %copy-done.14) | copy-start | bytes 7077892
  722.3 17.6 %all-to-all-start.9 = ((bf16[4,7,16,512]{3,2,1,0:T(8,128)(2,1)}), bf16[4,7,16,512]{3,2,1,0:T(8,128)(2,1)S(1)}, u32[]{:S(2)}, u32[]{:S(2)}) async-start(bf16[4,7,16,512]{3,2,1,0:T(8,128)(2,1)} %copy.106), calls=%async_computation.9 | async-start | bytes 917504 | tf_op jit(solution)/shard_map/all_to_all | solution.py:640
  725.9 20.4 %copy-start.81 = (f32[8]{0:T(128)S(1)}, f32[8]{0:T(128)}, u32[]{:S(2)}) copy-start(f32[8]{0:T(128)} %get-tuple-element.279) | copy-start | bytes 100
  725.9 20.4 %copy-start.82 = (f32[8]{0:T(128)S(1)}, f32[8]{0:T(128)}, u32[]{:S(2)}) copy-start(f32[8]{0:T(128)} %get-tuple-element.280) | copy-start | bytes 100
  726.2 20.5 %copy-start.73 = (f32[8]{0:T(128)S(1)}, f32[8]{0:T(128)}, u32[]{:S(2)}) copy-start(f32[8]{0:T(128)} %get-tuple-element.271) | copy-start | bytes 100
  726.2 20.5 %copy-start.74 = (f32[8]{0:T(128)S(1)}, f32[8]{0:T(128)}, u32[]{:S(2)}) copy-start(f32[8]{0:T(128)} %get-tuple-element.272) | copy-start | bytes 100
  726.3 20.5 %copy-start.75 = (f32[8]{0:T(128)S(1)}, f32[8]{0:T(128)}, u32[]{:S(2)}) copy-start(f32[8]{0:T(128)} %get-tuple-element.273) | copy-start | bytes 100
  726.3 20.5 %copy-start.76 = (f32[8]{0:T(128)S(1)}, f32[8]{0:T(128)}, u32[]{:S(2)}) copy-start(f32[8]{0:T(128)} %get-tuple-element.274) | copy-start | bytes 100
  740.0 34.9 %all-to-all-start.3 = ((bf16[4,288,512]{2,1,0:T(8,128)(2,1)}), bf16[4,288,512]{2,1,0:T(8,128)(2,1)}, u32[]{:S(2)}, u32[]{:S(2)}) async-start(bf16[4,288,512]{2,1,0:T(8,128)(2,1)} %bitcast.919), calls=%async_computation.3 | async-start | bytes 2359296 | tf_op jit(solution)/shard_map/all_to_all | solution.py:390
  746.1 62.8 %all-reduce.6.cloned.1.call-start = ((), (), s32[]{:S(2)}) async-start(), calls=%async_computation.13 | async-start | bytes 1835008 | tf_op jit(solution)/shard_map/psum | solution.py:642
  746.6 31.9 %copy-start.27 = (bf16[4,288,16]{2,1,0:T(8,128)(2,1)S(1)}, bf16[4,288,16]{2,1,0:T(8,128)(2,1)}, u32[]{:S(2)}) copy-start(bf16[4,288,16]{2,1,0:T(8,128)(2,1)} %get-tuple-element.73) | copy-start | bytes 110596
  774.9 20.8 %all-to-all-start.7 = ((bf16[4,288,512]{2,1,0:T(8,128)(2,1)}), bf16[4,288,512]{2,1,0:T(8,128)(2,1)S(1)}, u32[]{:S(2)}, u32[]{:S(2)}) async-start(bf16[4,288,512]{2,1,0:T(8,128)(2,1)} %bitcast.917), calls=%async_computation.7 | async-start | bytes 2359296 | tf_op jit(solution)/shard_map/all_to_all | solution.py:390
  778.4 62.4 %all-gather.11.cloned.1.call-start = ((), (), s32[]{:S(2)}) async-start(), calls=%async_computation.14 | async-start | bytes 2359296 | tf_op jit(solution)/shard_map/all_gather | solution.py:656
  795.7 15.5 %all-to-all-start.4 = ((bf16[4,288,512]{2,1,0:T(8,128)(2,1)}), bf16[4,288,512]{2,1,0:T(8,128)(2,1)S(1)}, u32[]{:S(2)}, u32[]{:S(2)}) async-start(bf16[4,288,512]{2,1,0:T(8,128)(2,1)} %all-to-all-done.3), calls=%async_computation.4 | async-start | bytes 2359296 | tf_op jit(solution)/shard_map/all_to_all | solution.py:391
  811.2 18.0 %all-to-all-start.8 = ((bf16[4,288,512]{2,1,0:T(8,128)(2,1)}), bf16[4,288,512]{2,1,0:T(8,128)(2,1)}, u32[]{:S(2)}, u32[]{:S(2)}) async-start(bf16[4,288,512]{2,1,0:T(8,128)(2,1)} %copy-done.20), calls=%async_computation.8 | async-start | bytes 2359296 | tf_op jit(solution)/shard_map/all_to_all | solution.py:391
  (84 other events, 572.1 us)
Sparse Core Ops, SparseCore 0:
  16.2 112.3 all-gather.4
  130.8 175.6 all-gather.6
  308.1 80.1 all-gather.8
  750.3 58.5 all-reduce.5
  810.9 29.8 all-gather.10

commit v3 on v2

v3 whole, which is shorter than its diff:
```python
import functools
import math

import jax
import jax.numpy as jnp
from jax import lax
from jax.experimental import pallas as pl
from jax.experimental.pallas import tpu as pltpu
from jax.sharding import PartitionSpec as P

D = 2048
HEAD_DIM = 128
RANK = 16
ADAPTERS = 8
PROMPT = 1024
CONT_LEN = 128
SLAB = 1152

adapter_scale = 2.0
norm_eps = 1e-06
rope_base = 500000.0
very_low = -1e30
bf16 = jnp.bfloat16
f32 = jnp.float32
log2_scale = math.log2(math.e) / math.sqrt(HEAD_DIM)
score_scale = 1.0 / math.sqrt(HEAD_DIM)
BLOCK = 384
TILE = 512
MESH = pl.DeviceIdType.MESH


def mm(left, right):
    return jnp.dot(left, right, preferred_element_type=f32)


def mm_nt(left, right):
    return lax.dot_general(left, right, (((1,), (1,)), ((), ())), preferred_element_type=f32)


class Links:
    def __init__(self, send_sem, recv_sem, local_sem):
        self.row, self.col = lax.axis_index("row"), lax.axis_index("col")
        self.xn, self.yn, self.dg = self.row ^ 1, self.row ^ 2, self.row ^ 3
        self.send_sem, self.recv_sem, self.local_sem = send_sem, recv_sem, local_sem
        self.used, self.local_used = 0, 0

    def take(self, count):
        self.used += count
        return self.used - count

    def copy(self, source, target, index, recv_index, row, col=None):
        return pltpu.make_async_remote_copy(
            src_ref=source,
            dst_ref=target,
            send_sem=self.send_sem.at[index],
            recv_sem=self.recv_sem.at[recv_index],
            device_id={"row": row, "col": self.col if col is None else col},
            device_id_type=MESH,
        )

    def local(self, source, target):
        self.local_used += 1
        return pltpu.make_async_copy(source, target, self.local_sem.at[self.local_used - 1])

    def greet(self, rows=2, columns=False):
        barrier = pltpu.get_barrier_semaphore()
        places = [(self.row ^ step, self.col) for step in range(1, rows + 1)]
        if columns:
            places += [(self.row, self.col ^ step) for step in range(1, 4)]
        for row, col in places:
            pl.semaphore_signal(
                barrier, inc=1, device_id={"row": row, "col": col}, device_id_type=MESH
            )
        pl.semaphore_wait(barrier, len(places))


class Exchange:
    def __init__(self, links, axis, piece_at, slot_at):
        self.links, self.axis = links, axis
        self.me = links.row if axis == "row" else links.col
        self.piece_at, self.slot_at = piece_at, slot_at
        self.base = links.take(3)
        self.own = links.local(piece_at(self.me), slot_at(self.me))

    def copy(self, source, target, step):
        links, other, index = self.links, self.me ^ step, self.base + step - 1
        row, col = (other, links.col) if self.axis == "row" else (links.row, other)
        return links.copy(source, target, index, index, row, col)

    def start(self):
        for step in range(1, 4):
            self.copy(self.piece_at(self.me ^ step), self.slot_at(self.me), step).start()
        self.own.start()

    def arrived(self):
        for step in range(1, 4):
            landed = self.slot_at(self.me ^ step)
            self.copy(landed, landed, step).wait_recv()
        self.own.wait()

    def sent(self):
        for step in range(1, 4):
            self.copy(self.piece_at(self.me ^ step), self.slot_at(self.me), step).wait_send()


class Turn:
    def __init__(self, links, inward, source_ref, middle_ref, target_ref, parts=1):
        size, width = middle_ref.shape[1], middle_ref.shape[2]
        self.hops = []
        for part in range(parts):
            start, count = part * (size // parts), size // parts
            rows = pl.ds(start, count)

            def features(ref, col, rows=rows):
                return ref.at[rows, pl.ds(pl.multiple_of(col * width, width), width)]

            def middle(key, rows=rows):
                return middle_ref.at[key, rows]

            if inward:
                first = Exchange(
                    links, "row", lambda key, rows=rows: source_ref.at[key, rows], middle
                )
                second = Exchange(
                    links, "col", middle, lambda key, features=features: features(target_ref, key)
                )
            else:
                first = Exchange(
                    links, "col", lambda key, features=features: features(source_ref, key), middle
                )
                second = Exchange(
                    links,
                    "row",
                    middle,
                    lambda key, start=start, count=count: target_ref.at[
                        pl.ds(pl.multiple_of(key * size + start, 16), count)
                    ],
                )
            self.hops.append((first, second))

    def start(self):
        for first, _ in self.hops:
            first.start()

    def relay(self):
        for first, second in self.hops:
            first.arrived()
            second.start()

    def finish(self):
        for _, second in self.hops:
            second.arrived()
        for first, second in self.hops:
            first.sent()
            second.sent()


def gather(links, all_ref, work, before=None, after=None):
    me, xn, yn, dg = links.row, links.xn, links.yn, links.dg
    half = all_ref.shape[1] // 2
    top, low = pl.ds(0, half), pl.ds(half, half)
    base = links.take(6)

    def move(owner, part, index, other):
        place = all_ref.at[owner, part]
        return links.copy(place, place, base + index, base + index, other)

    sends = [move(me, top, 0, xn), move(me, low, 1, yn), move(me, low, 2, xn), move(me, top, 3, yn)]
    for copy in sends:
        copy.start()
    if before:
        before()
    if work:
        work(me)
    move(xn, top, 0, xn).wait_recv()
    sends.append(move(xn, top, 4, yn))
    sends[-1].start()
    move(yn, low, 1, yn).wait_recv()
    sends.append(move(yn, low, 5, xn))
    sends[-1].start()
    if after:
        after()
    move(xn, low, 2, xn).wait_recv()
    if work:
        work(xn)
    move(yn, top, 3, yn).wait_recv()
    if work:
        work(yn)
    move(dg, top, 4, yn).wait_recv()
    move(dg, low, 5, xn).wait_recv()
    if work:
        work(dg)
    for copy in sends:
        copy.wait_send()


def scatter(links, product, o_ref, out_buf, relay_buf, final_buf, after=None):
    me, xn, yn, dg = links.row, links.xn, links.yn, links.dg
    count = o_ref.shape[0]
    half = count // 2
    top, low = slice(0, half), slice(half, count)
    base = links.take(6)

    def move(source, target, index, other):
        return links.copy(source, target, base + index, base + index, other)

    def keep(slot):
        def store(cols, value):
            out_buf[slot, :, cols] = value.astype(bf16)

        return store

    def own(cols, value):
        o_ref[:, cols] = value

    def add(slot, rows, relay):
        out_buf[slot, rows] = (
            out_buf[slot, rows].astype(f32) + relay_buf[relay].astype(f32)
        ).astype(bf16)

    product(dg, keep(0))
    copies = [
        move(out_buf.at[0, top], relay_buf.at[0], 0, xn),
        move(out_buf.at[0, low], relay_buf.at[1], 1, yn),
        move(out_buf.at[1, top], final_buf.at[0, top], 2, xn),
        move(out_buf.at[2, low], final_buf.at[1, low], 3, yn),
        move(out_buf.at[2, top], final_buf.at[1, top], 4, yn),
        move(out_buf.at[1, low], final_buf.at[0, low], 5, xn),
    ]
    copies[0].start()
    copies[1].start()
    product(xn, keep(1))
    copies[2].start()
    if after:
        after()
    product(yn, keep(2))
    copies[3].start()
    copies[0].wait_recv()
    add(2, top, 0)
    copies[4].start()
    copies[1].wait_recv()
    add(1, low, 1)
    copies[5].start()
    product(me, own)
    for copy in copies[2:]:
        copy.wait_recv()
    for copy in copies:
        copy.wait_send()


def each_tile(width, step, body):
    @pl.loop(0, width // step)
    def _(tile):
        body(pl.multiple_of(tile * step, step))


def lower(rows, factor):
    return (adapter_scale * mm_nt(rows, factor)).astype(bf16)


def leave_product(y_ref, w_ref, f1, f2_ref, f2_rows, low_ref):
    def product(owner, store):
        lowered = lower(y_ref[owner], f1)
        low_ref[owner] = lowered

        def body(at):
            cols = pl.ds(at, TILE)
            store(cols, mm_nt(y_ref[owner], w_ref[cols, :]) + mm(lowered, f2_ref[f2_rows, cols]))

        each_tile(w_ref.shape[0], TILE, body)

    return product


def inverse_of(values):
    return lax.rsqrt(jnp.mean(values * values, axis=1, keepdims=True) + norm_eps)


def norm_back(values, weighted):
    inverse = inverse_of(values)
    inner = jnp.mean(values * weighted, axis=1, keepdims=True)
    return inverse * weighted - values * (inverse**3 * inner)


def gated(gate, up):
    return gate * jax.nn.sigmoid(gate) * up


def gated_back(grad, gate, up):
    sig = jax.nn.sigmoid(gate)
    act = gate * sig
    return (grad * up * (sig + act * (1.0 - sig)), grad * act)


QKV_A, OUT_B, FFN_A, DOWN_B = slice(0, 48), slice(48, 64), slice(64, 96), slice(96, 112)
GAIN0, GAIN1 = slice(112, 113), slice(113, 114)


def share_stats(links, stat_ref, first, second):
    blank = jnp.zeros((6, first.shape[0]), f32)
    sums = [jnp.sum(value.T, axis=0, keepdims=True) for value in (first, second)]
    stat_ref[links.row] = jnp.concatenate(sums + [blank], axis=0)
    base = links.take(3)
    mine = stat_ref.at[links.row]
    copies = []
    for index, other in enumerate((links.xn, links.yn, links.dg)):
        copies.append(links.copy(mine, mine, base + index, base + index, other))
        copies[-1].start()
    for index, other in enumerate((links.xn, links.yn, links.dg)):
        theirs = stat_ref.at[other]
        links.copy(theirs, theirs, base + index, base + index, other).wait_recv()
    for copy in copies:
        copy.wait_send()
    return stat_ref[0] + stat_ref[1] + stat_ref[2] + stat_ref[3]


def lane_sums(values):
    return functools.reduce(
        jnp.add, [values[:, at : at + 128] for at in range(0, values.shape[1], 128)]
    )


def intake_kernel(
    x_ref, pieces_ref,
    own_ref, factors_ref,
    middle_ref, send_sem, recv_sem, local_sem,
):
    links = Links(send_sem, recv_sem, local_sem)
    links.greet(rows=3, columns=True)
    width = pieces_ref.shape[2]
    turn = Turn(links, True, x_ref, middle_ref, own_ref, 2)
    spread = Exchange(
        links,
        "col",
        lambda key: pieces_ref.at[key],
        lambda key: factors_ref.at[:, pl.ds(pl.multiple_of(key * width, width), width)],
    )
    turn.start()
    spread.start()
    turn.relay()
    spread.arrived()
    turn.finish()
    spread.sent()


def enter_qkv_kernel(
    x_ref, w_hbm, factors_ref, f2_ref,
    all_ref, low_ref, lin_ref, inv_ref,
    w_ref, sq_ref, stat_ref, send_sem, recv_sem, local_sem,
):
    links = Links(send_sem, recv_sem, local_sem)
    width = w_ref.shape[1]
    load = links.local(w_hbm.at[:, pl.ds(0, width)], w_ref)
    load.start()
    links.greet(rows=3)
    count = x_ref.shape[0]
    all_ref[links.row] = x_ref[...]

    def work(owner):
        lowered = lower(all_ref[owner], factors_ref[QKV_A])
        low_ref[owner] = lowered
        rows = all_ref[owner]
        third = width // 3
        for index in range(3):
            cols = slice(index * third, (index + 1) * third)
            value = mm(rows, w_ref[:, cols]) + mm(lowered, f2_ref[:, cols])
            lin_ref[owner, :, cols] = value
            if index < 2:
                place = pl.ds(pl.multiple_of(owner * count, 8), count)
                sq_ref[index, place] = lane_sums(value * value)

    gather(links, all_ref, work, load.wait)
    total = share_stats(links, stat_ref, sq_ref[0], sq_ref[1])
    inv_ref[...] = lax.rsqrt(total / D + norm_eps).T


def leave_out_kernel(
    y_ref, w_hbm, f1_ref, factors_ref, x_ref,
    lin_ref, low_ref, hidden_ref, all_ref,
    w_ref, out_buf, relay_buf, final_buf, send_sem, recv_sem, local_sem,
):
    links = Links(send_sem, recv_sem, local_sem)
    width = w_ref.shape[1]
    load = links.local(w_hbm.at[:, pl.ds(w_hbm.shape[1] - width, width)], w_ref)
    load.start()
    links.greet()
    load.wait()
    product = leave_product(y_ref, w_ref, f1_ref[...], factors_ref, OUT_B, low_ref)
    scatter(links, product, lin_ref, out_buf, relay_buf, final_buf)
    gain = factors_ref[GAIN0].astype(f32)

    @pl.loop(0, lin_ref.shape[0] // 16)
    def _(tile):
        rows = pl.ds(pl.multiple_of(tile * 16, 16), 16)
        value = lin_ref[rows] + final_buf[0, rows].astype(f32) + final_buf[1, rows].astype(f32)
        lin_ref[rows] = value
        hidden = x_ref[rows].astype(f32) + value * inverse_of(value) * gain
        hidden_ref[rows] = hidden
        all_ref[links.row, rows] = hidden.astype(bf16)

    gather(links, all_ref, None)


def ffn_kernel(h_ref, wg_ref, wu_ref, factors_ref, fg_ref, fu_ref, low_ref, gate_ref, up_ref, act_ref):
    @pl.when(pl.program_id(0) == 0)
    def _():
        low_ref[...] = lower(h_ref[...], factors_ref[FFN_A])

    lowered = low_ref[...]
    rank = lowered.shape[1] // 2
    for at in range(0, SLAB, BLOCK):
        rows = slice(at, at + BLOCK)
        gate = mm(h_ref[rows], wg_ref[...]) + mm(lowered[rows], fg_ref[...])
        up = mm(h_ref[rows], wu_ref[...]) + mm(lowered[rows], fu_ref[...])
        gate_ref[rows] = gate.astype(bf16)
        up_ref[rows] = up.astype(bf16)
        act_ref[rows] = gated(gate, up).astype(bf16)


def ffn(h_all, w, factors, f2):
    width = f2.shape[1] // 2
    step = 256
    tiles = width // step
    low = jax.ShapeDtypeStruct((SLAB, f2.shape[0]), bf16)
    wide = jax.ShapeDtypeStruct((SLAB, width), bf16)
    whole = lambda value: pl.BlockSpec(value.shape, lambda t: (0, 0))
    cols = lambda rows, base: pl.BlockSpec((rows, step), lambda t: (0, base * tiles + t))
    return pl.pallas_call(
        ffn_kernel,
        grid=(tiles,),
        in_specs=[whole(h_all), cols(D, 0), cols(D, 1), whole(factors)]
        + [cols(f2.shape[0], 0), cols(f2.shape[0], 1)],
        out_specs=[whole(low)] + [cols(SLAB, 0)] * 3,
        out_shape=[low, wide, wide, wide],
        compiler_params=pltpu.CompilerParams(vmem_limit_bytes=48 << 20),
        cost_estimate=pl.CostEstimate(
            flops=4 * SLAB * D * width, bytes_accessed=4 * D * width + 10 * SLAB * width,
            transcendentals=SLAB * width,
        ),
        name="ffn",
    )(h_all, w, w, factors, f2, f2)


def leave_down_kernel(
    y_ref, w_hbm, f1_ref, factors_ref, hidden_ref, cot_ref,
    low_ref, out_ref, dm_ref, own_cot_ref,
    w_ref, lin_ref, middle_ref, out_buf, relay_buf, final_buf, send_sem, recv_sem, local_sem,
):
    links = Links(send_sem, recv_sem, local_sem)
    load = links.local(w_hbm, w_ref)
    load.start()
    links.greet(rows=3, columns=True)
    turn = Turn(links, True, cot_ref, middle_ref, own_cot_ref)
    turn.start()
    load.wait()
    product = leave_product(y_ref, w_ref, f1_ref[...], factors_ref, DOWN_B, low_ref)
    scatter(links, product, lin_ref, out_buf, relay_buf, final_buf, turn.relay)
    turn.finish()
    gain = factors_ref[GAIN1].astype(f32)

    @pl.loop(0, lin_ref.shape[0] // 16)
    def _(tile):
        rows = pl.ds(pl.multiple_of(tile * 16, 16), 16)
        value = lin_ref[rows] + final_buf[0, rows].astype(f32) + final_buf[1, rows].astype(f32)
        out_ref[rows] = (hidden_ref[rows] + value * inverse_of(value) * gain).astype(bf16)
        dm_ref[rows] = norm_back(value, own_cot_ref[rows].astype(f32) * gain).astype(bf16)


def widen(source_ref, target_ref):
    @pl.loop(0, source_ref.shape[0] // 64)
    def _(tile):
        rows = pl.ds(pl.multiple_of(tile * 64, 64), 64)
        target_ref[rows] = source_ref[rows].astype(f32)


def back_down_kernel(
    dm_ref, w_hbm, factors_ref, f2_ref, gate_ref, up_ref, out_ref,
    all_ref, low_ref, grad_ref, final_ref,
    w_ref, middle_ref, out_buf, send_sem, recv_sem, local_sem,
):
    links = Links(send_sem, recv_sem, local_sem)
    load = links.local(w_hbm, w_ref)
    load.start()
    links.greet(rows=3, columns=True)
    width = w_ref.shape[1]
    all_ref[links.row] = dm_ref[...]
    turn = Turn(links, False, out_ref, middle_ref, out_buf)

    def before():
        turn.start()
        load.wait()

    def work(owner):
        lowered = lower(all_ref[owner], factors_ref[DOWN_B])
        low_ref[owner] = lowered

        def body(at):
            cols, far = pl.ds(at, TILE), pl.ds(pl.multiple_of(width + at, TILE), TILE)
            grad = mm(all_ref[owner], w_ref[:, cols]) + mm(lowered, f2_ref[:, cols])
            gate, up = gate_ref[owner, :, cols].astype(f32), up_ref[owner, :, cols].astype(f32)
            grad_gate, grad_up = gated_back(grad, gate, up)
            grad_ref[owner, :, cols] = grad_gate.astype(bf16)
            grad_ref[owner, :, far] = grad_up.astype(bf16)

        each_tile(width, TILE, body)

    waited = []

    def work_and_relay(owner):
        work(owner)
        waited.append(True)
        if len(waited) == 3:
            turn.relay()

    gather(links, all_ref, work_and_relay, before)
    turn.finish()
    widen(out_buf, final_ref)


def back_ffn_kernel(
    y_ref, w_hbm, f1_ref, factors_ref, cot_ref, attn_ref,
    low_ref, hidden_ref, da_ref,
    w_ref, lin_ref, out_buf, relay_buf, final_buf, send_sem, recv_sem, local_sem,
):
    links = Links(send_sem, recv_sem, local_sem)
    load = links.local(w_hbm, w_ref)
    load.start()
    links.greet()
    load.wait()
    product = leave_product(y_ref, w_ref, f1_ref[...], factors_ref, FFN_A, low_ref)
    scatter(links, product, lin_ref, out_buf, relay_buf, final_buf)
    gain = factors_ref[GAIN0].astype(f32)

    @pl.loop(0, lin_ref.shape[0] // 16)
    def _(tile):
        rows = pl.ds(pl.multiple_of(tile * 16, 16), 16)
        value = lin_ref[rows] + final_buf[0, rows].astype(f32) + final_buf[1, rows].astype(f32)
        value = value + cot_ref[rows].astype(f32)
        hidden_ref[rows] = value
        da_ref[rows] = norm_back(attn_ref[rows], value * gain).astype(bf16)


def mm_tn(left, right):
    return lax.dot_general(left, right, (((0,), (0,)), ((), ())), preferred_element_type=f32)


def back_out_kernel(
    da_ref, w_hbm, factors_ref, f2_ref, out_low_ref, attn_ref, down_low_ref, down_dlow_ref,
    ffn_low_ref, ffn_dlow_ref, dm_hbm, act_hbm, grad_hbm, h_hbm,
    all_ref, low_ref, heads_ref, down_raise_ref, down_lower_ref, ffn_raise_ref, ffn_lower_ref,
    out_raise_ref, out_lower_ref,
    w_ref, dm_ref, act_ref, grad_ref, h_ref, send_sem, recv_sem, local_sem,
):
    links = Links(send_sem, recv_sem, local_sem)
    width = w_ref.shape[1]
    load = links.local(w_hbm.at[:, pl.ds(w_hbm.shape[1] - width, width)], w_ref)
    loads = [
        links.local(source, target)
        for source, target in (
            (dm_hbm, dm_ref), (act_hbm, act_ref), (grad_hbm, grad_ref), (h_hbm, h_ref)
        )
    ]
    load.start()
    all_ref[links.row] = da_ref[...]
    links.greet()

    def before():
        for copy in loads:
            copy.start()
        load.wait()

    def after():
        for copy in loads:
            copy.wait()
        rank, half = down_low_ref.shape[1], grad_ref.shape[1] // 2
        down_raise_ref[...] = mm_tn(down_low_ref[...], dm_ref[...])
        down_lower_ref[...] = mm_tn(down_dlow_ref[...], act_ref[...])
        ffn_lower_ref[...] = mm_tn(ffn_dlow_ref[...], h_ref[...])
        both = mm_tn(ffn_low_ref[...], grad_ref[...])
        ffn_raise_ref[:, :half] = both[:rank, :half]
        ffn_raise_ref[:, half:] = both[rank:, half:]

    def work(owner):
        lowered = lower(all_ref[owner], factors_ref[OUT_B])
        low_ref[owner] = lowered
        heads_ref[owner] = (mm(all_ref[owner], w_ref[...]) + mm(lowered, f2_ref[...])).astype(bf16)

    gather(links, all_ref, work, before, after)
    raised, lowered = 0.0, 0.0
    for owner in range(4):
        raised = raised + mm_tn(out_low_ref[owner], all_ref[owner])
        lowered = lowered + mm_tn(low_ref[owner], attn_ref[owner])
    out_raise_ref[...] = raised
    out_lower_ref[...] = lowered


def prepare_kernel(
    wq_ref, wk_ref, dv_ref, lin_ref, inv_ref, inner_ref, f1_ref, low_ref, x_hbm,
    grad_ref, dlow_ref, raise_ref, lower_ref,
    x_ref, total_ref, stat_ref, send_sem, recv_sem, local_sem,
):
    links = Links(send_sem, recv_sem, local_sem)
    load = links.local(x_hbm, x_ref)
    load.start()
    third = wq_ref.shape[1]
    links.greet(rows=3)
    total = share_stats(links, stat_ref, inner_ref[0], inner_ref[1])
    total_ref[...] = total.T / D

    @pl.loop(0, SLAB // 32)
    def _(tile):
        rows = pl.ds(pl.multiple_of(tile * 32, 32), 32)
        inverse = inv_ref[rows]
        factor = inverse**3 * total_ref[rows]
        for index, source in enumerate((wq_ref, wk_ref)):
            cols = slice(index * third, (index + 1) * third)
            one = slice(index, index + 1)
            value = inverse[:, one] * source[rows] - lin_ref[rows, cols] * factor[:, one]
            grad_ref[rows, cols] = value.astype(bf16)
        grad_ref[rows, 2 * third :] = dv_ref[rows]

    dlow_ref[...] = lower(grad_ref[...], f1_ref[...])
    raised = mm_tn(low_ref[...], grad_ref[...])
    for index in range(3):
        cols = slice(index * third, (index + 1) * third)
        raise_ref[:, cols] = raised[index * RANK : (index + 1) * RANK, cols]
    load.wait()
    lower_ref[...] = mm_tn(dlow_ref[...], x_ref[...])


def back_qkv_kernel(
    grad_ref, dlow_ref, w_hbm, factors_ref, hidden_ref,
    final_ref,
    w_ref, sum_ref, own_ref, middle_ref, turn_buf, out_buf, relay_buf, final_buf,
    send_sem, recv_sem, local_sem,
):
    links = Links(send_sem, recv_sem, local_sem)
    load = links.local(w_hbm.at[:, pl.ds(0, w_ref.shape[1])], w_ref)
    load.start()
    links.greet(rows=3, columns=True)
    count = grad_ref.shape[1]

    def product(owner, store):
        def body(at):
            cols = pl.ds(at, TILE)
            value = mm_nt(grad_ref[owner], w_ref[cols, :])
            store(cols, value + mm(dlow_ref[owner], factors_ref[QKV_A, cols]))

        each_tile(w_ref.shape[0], TILE, body)

    load.wait()
    scatter(links, product, sum_ref, out_buf, relay_buf, final_buf)

    @pl.loop(0, count // 16)
    def _(tile):
        rows = pl.ds(pl.multiple_of(tile * 16, 16), 16)
        value = sum_ref[rows] + final_buf[0, rows].astype(f32) + final_buf[1, rows].astype(f32)
        own_ref[rows] = (value + hidden_ref[rows]).astype(bf16)

    turn = Turn(links, False, own_ref, middle_ref, turn_buf, 2)
    turn.start()
    turn.relay()
    turn.finish()
    widen(turn_buf, final_ref)


VMEM = pl.BlockSpec(memory_space=pltpu.VMEM)
ANY = pl.BlockSpec(memory_space=pl.ANY)


def linked(kernel, number, operands, outs, scratch, flops):
    specs = [ANY if isinstance(value, tuple) else VMEM for value in operands]
    values = [value[0] if isinstance(value, tuple) else value for value in operands]
    return pl.pallas_call(
        kernel,
        in_specs=specs,
        out_specs=[VMEM] * len(outs),
        out_shape=[jax.ShapeDtypeStruct(shape, kind) for shape, kind in outs],
        scratch_shapes=[pltpu.VMEM(shape, kind) for shape, kind in scratch]
        + [
            pltpu.SemaphoreType.DMA((32,)),
            pltpu.SemaphoreType.DMA((32,)),
            pltpu.SemaphoreType.DMA((8,)),
        ],
        compiler_params=pltpu.CompilerParams(
            collective_id=number, has_side_effects=True, vmem_limit_bytes=60 << 20
        ),
        cost_estimate=pl.CostEstimate(
            flops=flops, bytes_accessed=flops // 400, transcendentals=0
        ),
        name=kernel.__name__,
    )(*values)


def scatter_buffers(count):
    return [((3, count, D), bf16), ((2, count // 2, D), bf16), ((2, count, D), bf16)]


def score_blocks(k_ref, q_block, bias_ref, start, stop):
    parts = []
    if start:
        parts.append(mm_nt(k_ref[0:start], q_block) + bias_ref[0:start])
    own = mm_nt(k_ref[start:stop], q_block) + bias_ref[start:stop]
    keys = lax.broadcasted_iota(jnp.int32, own.shape, 0)
    queries = lax.broadcasted_iota(jnp.int32, own.shape, 1)
    parts.append(jnp.where(keys <= queries, own, very_low))
    return parts

def attend_kernel(q_ref, k_ref, v_ref, inv_ref, gain_ref, cos_ref, sin_ref, bias_ref,
                  ql_ref, kl_ref, vl_ref, o_ref, lse_ref):
    for source, target, index in ((q_ref, ql_ref, 0), (k_ref, kl_ref, 1)):
        normed = source[...] * inv_ref[:, index:index+1] * gain_ref[index:index+1, :]
        target[...] = (normed * cos_ref[...] + pltpu.roll(normed, HEAD_DIM // 2, 1) * sin_ref[...]).astype(bf16)
    values = v_ref[...].astype(bf16)
    vl_ref[...] = values
    values_t = v_ref[...].T.astype(bf16)
    for start in range(0, SLAB, BLOCK):
        stop = start + BLOCK
        parts = score_blocks(kl_ref, ql_ref[start:stop], bias_ref, start, stop)
        top = functools.reduce(jnp.maximum, [jnp.max(p, axis=0, keepdims=True) for p in parts]) * log2_scale
        total, out, at = 0.0, 0.0, 0
        for part in parts:
            shifted = jnp.exp2(part * log2_scale - top)
            total = total + jnp.sum(shifted, axis=0, keepdims=True)
            out = out + mm(values_t[:, at:at+part.shape[0]], shifted.astype(bf16))
            at += part.shape[0]
        o_ref[start:stop] = (out / total).T.astype(bf16)
        lse_ref[0, :, start:stop] = top + jnp.log2(total)

def attend_back_kernel(ql_ref, kl_ref, vl_ref, o_ref, do_ref, lse_ref, q_ref, k_ref, gain_ref, cos_ref, sin_ref, bias_ref,
                       wq_ref, wk_ref, dv_ref, sum_ref, dk_sum, dv_sum):
    keys_t = kl_ref[...].astype(f32).T.astype(bf16)
    delta_all = jnp.sum((do_ref[...].astype(f32) * o_ref[...].astype(f32)).T, axis=0, keepdims=True)
    dk_sum[...] = jnp.zeros_like(dk_sum)
    dv_sum[...] = jnp.zeros_like(dv_sum)
    def unrotate(values):
        return values * cos_ref[...] - pltpu.roll(values, HEAD_DIM // 2, 1) * sin_ref[...]
    dq_parts = []
    for start in range(0, SLAB, BLOCK):
        stop = start + BLOCK
        queries, grads = ql_ref[start:stop], do_ref[start:stop]
        parts = score_blocks(kl_ref, queries, bias_ref, start, stop)
        lse, delta = lse_ref[0, :, start:stop], delta_all[:, start:stop]
        at, dq = 0, 0.0
        for part in parts:
            span = slice(at, at + part.shape[0])
            probs = jnp.exp2(part * log2_scale - lse)
            dv_sum[span] += mm(probs.astype(bf16), grads)
            dscore = (probs * (mm_nt(vl_ref[span], grads) - delta)).astype(bf16)
            dk_sum[span] += mm(dscore, queries)
            dq = dq + mm(keys_t[:, span], dscore)
            at += part.shape[0]
        dq_parts.append(dq.T)
    dq_all = jnp.concatenate(dq_parts, axis=0) * score_scale
    dv_ref[...] = dv_sum[...].astype(bf16)
    wq = unrotate(dq_all) * gain_ref[0:1, :]
    wk = unrotate(dk_sum[...] * score_scale) * gain_ref[1:2, :]
    wq_ref[...] = wq.astype(wq_ref.dtype)
    wk_ref[...] = wk.astype(wk_ref.dtype)
    first = pl.program_id(0) == 0
    for index, (weighted, source) in enumerate(((wq, q_ref), (wk, k_ref))):
        product = weighted * source[...]

        @pl.when(first)
        def _():
            sum_ref[index] = product

        @pl.when(jnp.logical_not(first))
        def _():
            sum_ref[index] += product


def attend_specs(heads):
    col = lambda base: pl.BlockSpec((SLAB, HEAD_DIM), lambda h: (0, base * heads + h))
    whole = lambda shape: pl.BlockSpec(shape, lambda h: (0,) * len(shape))
    return col, whole

def attend(qkv_lin, inverses, gains, cosine, sine, bias):
    heads = qkv_lin.shape[1] // (3 * HEAD_DIM)
    col, whole = attend_specs(heads)
    low = jax.ShapeDtypeStruct((SLAB, heads * HEAD_DIM), bf16)
    return pl.pallas_call(
        attend_kernel, grid=(heads,),
        in_specs=[col(0), col(1), col(2), whole((SLAB, 8)), pl.BlockSpec((2, HEAD_DIM), lambda h: (0, h)),
                  whole((SLAB, HEAD_DIM)), whole((SLAB, HEAD_DIM)), whole((SLAB, 1))],
        out_specs=[col(0)] * 4 + [pl.BlockSpec((1, 1, SLAB), lambda h: (h, 0, 0))],
        out_shape=[low] * 4 + [jax.ShapeDtypeStruct((heads, 1, SLAB), f32)],
        compiler_params=pltpu.CompilerParams(vmem_limit_bytes=48 << 20),
        cost_estimate=pl.CostEstimate(flops=heads*4*SLAB*SLAB*HEAD_DIM, bytes_accessed=heads*SLAB*HEAD_DIM*20, transcendentals=heads*SLAB*SLAB),
        name="attend",
    )(qkv_lin, qkv_lin, qkv_lin, inverses, gains, cosine, sine, bias)

def attend_back(ql, kl, vl, o, do, lse, qkv_lin, gains, cosine, sine, bias):
    heads = ql.shape[1] // HEAD_DIM
    col, whole = attend_specs(heads)
    wide = jax.ShapeDtypeStruct(ql.shape, f32)
    return pl.pallas_call(
        attend_back_kernel, grid=(heads,),
        in_specs=[col(0)] * 5 + [pl.BlockSpec((1, 1, SLAB), lambda h: (h, 0, 0)), col(0), col(1), pl.BlockSpec((2, HEAD_DIM), lambda h: (0, h)),
                  whole((SLAB, HEAD_DIM)), whole((SLAB, HEAD_DIM)), whole((SLAB, 1))],
        out_specs=[col(0)] * 3 + [whole((2, SLAB, HEAD_DIM))],
        out_shape=[wide, wide, jax.ShapeDtypeStruct(ql.shape, bf16), jax.ShapeDtypeStruct((2, SLAB, HEAD_DIM), f32)],
        scratch_shapes=[pltpu.VMEM((SLAB, HEAD_DIM), f32)] * 2,
        compiler_params=pltpu.CompilerParams(vmem_limit_bytes=48 << 20),
        cost_estimate=pl.CostEstimate(flops=heads*10*SLAB*SLAB*HEAD_DIM, bytes_accessed=heads*SLAB*HEAD_DIM*30, transcendentals=heads*SLAB*SLAB),
        name="attend_back",
    )(ql, kl, vl, o, do, lse, qkv_lin, qkv_lin, gains, cosine, sine, bias)


def dot(left, right):
    return jnp.dot(left, right, preferred_element_type=f32)


def dot_nt(left, right):
    return lax.dot_general(left, right, (((1,), (1,)), ((), ())), preferred_element_type=f32)


def dot_tn(left, right):
    return lax.dot_general(left, right, (((0,), (0,)), ((), ())), preferred_element_type=f32)


def gather_weight(local):
    half = local.shape[0] // lax.axis_size("tok")
    part = lax.dynamic_slice_in_dim(local, lax.axis_index("tok") * half, half, 0)
    return lax.all_gather(part, ("col", "tok"), axis=0, tiled=True)


def to_tokens(values):
    rows, cols = lax.axis_size("row"), lax.axis_size("col")
    width = values.shape[1]
    mixed = lax.all_to_all(values, "row", 0, 0, tiled=True)
    mixed = lax.all_to_all(mixed, "col", 0, 0, tiled=True)
    return mixed.reshape(cols, SLAB // rows, width).transpose(1, 0, 2).reshape(SLAB // rows, -1)


def from_tokens(values):
    rows, cols = lax.axis_size("row"), lax.axis_size("col")
    count = values.shape[0]
    mixed = values.reshape(count, cols, -1).transpose(1, 0, 2).reshape(cols * count, -1)
    mixed = lax.all_to_all(mixed, "col", 0, 0, tiled=True)
    return lax.all_to_all(mixed, "row", 0, 0, tiled=True)


def reorder(values, outer, inner):
    if outer == 1 or inner == 1:
        return values
    rest = values.shape[0] // (outer * inner)
    shape = (outer, inner, rest) + values.shape[1:]
    return values.reshape(shape).swapaxes(0, 1).reshape(values.shape)


def gather_tokens(values):
    rows, per_slab = lax.axis_size("row"), lax.axis_size("row") // lax.axis_size("col")
    return reorder(lax.all_gather(values, "row", axis=0, tiled=True), rows, per_slab)


def scatter_tokens(values):
    rows, per_slab = lax.axis_size("row"), lax.axis_size("row") // lax.axis_size("col")
    values = reorder(values.astype(bf16), per_slab, rows)
    return lax.psum_scatter(values, "row", scatter_dimension=0, tiled=True).astype(f32)


def token_places(length):
    slot_ids = jnp.arange(SLAB, dtype=jnp.int32)
    return jnp.where(slot_ids < PROMPT, slot_ids, length + (slot_ids - PROMPT) % CONT_LEN)


def rotation(places, head_size):
    half_dim = head_size // 2
    frequency = jnp.exp(
        -(2.0 * jnp.arange(half_dim, dtype=f32) / head_size) * math.log(rope_base)
    )
    angles = places.astype(f32)[:, None] * frequency[None, :]
    return (jnp.cos(angles), jnp.sin(angles))


def pick(adapters, ids):
    onehot = (ids[:, None] == jnp.arange(adapters.shape[0], dtype=jnp.int32)).astype(adapters.dtype)
    return jnp.tensordot(onehot, adapters, axes=1)


def place(ids, gradients):
    onehot = (jnp.arange(ADAPTERS, dtype=jnp.int32)[:, None] == ids[None, :]).astype(f32)
    total = 0.0
    for index in range(gradients.shape[0]):
        weight = onehot[:, index].reshape((ADAPTERS,) + (1,) * (gradients.ndim - 1))
        total = total + weight * gradients[index][None].astype(f32)
    return total


def block_diagonal(factors):
    count = len(factors)
    lines = []
    for index, factor in enumerate(factors):
        blank = jnp.zeros_like(factor)
        lines.append(
            jnp.concatenate([factor if k == index else blank for k in range(count)], axis=1)
        )
    return jnp.concatenate(lines, axis=0)


def enter(x, w, f1, f2):
    everything = gather_tokens(x)
    lowered = (adapter_scale * dot_nt(everything, f1)).astype(bf16)
    return everything, lowered, dot(everything, w) + dot(lowered, f2)


def leave(y, w, f1, f2):
    lowered = (adapter_scale * dot_nt(y, f1)).astype(bf16)
    return scatter_tokens(dot_nt(y, w) + dot(lowered, f2)), lowered


def split_layer(
    layer_in, cotangent, attn_full, ffn_full, down_full, pieces, head_gain, qkv_b, out_a, ffn_b,
    down_a, tables,
):
    factors = lax.all_to_all(pieces, "col", 0, 0, tiled=True)
    factors = factors.transpose(1, 0, 2).reshape(-1, D)
    qkv_a, out_b, ffn_a, down_b = (factors[part] for part in (QKV_A, OUT_B, FFN_A, DOWN_B))
    gains = factors[GAIN0.start : GAIN1.stop].astype(f32)
    width = qkv_b.shape[1]
    head_width, ff_width = width // 3, ffn_b.shape[1] // 2
    x_own = to_tokens(layer_in)
    x_all, qkv_low, qkv_lin = enter(x_own, attn_full[:, :width], qkv_a, qkv_b)
    q_lin, k_lin = qkv_lin[:, :head_width], qkv_lin[:, head_width : 2 * head_width]
    squares = jnp.stack([jnp.sum(q_lin * q_lin, axis=1), jnp.sum(k_lin * k_lin, axis=1)], axis=1)
    inverses = lax.rsqrt(lax.psum(squares, "row") / D + norm_eps)
    inverses = jnp.concatenate([inverses] * 4, axis=1)
    q_low, k_low, v_low, attn_low, log_sums = attend(qkv_lin, inverses, head_gain, *tables)
    attn_lin, out_low = leave(attn_low, attn_full[:, width:], out_a, out_b)
    hidden = x_own.astype(f32) + attn_lin * inverse_of(attn_lin) * gains[0]
    h_all, ffn_low, ffn_lin = enter(hidden.astype(bf16), ffn_full, ffn_a, ffn_b)
    gate_lin, up_lin = ffn_lin[:, :ff_width], ffn_lin[:, ff_width:]
    act_low = gated(gate_lin, up_lin).astype(bf16)
    mlp_lin, down_low = leave(act_low, down_full, down_a, down_b)
    layer_out = hidden + mlp_lin * inverse_of(mlp_lin) * gains[1]
    layer_out = from_tokens(layer_out.astype(bf16)).astype(f32)
    grad_out = to_tokens(cotangent).astype(f32)
    grad_mlp = norm_back(mlp_lin, grad_out * gains[1]).astype(bf16)
    dm_all, down_dlow, grad_act = enter(grad_mlp, down_full, down_b, down_a)
    grad_ffn = jnp.concatenate(gated_back(grad_act, gate_lin, up_lin), axis=1).astype(bf16)
    grad_ffn_in, ffn_dlow = leave(grad_ffn, ffn_full, ffn_b, ffn_a)
    grad_hidden = grad_out + grad_ffn_in
    grad_attn = norm_back(attn_lin, grad_hidden * gains[0]).astype(bf16)
    da_all, out_dlow, grad_heads = enter(grad_attn, attn_full[:, width:], out_b, out_a)
    weighted_q, weighted_k, grad_v, inner = attend_back(
        q_low, k_low, v_low, attn_low, grad_heads.astype(bf16), log_sums, qkv_lin, head_gain, *tables
    )
    inner = lax.psum(jnp.sum(inner, axis=2).T, "row")
    factor = inverses[:, :2] ** 3 * inner / D
    grad_qkv = jnp.concatenate(
        [
            (inverses[:, 0:1] * weighted_q - q_lin * factor[:, 0:1]).astype(bf16),
            (inverses[:, 1:2] * weighted_k - k_lin * factor[:, 1:2]).astype(bf16),
            grad_v,
        ],
        axis=1,
    )
    grad_qkv_in, qkv_dlow = leave(grad_qkv, attn_full[:, :width], qkv_b, qkv_a)
    grad_in = from_tokens((grad_hidden + grad_qkv_in).astype(bf16)).astype(f32)
    return (
        layer_out, grad_in,
        dot_tn(down_low, dm_all), dot_tn(down_dlow, act_low),
        diagonal(dot_tn(ffn_low, grad_ffn), 2), dot_tn(ffn_dlow, h_all),
        dot_tn(out_low, da_all), dot_tn(out_dlow, attn_low),
        diagonal(dot_tn(qkv_low, grad_qkv), 3), dot_tn(qkv_dlow, x_all),
    )


def flat(values):
    return values.reshape((SLAB,) + values.shape[2:])


def cube(values):
    return values.reshape((4, SLAB // 4) + values.shape[1:])


def linked_layer(
    layer_in, cotangent, attn_full, ffn_full, down_full, pieces, head_gain, qkv_b, out_a, ffn_b,
    down_a, tables,
):
    count = SLAB // 4
    width = qkv_b.shape[1]
    head_width, ff_width = width // 3, ffn_b.shape[1] // 2
    buffers = scatter_buffers(count)
    per = 2 * SLAB * D
    tokens = ((4, count, D), bf16)

    def low_rows(size):
        return ((4, count, size), bf16)

    piece = (4, count, layer_in.shape[1])
    x_own, factors = linked(
        intake_kernel, 1,
        [cube(layer_in), pieces],
        [((count, D), bf16), ((128, D), bf16)],
        [(piece, bf16)],
        per * 128,
    )
    x_all, qkv_low, qkv_lin, inverses = linked(
        enter_qkv_kernel, 2,
        [x_own, (attn_full,), factors, qkv_b],
        [tokens, low_rows(48), ((4, count, width), f32), ((SLAB, 8), f32)],
        [((D, width), bf16), ((2, SLAB, 128), f32), ((4, 8, SLAB), f32)],
        per * width,
    )
    qkv_lin = flat(qkv_lin)
    q_low, k_low, v_low, attn_low, log_sums = attend(qkv_lin, inverses, head_gain, *tables)
    attn_lin, out_low, hidden, h_all = linked(
        leave_out_kernel, 3,
        [cube(attn_low), (attn_full,), out_a, factors, x_own],
        [((count, D), f32), low_rows(16), ((count, D), f32), tokens],
        [((D, head_width), bf16)] + buffers,
        per * head_width,
    )
    h_all = flat(h_all)
    ffn_low, gate_lin, up_lin, act_low = ffn(h_all, ffn_full, factors, ffn_b)
    down_low, own_out, grad_mlp, own_cot = linked(
        leave_down_kernel, 4,
        [cube(act_low), (down_full,), down_a, factors, hidden, cube(cotangent)],
        [low_rows(16)] + [((count, D), bf16)] * 3,
        [((D, ff_width), bf16), ((count, D), f32), (piece, bf16)] + buffers,
        per * ff_width,
    )
    dm_all, down_dlow, grad_ffn, layer_out = linked(
        back_down_kernel, 5,
        [grad_mlp, (down_full,), factors, down_a, cube(gate_lin), cube(up_lin), own_out],
        [tokens, low_rows(16), ((4, count, 2 * ff_width), bf16), (layer_in.shape, f32)],
        [((D, ff_width), bf16), (piece, bf16), (layer_in.shape, bf16)],
        per * ff_width,
    )
    ffn_dlow, grad_hidden, grad_attn = linked(
        back_ffn_kernel, 6,
        [grad_ffn, (ffn_full,), ffn_b, factors, own_cot, attn_lin],
        [low_rows(32), ((count, D), f32), ((count, D), bf16)],
        [((D, 2 * ff_width), bf16), ((count, D), f32)] + buffers,
        per * 2 * ff_width,
    )
    da_all, out_dlow, grad_heads, *early = linked(
        back_out_kernel, 7,
        [grad_attn, (attn_full,), factors, out_a, out_low, cube(attn_low), flat(down_low)]
        + [flat(down_dlow), ffn_low, flat(ffn_dlow), (flat(dm_all),), (act_low,)]
        + [(flat(grad_ffn),), (h_all,)],
        [tokens, low_rows(16), ((4, count, head_width), bf16), ((16, D), f32)]
        + [((16, ff_width), f32), ((16, 2 * ff_width), f32), ((32, D), f32)]
        + [((16, D), f32), ((16, head_width), f32)],
        [((D, head_width), bf16), ((SLAB, D), bf16), ((SLAB, ff_width), bf16)]
        + [((SLAB, 2 * ff_width), bf16), ((SLAB, D), bf16)],
        per * head_width,
    )
    weighted_q, weighted_k, grad_v, inner = attend_back(
        q_low, k_low, v_low, attn_low, flat(grad_heads), log_sums, qkv_lin, head_gain, *tables
    )
    grad_qkv, qkv_dlow, *late = linked(
        prepare_kernel, 8,
        [weighted_q, weighted_k, grad_v, qkv_lin, inverses, inner, qkv_b, flat(qkv_low)]
        + [(flat(x_all),)],
        [((SLAB, width), bf16), ((SLAB, 48), bf16), ((16, width), f32), ((48, D), f32)],
        [((SLAB, D), bf16), ((SLAB, 8), f32), ((4, 8, SLAB), f32)],
        per * 128,
    )
    (grad_in,) = linked(
        back_qkv_kernel, 9,
        [cube(grad_qkv), cube(qkv_dlow), (attn_full,), factors, grad_hidden],
        [(layer_in.shape, f32)],
        [((D, width), bf16), ((count, D), f32), ((count, D), bf16), (piece, bf16)]
        + [(layer_in.shape, bf16)]
        + buffers,
        per * width,
    )
    return (layer_out, grad_in, *early, *late)


def diagonal(values, count):
    width = values.shape[1] // count
    return jnp.concatenate(
        [
            values[k * RANK : (k + 1) * RANK, k * width : (k + 1) * width]
            for k in range(count)
        ],
        axis=1,
    )


def on_device(
    layer_in,
    cotangent,
    qkv_weight,
    out_weight,
    ffn_weight,
    down_weight,
    qk_gain,
    post_gain,
    qkv_lower,
    qkv_raise,
    out_lower,
    out_raise,
    ffn_lower,
    ffn_raise,
    down_lower,
    down_raise,
    adapter_ids,
    prompt_len,
):
    col_count = lax.axis_size("col")
    group_base = lax.axis_index("tok") * col_count
    group = group_base + lax.axis_index("col")
    slab_ids = lax.dynamic_slice_in_dim(adapter_ids, group_base, col_count, 0)
    own_ids = lax.dynamic_index_in_dim(adapter_ids, group, 0, keepdims=False)
    length = lax.dynamic_index_in_dim(prompt_len, group, 0, keepdims=False)
    width = layer_in.shape[1]
    head_width = qkv_weight.shape[2]
    ff_width = ffn_weight.shape[2]

    local = jnp.concatenate([qkv_weight.transpose(1, 0, 2).reshape(width, -1), out_weight.T], axis=1)
    attn_full = gather_weight(local)
    ffn_full = gather_weight(ffn_weight.transpose(1, 0, 2).reshape(width, -1))
    down_full = gather_weight(down_weight.T)

    pieces = jnp.concatenate(
        [pick(qkv_lower[p].swapaxes(1, 2), slab_ids[:, p]) for p in range(3)]
        + [pick(out_raise, slab_ids[:, 3])]
        + [pick(ffn_lower[p].swapaxes(1, 2), slab_ids[:, 4 + p]) for p in range(2)]
        + [pick(down_raise, slab_ids[:, 6])]
        + [jnp.broadcast_to(jnp.pad(post_gain, ((0, 14), (0, 0))), (col_count, RANK, width))],
        axis=1,
    )
    qkv_b = block_diagonal([pick(qkv_raise[p], own_ids[p : p + 1])[0] for p in range(3)])
    out_a = pick(out_lower, own_ids[3:4])[0].T
    ffn_b = block_diagonal([pick(ffn_raise[p], own_ids[4 + p : 5 + p])[0] for p in range(2)])
    down_a = pick(down_lower, own_ids[6:7])[0].T

    cosine, sine = rotation(token_places(length), HEAD_DIM)
    cosine = jnp.concatenate([cosine, cosine], axis=1)
    sine = jnp.concatenate([-sine, sine], axis=1)
    slots = jnp.arange(SLAB, dtype=jnp.int32)
    bias = jnp.where((slots < length) | (slots >= PROMPT), 0.0, very_low)[:, None].astype(f32)

    layer = linked_layer if (lax.axis_size("row"), col_count) == (4, 4) else split_layer
    (
        layer_out, grad_in, down_raise_part, down_lower_part, ffn_raise_part, ffn_lower_part,
        out_raise_part, out_lower_part, qkv_raise_part, qkv_lower_part,
    ) = layer(
        layer_in, cotangent, attn_full, ffn_full, down_full, pieces, qk_gain.astype(f32), qkv_b,
        out_a, ffn_b, down_a, (cosine, sine, bias),
    )

    def col_sums(parts, numbers):
        count = len(numbers)
        parts = jnp.concatenate(parts).astype(bf16).reshape(count, RANK, col_count, width)
        parts = lax.all_to_all(parts.transpose(2, 0, 1, 3), "col", 0, 0, tiled=True)
        placed = [place(slab_ids[:, p], parts[:, k]) for k, p in enumerate(numbers)]
        return lax.psum(jnp.stack(placed).astype(bf16), ("tok", "row")).astype(f32)

    def row_sums(parts, numbers):
        own = jnp.concatenate(parts, axis=1).astype(bf16)
        every = lax.all_gather(own, ("tok", "col"), axis=0)
        sums, at = [], 0
        for p in numbers:
            size = ff_width if p > 3 else head_width
            sums.append(place(adapter_ids[:, p], every[:, :, at : at + size]))
            at += size
        return sums

    early_cols = col_sums([out_raise_part, ffn_lower_part, down_raise_part], [3, 4, 5, 6])
    early_rows = row_sums([out_lower_part, ffn_raise_part, down_lower_part], [3, 4, 5, 6])
    late_cols = col_sums([qkv_lower_part], [0, 1, 2])
    late_rows = row_sums([qkv_raise_part], [0, 1, 2])
    return (
        layer_out,
        grad_in,
        late_cols.swapaxes(2, 3),
        jnp.stack(late_rows),
        early_rows[0].swapaxes(1, 2),
        early_cols[0],
        early_cols[1:3].swapaxes(2, 3),
        jnp.stack(early_rows[1:3]),
        early_rows[3].swapaxes(1, 2),
        early_cols[3],
    )


def solution(mesh):
    return jax.shard_map(
        on_device,
        mesh=mesh,
        in_specs=(
            P(("tok", "row"), "col"),
            P(("tok", "row"), "col"),
            P(None, "col", "row"),
            P("row", "col"),
            P(None, "col", "row"),
            P("row", "col"),
            P(None, "row"),
            P(None, "col"),
            P(None, None, "col", None),
            P(None, None, None, "row"),
            P(None, "row", None),
            P(None, None, "col"),
            P(None, None, "col", None),
            P(None, None, None, "row"),
            P(None, "row", None),
            P(None, None, "col"),
            P(),
            P(),
        ),
        out_specs=(
            P(("tok", "row"), "col"),
            P(("tok", "row"), "col"),
            P(None, None, "col", None),
            P(None, None, None, "row"),
            P(None, "row", None),
            P(None, None, "col"),
            P(None, None, "col", None),
            P(None, None, None, "row"),
            P(None, "row", None),
            P(None, None, "col"),
        ),
        check_vma=False,
    )
```

time: 870 us -> 823 us (0.946)
  Pallas kernels: 382 us -> 618 us
  waiting for transfers between devices: 161 us -> 49 us
  blocking collectives: 91.7 us -> 39.5 us
  starting transfers between devices: 44.4 us -> 6.98 us
  local copies, waits for them, and re-layouts: 71.9 us -> 42.4 us
  matrix products: 39.6 us -> 15.2 us
  other arithmetic: 52.8 us -> 30.2 us
    pallas_call x8 -> x10, Pallas kernels: 351 us -> 589 us  [the longest x9 560 us: linked(): pl.pallas_call(kernel, in_specs=specs, out_specs=[VMEM] * len(outs), out_...]
    all_to_all x10 -> x2, waiting for transfers between devices: 143 us -> 10.6 us  [col_sums(): parts = lax.all_to_all(parts.transpose(2, 0, 1, 3), 'col', 0, 0, tiled=True)]
    psum x2 -> x0, blocking collectives: 51.2 us -> none  [the longest x1 25.7 us: on_device(): factor = inverses ** 3 * lax.psum(inner, 'row') / D]
    all_gather x3, waiting for transfers between devices: 0.02 us -> 38.3 us  [gather_weight(): return lax.all_gather(part, ('col', 'tok'), axis=0, tiled=True)]
    all_to_all x10 -> x2, starting transfers between devices: 44.2 us -> 6.77 us  [col_sums(): parts = lax.all_to_all(parts.transpose(2, 0, 1, 3), 'col', 0, 0, tiled=True)]
    dot_general x8 -> x0, matrix products: 24.1 us -> none  [dot_tn(): lax.dot_general(left, right, (((0,), (0,)), ((), ())), preferred_element_...]
    convert_element_type x9 -> x4, other arithmetic: 18.1 us -> 2.2 us  [the longest x1 1.16 us: col_sums(): return lax.psum(jnp.stack(placed).astype(bf16), ('tok', 'row')).astype(f32)]
    dot_general x4 -> x0, local copies, waits for them, and re-layouts: 14.7 us -> none  [dot_tn(): lax.dot_general(left, right, (((0,), (0,)), ((), ())), preferred_element_...]
  transfers between devices with their start and end apart: 15 -> 7, of which waited for: 9 -> 4; matrix products, arithmetic and copies ran while one was open for 10% -> 6% of each run, Pallas kernels for 16% -> 42%
where the time goes in v3:
time: 823 us; the launch traced here: 817 us
  Pallas kernels  618 us (75%)
  waiting for transfers between devices  49 us (6%)
  local copies, waits for them, and re-layouts  42.4 us (5%)
  blocking collectives  39.5 us (5%)
  other arithmetic  30.2 us (4%)
  matrix products  15.2 us (2%)
  between operations  15.1 us (2%)
    pallas_call x9, Pallas kernels, linked(): pl.pallas_call(kernel, in_specs=specs, out_specs=[VMEM] * len(outs), out_...  560 us
    all_gather x1, blocking collectives, row_sums(): every = lax.all_gather(own, ('tok', 'col'), axis=0)  39.5 us
    all_gather x3, waiting for transfers between devices, gather_weight(): return lax.all_gather(part, ('col', 'tok'), axis=0, tiled=True)  38.3 us
    pallas_call x1, Pallas kernels, ffn(): pl.pallas_call(ffn_kernel, grid=(tiles,), in_specs=[whole(h_all), cols(D,...  29.4 us
    unnamed x74, local copies, waits for them, and re-layouts  19.5 us
  transfers between devices with their start and end apart: 7, of which 4 were waited for; matrix products, arithmetic and copies ran while one was open for 6% of the time, Pallas kernels for 42%

profile of v3, /device:TPU:0, one launch (start us, length us, event | category | flops | bytes accessed | tf_op | source)
XLA Modules:
  0.0 816.5 jit_solution(9350654522862483142)
XLA Ops:
  7.2 2.7 copy.79
  10.0 2.6 copy.81
  12.8 2.2 fusion
  15.1 2.5 copy.106
  23.1 2.9 fusion.22
  26.0 6.2 fusion.3
  32.8 2.6 copy.93
  35.5 7.9 copy.99
  45.6 80.7 %intake_kernel.1 = (bf16[288,2048]{1,0:T(8,128)(2,1)}, bf16[128,2048]{1,0:T(8,128)(2,1)}) custom-call(bf16[4,288,512]{2,1,0:T(8,128)(2,1)} %bitcast.811, bf16[4,128,512]{2,1,0:T(8,128)(2,1)} %copy-done.27), custom_call_target="tpu_custom_call" | custom-call | flops 603979776 | bytes 1509949 | tf_op jit(solution)/shard_map/intake_kernel/pallas_call | solution.py:674
  133.3 2.1 fusion.14
  136.2 56.5 %enter_qkv_kernel.1 = (bf16[4,288,2048]{2,1,0:T(8,128)(2,1)}, bf16[4,288,48]{2,1,0:T(8,128)(2,1)}, f32[4,288,1536]{2,1,0:T(8,128)}, f32[1152,8]{1,0:T(8,128)}) custom-call(bf16[288,2048]{1,0:T(8,128)(2,1)} %get-tuple-element.55.x_ref, bf16[2048,2048]{1,0:T(8,128)(2,1)} %all-gather.6.cloned.1.call-done.w_hbm, ...), custom_call_target="tpu_custom_call" | custom-call | flops 7247757312 | bytes 18119392 | tf_op jit(solution)/shard_map/enter_qkv_kernel/pallas_call | solution.py:674
  193.8 13.2 %attend.1 = (bf16[1152,512]{1,0:T(8,128)(2,1)S(1)}, bf16[1152,512]{1,0:T(8,128)(2,1)S(1)}, bf16[1152,512]{1,0:T(8,128)(2,1)S(1)}, bf16[1152,512]{1,0:T(8,128)(2,1)}, f32[4,1,1152]{2,1,0:T(1,128)S(1)}) custom-call(f32[1152,1536]{1,0:T(8,128)} %bitcast.780, f32[1152,1536]{1,0:T(8,128)} %bitcast.781, f32[1152,1536]{1,0:T(8,128)} %bitcast.782, ...), custom_call_target="tpu_custom_call" | custom-call | flops 2717908992 | bytes 11796480 | tf_op jit(solution)/shard_map/attend/pallas_call | solution.py:782
  210.1 89.6 %leave_out_kernel.1 = (f32[288,2048]{1,0:T(8,128)}, bf16[4,288,16]{2,1,0:T(8,128)(2,1)}, f32[288,2048]{1,0:T(8,128)}, bf16[4,288,2048]{2,1,0:T(8,128)(2,1)}) custom-call(bf16[4,288,512]{2,1,0:T(8,128)(2,1)} %bitcast.793, bf16[2048,2048]{1,0:T(8,128)(2,1)} %all-gather.6.cloned.1.call-done.w_hbm, bf16[16,512]{1,0:T(8,128)(2,1)} %bitcast.805, ...), custom_call_target="tpu_custom_call" | custom-call | flops 2415919104 | bytes 6039797 | tf_op jit(solution)/shard_map/leave_out_kernel/pallas_call | solution.py:674
  299.7 29.4 %ffn.1 = (bf16[1152,32]{1,0:T(8,128)(2,1)S(1)}, bf16[1152,2048]{1,0:T(8,128)(2,1)S(1)}, bf16[1152,2048]{1,0:T(8,128)(2,1)}, bf16[1152,2048]{1,0:T(8,128)(2,1)}) custom-call(bf16[1152,2048]{1,0:T(8,128)(2,1)} %bitcast.789, bf16[2048,4096]{1,0:T(8,128)(2,1)} %all-gather.8.cloned.1.call-done.wg_ref.wu_ref.w_hbm, ...), custom_call_target="tpu_custom_call" | custom-call | flops 19327352832 | bytes 40370176 | tf_op jit(solution)/shard_map/ffn/pallas_call | solution.py:428
  329.8 2.1 copy-done.12
  331.9 37.9 %all-gather.10.cloned.1.call-done.w_hbm = bf16[2048,2048]{1,0:T(8,128)(2,1)} async-done(((bf16[256,2048]{1,0:T(8,128)(2,1)}), bf16[2048,2048]{1,0:T(8,128)(2,1)}) %all-gather.10.cloned.1.call-update) | async-done | bytes 8388624 | tf_op jit(solution)/shard_map/all_gather | solution.py:825
  369.9 63.1 %leave_down_kernel.1 = (bf16[4,288,16]{2,1,0:T(8,128)(2,1)}, bf16[288,2048]{1,0:T(8,128)(2,1)}, bf16[288,2048]{1,0:T(8,128)(2,1)}, bf16[288,2048]{1,0:T(8,128)(2,1)}) custom-call(bf16[4,288,2048]{2,1,0:T(8,128)(2,1)} %bitcast.791, bf16[2048,2048]{1,0:T(8,128)(2,1)} %all-gather.10.cloned.1.call-done.w_hbm, bf16[16,2048]{1,0:T(8,128)(2,1)} %bitcast.807, ...), custom_call_target="tpu_custom_call" | custom-call | flops 9663676416 | bytes 24159192 | tf_op jit(solution)/shard_map/leave_down_kernel/pallas_call | solution.py:674
  432.9 66.0 %back_down_kernel.1 = (bf16[4,288,2048]{2,1,0:T(8,128)(2,1)}, bf16[4,288,16]{2,1,0:T(8,128)(2,1)}, bf16[4,288,4096]{2,1,0:T(8,128)(2,1)}, f32[1152,512]{1,0:T(8,128)}) custom-call(bf16[288,2048]{1,0:T(8,128)(2,1)} %get-tuple-element.63.dm_ref, bf16[2048,2048]{1,0:T(8,128)(2,1)} %all-gather.10.cloned.1.call-done.w_hbm, ...), custom_call_target="tpu_custom_call" | custom-call | flops 9663676416 | bytes 24159192 | tf_op jit(solution)/shard_map/back_down_kernel/pallas_call | solution.py:674
  498.9 61.2 %back_ffn_kernel.1 = (bf16[4,288,32]{2,1,0:T(8,128)(2,1)}, f32[288,2048]{1,0:T(8,128)}, bf16[288,2048]{1,0:T(8,128)(2,1)}) custom-call(bf16[4,288,4096]{2,1,0:T(8,128)(2,1)} %get-tuple-element.71.y_ref, bf16[2048,4096]{1,0:T(8,128)(2,1)} %all-gather.8.cloned.1.call-done.wg_ref.wu_ref.w_hbm, bf16[32,4096]{1,0:T(8,128)(2,1)} %copy-done.7, ...), custom_call_target="tpu_custom_call" | custom-call | flops 19327352832 | bytes 48318384 | tf_op jit(solution)/shard_map/back_ffn_kernel/pallas_call | solution.py:674
  560.1 46.5 %back_out_kernel.1 = (bf16[4,288,2048]{2,1,0:T(8,128)(2,1)}, bf16[4,288,16]{2,1,0:T(8,128)(2,1)}, bf16[4,288,512]{2,1,0:T(8,128)(2,1)}, f32[16,2048]{1,0:T(8,128...) custom-call(bf16[288,2048]{1,0:T(8,128)(2,1)} %get-tuple-element.74., ...), custom_call_target="tpu_custom_call" | custom-call | flops 2415919104 | bytes 6039797 | tf_op jit(solution)/shard_map/back_out_kernel/pallas_call | solution.py:674
  612.5 15.9 %attend_back.1 = (f32[1152,512]{1,0:T(8,128)}, f32[1152,512]{1,0:T(8,128)}, bf16[1152,512]{1,0:T(8,128)(2,1)S(1)}, f32[2,1152,128]{2,1,0:T(8,128)S(1)}) custom-call(bf16[1152,512]{1,0:T(8,128)(2,1)S(1)} %copy-done.9, bf16[1152,512]{1,0:T(8,128)(2,1)} %copy-done.10, bf16[1152,512]{1,0:T(8,128)(2,1)} %copy-done.11, bf16[1152,512]{1,0:T(8,128)(2,1)} %get-tuple-element.59.o_ref, ...), custom_call_target="tpu_custom_call" | custom-call | flops 6794772480 | bytes 17694720 | tf_op jit(solution)/shard_map/attend_back/pallas_call | solution.py:797
  630.5 19.2 %prepare_kernel.1 = (bf16[1152,1536]{1,0:T(8,128)(2,1)}, bf16[1152,48]{1,0:T(8,128)(2,1)}, f32[16,1536]{1,0:T(8,128)}, f32[48,2048]{1,0:T(8,128)}) custom-call(f32[1152,512]{1,0:T(8,128)} %get-tuple-element.83.wq_ref, f32[1152,512]{1,0:T(8,128)} %get-tuple-element.84.wk_ref, bf16[1152,512]{1,0:T(8,128)(2,1)} %copy-done.4, f32[1152,1536]{1,0:T(8,128)} %bitcast.785, ...), custom_call_target="tpu_custom_call" | custom-call | flops 603979776 | bytes 1509949 | tf_op jit(solution)/shard_map/prepare_kernel/pallas_call | solution.py:674
  651.6 3.4 all-to-all-start
  655.9 5.2 all-to-all-done
  661.2 3.4 all-to-all-start.1
  665.9 5.4 all-to-all-done.1
  673.7 76.9 %back_qkv_kernel.1 = f32[1152,512]{1,0:T(8,128)} custom-call(bf16[4,288,1536]{2,1,0:T(8,128)(2,1)} %bitcast.810, bf16[4,288,48]{2,1,0:T(8,128)(2,1)} %bitcast.814, bf16[2048,2048]{1,0:T(8,128)(2,1)} %all-gather.6.cloned.1.call-done.w_hbm, bf16[128,2048]{1,0:T(8,128)(2,1)} %get-tuple-element.56.factors_ref, f32[288,2048]{1,0:T(8,128)} %get-tuple-element.91.hidden_ref), custom_call_target="tpu_custom_call" | custom-call | flops 7247757312 | bytes 18119392 | tf_op jit(solution)/shard_map/back_qkv_kernel/pallas_call | solution.py:674
  750.6 39.5 %all-gather = bf16[128,1536]{1,0:T(8,128)(2,1)S(1)} all-gather(bf16[16,1536]{1,0:T(8,128)(2,1)S(1)} %convert_element_type.488), channel_id=2, replica_groups=mesh['tok'=2,'row'=4,'col'=4] {'tok','col'}, dimensions={0}, use_global_device_ids=true | all-gather | bytes 442368 | tf_op jit(solution)/shard_map/all_gather | solution.py:1157
  793.0 2.0 transpose.293
  796.7 1.6 convert_bitcast_fusion.7
  800.6 1.5 pad_maximum_fusion
  802.2 1.6 multiply_add_fusion
  (184 shorter events, 47.8 us)
Async XLA Ops:
  7.2 12.0 %copy-start = (bf16[2048,512]{1,0:T(8,128)(2,1)S(1)}, bf16[2048,512]{1,0:T(8,128)(2,1)}, u32[]{:S(2)}) copy-start(bf16[2048,512]{1,0:T(8,128)(2,1)} %param.23) | copy-start | bytes 6291460
  7.2 129.0 %all-gather.6.cloned.1.call-start = ((), (), s32[]{:S(2)}) async-start(), calls=%async_computation.2 | async-start | bytes 9437184 | tf_op jit(solution)/shard_map/all_gather | solution.py:825
  10.0 2.6 copy-start.17
  15.1 284.6 %all-gather.8.cloned.1.call-start = ((), (), s32[]{:S(2)}) async-start(), calls=%async_computation.3 | async-start | bytes 18874368 | tf_op jit(solution)/shard_map/all_gather | solution.py:825
  19.1 350.7 %all-gather.10.cloned.1.call-start = ((), (), s32[]{:S(2)}) async-start(), calls=%async_computation.4 | async-start | bytes 9437184 | tf_op jit(solution)/shard_map/all_gather | solution.py:825
  19.3 1.5 copy-start.21
  19.3 1.8 copy-start.18
  19.3 2.5 copy-start.19
  20.7 2.4 copy-start.22
  21.1 4.9 copy-start.16
  26.0 6.2 copy-start.30
  26.0 6.8 copy-start.28
  35.4 7.9 copy-start.29
  35.4 8.2 %copy-start.23 = (bf16[8,16,512]{2,1,0:T(8,128)(2,1)S(1)}, bf16[8,16,512]{2,1,0:T(8,128)(2,1)}, u32[]{:S(2)}) copy-start(bf16[8,16,512]{2,1,0:T(8,128)(2,1)} %param.29) | copy-start | bytes 393220
  35.4 8.5 %copy-start.20 = (bf16[2,8,512,16]{2,3,1,0:T(8,128)(2,1)S(1)}, bf16[2,8,512,16]{2,3,1,0:T(8,128)(2,1)}, u32[]{:S(2)}) copy-start(bf16[2,8,512,16]{2,3,1,0:T(8,128)(2,1)} %param.30) | copy-start | bytes 786436
  35.4 9.1 %copy-start.24 = (bf16[8,16,512]{2,1,0:T(8,128)(2,1)S(1)}, bf16[8,16,512]{2,1,0:T(8,128)(2,1)}, u32[]{:S(2)}) copy-start(bf16[8,16,512]{2,1,0:T(8,128)(2,1)} %param.33) | copy-start | bytes 393220
  44.0 86.3 %copy-start.15 = (bf16[2,8,16,2048]{3,2,1,0:T(8,128)(2,1)S(1)}, bf16[2,8,16,2048]{3,2,1,0:T(8,128)(2,1)}, u32[]{:S(2)}) copy-start(bf16[2,8,16,2048]{3,2,1,0:T(8,128)(2,1)} %param.31) | copy-start | bytes 3145732
  135.9 163.8 %copy-start.7 = (bf16[32,4096]{1,0:T(8,128)(2,1)}, bf16[32,4096]{1,0:T(8,128)(2,1)S(1)}, u32[]{:S(2)}) copy-start(bf16[32,4096]{1,0:T(8,128)(2,1)S(1)} %fusion.13.fg_ref.fu_ref.f1_ref) | copy-start | bytes 786436
  192.8 1.1 copy-start.2
  209.0 1.1 copy-start.11
  210.1 89.6 %copy-start.3 = (bf16[128,2048]{1,0:T(8,128)(2,1)S(1)}, bf16[128,2048]{1,0:T(8,128)(2,1)}, u32[]{:S(2)}) copy-start(bf16[128,2048]{1,0:T(8,128)(2,1)} %get-tuple-element.56.factors_ref) | copy-start | bytes 1572868
  329.8 2.1 copy-start.12
  611.3 1.3 copy-start.9
  649.7 6.2 copy-start.26
  651.6 9.6 %all-to-all-start = ((bf16[4,3,16,512]{3,2,1,0:T(8,128)(2,1)}), bf16[4,3,16,512]{3,2,1,0:T(8,128)(2,1)S(1)}, u32[]{:S(2)}, u32[]{:S(2)}) async-start(bf16[4,3,16,512]{3,2,1,0:T(8,128)(2,1)} %bitcast.777), calls=%async_computation | async-start | bytes 393216 | tf_op jit(solution)/shard_map/all_to_all | solution.py:1151
  661.2 10.2 %all-to-all-start.1 = ((bf16[4,4,16,512]{3,2,1,0:T(8,128)(2,1)}), bf16[4,4,16,512]{3,2,1,0:T(8,128)(2,1)S(1)}, u32[]{:S(2)}, u32[]{:S(2)}) async-start(bf16[4,4,16,512]{3,2,1,0:T(8,128)(2,1)} %bitcast.776), calls=%async_computation.1 | async-start | bytes 524288 | tf_op jit(solution)/shard_map/all_to_all | solution.py:1151
  664.6 127.2 %all-reduce.8.cloned.1.call-start = ((), (), s32[]{:S(2)}) async-start(), calls=%async_computation.6 | async-start | bytes 1835008 | tf_op jit(solution)/shard_map/psum | solution.py:1153
  665.9 7.8 copy-start.25
  672.9 123.8 %all-gather.12.cloned.1.call-start = ((), (), s32[]{:S(2)}) async-start(), calls=%async_computation.5 | async-start | bytes 1916928 | tf_op jit(solution)/shard_map/all_gather | solution.py:1157
  802.2 3.4 copy-start.13
  805.6 2.5 copy-start.14
  805.6 3.9 copy-start.1
  (6 other events, 5.6 us)
Sparse Core Ops, SparseCore 0:
  15.2 120.9 all-gather.5
  138.4 149.5 all-gather.7
  289.6 80.2 all-gather.9
  673.0 58.1 all-reduce.7
  733.3 25.6 all-gather.11

commit v4 on v3

v4 whole, which is shorter than its diff:
```python
import functools
import math

import jax
import jax.numpy as jnp
from jax import lax
from jax.experimental import pallas as pl
from jax.experimental.pallas import tpu as pltpu
from jax.sharding import PartitionSpec as P

D = 2048
HEAD_DIM = 128
RANK = 16
ADAPTERS = 8
PROMPT = 1024
CONT_LEN = 128
SLAB = 1152

adapter_scale = 2.0
norm_eps = 1e-06
rope_base = 500000.0
very_low = -1e30
bf16 = jnp.bfloat16
f32 = jnp.float32
log2_scale = math.log2(math.e) / math.sqrt(HEAD_DIM)
score_scale = 1.0 / math.sqrt(HEAD_DIM)
BLOCK = 384
TILE = 512
MESH = pl.DeviceIdType.MESH


def mm(left, right):
    return jnp.dot(left, right, preferred_element_type=f32)


def mm_nt(left, right):
    return lax.dot_general(left, right, (((1,), (1,)), ((), ())), preferred_element_type=f32)


class Links:
    def __init__(self, send_sem, recv_sem, local_sem):
        self.tok = lax.axis_index("tok")
        self.row, self.col = lax.axis_index("row"), lax.axis_index("col")
        self.xn, self.yn, self.dg = self.row ^ 1, self.row ^ 2, self.row ^ 3
        self.send_sem, self.recv_sem, self.local_sem = send_sem, recv_sem, local_sem
        self.used, self.local_used = 0, 0

    def take(self, count):
        self.used += count
        return self.used - count

    def copy(self, source, target, index, recv_index, row, col=None, tok=None):
        return pltpu.make_async_remote_copy(
            src_ref=source,
            dst_ref=target,
            send_sem=self.send_sem.at[index],
            recv_sem=self.recv_sem.at[recv_index],
            device_id={
                "tok": self.tok if tok is None else tok,
                "row": row,
                "col": self.col if col is None else col,
            },
            device_id_type=MESH,
        )

    def local(self, source, target):
        self.local_used += 1
        return pltpu.make_async_copy(source, target, self.local_sem.at[self.local_used - 1])

    def plan(self, *pairs):
        return [self.local(source, target) for source, target in pairs]

    def fetch(self, *pairs):
        return start_all(self.plan(*pairs))

    def greet(self, rows=2, columns=False, twin=False):
        barrier = pltpu.get_barrier_semaphore()
        places = [(self.tok, self.row ^ step, self.col) for step in range(1, rows + 1)]
        if columns:
            places += [(self.tok, self.row, self.col ^ step) for step in range(1, 4)]
        if twin:
            places += [(self.tok ^ 1, self.row, self.col)]
        for tok, row, col in places:
            pl.semaphore_signal(
                barrier,
                inc=1,
                device_id={"tok": tok, "row": row, "col": col},
                device_id_type=MESH,
            )
        pl.semaphore_wait(barrier, len(places))


def start_all(copies):
    for copy in copies:
        copy.start()
    return copies


def wait_all(copies):
    for copy in copies:
        copy.wait()


class Exchange:
    def __init__(self, links, axis, piece_at, slot_at):
        self.links, self.axis = links, axis
        self.me = links.row if axis == "row" else links.col
        self.piece_at, self.slot_at = piece_at, slot_at
        self.base = links.take(3)
        self.own = links.local(piece_at(self.me), slot_at(self.me))

    def copy(self, source, target, step):
        links, other, index = self.links, self.me ^ step, self.base + step - 1
        row, col = (other, links.col) if self.axis == "row" else (links.row, other)
        return links.copy(source, target, index, index, row, col)

    def start(self):
        for step in range(1, 4):
            self.copy(self.piece_at(self.me ^ step), self.slot_at(self.me), step).start()
        self.own.start()

    def arrived(self):
        for step in range(1, 4):
            landed = self.slot_at(self.me ^ step)
            self.copy(landed, landed, step).wait_recv()
        self.own.wait()

    def sent(self):
        for step in range(1, 4):
            self.copy(self.piece_at(self.me ^ step), self.slot_at(self.me), step).wait_send()


def features(ref, width):
    return lambda col: ref.at[:, pl.ds(pl.multiple_of(col * width, width), width)]


def slot(ref):
    return lambda key: ref.at[key]


def token_rows(ref, count):
    return lambda row: ref.at[pl.ds(pl.multiple_of(row * count, 16), count)]


def gather(links, all_ref, work, before=None, after=None):
    me, xn, yn, dg = links.row, links.xn, links.yn, links.dg
    half = all_ref.shape[1] // 2
    top, low = pl.ds(0, half), pl.ds(half, half)
    base = links.take(6)

    def move(owner, part, index, other):
        place = all_ref.at[owner, part]
        return links.copy(place, place, base + index, base + index, other)

    sends = [move(me, top, 0, xn), move(me, low, 1, yn), move(me, low, 2, xn), move(me, top, 3, yn)]
    for copy in sends:
        copy.start()
    if before:
        before()
    if work:
        work(me)
    move(xn, top, 0, xn).wait_recv()
    sends.append(move(xn, top, 4, yn))
    sends[-1].start()
    move(yn, low, 1, yn).wait_recv()
    sends.append(move(yn, low, 5, xn))
    sends[-1].start()
    if after:
        after()
    move(xn, low, 2, xn).wait_recv()
    if work:
        work(xn)
    move(yn, top, 3, yn).wait_recv()
    if work:
        work(yn)
    move(dg, top, 4, yn).wait_recv()
    move(dg, low, 5, xn).wait_recv()
    if work:
        work(dg)
    for copy in sends:
        copy.wait_send()


SLICES = 4


def scatter(links, product, o_ref, out_buf, relay_buf, final_buf, block=None, ready=None, hooks=None):
    me, xn, yn, dg = links.row, links.xn, links.yn, links.dg
    count, width = o_ref.shape[0], o_ref.shape[1] // SLICES
    half = count // 2
    top, low = pl.ds(0, half), pl.ds(half, half)
    base = links.take(6 * SLICES)
    all_copies = []

    def columns(k):
        at = block(k) * width if block else k * width
        return pl.ds(pl.multiple_of(at, width), width)

    def add(place, k, rows, relay):
        out_buf[place, k, rows] = (
            out_buf[place, k, rows].astype(f32) + relay_buf[relay, k].astype(f32)
        ).astype(bf16)

    def relay(k):
        copies = all_copies[k]
        copies[0].wait_recv()
        add(2, k, top, 0)
        copies[4].start()
        copies[1].wait_recv()
        add(1, k, low, 1)
        copies[5].start()

    def finish(k):
        for copy in all_copies[k][2:]:
            copy.wait_recv()

    for k in range(SLICES):
        cols = columns(k)

        def move(source, target, index, other, k=k):
            at = base + 6 * k + index
            return links.copy(source, target, at, at, other)

        copies = [
            move(out_buf.at[0, k, top], relay_buf.at[0, k], 0, xn),
            move(out_buf.at[0, k, low], relay_buf.at[1, k], 1, yn),
            move(out_buf.at[1, k, top], final_buf.at[0, k, top], 2, xn),
            move(out_buf.at[2, k, low], final_buf.at[1, k, low], 3, yn),
            move(out_buf.at[2, k, top], final_buf.at[1, k, top], 4, yn),
            move(out_buf.at[1, k, low], final_buf.at[0, k, low], 5, xn),
        ]
        all_copies.append(copies)
        if ready:
            ready(k)
        for place, (owner, first) in enumerate(((dg, (0, 1)), (xn, (2,)), (yn, (3,)))):
            out_buf[place, k] = product(owner, k, cols).astype(bf16)
            for index in first:
                copies[index].start()
        if k:
            relay(k - 1)
        o_ref[:, cols] = product(me, k, cols)
        if hooks:
            hooks[k](columns, finish)
    relay(SLICES - 1)

    def sent():
        for copies in all_copies:
            for copy in copies:
                copy.wait_send()

    return columns, finish, sent


def finish_all(result):
    _, finish, sent = result
    for k in range(SLICES):
        finish(k)
    sent()


def each_tile(width, step, body):
    @pl.loop(0, width // step)
    def _(tile):
        body(pl.multiple_of(tile * step, step))


def lower(rows, factor):
    return (adapter_scale * mm_nt(rows, factor)).astype(bf16)


def leave_product(y_ref, weight, f1, f2_ref, f2_rows, low_ref, loads):
    lowered = {}

    def product(owner, k, cols):
        place = len(lowered) % 4 if k == 0 else None
        if k == 0:
            loads[place].wait()
            low_ref[owner] = lower(y_ref[owner], f1)
            lowered[place] = True
        return weight(y_ref[owner], cols) + mm(low_ref[owner], f2_ref[f2_rows, cols])

    return product


class Streams:
    def __init__(self, links, rows, blocks, late=()):
        order = (links.dg, links.xn, links.yn, links.row)
        self.rows = links.plan(*[(rows[0].at[k], rows[1].at[k]) for k in order]) if rows else []
        self.blocks = blocks
        self.late = links.plan(*late)
        start_all(self.rows[:1])
        start_all(blocks[0])

    def ready(self, k):
        wait_all(self.blocks[k])
        if k == 0:
            start_all(self.rows[1:])
        if k < SLICES - 1:
            start_all(self.blocks[k + 1])
        if k == 1:
            start_all(self.late)


def load_qkv(links, w_hbm, w_ref, blocks):
    half, width = w_hbm.shape[1] // 4, w_hbm.shape[2]
    return [
        links.plan(
            *[
                (
                    w_hbm.at[2 * c + t, pl.ds(p * half, half)],
                    w_ref.at[
                        pl.ds(pl.multiple_of((2 * c + t) * half, half), half),
                        pl.ds(p * width, width),
                    ],
                )
                for t in range(2)
                for p in range(3)
            ]
        )
        for c in blocks
    ]


def load_out(links, w_hbm, w_ref):
    half, width = w_hbm.shape[1] // 4, w_hbm.shape[2]
    return [
        links.plan(
            *[
                (
                    w_hbm.at[2 * c + t, pl.ds(3 * half, half)],
                    w_ref.at[pl.ds(t * half, half), pl.ds(c * width, width)],
                )
                for t in range(2)
            ]
        )
        for c in range(4)
    ]


def load_down(links, w_hbm, w_ref):
    half, width = w_hbm.shape[1:]
    return [
        links.plan(
            *[
                (
                    w_hbm.at[2 * c + t],
                    w_ref.at[pl.ds(t * half, half), pl.ds(c * width, width)],
                )
                for t in range(2)
            ]
        )
        for c in range(4)
    ]


def load_ffn(links, w_hbm, w_ref):
    half, width = w_hbm.shape[2:]
    return [
        links.plan(
            *[
                (
                    w_hbm.at[2 * c + t, g],
                    w_ref.at[pl.ds((2 * c + t) * half, half), pl.ds(g * width, width)],
                )
                for t in range(2)
                for g in range(2)
            ]
        )
        for c in range(4)
    ]


def inverse_of(values):
    return lax.rsqrt(jnp.mean(values * values, axis=1, keepdims=True) + norm_eps)


def norm_back(values, weighted):
    inverse = inverse_of(values)
    inner = jnp.mean(values * weighted, axis=1, keepdims=True)
    return inverse * weighted - values * (inverse**3 * inner)


def gated(gate, up):
    return gate * jax.nn.sigmoid(gate) * up


def gated_back(grad, gate, up):
    sig = jax.nn.sigmoid(gate)
    act = gate * sig
    return (grad * up * (sig + act * (1.0 - sig)), grad * act)


QKV_A, OUT_B, FFN_A, DOWN_B = slice(0, 48), slice(48, 64), slice(64, 96), slice(96, 112)
GAIN0, GAIN1 = slice(112, 113), slice(113, 114)


def share_stats(links, stat_ref, first, second):
    blank = jnp.zeros((6, first.shape[0]), f32)
    sums = [jnp.sum(value.T, axis=0, keepdims=True) for value in (first, second)]
    stat_ref[links.row] = jnp.concatenate(sums + [blank], axis=0)
    base = links.take(3)
    mine = stat_ref.at[links.row]
    copies = []
    for index, other in enumerate((links.xn, links.yn, links.dg)):
        copies.append(links.copy(mine, mine, base + index, base + index, other))
        copies[-1].start()
    for index, other in enumerate((links.xn, links.yn, links.dg)):
        theirs = stat_ref.at[other]
        links.copy(theirs, theirs, base + index, base + index, other).wait_recv()
    for copy in copies:
        copy.wait_send()
    return stat_ref[0] + stat_ref[1] + stat_ref[2] + stat_ref[3]


def lane_sums(values):
    return functools.reduce(
        jnp.add, [values[:, at : at + 128] for at in range(0, values.shape[1], 128)]
    )


def intake_kernel(
    x_hbm, cot_hbm, ids_ref, gain_ref, qkv_lower_ref, out_raise_ref, ffn_lower_ref, down_raise_ref,
    qkv_raise_ref, out_lower_ref, ffn_raise_ref, down_lower_ref,
    own_ref, cot_ref, factors_ref, qkv_b_ref, out_a_ref, ffn_b_ref, down_a_ref,
    middle_ref, pieces_ref, send_sem, recv_sem, local_sem,
):
    links = Links(send_sem, recv_sem, local_sem)
    links.greet(rows=3, columns=True)
    width = pieces_ref.shape[2]
    first = Exchange(links, "row", slot(x_hbm), slot(middle_ref))
    second = Exchange(links, "col", slot(middle_ref), features(own_ref, width))
    turned = Exchange(links, "row", slot(cot_hbm), slot(cot_ref))
    spread = Exchange(links, "col", slot(pieces_ref), features(factors_ref, width))
    first.start()
    base = 4 * links.tok
    for place in range(4):
        for p in range(7):
            chosen = ids_ref[base + place, p]
            if p < 3:
                value = qkv_lower_ref[p, chosen]
            elif p == 3:
                value = out_raise_ref[chosen]
            elif p < 6:
                value = ffn_lower_ref[p - 4, chosen]
            else:
                value = down_raise_ref[chosen]
            pieces_ref[place, p * RANK : (p + 1) * RANK] = value
        pieces_ref[place, 7 * RANK :] = gain_ref[...]
    spread.start()
    first.arrived()
    second.start()
    turned.start()
    own = base + links.col
    qkv_b_ref[...] = jnp.zeros_like(qkv_b_ref)
    ffn_b_ref[...] = jnp.zeros_like(ffn_b_ref)
    for p in range(3):
        cols = slice(p * qkv_raise_ref.shape[3], (p + 1) * qkv_raise_ref.shape[3])
        qkv_b_ref[p * RANK : (p + 1) * RANK, cols] = qkv_raise_ref[p, ids_ref[own, p]]
    for p in range(2):
        cols = slice(p * ffn_raise_ref.shape[3], (p + 1) * ffn_raise_ref.shape[3])
        ffn_b_ref[p * RANK : (p + 1) * RANK, cols] = ffn_raise_ref[p, ids_ref[own, 4 + p]]
    out_a_ref[...] = out_lower_ref[ids_ref[own, 3]]
    down_a_ref[...] = down_lower_ref[ids_ref[own, 6]]
    for exchange in (spread, second, turned):
        exchange.arrived()
    for exchange in (first, spread, second, turned):
        exchange.sent()


def enter_qkv_kernel(
    x_ref, w_hbm, factors_ref, f2_ref,
    all_hbm, low_ref, lin_hbm, inv_ref,
    all_ref, lin_ref, w_ref, sq_ref, stat_ref, send_sem, recv_sem, local_sem,
):
    links = Links(send_sem, recv_sem, local_sem)
    width = w_ref.shape[1]
    loads = start_all(sum(load_qkv(links, w_hbm, w_ref, range(4)), []))
    all_ref[links.row] = x_ref[...]
    links.greet(rows=3)
    count = x_ref.shape[0]
    stores = []

    def work(owner):
        lowered = lower(all_ref[owner], factors_ref[QKV_A])
        low_ref[owner] = lowered
        rows = all_ref[owner]
        third = width // 3
        for index in range(3):
            cols = slice(index * third, (index + 1) * third)
            value = mm(rows, w_ref[:, cols]) + mm(lowered, f2_ref[:, cols])
            lin_ref[owner, :, cols] = value
            if index < 2:
                place = pl.ds(pl.multiple_of(owner * count, 8), count)
                sq_ref[index, place] = lane_sums(value * value)
        stores.extend(
            links.fetch(
                (lin_ref.at[owner], lin_hbm.at[owner]), (all_ref.at[owner], all_hbm.at[owner])
            )
        )

    gather(links, all_ref, work, lambda: wait_all(loads))
    total = share_stats(links, stat_ref, sq_ref[0], sq_ref[1])
    inv_ref[...] = lax.rsqrt(total / D + norm_eps).T
    wait_all(stores)


def summed(o_ref, final_buf, rows):
    return o_ref[rows] + jnp.concatenate(
        [
            final_buf[0, k, rows].astype(f32) + final_buf[1, k, rows].astype(f32)
            for k in range(SLICES)
        ],
        axis=1,
    )


def leave_out_kernel(
    y_ref, w_hbm, f1_ref, factors_ref, x_ref,
    lin_ref, low_ref, hidden_ref, all_ref,
    w_ref, out_buf, relay_buf, final_buf, send_sem, recv_sem, local_sem,
):
    links = Links(send_sem, recv_sem, local_sem)
    streams = Streams(links, None, load_out(links, w_hbm, w_ref))
    links.greet()

    def product(owner, k, cols):
        if k == 0:
            low_ref[owner] = lower(y_ref[owner], f1_ref[...])
        return mm(y_ref[owner], w_ref[:, cols]) + mm(low_ref[owner], factors_ref[OUT_B, cols])

    finish_all(
        scatter(
            links, product, lin_ref, out_buf, relay_buf, final_buf,
            ready=streams.ready,
        )
    )
    gain = factors_ref[GAIN0].astype(f32)

    @pl.loop(0, lin_ref.shape[0] // 16)
    def _(tile):
        rows = pl.ds(pl.multiple_of(tile * 16, 16), 16)
        value = summed(lin_ref, final_buf, rows)
        lin_ref[rows] = value
        hidden = x_ref[rows].astype(f32) + value * inverse_of(value) * gain
        hidden_ref[rows] = hidden
        all_ref[links.row, rows] = hidden.astype(bf16)

    gather(links, all_ref, None)


def flat_weight(ref):
    return ref[...].reshape(D, ref.shape[3])


def ffn_kernel(h_ref, wg_ref, wu_ref, factors_ref, fg_ref, fu_ref, low_ref, gate_ref, up_ref, act_ref):
    @pl.when(pl.program_id(0) == 0)
    def _():
        low_ref[...] = lower(h_ref[...], factors_ref[FFN_A])

    lowered = low_ref[...]
    rank = lowered.shape[1] // 2
    for at in range(0, SLAB, BLOCK):
        rows = slice(at, at + BLOCK)
        gate = mm(h_ref[rows], flat_weight(wg_ref)) + mm(lowered[rows], fg_ref[...])
        up = mm(h_ref[rows], flat_weight(wu_ref)) + mm(lowered[rows], fu_ref[...])
        gate_ref[rows] = gate.astype(bf16)
        up_ref[rows] = up.astype(bf16)
        act_ref[rows] = gated(gate, up).astype(bf16)


def ffn(h_all, w, factors, f2):
    width = f2.shape[1] // 2
    step = 256
    tiles = width // step
    low = jax.ShapeDtypeStruct((SLAB, f2.shape[0]), bf16)
    wide = jax.ShapeDtypeStruct((SLAB, width), bf16)
    whole = lambda value: pl.BlockSpec(value.shape, lambda t: (0, 0))
    cols = lambda rows, base: pl.BlockSpec((rows, step), lambda t: (0, base * tiles + t))
    block = (w.shape[0], 1, w.shape[2], step)
    part = lambda which: pl.BlockSpec(block, lambda t: (0, which, 0, t))
    return pl.pallas_call(
        ffn_kernel,
        grid=(tiles,),
        in_specs=[whole(h_all), part(0), part(1), whole(factors)]
        + [cols(f2.shape[0], 0), cols(f2.shape[0], 1)],
        out_specs=[whole(low)] + [cols(SLAB, 0)] * 3,
        out_shape=[low, wide, wide, wide],
        compiler_params=pltpu.CompilerParams(vmem_limit_bytes=48 << 20),
        cost_estimate=pl.CostEstimate(
            flops=4 * SLAB * D * width, bytes_accessed=4 * D * width + 10 * SLAB * width,
            transcendentals=SLAB * width,
        ),
        name="ffn",
    )(h_all, w, w, factors, f2, f2)


def leave_down_kernel(
    y_hbm, w_hbm, f1_ref, factors_ref, hidden_hbm, cot_ref,
    low_ref, out_ref, dm_ref, own_cot_ref,
    y_ref, w_ref, hidden_ref, lin_ref, out_buf, relay_buf, final_buf,
    send_sem, recv_sem, local_sem,
):
    links = Links(send_sem, recv_sem, local_sem)
    streams = Streams(
        links, (y_hbm, y_ref), load_down(links, w_hbm, w_ref), [(hidden_hbm, hidden_ref)]
    )
    links.greet(columns=True)
    turned = Exchange(links, "col", slot(cot_ref), features(own_cot_ref, cot_ref.shape[2]))
    turned.start()
    product = leave_product(
        y_ref, lambda rows, cols: mm(rows, w_ref[:, cols]), f1_ref[...], factors_ref, DOWN_B,
        low_ref, streams.rows,
    )
    finish_all(
        scatter(
            links, product, lin_ref, out_buf, relay_buf, final_buf,
            ready=streams.ready,
        )
    )
    turned.arrived()
    wait_all(streams.late)
    gain = factors_ref[GAIN1].astype(f32)

    @pl.loop(0, lin_ref.shape[0] // 16)
    def _(tile):
        rows = pl.ds(pl.multiple_of(tile * 16, 16), 16)
        value = summed(lin_ref, final_buf, rows)
        out_ref[rows] = (hidden_ref[rows] + value * inverse_of(value) * gain).astype(bf16)
        dm_ref[rows] = norm_back(value, own_cot_ref[rows].astype(f32) * gain).astype(bf16)

    turned.sent()


def widen(source_ref, target_ref):
    @pl.loop(0, source_ref.shape[0] // 64)
    def _(tile):
        rows = pl.ds(pl.multiple_of(tile * 64, 64), 64)
        target_ref[rows] = source_ref[rows].astype(f32)


def back_down_kernel(
    dm_ref, w_hbm, factors_ref, f2_ref, gate_hbm, up_hbm, out_ref,
    all_hbm, low_ref, grad_hbm, out_mid_ref,
    all_ref, w_ref, gate_ref, up_ref, grad_ref, send_sem, recv_sem, local_sem,
):
    links = Links(send_sem, recv_sem, local_sem)
    loads = start_all(sum(load_down(links, w_hbm, w_ref), []))
    order = (links.row, links.xn, links.yn, links.dg)
    gates = [
        links.plan((gate_hbm.at[k], gate_ref.at[k]), (up_hbm.at[k], up_ref.at[k])) for k in order
    ]
    start_all(gates[0])
    all_ref[links.row] = dm_ref[...]
    links.greet(columns=True)
    width = w_ref.shape[0]
    turned = Exchange(links, "col", features(out_ref, out_mid_ref.shape[2]), slot(out_mid_ref))
    stores = []

    def before():
        turned.start()
        wait_all(loads)
        for gate in gates[1:]:
            start_all(gate)

    def work(owner):
        wait_all(gates[len(stores) // 2])
        lowered = lower(all_ref[owner], factors_ref[DOWN_B])
        low_ref[owner] = lowered

        def body(at):
            cols, far = pl.ds(at, TILE), pl.ds(pl.multiple_of(width + at, TILE), TILE)
            grad = mm_nt(all_ref[owner], w_ref[cols, :]) + mm(lowered, f2_ref[:, cols])
            gate, up = gate_ref[owner, :, cols].astype(f32), up_ref[owner, :, cols].astype(f32)
            grad_gate, grad_up = gated_back(grad, gate, up)
            grad_ref[owner, :, cols] = grad_gate.astype(bf16)
            grad_ref[owner, :, far] = grad_up.astype(bf16)

        each_tile(width, TILE, body)
        stores.extend(
            links.fetch(
                (grad_ref.at[owner], grad_hbm.at[owner]), (all_ref.at[owner], all_hbm.at[owner])
            )
        )

    gather(links, all_ref, work, before)
    turned.arrived()
    turned.sent()
    wait_all(stores)


def back_ffn_kernel(
    y_hbm, w_hbm, f1_ref, factors_ref, cot_hbm, attn_hbm,
    low_ref, hidden_ref, da_ref,
    y_ref, w_ref, cot_ref, attn_ref, lin_ref, out_buf, relay_buf, final_buf,
    send_sem, recv_sem, local_sem,
):
    links = Links(send_sem, recv_sem, local_sem)
    streams = Streams(
        links,
        (y_hbm, y_ref),
        load_ffn(links, w_hbm, w_ref),
        [(cot_hbm, cot_ref), (attn_hbm, attn_ref)],
    )
    links.greet()
    product = leave_product(
        y_ref, lambda rows, cols: mm_nt(rows, w_ref[cols, :]), f1_ref[...], factors_ref, FFN_A,
        low_ref, streams.rows,
    )
    finish_all(
        scatter(
            links, product, lin_ref, out_buf, relay_buf, final_buf,
            ready=streams.ready,
        )
    )
    wait_all(streams.late)
    gain = factors_ref[GAIN0].astype(f32)

    @pl.loop(0, lin_ref.shape[0] // 16)
    def _(tile):
        rows = pl.ds(pl.multiple_of(tile * 16, 16), 16)
        value = summed(lin_ref, final_buf, rows) + cot_ref[rows].astype(f32)
        hidden_ref[rows] = value
        da_ref[rows] = norm_back(attn_ref[rows], value * gain).astype(bf16)


def mm_tn(left, right):
    return lax.dot_general(left, right, (((0,), (0,)), ((), ())), preferred_element_type=f32)


def back_out_kernel(
    da_ref, w_hbm, factors_ref, f2_ref, out_low_ref, attn_ref, down_low_ref, down_dlow_ref,
    ffn_low_ref, ffn_dlow_ref, dm_hbm, act_hbm, grad_hbm, h_hbm,
    heads_ref, cols_ref, rows_ref,
    all_ref, low_ref, w_ref, dm_ref, act_ref, grad_ref, h_ref, raise_ref, lower_ref, send_sem, recv_sem, local_sem,
):
    links = Links(send_sem, recv_sem, local_sem)
    load = start_all(sum(load_out(links, w_hbm, w_ref), []))
    all_ref[links.row] = da_ref[...]
    links.greet()
    loads = []

    def before():
        loads.extend(
            links.fetch((dm_hbm, dm_ref), (act_hbm, act_ref), (grad_hbm, grad_ref), (h_hbm, h_ref))
        )
        wait_all(load)

    heads, half = heads_ref.shape[2], grad_ref.shape[1] // 2

    def after():
        wait_all(loads)
        down_raise = mm_tn(down_low_ref[...], dm_ref[...])
        cols_ref[3 * RANK : 4 * RANK] = down_raise.astype(bf16)
        cols_ref[RANK : 3 * RANK] = mm_tn(ffn_dlow_ref[...], h_ref[...]).astype(bf16)
        both = mm_tn(ffn_low_ref[...], grad_ref[...]).astype(bf16)
        rows_ref[:, heads : heads + half] = both[:RANK, :half]
        rows_ref[:, heads + half : heads + 2 * half] = both[RANK:, half:]
        rows_ref[:, heads + 2 * half :] = mm_tn(down_dlow_ref[...], act_ref[...]).astype(bf16)

    def work(owner):
        lowered = lower(all_ref[owner], factors_ref[OUT_B])
        low_ref[owner] = lowered
        value = mm_nt(all_ref[owner], w_ref[...]) + mm(lowered, f2_ref[...])
        heads_ref[owner] = value.astype(bf16)
        raise_ref[...] += mm_tn(out_low_ref[owner], all_ref[owner])
        lower_ref[...] += mm_tn(low_ref[owner], attn_ref[owner])

    raise_ref[...] = jnp.zeros_like(raise_ref)
    lower_ref[...] = jnp.zeros_like(lower_ref)
    gather(links, all_ref, work, before, after)
    cols_ref[0:RANK] = raise_ref[...].astype(bf16)
    rows_ref[:, :heads] = lower_ref[...].astype(bf16)


def prepare_kernel(
    wq_hbm, wk_hbm, dv_ref, lin_hbm, inv_ref, inner_ref, f1_ref, low_ref, early_ref,
    grad_ref, dlow_ref, rows_ref,
    wq_ref, wk_ref, lin_ref, total_ref, stat_ref, send_sem, recv_sem, local_sem,
):
    links = Links(send_sem, recv_sem, local_sem)
    third = wq_ref.shape[1]
    loads = links.fetch(
        (wq_hbm, wq_ref),
        (wk_hbm, wk_ref),
        (lin_hbm.at[:, pl.ds(0, 2 * third)], lin_ref),
    )
    links.greet(rows=3)
    total = share_stats(links, stat_ref, inner_ref[0], inner_ref[1])
    total_ref[...] = total.T / D
    wait_all(loads)

    @pl.loop(0, SLAB // 96)
    def _(tile):
        rows = pl.ds(pl.multiple_of(tile * 96, 96), 96)
        inverse = inv_ref[rows]
        factor = inverse**3 * total_ref[rows]
        for index, source in enumerate((wq_ref, wk_ref)):
            cols = slice(index * third, (index + 1) * third)
            one = slice(index, index + 1)
            value = inverse[:, one] * source[rows] - lin_ref[rows, cols] * factor[:, one]
            grad_ref[rows, cols] = value.astype(bf16)
        grad_ref[rows, 2 * third :] = dv_ref[rows]

    dlow_ref[...] = lower(grad_ref[...], f1_ref[...])
    for index in range(3):
        cols = slice(index * third, (index + 1) * third)
        low = low_ref[:, index * RANK : (index + 1) * RANK]
        rows_ref[:, cols] = mm_tn(low, grad_ref[:, cols]).astype(bf16)
    rows_ref[:, 3 * third :] = early_ref[...]


def back_qkv_kernel(
    grad_ref, dlow_ref, w_hbm, factors_ref, hidden_hbm, x_hbm, early_ref, chosen_ref,
    final_ref, sums_ref,
    w_ref, hidden_ref, x_ref, sum_ref, own_ref, middle_ref, turn_buf, parts_ref, got_ref, total_ref, groups_ref,
    placed_ref, out_buf, relay_buf, final_buf, send_sem, recv_sem, local_sem,
):
    links = Links(send_sem, recv_sem, local_sem)
    steps = (2, 3, 1, 0)
    streams = Streams(
        links,
        None,
        load_qkv(links, w_hbm, w_ref, [links.col ^ step for step in steps]),
        [(hidden_hbm, hidden_ref)],
    )
    x_load = links.fetch((x_hbm, x_ref))
    links.greet(rows=3, columns=True, twin=True)
    width = own_ref.shape[2]
    count = grad_ref.shape[1]
    by_row = Exchange(links, "row", slot(parts_ref), slot(got_ref))
    base = 4 * links.tok
    by_col = Exchange(
        links, "col", slot(total_ref), lambda key: groups_ref.at[base + key]
    )
    index = links.take(1)
    mine, theirs = groups_ref.at[pl.ds(base, 4)], groups_ref.at[pl.ds(4 - base, 4)]
    to_twin = links.copy(mine, mine, index, index, links.row, tok=links.tok ^ 1)
    from_twin = links.copy(theirs, theirs, index, index, links.row, tok=links.tok ^ 1)
    spread = Exchange(links, "row", lambda key: placed_ref, slot(sums_ref))

    def lower_grad():
        wait_all(x_load)
        late = 0.0
        for owner in range(4):
            late = late + mm_tn(dlow_ref[owner], x_ref[owner])
        late = late.astype(bf16)
        parts_ref[0] = late[0 : 2 * RANK]
        parts_ref[1, :RANK] = late[2 * RANK :]
        parts_ref[1, RANK:] = early_ref[:RANK]
        parts_ref[2] = early_ref[RANK : 3 * RANK]
        parts_ref[3, :RANK] = early_ref[3 * RANK :]
        parts_ref[3, RANK:] = jnp.zeros((RANK, D), bf16)
        by_row.start()

    def add_rows():
        by_row.arrived()
        for f in range(4):
            cols = slice(f * width, (f + 1) * width)
            value = got_ref[0, :, cols].astype(f32)
            for q in range(1, 4):
                value = value + got_ref[q, :, cols].astype(f32)
            total_ref[f] = value.astype(bf16)
        by_col.start()

    def share():
        by_col.arrived()
        to_twin.start()

    def place_groups():
        from_twin.wait_recv()
        for half in range(2):
            rows = slice(half * RANK, (half + 1) * RANK)
            values = [groups_ref[g, rows].astype(f32) for g in range(8)]
            for adapter in range(ADAPTERS):
                value = 0.0
                for g in range(8):
                    value = value + chosen_ref[2 * links.row + half, adapter * 8 + g] * values[g]
                placed_ref[adapter, rows] = value.astype(bf16)
        spread.start()

    def product(owner, k, cols):
        value = mm_nt(grad_ref[owner], w_ref[cols, :])
        return value + mm(dlow_ref[owner], factors_ref[QKV_A, cols])

    z_base, row_base = links.take(3), links.take(4)
    near = links.local(middle_ref.at[links.row], token_rows(turn_buf, count)(links.row))
    z_copies = []

    def leave_col(k, columns, finish):
        finish(k)
        cols, step = columns(k), steps[k]
        value = (
            sum_ref[:, cols]
            + final_buf[0, k].astype(f32)
            + final_buf[1, k].astype(f32)
            + hidden_ref[:, cols]
        ).astype(bf16)
        if step == 0:
            middle_ref[links.col] = value
            return
        own_ref[k] = value
        at = z_base + k
        copy = links.copy(
            own_ref.at[k], middle_ref.at[links.col], at, at, links.row, links.col ^ step
        )
        copy.start()
        z_copies.append(copy)

    def to_row(step):
        other = links.row ^ step
        return links.copy(
            middle_ref.at[other],
            token_rows(turn_buf, count)(links.row),
            row_base + step,
            row_base + step,
            other,
        )

    def leave_row(k):
        source = links.col ^ steps[k]
        if steps[k]:
            at = z_base + k
            landed = middle_ref.at[source]
            links.copy(landed, landed, at, at, links.row, source).wait_recv()
        step = links.row ^ source

        @pl.when(step == 0)
        def _():
            near.start()

        @pl.when(step != 0)
        def _():
            to_row(step).start()

    def second(columns, finish):
        add_rows()

    def third(columns, finish):
        share()
        wait_all(streams.late)
        leave_col(0, columns, finish)

    def fourth(columns, finish):
        place_groups()
        leave_col(1, columns, finish)

    columns, finish, sent = scatter(
        links, product, sum_ref, out_buf, relay_buf, final_buf,
        block=lambda k: links.col ^ steps[k],
        ready=streams.ready,
        hooks=[lambda columns, finish: lower_grad(), second, third, fourth],
    )
    leave_row(0)
    leave_col(2, columns, finish)
    leave_row(1)
    leave_col(3, columns, finish)
    leave_row(3)
    leave_row(2)
    near.wait()
    for step in range(1, 4):
        landed = token_rows(turn_buf, count)(links.row ^ step)
        at = row_base + step
        links.copy(landed, landed, at, at, links.row ^ step).wait_recv()
    widen(turn_buf, final_ref)
    spread.arrived()
    for step in range(1, 4):
        to_row(step).wait_send()
    for copy in z_copies:
        copy.wait_send()
    to_twin.wait_send()
    for exchange in (by_row, by_col, spread):
        exchange.sent()
    sent()


VMEM = pl.BlockSpec(memory_space=pltpu.VMEM)
ANY = pl.BlockSpec(memory_space=pl.ANY)
SMEM = pl.BlockSpec(memory_space=pltpu.SMEM)


def linked(kernel, number, operands, outs, scratch, flops):
    specs = [ANY if isinstance(value, tuple) else VMEM for value in operands]
    values = [value[0] if isinstance(value, tuple) else value for value in operands]
    specs = [
        SMEM if value.ndim == 2 and value.shape[0] == 8 and value.dtype != bf16 else spec
        for spec, value in zip(specs, values)
    ]
    return pl.pallas_call(
        kernel,
        in_specs=specs,
        out_specs=[ANY if len(out) == 3 else VMEM for out in outs],
        out_shape=[jax.ShapeDtypeStruct(out[0], out[1]) for out in outs],
        scratch_shapes=[pltpu.VMEM(shape, kind) for shape, kind in scratch]
        + [
            pltpu.SemaphoreType.DMA((48,)),
            pltpu.SemaphoreType.DMA((48,)),
            pltpu.SemaphoreType.DMA((48,)),
        ],
        compiler_params=pltpu.CompilerParams(
            collective_id=number, has_side_effects=True, vmem_limit_bytes=60 << 20
        ),
        cost_estimate=pl.CostEstimate(
            flops=flops, bytes_accessed=flops // 400, transcendentals=0
        ),
        name=kernel.__name__,
    )(*values)


def scatter_buffers(count):
    part = D // SLICES
    return [
        ((3, SLICES, count, part), bf16),
        ((2, SLICES, count // 2, part), bf16),
        ((2, SLICES, count, part), bf16),
    ]


def score_blocks(k_ref, q_block, bias_ref, start, stop):
    parts = []
    if start:
        parts.append(mm_nt(k_ref[0:start], q_block) + bias_ref[0:start])
    own = mm_nt(k_ref[start:stop], q_block) + bias_ref[start:stop]
    keys = lax.broadcasted_iota(jnp.int32, own.shape, 0)
    queries = lax.broadcasted_iota(jnp.int32, own.shape, 1)
    parts.append(jnp.where(keys <= queries, own, very_low))
    return parts

def attend_kernel(q_ref, k_ref, v_ref, inv_ref, gain_ref, cos_ref, sin_ref, bias_ref,
                  ql_ref, kl_ref, vl_ref, o_ref, lse_ref):
    for source, target, index in ((q_ref, ql_ref, 0), (k_ref, kl_ref, 1)):
        normed = source[...] * inv_ref[:, index:index+1] * gain_ref[index:index+1, :]
        target[...] = (normed * cos_ref[...] + pltpu.roll(normed, HEAD_DIM // 2, 1) * sin_ref[...]).astype(bf16)
    values = v_ref[...].astype(bf16)
    vl_ref[...] = values
    values_t = v_ref[...].T.astype(bf16)
    for start in range(0, SLAB, BLOCK):
        stop = start + BLOCK
        parts = score_blocks(kl_ref, ql_ref[start:stop], bias_ref, start, stop)
        top = functools.reduce(jnp.maximum, [jnp.max(p, axis=0, keepdims=True) for p in parts]) * log2_scale
        total, out, at = 0.0, 0.0, 0
        for part in parts:
            shifted = jnp.exp2(part * log2_scale - top)
            total = total + jnp.sum(shifted, axis=0, keepdims=True)
            out = out + mm(values_t[:, at:at+part.shape[0]], shifted.astype(bf16))
            at += part.shape[0]
        o_ref[start:stop] = (out / total).T.astype(bf16)
        lse_ref[0, :, start:stop] = top + jnp.log2(total)

def attend_back_kernel(ql_ref, kl_ref, vl_ref, o_ref, do_ref, lse_ref, q_ref, k_ref, gain_ref, cos_ref, sin_ref, bias_ref, *refs):
    mid_ref, wq_ref, wk_ref, dv_ref, sum_ref, turn_ref, dk_sum, dv_sum, *sems = refs if len(refs) > 8 else (None, *refs[:4], None, *refs[4:])
    if sems:
        links = Links(*sems)
        turned = Exchange(links, "row", slot(mid_ref), token_rows(turn_ref, mid_ref.shape[1]))

        @pl.when(pl.program_id(0) == 0)
        def _():
            links.greet(rows=3)
            turned.start()

    keys_t = kl_ref[...].astype(f32).T.astype(bf16)
    delta_all = jnp.sum((do_ref[...].astype(f32) * o_ref[...].astype(f32)).T, axis=0, keepdims=True)
    dk_sum[...] = jnp.zeros_like(dk_sum)
    dv_sum[...] = jnp.zeros_like(dv_sum)
    def unrotate(values):
        return values * cos_ref[...] - pltpu.roll(values, HEAD_DIM // 2, 1) * sin_ref[...]
    dq_parts = []
    for start in range(0, SLAB, BLOCK):
        stop = start + BLOCK
        queries, grads = ql_ref[start:stop], do_ref[start:stop]
        parts = score_blocks(kl_ref, queries, bias_ref, start, stop)
        lse, delta = lse_ref[0, :, start:stop], delta_all[:, start:stop]
        at, dq = 0, 0.0
        for part in parts:
            span = slice(at, at + part.shape[0])
            probs = jnp.exp2(part * log2_scale - lse)
            dv_sum[span] += mm(probs.astype(bf16), grads)
            dscore = (probs * (mm_nt(vl_ref[span], grads) - delta)).astype(bf16)
            dk_sum[span] += mm(dscore, queries)
            dq = dq + mm(keys_t[:, span], dscore)
            at += part.shape[0]
        dq_parts.append(dq.T)
    dq_all = jnp.concatenate(dq_parts, axis=0) * score_scale
    dv_ref[...] = dv_sum[...].astype(bf16)
    wq = unrotate(dq_all) * gain_ref[0:1, :]
    wk = unrotate(dk_sum[...] * score_scale) * gain_ref[1:2, :]
    wq_ref[...] = wq.astype(wq_ref.dtype)
    wk_ref[...] = wk.astype(wk_ref.dtype)
    first = pl.program_id(0) == 0
    for index, (weighted, source) in enumerate(((wq, q_ref), (wk, k_ref))):
        product = weighted * source[...]

        @pl.when(first)
        def _():
            sum_ref[index] = product

        @pl.when(jnp.logical_not(first))
        def _():
            sum_ref[index] += product

    if sems:

        @pl.when(pl.program_id(0) == pl.num_programs(0) - 1)
        def _():
            turned.arrived()
            turned.sent()


def attend_specs(heads):
    col = lambda base: pl.BlockSpec((SLAB, HEAD_DIM), lambda h: (0, base * heads + h))
    whole = lambda shape: pl.BlockSpec(shape, lambda h: (0,) * len(shape))
    return col, whole

def attend(qkv_lin, inverses, gains, cosine, sine, bias):
    heads = qkv_lin.shape[1] // (3 * HEAD_DIM)
    col, whole = attend_specs(heads)
    low = jax.ShapeDtypeStruct((SLAB, heads * HEAD_DIM), bf16)
    return pl.pallas_call(
        attend_kernel, grid=(heads,),
        in_specs=[col(0), col(1), col(2), whole((SLAB, 8)), pl.BlockSpec((2, HEAD_DIM), lambda h: (0, h)),
                  whole((SLAB, HEAD_DIM)), whole((SLAB, HEAD_DIM)), whole((SLAB, 1))],
        out_specs=[col(0)] * 4 + [pl.BlockSpec((1, 1, SLAB), lambda h: (h, 0, 0))],
        out_shape=[low] * 4 + [jax.ShapeDtypeStruct((heads, 1, SLAB), f32)],
        compiler_params=pltpu.CompilerParams(vmem_limit_bytes=48 << 20),
        cost_estimate=pl.CostEstimate(flops=heads*4*SLAB*SLAB*HEAD_DIM, bytes_accessed=heads*SLAB*HEAD_DIM*20, transcendentals=heads*SLAB*SLAB),
        name="attend",
    )(qkv_lin, qkv_lin, qkv_lin, inverses, gains, cosine, sine, bias)

def attend_back(ql, kl, vl, o, do, lse, qkv_lin, gains, cosine, sine, bias, middle=None):
    heads = ql.shape[1] // HEAD_DIM
    col, whole = attend_specs(heads)
    wide = jax.ShapeDtypeStruct(ql.shape, f32)
    outs = [wide, wide, jax.ShapeDtypeStruct(ql.shape, bf16)]
    outs.append(jax.ShapeDtypeStruct((2, SLAB, HEAD_DIM), f32))
    moved, turned, params, sems = [], [], dict(vmem_limit_bytes=48 << 20), []
    if middle is not None:
        moved, turned = [middle], [jax.ShapeDtypeStruct((SLAB, middle.shape[2]), bf16)]
        params.update(collective_id=10, has_side_effects=True)
        sems = [pltpu.SemaphoreType.DMA((4,))] * 3
    hbm = pl.BlockSpec(memory_space=pl.ANY)
    return pl.pallas_call(
        attend_back_kernel,
        grid=(heads,),
        in_specs=[col(0)] * 5
        + [pl.BlockSpec((1, 1, SLAB), lambda h: (h, 0, 0)), col(0), col(1)]
        + [pl.BlockSpec((2, HEAD_DIM), lambda h: (0, h))]
        + [whole((SLAB, HEAD_DIM)), whole((SLAB, HEAD_DIM)), whole((SLAB, 1))]
        + [hbm] * len(moved),
        out_specs=[col(0)] * 3 + [whole((2, SLAB, HEAD_DIM))] + [hbm] * len(turned),
        out_shape=outs + turned,
        scratch_shapes=[pltpu.VMEM((SLAB, HEAD_DIM), f32)] * 2 + sems,
        compiler_params=pltpu.CompilerParams(**params),
        cost_estimate=pl.CostEstimate(
            flops=heads * 10 * SLAB * SLAB * HEAD_DIM,
            bytes_accessed=heads * SLAB * HEAD_DIM * 30,
            transcendentals=heads * SLAB * SLAB,
        ),
        name="attend_back",
    )(ql, kl, vl, o, do, lse, qkv_lin, qkv_lin, gains, cosine, sine, bias, *moved)


def dot(left, right):
    return jnp.dot(left, right, preferred_element_type=f32)


def dot_nt(left, right):
    return lax.dot_general(left, right, (((1,), (1,)), ((), ())), preferred_element_type=f32)


def dot_tn(left, right):
    return lax.dot_general(left, right, (((0,), (0,)), ((), ())), preferred_element_type=f32)


def gather_weight(local):
    half = local.shape[0] // lax.axis_size("tok")
    part = lax.dynamic_slice_in_dim(local, lax.axis_index("tok") * half, half, 0)
    return lax.all_gather(part, ("col", "tok"), axis=0, tiled=True)


def to_tokens(values):
    rows, cols = lax.axis_size("row"), lax.axis_size("col")
    width = values.shape[1]
    mixed = lax.all_to_all(values, "row", 0, 0, tiled=True)
    mixed = lax.all_to_all(mixed, "col", 0, 0, tiled=True)
    return mixed.reshape(cols, SLAB // rows, width).transpose(1, 0, 2).reshape(SLAB // rows, -1)


def from_tokens(values):
    rows, cols = lax.axis_size("row"), lax.axis_size("col")
    count = values.shape[0]
    mixed = values.reshape(count, cols, -1).transpose(1, 0, 2).reshape(cols * count, -1)
    mixed = lax.all_to_all(mixed, "col", 0, 0, tiled=True)
    return lax.all_to_all(mixed, "row", 0, 0, tiled=True)


def reorder(values, outer, inner):
    if outer == 1 or inner == 1:
        return values
    rest = values.shape[0] // (outer * inner)
    shape = (outer, inner, rest) + values.shape[1:]
    return values.reshape(shape).swapaxes(0, 1).reshape(values.shape)


def gather_tokens(values):
    rows, per_slab = lax.axis_size("row"), lax.axis_size("row") // lax.axis_size("col")
    return reorder(lax.all_gather(values, "row", axis=0, tiled=True), rows, per_slab)


def scatter_tokens(values):
    rows, per_slab = lax.axis_size("row"), lax.axis_size("row") // lax.axis_size("col")
    values = reorder(values.astype(bf16), per_slab, rows)
    return lax.psum_scatter(values, "row", scatter_dimension=0, tiled=True).astype(f32)


def token_places(length):
    slot_ids = jnp.arange(SLAB, dtype=jnp.int32)
    return jnp.where(slot_ids < PROMPT, slot_ids, length + (slot_ids - PROMPT) % CONT_LEN)


def rotation(places, head_size):
    half_dim = head_size // 2
    frequency = jnp.exp(
        -(2.0 * jnp.arange(half_dim, dtype=f32) / head_size) * math.log(rope_base)
    )
    angles = places.astype(f32)[:, None] * frequency[None, :]
    return (jnp.cos(angles), jnp.sin(angles))


def pick(adapters, ids):
    onehot = (ids[:, None] == jnp.arange(adapters.shape[0], dtype=jnp.int32)).astype(adapters.dtype)
    return jnp.tensordot(onehot, adapters, axes=1)


def place(ids, gradients):
    onehot = (jnp.arange(ADAPTERS, dtype=jnp.int32)[:, None] == ids[None, :]).astype(f32)
    total = 0.0
    for index in range(gradients.shape[0]):
        weight = onehot[:, index].reshape((ADAPTERS,) + (1,) * (gradients.ndim - 1))
        total = total + weight * gradients[index][None].astype(f32)
    return total


def block_diagonal(factors):
    count = len(factors)
    lines = []
    for index, factor in enumerate(factors):
        blank = jnp.zeros_like(factor)
        lines.append(
            jnp.concatenate([factor if k == index else blank for k in range(count)], axis=1)
        )
    return jnp.concatenate(lines, axis=0)


def enter(x, w, f1, f2):
    everything = gather_tokens(x)
    lowered = (adapter_scale * dot_nt(everything, f1)).astype(bf16)
    return everything, lowered, dot(everything, w) + dot(lowered, f2)


def leave(y, w, f1, f2):
    lowered = (adapter_scale * dot_nt(y, f1)).astype(bf16)
    return scatter_tokens(dot_nt(y, w) + dot(lowered, f2)), lowered


def split_layer(
    layer_in, cotangent, qkv_weight, out_weight, ffn_weight, down_weight, head_gain, post_gain,
    adapters, adapter_ids, tables,
):
    qkv_lower, out_raise, ffn_lower, down_raise, qkv_raise, out_lower, ffn_raise, down_lower = (
        adapters
    )
    col_count = lax.axis_size("col")
    group_base = lax.axis_index("tok") * col_count
    group = group_base + lax.axis_index("col")
    slab_ids = lax.dynamic_slice_in_dim(adapter_ids, group_base, col_count, 0)
    own_ids = lax.dynamic_index_in_dim(adapter_ids, group, 0, keepdims=False)
    size = layer_in.shape[1]
    local = jnp.concatenate([qkv_weight.transpose(1, 0, 2).reshape(size, -1), out_weight.T], axis=1)
    attn_full = gather_weight(local)
    ffn_full = gather_weight(ffn_weight.transpose(1, 0, 2).reshape(size, -1))
    down_full = gather_weight(down_weight.T)
    pieces = jnp.concatenate(
        [pick(qkv_lower[p], slab_ids[:, p]) for p in range(3)]
        + [pick(out_raise, slab_ids[:, 3])]
        + [pick(ffn_lower[p], slab_ids[:, 4 + p]) for p in range(2)]
        + [pick(down_raise, slab_ids[:, 6])]
        + [jnp.broadcast_to(jnp.pad(post_gain, ((0, 14), (0, 0))), (col_count, RANK, size))],
        axis=1,
    )
    qkv_b = block_diagonal([pick(qkv_raise[p], own_ids[p : p + 1])[0] for p in range(3)])
    out_a = pick(out_lower, own_ids[3:4])[0]
    ffn_b = block_diagonal([pick(ffn_raise[p], own_ids[4 + p : 5 + p])[0] for p in range(2)])
    down_a = pick(down_lower, own_ids[6:7])[0]
    factors = lax.all_to_all(pieces, "col", 0, 0, tiled=True)
    factors = factors.transpose(1, 0, 2).reshape(-1, D)
    qkv_a, out_b, ffn_a, down_b = (factors[part] for part in (QKV_A, OUT_B, FFN_A, DOWN_B))
    gains = factors[GAIN0.start : GAIN1.stop].astype(f32)
    width = qkv_b.shape[1]
    head_width, ff_width = width // 3, ffn_b.shape[1] // 2
    x_own = to_tokens(layer_in)
    x_all, qkv_low, qkv_lin = enter(x_own, attn_full[:, :width], qkv_a, qkv_b)
    q_lin, k_lin = qkv_lin[:, :head_width], qkv_lin[:, head_width : 2 * head_width]
    squares = jnp.stack([jnp.sum(q_lin * q_lin, axis=1), jnp.sum(k_lin * k_lin, axis=1)], axis=1)
    inverses = lax.rsqrt(lax.psum(squares, "row") / D + norm_eps)
    inverses = jnp.concatenate([inverses] * 4, axis=1)
    q_low, k_low, v_low, attn_low, log_sums = attend(qkv_lin, inverses, head_gain, *tables)
    attn_lin, out_low = leave(attn_low, attn_full[:, width:], out_a, out_b)
    hidden = x_own.astype(f32) + attn_lin * inverse_of(attn_lin) * gains[0]
    h_all, ffn_low, ffn_lin = enter(hidden.astype(bf16), ffn_full, ffn_a, ffn_b)
    gate_lin, up_lin = ffn_lin[:, :ff_width], ffn_lin[:, ff_width:]
    act_low = gated(gate_lin, up_lin).astype(bf16)
    mlp_lin, down_low = leave(act_low, down_full, down_a, down_b)
    layer_out = hidden + mlp_lin * inverse_of(mlp_lin) * gains[1]
    layer_out = from_tokens(layer_out.astype(bf16)).astype(f32)
    grad_out = to_tokens(cotangent).astype(f32)
    grad_mlp = norm_back(mlp_lin, grad_out * gains[1]).astype(bf16)
    dm_all, down_dlow, grad_act = enter(grad_mlp, down_full, down_b, down_a)
    grad_ffn = jnp.concatenate(gated_back(grad_act, gate_lin, up_lin), axis=1).astype(bf16)
    grad_ffn_in, ffn_dlow = leave(grad_ffn, ffn_full, ffn_b, ffn_a)
    grad_hidden = grad_out + grad_ffn_in
    grad_attn = norm_back(attn_lin, grad_hidden * gains[0]).astype(bf16)
    da_all, out_dlow, grad_heads = enter(grad_attn, attn_full[:, width:], out_b, out_a)
    weighted_q, weighted_k, grad_v, inner = attend_back(
        q_low, k_low, v_low, attn_low, grad_heads.astype(bf16), log_sums, qkv_lin, head_gain, *tables
    )
    inner = lax.psum(jnp.sum(inner, axis=2).T, "row")
    factor = inverses[:, :2] ** 3 * inner / D
    grad_qkv = jnp.concatenate(
        [
            (inverses[:, 0:1] * weighted_q - q_lin * factor[:, 0:1]).astype(bf16),
            (inverses[:, 1:2] * weighted_k - k_lin * factor[:, 1:2]).astype(bf16),
            grad_v,
        ],
        axis=1,
    )
    grad_qkv_in, qkv_dlow = leave(grad_qkv, attn_full[:, :width], qkv_b, qkv_a)
    grad_in = from_tokens((grad_hidden + grad_qkv_in).astype(bf16)).astype(f32)
    parts = jnp.concatenate(
        [dot_tn(qkv_dlow, x_all), dot_tn(out_low, da_all), dot_tn(ffn_dlow, h_all)]
        + [dot_tn(down_low, dm_all)]
    )
    parts = parts.astype(bf16).reshape(7, RANK, col_count, size).transpose(2, 0, 1, 3)
    parts = lax.all_to_all(parts, "col", 0, 0, tiled=True)
    placed = [place(slab_ids[:, p], parts[:, p]) for p in range(7)]
    col_grads = list(lax.psum(jnp.stack(placed).astype(bf16), ("tok", "row")).astype(f32))
    own_rows = jnp.concatenate(
        [diagonal(dot_tn(qkv_low, grad_qkv), 3), dot_tn(out_dlow, attn_low)]
        + [diagonal(dot_tn(ffn_low, grad_ffn), 2), dot_tn(down_dlow, act_low)],
        axis=1,
    )
    every = lax.all_gather(own_rows.astype(bf16), ("tok", "col"), axis=0)
    row_grads, at = [], 0
    for p in range(7):
        part = ff_width if p > 3 else head_width
        row_grads.append(place(adapter_ids[:, p], every[:, :, at : at + part]))
        at += part
    return layer_out, grad_in, col_grads, row_grads


def flat(values):
    return values.reshape((SLAB,) + values.shape[2:])


def cube(values):
    return values.reshape((4, SLAB // 4) + values.shape[1:])


def linked_layer(
    layer_in, cotangent, qkv_weight, out_weight, ffn_weight, down_weight, head_gain, post_gain,
    adapters, adapter_ids, tables,
):
    count = SLAB // 4
    piece = (4, count, layer_in.shape[1])
    head_width, ff_width = qkv_weight.shape[2], ffn_weight.shape[2]
    width = 3 * head_width
    buffers = scatter_buffers(count)
    per = 2 * SLAB * D
    tokens = ((4, count, D), bf16)
    own = ((count, D), bf16)
    wide = ((count, D), f32)

    def low_rows(size):
        return ((4, count, size), bf16)

    def gather_halves(local, axis):
        half = local.shape[axis] // 2
        return lax.dynamic_slice_in_dim(local, lax.axis_index("tok") * half, half, axis)

    def gathered(local):
        return lax.all_gather(local, ("col", "tok"), axis=0)

    attn_full = gathered(
        jnp.concatenate(
            [gather_halves(qkv_weight, 1).reshape(-1, head_width), gather_halves(out_weight, 0)]
        )
    )
    ffn_full = gathered(gather_halves(ffn_weight, 1))
    down_full = gathered(gather_halves(down_weight, 0))

    x_own, cot_mid, factors, qkv_b, out_a, ffn_b, down_a = linked(
        intake_kernel, 1,
        [(cube(layer_in),), (cube(cotangent),), adapter_ids]
        + [jnp.pad(post_gain, ((0, RANK - 2), (0, 0)))]
        + adapters,
        [own, (piece, bf16), ((128, D), bf16), ((48, width), bf16), ((16, head_width), bf16)]
        + [((32, 2 * ff_width), bf16), ((16, ff_width), bf16)],
        [(piece, bf16), ((4, 128, piece[2]), bf16)],
        per * 128,
    )
    x_all, qkv_low, qkv_lin, inverses = linked(
        enter_qkv_kernel, 2,
        [x_own, (attn_full,), factors, qkv_b],
        [tokens + (ANY,), low_rows(48), ((4, count, width), f32, ANY), ((SLAB, 8), f32)],
        [tokens, ((4, count, width), f32), ((D, width), bf16), ((2, SLAB, 128), f32)]
        + [((4, 8, SLAB), f32)],
        per * width,
    )
    qkv_lin = flat(qkv_lin)
    q_low, k_low, v_low, attn_low, log_sums = attend(qkv_lin, inverses, head_gain, *tables)
    attn_lin, out_low, hidden, h_all = linked(
        leave_out_kernel, 3,
        [cube(attn_low), (attn_full,), out_a, factors, x_own],
        [wide, low_rows(16), wide, tokens],
        [((head_width, D), bf16)] + buffers,
        per * head_width,
    )
    h_all = flat(h_all)
    ffn_low, gate_lin, up_lin, act_low = ffn(h_all, ffn_full, factors, ffn_b)
    down_low, own_out, grad_mlp, own_cot = linked(
        leave_down_kernel, 4,
        [(cube(act_low),), (down_full,), down_a, factors, (hidden,), cot_mid],
        [low_rows(16), own, own, own],
        [((4, count, ff_width), bf16), ((ff_width, D), bf16), wide, wide] + buffers,
        per * ff_width,
    )
    dm_all, down_dlow, grad_ffn, out_mid = linked(
        back_down_kernel, 5,
        [grad_mlp, (down_full,), factors, down_a, (cube(gate_lin),), (cube(up_lin),), own_out],
        [tokens + (ANY,), low_rows(16), ((4, count, 2 * ff_width), bf16, ANY), (piece, bf16)],
        [tokens, ((ff_width, D), bf16)]
        + [((4, count, ff_width), bf16)] * 2
        + [((4, count, 2 * ff_width), bf16)],
        per * ff_width,
    )
    ffn_dlow, grad_hidden, grad_attn = linked(
        back_ffn_kernel, 6,
        [(grad_ffn,), (ffn_full,), ffn_b, factors, (own_cot,), (attn_lin,)],
        [low_rows(32), wide, own],
        [((4, count, 2 * ff_width), bf16), ((D, 2 * ff_width), bf16), own, wide, wide] + buffers,
        per * 2 * ff_width,
    )
    grad_heads, early_cols, early_rows = linked(
        back_out_kernel, 7,
        [grad_attn, (attn_full,), factors, out_a, out_low, cube(attn_low), flat(down_low)]
        + [flat(down_dlow), ffn_low, flat(ffn_dlow), (flat(dm_all),), (act_low,)]
        + [(flat(grad_ffn),), (h_all,)],
        [((4, count, head_width), bf16), ((64, D), bf16)]
        + [((16, head_width + 3 * ff_width), bf16)],
        [tokens, low_rows(16), ((head_width, D), bf16), ((SLAB, D), bf16)]
        + [((SLAB, ff_width), bf16), ((SLAB, 2 * ff_width), bf16), ((SLAB, D), bf16)]
        + [((16, D), f32), ((16, head_width), f32)],
        per * head_width,
    )
    weighted_q, weighted_k, grad_v, inner, layer_out = attend_back(
        q_low, k_low, v_low, attn_low, flat(grad_heads), log_sums, qkv_lin, head_gain, *tables,
        out_mid,
    )
    grad_qkv, qkv_dlow, own_rows = linked(
        prepare_kernel, 8,
        [(weighted_q,), (weighted_k,), grad_v, (qkv_lin,), inverses, inner, qkv_b, flat(qkv_low)]
        + [early_rows],
        [((SLAB, width), bf16), ((SLAB, 48), bf16)]
        + [((16, width + head_width + 3 * ff_width), bf16)],
        [((SLAB, head_width), f32)] * 2
        + [((SLAB, 2 * head_width), f32), ((SLAB, 8), f32), ((4, 8, SLAB), f32)],
        per * 128,
    )
    every = lax.all_gather(own_rows, ("tok", "col"), axis=0)
    numbers = jnp.arange(ADAPTERS, dtype=jnp.int32)
    chosen = (adapter_ids.T[:, None, :] == numbers[None, :, None]).astype(f32).reshape(7, -1)
    chosen = jnp.pad(chosen, ((0, 1), (0, 0)))
    grad_in, col_parts = linked(
        back_qkv_kernel, 9,
        [cube(grad_qkv), cube(qkv_dlow), (attn_full,), factors, (grad_hidden,), (x_all,)]
        + [early_cols, chosen],
        [(layer_in.shape, f32), ((4, ADAPTERS, 32, piece[2]), bf16)],
        [((D, width), bf16), wide, tokens, wide, (piece, bf16), (piece, bf16)]
        + [(layer_in.shape, bf16)]
        + [((4, 32, D), bf16)] * 2
        + [((4, 32, piece[2]), bf16), ((8, 32, piece[2]), bf16)]
        + [((ADAPTERS, 32, piece[2]), bf16)]
        + buffers,
        per * width,
    )
    col_grads = []
    for p in range(7):
        rows = slice(p % 2 * RANK, (p % 2 + 1) * RANK)
        col_grads.append(col_parts[p // 2, :, rows].astype(f32))
    row_grads, at = [], 0
    for p in range(7):
        size = ff_width if p > 3 else head_width
        row_grads.append(place(adapter_ids[:, p], every[:, :, at : at + size]))
        at += size
    return layer_out.astype(f32), grad_in, col_grads, row_grads


def diagonal(values, count):
    width = values.shape[1] // count
    return jnp.concatenate(
        [
            values[k * RANK : (k + 1) * RANK, k * width : (k + 1) * width]
            for k in range(count)
        ],
        axis=1,
    )


def on_device(
    layer_in,
    cotangent,
    qkv_weight,
    out_weight,
    ffn_weight,
    down_weight,
    qk_gain,
    post_gain,
    qkv_lower,
    qkv_raise,
    out_lower,
    out_raise,
    ffn_lower,
    ffn_raise,
    down_lower,
    down_raise,
    adapter_ids,
    prompt_len,
):
    group = lax.axis_index("tok") * lax.axis_size("col") + lax.axis_index("col")
    length = lax.dynamic_index_in_dim(prompt_len, group, 0, keepdims=False)
    cosine, sine = rotation(token_places(length), HEAD_DIM)
    cosine = jnp.concatenate([cosine, cosine], axis=1)
    sine = jnp.concatenate([-sine, sine], axis=1)
    slots = jnp.arange(SLAB, dtype=jnp.int32)
    bias = jnp.where((slots < length) | (slots >= PROMPT), 0.0, very_low)[:, None].astype(f32)

    plane = (lax.axis_size("tok"), lax.axis_size("row"), lax.axis_size("col"))
    layer = linked_layer if plane == (2, 4, 4) else split_layer
    adapters = [
        qkv_lower.swapaxes(2, 3), out_raise, ffn_lower.swapaxes(2, 3), down_raise,
        qkv_raise, out_lower.swapaxes(1, 2), ffn_raise, down_lower.swapaxes(1, 2),
    ]
    layer_out, grad_in, col_grads, row_grads = layer(
        layer_in, cotangent, qkv_weight, out_weight, ffn_weight, down_weight, qk_gain.astype(f32),
        post_gain, adapters, adapter_ids, (cosine, sine, bias),
    )
    return (
        layer_out,
        grad_in,
        jnp.stack(col_grads[0:3]).swapaxes(2, 3),
        jnp.stack(row_grads[0:3]),
        row_grads[3].swapaxes(1, 2),
        col_grads[3],
        jnp.stack(col_grads[4:6]).swapaxes(2, 3),
        jnp.stack(row_grads[4:6]),
        row_grads[6].swapaxes(1, 2),
        col_grads[6],
    )


def solution(mesh):
    return jax.shard_map(
        on_device,
        mesh=mesh,
        in_specs=(
            P(("tok", "row"), "col"),
            P(("tok", "row"), "col"),
            P(None, "col", "row"),
            P("row", "col"),
            P(None, "col", "row"),
            P("row", "col"),
            P(None, "row"),
            P(None, "col"),
            P(None, None, "col", None),
            P(None, None, None, "row"),
            P(None, "row", None),
            P(None, None, "col"),
            P(None, None, "col", None),
            P(None, None, None, "row"),
            P(None, "row", None),
            P(None, None, "col"),
            P(),
            P(),
        ),
        out_specs=(
            P(("tok", "row"), "col"),
            P(("tok", "row"), "col"),
            P(None, None, "col", None),
            P(None, None, None, "row"),
            P(None, "row", None),
            P(None, None, "col"),
            P(None, None, "col", None),
            P(None, None, None, "row"),
            P(None, "row", None),
            P(None, None, "col"),
        ),
        check_vma=False,
    )
```

time: 823 us -> 732 us (0.89)
  blocking collectives: 39.5 us -> 0 us
  Pallas kernels: 618 us -> 586 us
  waiting for transfers between devices: 49 us -> 80.7 us
  local copies, waits for them, and re-layouts: 42.4 us -> 19.8 us
  matrix products: 15.2 us -> 0 us
  other arithmetic: 30.2 us -> 21.6 us
    all_gather x4, waiting for transfers between devices: 38.3 us -> 80.6 us  [the longest x3 80.6 us: gathered(): return lax.all_gather(local, ('col', 'tok'), axis=0)]
    all_gather x1 -> x0, blocking collectives: 39.5 us -> none  [row_sums(): every = lax.all_gather(own, ('tok', 'col'), axis=0)]
    pallas_call x10, Pallas kernels: 589 us -> 554 us  [the longest x9 524 us: linked(): pl.pallas_call(kernel, in_specs=specs, out_specs=[ANY if len(out) == 3 el...]
    dot_general x14 -> x0, matrix products: 15.2 us -> none  [pick(): return jnp.tensordot(onehot, adapters, axes=1)]
    dot_general x5 -> x0, local copies, waits for them, and re-layouts: 10.6 us -> none  [pick(): return jnp.tensordot(onehot, adapters, axes=1)]
    all_to_all x2 -> x0, waiting for transfers between devices: 10.6 us -> none  [col_sums(): parts = lax.all_to_all(parts.transpose(2, 0, 1, 3), 'col', 0, 0, tiled=True)]
    unnamed x74 -> x39, local copies, waits for them, and re-layouts: 19.5 us -> 11.5 us
  transfers between devices with their start and end apart: 7 -> 4, of which waited for: 4 -> 2; matrix products, arithmetic and copies ran while one was open for 6% -> 2% of each run, Pallas kernels for 42% -> 47%
where the time goes in v4:
time: 732 us; the launch traced here: 723 us
  Pallas kernels  586 us (80%)
  waiting for transfers between devices  80.7 us (11%)
  other arithmetic  21.6 us (3%)
  local copies, waits for them, and re-layouts  19.8 us (3%)
  between operations  14.4 us (2%)
    pallas_call x9, Pallas kernels, linked(): pl.pallas_call(kernel, in_specs=specs, out_specs=[ANY if len(out) == 3 el...  524 us
    all_gather x3, waiting for transfers between devices, gathered(): return lax.all_gather(local, ('col', 'tok'), axis=0)  80.6 us
    pallas_call x1, Pallas kernels, ffn(): pl.pallas_call(ffn_kernel, grid=(tiles,), in_specs=[whole(h_all), part(0)...  30.4 us
    pallas_call x1, Pallas kernels, attend_back(): pl.pallas_call(attend_back_kernel, grid=(heads,), in_specs=[col(0)] * 5 +...  17.9 us
  transfers between devices with their start and end apart: 4, of which 2 were waited for; matrix products, arithmetic and copies ran while one was open for 2% of the time, Pallas kernels for 47%

profile of v4, /device:TPU:0, one launch (start us, length us, event | category | flops | bytes accessed | tf_op | source)
XLA Modules:
  0.0 722.6 jit_solution(13087871262404437669)
XLA Ops:
  7.2 1.3 constant_dynamic-slice_fusion.3
  9.6 1.0 pad_maximum_fusion.1
  10.7 3.2 constant_dynamic-slice_fusion.1
  14.0 1.1 constant_dynamic-slice_fusion
  16.6 71.5 %intake_kernel.1 = (bf16[288,2048]{1,0:T(8,128)(2,1)}, bf16[4,288,512]{2,1,0:T(8,128)(2,1)}, bf16[128,2048]{1,0:T(8,128)(2,1)}, bf16[48,1536]{1,0:T(8,128)(2,1)}...) custom-call(bf16[4,288,512]{2,1,0:T(8,128)(2,1)} %bitcast.485, ...), custom_call_target="tpu_custom_call" | custom-call | flops 603979776 | bytes 1509949 | tf_op jit(solution)/shard_map/intake_kernel/pallas_call | solution.py:988
  89.9 2.1 fusion.2
  92.4 38.6 %all-gather.9.cloned.1.call-done = bf16[8192,512]{1,0:T(8,128)(2,1)} async-done(((bf16[1024,512]{1,0:T(8,128)(2,1)}), bf16[8192,512]{1,0:T(8,128)(2,1)}) %all-gather.9.cloned.1.call-update) | async-done | bytes 8388624 | tf_op jit(solution)/shard_map/all_gather | solution.py:1389
  131.0 52.8 %enter_qkv_kernel.1 = (bf16[4,288,2048]{2,1,0:T(8,128)(2,1)}, bf16[4,288,48]{2,1,0:T(8,128)(2,1)}, f32[4,288,1536]{2,1,0:T(8,128)}, f32[1152,8]{1,0:T(8,128)}) custom-call(bf16[288,2048]{1,0:T(8,128)(2,1)} %get-tuple-element.58.x_ref, bf16[8,1024,512]{2,1,0:T(8,128)(2,1)} %bitcast.469, bf16[128,2048]{1,0:T(8,128)(2,1)} %get-tuple-element.59.factors_ref, ...), custom_call_target="tpu_custom_call" | custom-call | flops 7247757312 | bytes 18119392 | tf_op jit(solution)/shard_map/enter_qkv_kernel/pallas_call | solution.py:988
  183.8 1.1 copy-done.2
  184.8 13.6 %attend.1 = (bf16[1152,512]{1,0:T(8,128)(2,1)S(1)}, bf16[1152,512]{1,0:T(8,128)(2,1)S(1)}, bf16[1152,512]{1,0:T(8,128)(2,1)S(1)}, bf16[1152,512]{1,0:T(8,128)(2,1)}, f32[4,1,1152]{2,1,0:T(1,128)S(1)}) custom-call(f32[1152,1536]{1,0:T(8,128)} %bitcast.463, f32[1152,1536]{1,0:T(8,128)} %bitcast.464, f32[1152,1536]{1,0:T(8,128)} %bitcast.465, ...), custom_call_target="tpu_custom_call" | custom-call | flops 2717908992 | bytes 11796480 | tf_op jit(solution)/shard_map/attend/pallas_call | solution.py:1117
  198.5 1.0 copy-done.7
  199.5 1.0 copy-done.8
  200.5 1.0 copy-done.9
  201.5 88.4 %leave_out_kernel.1 = (f32[288,2048]{1,0:T(8,128)}, bf16[4,288,16]{2,1,0:T(8,128)(2,1)}, f32[288,2048]{1,0:T(8,128)}, bf16[4,288,2048]{2,1,0:T(8,128)(2,1)}) custom-call(bf16[4,288,512]{2,1,0:T(8,128)(2,1)} %bitcast.478, bf16[8,1024,512]{2,1,0:T(8,128)(2,1)} %bitcast.470, bf16[16,512]{1,0:T(8,128)(2,1)} %get-tuple-element.67.f1_ref.f2_ref, ...), custom_call_target="tpu_custom_call" | custom-call | flops 2415919104 | bytes 6039797 | tf_op jit(solution)/shard_map/leave_out_kernel/pallas_call | solution.py:988
  289.9 30.4 %ffn.1 = (bf16[1152,32]{1,0:T(8,128)(2,1)S(1)}, bf16[1152,2048]{1,0:T(8,128)(2,1)S(1)}, bf16[1152,2048]{1,0:T(8,128)(2,1)}, bf16[1152,2048]{1,0:T(8,128)(2,1)}) custom-call(bf16[1152,2048]{1,0:T(8,128)(2,1)} %bitcast.474, bf16[8,2,256,2048]{3,2,1,0:T(8,128)(2,1)} %bitcast.496, bf16[8,2,256,2048]{3,2,1,0:T(8,128)(2,1)} %bitcast.497, ...), custom_call_target="tpu_custom_call" | custom-call | flops 19327352832 | bytes 40370176 | tf_op jit(solution)/shard_map/ffn/pallas_call | solution.py:581
  321.1 2.1 copy-done.11
  323.2 42.0 %all-gather.13.cloned.1.call-done = bf16[8192,512]{1,0:T(8,128)(2,1)} async-done(((bf16[1024,512]{1,0:T(8,128)(2,1)}), bf16[8192,512]{1,0:T(8,128)(2,1)}) %all-gather.13.cloned.1.call-update) | async-done | bytes 8388624 | tf_op jit(solution)/shard_map/all_gather | solution.py:1389
  365.2 53.7 %leave_down_kernel.1 = (bf16[4,288,16]{2,1,0:T(8,128)(2,1)}, bf16[288,2048]{1,0:T(8,128)(2,1)}, bf16[288,2048]{1,0:T(8,128)(2,1)}, bf16[288,2048]{1,0:T(8,128)(2,1)}) custom-call(bf16[4,288,2048]{2,1,0:T(8,128)(2,1)} %bitcast.476, bf16[8,1024,512]{2,1,0:T(8,128)(2,1)} %bitcast.499, bf16[16,2048]{1,0:T(8,128)(2,1)} %get-tuple-element.71.f1_ref.f2_ref, ...), custom_call_target="tpu_custom_call" | custom-call | flops 9663676416 | bytes 24159192 | tf_op jit(solution)/shard_map/leave_down_kernel/pallas_call | solution.py:988
  418.9 52.2 %back_down_kernel.1 = (bf16[4,288,2048]{2,1,0:T(8,128)(2,1)}, bf16[4,288,16]{2,1,0:T(8,128)(2,1)}, bf16[4,288,4096]{2,1,0:T(8,128)(2,1)}, bf16[4,288,512]{2,1,0:T(8,128)(2,1)}) custom-call(bf16[288,2048]{1,0:T(8,128)(2,1)} %get-tuple-element.74.dm_ref, bf16[8,1024,512]{2,1,0:T(8,128)(2,1)} %bitcast.500, bf16[128,2048]{1,0:T(8,128)(2,1)} %get-tuple-element.59.factors_ref, ...), custom_call_target="tpu_custom_call" | custom-call | flops 9663676416 | bytes 24159192 | tf_op jit(solution)/shard_map/back_down_kernel/pallas_call | solution.py:988
  471.1 65.6 %back_ffn_kernel.1 = (bf16[4,288,32]{2,1,0:T(8,128)(2,1)}, f32[288,2048]{1,0:T(8,128)}, bf16[288,2048]{1,0:T(8,128)(2,1)}) custom-call(bf16[4,288,4096]{2,1,0:T(8,128)(2,1)} %get-tuple-element.78.y_hbm, bf16[8,2,256,2048]{3,2,1,0:T(8,128)(2,1)} %bitcast.498, bf16[32,4096]{1,0:T(8,128)(2,1)} %get-tuple-element.69.fg_ref.fu_ref.f1_ref, ...), custom_call_target="tpu_custom_call" | custom-call | flops 19327352832 | bytes 48318384 | tf_op jit(solution)/shard_map/back_ffn_kernel/pallas_call | solution.py:988
  536.7 46.0 %back_out_kernel.1 = (bf16[4,288,512]{2,1,0:T(8,128)(2,1)}, bf16[64,2048]{1,0:T(8,128)(2,1)}, bf16[16,6656]{1,0:T(8,128)(2,1)}) custom-call(bf16[288,2048]{1,0:T(8,128)(2,1)} %get-tuple-element.81.da_ref, bf16[8,1024,512]{2,1,0:T(8,128)(2,1)} %bitcast.471, bf16[128,2048]{1,0:T(8,128)(2,1)} %get-tuple-element.59.factors_ref, ...), custom_call_target="tpu_custom_call" | custom-call | flops 2415919104 | bytes 6039797 | tf_op jit(solution)/shard_map/back_out_kernel/pallas_call | solution.py:988
  582.7 17.9 %attend_back.1 = (f32[1152,512]{1,0:T(8,128)}, f32[1152,512]{1,0:T(8,128)}, bf16[1152,512]{1,0:T(8,128)(2,1)S(1)}, f32[2,1152,128]{2,1,0:T(8,128)S(1)}, bf16[1152,512]{1,0:T(8,128)(2,1)S(1)}) custom-call(bf16[1152,512]{1,0:T(8,128)(2,1)} %copy-done.7, bf16[1152,512]{1,0:T(8,128)(2,1)} %copy-done.8, bf16[1152,512]{1,0:T(8,128)(2,1)} %copy-done.9, ...), custom_call_target="tpu_custom_call" | custom-call | flops 6794772480 | bytes 17694720 | tf_op jit(solution)/shard_map/attend_back/pallas_call | solution.py:1140
  601.6 1.0 copy-done.5
  602.6 13.0 %prepare_kernel.1 = (bf16[1152,1536]{1,0:T(8,128)(2,1)}, bf16[1152,48]{1,0:T(8,128)(2,1)}, bf16[16,8192]{1,0:T(8,128)(2,1)}) custom-call(f32[1152,512]{1,0:T(8,128)} %get-tuple-element.92.wq_hbm, f32[1152,512]{1,0:T(8,128)} %get-tuple-element.93.wk_hbm, bf16[1152,512]{1,0:T(8,128)(2,1)} %copy-done.4, f32[1152,1536]{1,0:T(8,128)} %bitcast.468, ...), custom_call_target="tpu_custom_call" | custom-call | flops 603979776 | bytes 1509949 | tf_op jit(solution)/shard_map/prepare_kernel/pallas_call | solution.py:988
  616.6 80.9 %back_qkv_kernel.1 = (f32[1152,512]{1,0:T(8,128)}, bf16[4,8,32,512]{3,2,1,0:T(8,128)(2,1)}) custom-call(bf16[4,288,1536]{2,1,0:T(8,128)(2,1)} %bitcast.501, bf16[4,288,48]{2,1,0:T(8,128)(2,1)} %bitcast.503, bf16[8,1024,512]{2,1,0:T(8,128)(2,1)} %bitcast.472, bf16[128,2048]{1,0:T(8,128)(2,1)} %get-tuple-element.59.factors_ref, ...), custom_call_target="tpu_custom_call" | custom-call | flops 7247757312 | bytes 18119392 | tf_op jit(solution)/shard_map/back_qkv_kernel/pallas_call | solution.py:988
  697.5 1.7 convert_element_type.46
  702.0 1.6 convert_bitcast_fusion.9
  703.5 1.0 fusion.18
  707.8 1.5 pad_maximum_fusion
  710.9 1.6 multiply_add_fusion
  713.4 1.4 copy.31
  714.8 1.0 copy-done.1
  (80 shorter events, 15.9 us)
Async XLA Ops:
  7.2 6.8 copy-start
  7.2 123.8 %all-gather.9.cloned.1.call-start = ((), (), s32[]{:S(2)}) async-start(), calls=%async_computation | async-start | bytes 9437184 | tf_op jit(solution)/shard_map/all_gather | solution.py:1389
  10.6 279.3 %all-gather.11.cloned.1.call-start = ((), (), s32[]{:S(2)}) async-start(), calls=%async_computation.1 | async-start | bytes 18874368 | tf_op jit(solution)/shard_map/all_gather | solution.py:1389
  13.9 1.3 copy-start.16
  13.9 1.3 copy-start.14
  13.9 1.5 copy-start.17
  13.9 2.2 copy-start.18
  13.9 351.3 %all-gather.13.cloned.1.call-start = ((), (), s32[]{:S(2)}) async-start(), calls=%async_computation.2 | async-start | bytes 9437184 | tf_op jit(solution)/shard_map/all_gather | solution.py:1389
  15.1 686.9 %all-gather.15.cloned.1.call-start = ((), (), s32[]{:S(2)}) async-start(), calls=%async_computation.3 | async-start | bytes 2359296 | tf_op jit(solution)/shard_map/all_gather | solution.py:1477
  16.6 72.2 %copy-start.15 = (s32[8,7]{1,0:T(8,128)S(1)}, s32[8,7]{1,0:T(8,128)}, u32[]{:S(2)}) copy-start(s32[8,7]{1,0:T(8,128)} %ids_ref.1) | copy-start | bytes 676
  183.8 1.1 copy-start.2
  198.5 1.0 copy-start.7
  199.5 1.0 copy-start.8
  200.5 1.0 copy-start.9
  201.5 88.4 %copy-start.3 = (bf16[128,2048]{1,0:T(8,128)(2,1)S(1)}, bf16[128,2048]{1,0:T(8,128)(2,1)}, u32[]{:S(2)}) copy-start(bf16[128,2048]{1,0:T(8,128)(2,1)} %get-tuple-element.59.factors_ref) | copy-start | bytes 1572868
  201.5 88.4 %copy-start.10 = (bf16[32,4096]{1,0:T(8,128)(2,1)S(1)}, bf16[32,4096]{1,0:T(8,128)(2,1)}, u32[]{:S(2)}) copy-start(bf16[32,4096]{1,0:T(8,128)(2,1)} %get-tuple-element.69.fg_ref.fu_ref.f1_ref) | copy-start | bytes 786436
  320.4 0.7 copy-start.6
  321.1 2.1 copy-start.11
  600.6 1.0 copy-start.4
  601.6 1.0 copy-start.5
  697.5 1.7 copy-start.13
  709.9 3.5 copy-start.12
  713.4 2.4 copy-start.1
Sparse Core Ops, SparseCore 0:
  10.7 120.1 all-gather.8
  133.2 150.0 all-gather.10
  284.9 80.2 all-gather.12
  615.8 35.6 all-gather.14

commit v5 on v4

--- a/solution.py
+++ b/solution.py
@@ -149,7 +149,7 @@
     base = links.take(6)
 
     def move(owner, part, index, other):
-        place = all_ref.at[owner, part]
+        place = all_ref.at[owner, part, pl.ds(0, D)]
         return links.copy(place, place, base + index, base + index, other)
 
     sends = [move(me, top, 0, xn), move(me, low, 1, yn), move(me, low, 2, xn), move(me, top, 3, yn)]
@@ -238,10 +238,14 @@
                 copies[index].start()
         if k:
             relay(k - 1)
-        o_ref[:, cols] = product(me, k, cols)
         if hooks:
+            o_ref[:, cols] = product(me, k, cols)
             hooks[k](columns, finish)
-    relay(SLICES - 1)
+    for k in range(SLICES):
+        if k == (0 if hooks else SLICES // 2):
+            relay(SLICES - 1)
+        if not hooks:
+            o_ref[:, columns(k)] = product(me, k, columns(k))
 
     def sent():
         for copies in all_copies:
@@ -265,19 +269,27 @@
 
 
 def lower(rows, factor):
-    return (adapter_scale * mm_nt(rows, factor)).astype(bf16)
-
-
-def leave_product(y_ref, weight, f1, f2_ref, f2_rows, low_ref, loads):
-    lowered = {}
+    step = rows.shape[1] // 4
+    parts = [
+        mm_nt(rows[:, at : at + step], factor[:, at : at + step])
+        for at in range(0, rows.shape[1], step)
+    ]
+    return (adapter_scale * functools.reduce(jnp.add, parts)).astype(bf16)
+
+
+def leave_product(y_ref, weight, f1_ref, low_ref, loads):
+    depth = f1_ref.shape[1]
+    used = []
 
     def product(owner, k, cols):
-        place = len(lowered) % 4 if k == 0 else None
         if k == 0:
-            loads[place].wait()
-            low_ref[owner] = lower(y_ref[owner], f1)
-            lowered[place] = True
-        return weight(y_ref[owner], cols) + mm(low_ref[owner], f2_ref[f2_rows, cols])
+            if loads:
+                loads[len(used)].wait()
+            used.append(True)
+            lowered = lower(y_ref[owner, :, :depth], f1_ref[...])
+            low_ref[owner] = lowered
+            y_ref[owner, :, depth:] = lowered
+        return weight(y_ref[owner], cols)
 
     return product
 
@@ -285,7 +297,10 @@
 class Streams:
     def __init__(self, links, rows, blocks, late=()):
         order = (links.dg, links.xn, links.yn, links.row)
-        self.rows = links.plan(*[(rows[0].at[k], rows[1].at[k]) for k in order]) if rows else []
+        self.rows = []
+        if rows:
+            cols = pl.ds(0, rows[0].shape[2])
+            self.rows = links.plan(*[(rows[0].at[k], rows[1].at[k, :, cols]) for k in order])
         self.blocks = blocks
         self.late = links.plan(*late)
         start_all(self.rows[:1])
@@ -421,7 +436,8 @@
 def intake_kernel(
     x_hbm, cot_hbm, ids_ref, gain_ref, qkv_lower_ref, out_raise_ref, ffn_lower_ref, down_raise_ref,
     qkv_raise_ref, out_lower_ref, ffn_raise_ref, down_lower_ref,
-    own_ref, cot_ref, factors_ref, qkv_b_ref, out_a_ref, ffn_b_ref, down_a_ref,
+    own_ref, cot_ref, factors_ref, factors_t_ref, qkv_b_ref, out_a_ref, out_at_ref, ffn_b_ref,
+    down_a_ref, down_at_ref,
     middle_ref, pieces_ref, send_sem, recv_sem, local_sem,
 ):
     links = Links(send_sem, recv_sem, local_sem)
@@ -451,17 +467,23 @@
     second.start()
     turned.start()
     own = base + links.col
-    qkv_b_ref[...] = jnp.zeros_like(qkv_b_ref)
-    ffn_b_ref[...] = jnp.zeros_like(ffn_b_ref)
+    for ref in (qkv_b_ref, out_a_ref, ffn_b_ref, down_a_ref):
+        ref[...] = jnp.zeros_like(ref)
     for p in range(3):
         cols = slice(p * qkv_raise_ref.shape[3], (p + 1) * qkv_raise_ref.shape[3])
         qkv_b_ref[p * RANK : (p + 1) * RANK, cols] = qkv_raise_ref[p, ids_ref[own, p]]
     for p in range(2):
         cols = slice(p * ffn_raise_ref.shape[3], (p + 1) * ffn_raise_ref.shape[3])
-        ffn_b_ref[p * RANK : (p + 1) * RANK, cols] = ffn_raise_ref[p, ids_ref[own, 4 + p]]
-    out_a_ref[...] = out_lower_ref[ids_ref[own, 3]]
-    down_a_ref[...] = down_lower_ref[ids_ref[own, 6]]
-    for exchange in (spread, second, turned):
+        rows = slice((4 + p) * RANK, (5 + p) * RANK)
+        ffn_b_ref[rows, cols] = ffn_raise_ref[p, ids_ref[own, 4 + p]]
+    out_a_ref[OUT_B] = out_lower_ref[ids_ref[own, 3]]
+    down_a_ref[DOWN_B] = down_lower_ref[ids_ref[own, 6]]
+    spread.arrived()
+    for source, target in (
+        (out_a_ref, out_at_ref), (down_a_ref, down_at_ref), (factors_ref, factors_t_ref)
+    ):
+        target[...] = source[...].astype(f32).T.astype(bf16)
+    for exchange in (second, turned):
         exchange.arrived()
     for exchange in (first, spread, second, turned):
         exchange.sent()
@@ -475,26 +497,29 @@
     links = Links(send_sem, recv_sem, local_sem)
     width = w_ref.shape[1]
     loads = start_all(sum(load_qkv(links, w_hbm, w_ref, range(4)), []))
-    all_ref[links.row] = x_ref[...]
+    loads += links.fetch((f2_ref, w_ref.at[pl.ds(D, 128)]))
+    all_ref[links.row, :, :D] = x_ref[...]
     links.greet(rows=3)
     count = x_ref.shape[0]
     stores = []
 
     def work(owner):
-        lowered = lower(all_ref[owner], factors_ref[QKV_A])
+        lowered = lower(all_ref[owner, :, :D], factors_ref[...])
         low_ref[owner] = lowered
+        all_ref[owner, :, D:] = lowered
         rows = all_ref[owner]
         third = width // 3
         for index in range(3):
             cols = slice(index * third, (index + 1) * third)
-            value = mm(rows, w_ref[:, cols]) + mm(lowered, f2_ref[:, cols])
+            value = mm(rows, w_ref[:, cols])
             lin_ref[owner, :, cols] = value
             if index < 2:
                 place = pl.ds(pl.multiple_of(owner * count, 8), count)
                 sq_ref[index, place] = lane_sums(value * value)
         stores.extend(
             links.fetch(
-                (lin_ref.at[owner], lin_hbm.at[owner]), (all_ref.at[owner], all_hbm.at[owner])
+                (lin_ref.at[owner], lin_hbm.at[owner]),
+                (all_ref.at[owner, :, pl.ds(0, D)], all_hbm.at[owner]),
             )
         )
 
@@ -515,24 +540,19 @@
 
 
 def leave_out_kernel(
-    y_ref, w_hbm, f1_ref, factors_ref, x_ref,
+    y_hbm, w_hbm, f1_ref, factors_ref, x_ref,
     lin_ref, low_ref, hidden_ref, all_ref,
-    w_ref, out_buf, relay_buf, final_buf, send_sem, recv_sem, local_sem,
+    y_ref, w_ref, out_buf, relay_buf, final_buf, send_sem, recv_sem, local_sem,
 ):
     links = Links(send_sem, recv_sem, local_sem)
-    streams = Streams(links, None, load_out(links, w_hbm, w_ref))
+    streams = Streams(links, (y_hbm, y_ref), load_out(links, w_hbm, w_ref))
+    w_ref[f1_ref.shape[1] :] = factors_ref[...]
     links.greet()
-
-    def product(owner, k, cols):
-        if k == 0:
-            low_ref[owner] = lower(y_ref[owner], f1_ref[...])
-        return mm(y_ref[owner], w_ref[:, cols]) + mm(low_ref[owner], factors_ref[OUT_B, cols])
-
+    product = leave_product(
+        y_ref, lambda rows, cols: mm(rows, w_ref[:, cols]), f1_ref, low_ref, streams.rows
+    )
     finish_all(
-        scatter(
-            links, product, lin_ref, out_buf, relay_buf, final_buf,
-            ready=streams.ready,
-        )
+        scatter(links, product, lin_ref, out_buf, relay_buf, final_buf, ready=streams.ready)
     )
     gain = factors_ref[GAIN0].astype(f32)
 
@@ -555,7 +575,7 @@
 def ffn_kernel(h_ref, wg_ref, wu_ref, factors_ref, fg_ref, fu_ref, low_ref, gate_ref, up_ref, act_ref):
     @pl.when(pl.program_id(0) == 0)
     def _():
-        low_ref[...] = lower(h_ref[...], factors_ref[FFN_A])
+        low_ref[...] = lower(h_ref[...], factors_ref[...])
 
     lowered = low_ref[...]
     rank = lowered.shape[1] // 2
@@ -607,9 +627,9 @@
     links.greet(columns=True)
     turned = Exchange(links, "col", slot(cot_ref), features(own_cot_ref, cot_ref.shape[2]))
     turned.start()
+    w_ref[f1_ref.shape[1] :] = factors_ref[...]
     product = leave_product(
-        y_ref, lambda rows, cols: mm(rows, w_ref[:, cols]), f1_ref[...], factors_ref, DOWN_B,
-        low_ref, streams.rows,
+        y_ref, lambda rows, cols: mm(rows, w_ref[:, cols]), f1_ref, low_ref, streams.rows
     )
     finish_all(
         scatter(
@@ -636,6 +656,61 @@
     def _(tile):
         rows = pl.ds(pl.multiple_of(tile * 64, 64), 64)
         target_ref[rows] = source_ref[rows].astype(f32)
+
+
+def finish_kernel(
+    chosen_ref, out_ref, grad_ref, parts_ref, every_ref,
+    out32_ref, grad32_ref, qkv_lower_ref, out_raise_ref, ffn_lower_ref, down_raise_ref,
+    qkv_raise_ref, out_lower_ref, ffn_raise_ref, down_lower_ref,
+):
+    widen(out_ref, out32_ref)
+    widen(grad_ref, grad32_ref)
+    targets = [qkv_lower_ref.at[p] for p in range(3)]
+    targets += [out_raise_ref, ffn_lower_ref.at[0], ffn_lower_ref.at[1], down_raise_ref]
+    for p, target in enumerate(targets):
+        rows = slice(p % 2 * RANK, (p % 2 + 1) * RANK)
+        for adapter in range(ADAPTERS):
+            target[adapter] = parts_ref[p // 2, adapter, rows].astype(f32)
+    targets = [qkv_raise_ref.at[p] for p in range(3)]
+    targets += [out_lower_ref, ffn_raise_ref.at[0], ffn_raise_ref.at[1], down_lower_ref]
+    base = 0
+    for p, target in enumerate(targets):
+        step = 256
+        weights = [chosen_ref[p, at] for at in range(64)]
+
+        @pl.loop(0, target.shape[2] // step)
+        def _(tile, p=p, target=target, base=base, weights=weights):
+            cols = pl.ds(pl.multiple_of(base + tile * step, step), step)
+            here = pl.ds(pl.multiple_of(tile * step, step), step)
+            values = [every_ref[g, :, cols].astype(f32) for g in range(8)]
+            for adapter in range(ADAPTERS):
+                terms = [weights[adapter * 8 + g] * values[g] for g in range(8)]
+                target[adapter, :, here] = functools.reduce(jnp.add, terms)
+
+        base += target.shape[2]
+
+
+def finish(chosen, layer_out, grad_in, col_parts, every, head_width, ff_width):
+    piece = col_parts.shape[3]
+
+    def out(*shape):
+        return jax.ShapeDtypeStruct(shape, f32)
+
+    return pl.pallas_call(
+        finish_kernel,
+        in_specs=[SMEM] + [VMEM] * 4,
+        out_specs=[VMEM] * 10,
+        out_shape=[
+            out(*layer_out.shape), out(*grad_in.shape),
+            out(3, ADAPTERS, RANK, piece), out(ADAPTERS, RANK, piece),
+            out(2, ADAPTERS, RANK, piece), out(ADAPTERS, RANK, piece),
+            out(3, ADAPTERS, RANK, head_width), out(ADAPTERS, RANK, head_width),
+            out(2, ADAPTERS, RANK, ff_width), out(ADAPTERS, RANK, ff_width),
+        ],
+        compiler_params=pltpu.CompilerParams(vmem_limit_bytes=48 << 20),
+        cost_estimate=pl.CostEstimate(flops=10**8, bytes_accessed=16 << 20, transcendentals=0),
+        name="finish",
+    )(chosen, layer_out, grad_in, col_parts, every)
 
 
 def back_down_kernel(
@@ -650,7 +725,8 @@
         links.plan((gate_hbm.at[k], gate_ref.at[k]), (up_hbm.at[k], up_ref.at[k])) for k in order
     ]
     start_all(gates[0])
-    all_ref[links.row] = dm_ref[...]
+    all_ref[links.row, :, :D] = dm_ref[...]
+    w_ref[:, D:] = f2_ref[...]
     links.greet(columns=True)
     width = w_ref.shape[0]
     turned = Exchange(links, "col", features(out_ref, out_mid_ref.shape[2]), slot(out_mid_ref))
@@ -664,12 +740,13 @@
 
     def work(owner):
         wait_all(gates[len(stores) // 2])
-        lowered = lower(all_ref[owner], factors_ref[DOWN_B])
+        lowered = lower(all_ref[owner, :, :D], factors_ref[...])
         low_ref[owner] = lowered
+        all_ref[owner, :, D:] = lowered
 
         def body(at):
             cols, far = pl.ds(at, TILE), pl.ds(pl.multiple_of(width + at, TILE), TILE)
-            grad = mm_nt(all_ref[owner], w_ref[cols, :]) + mm(lowered, f2_ref[:, cols])
+            grad = mm_nt(all_ref[owner], w_ref[cols, :])
             gate, up = gate_ref[owner, :, cols].astype(f32), up_ref[owner, :, cols].astype(f32)
             grad_gate, grad_up = gated_back(grad, gate, up)
             grad_ref[owner, :, cols] = grad_gate.astype(bf16)
@@ -678,7 +755,8 @@
         each_tile(width, TILE, body)
         stores.extend(
             links.fetch(
-                (grad_ref.at[owner], grad_hbm.at[owner]), (all_ref.at[owner], all_hbm.at[owner])
+                (grad_ref.at[owner], grad_hbm.at[owner]),
+                (all_ref.at[owner, :, pl.ds(0, D)], all_hbm.at[owner]),
             )
         )
 
@@ -689,7 +767,7 @@
 
 
 def back_ffn_kernel(
-    y_hbm, w_hbm, f1_ref, factors_ref, cot_hbm, attn_hbm,
+    y_hbm, w_hbm, f1_ref, factors_ref, factors_t_ref, cot_hbm, attn_hbm,
     low_ref, hidden_ref, da_ref,
     y_ref, w_ref, cot_ref, attn_ref, lin_ref, out_buf, relay_buf, final_buf,
     send_sem, recv_sem, local_sem,
@@ -702,9 +780,9 @@
         [(cot_hbm, cot_ref), (attn_hbm, attn_ref)],
     )
     links.greet()
+    w_ref[:, f1_ref.shape[1] :] = factors_t_ref[...]
     product = leave_product(
-        y_ref, lambda rows, cols: mm_nt(rows, w_ref[cols, :]), f1_ref[...], factors_ref, FFN_A,
-        low_ref, streams.rows,
+        y_ref, lambda rows, cols: mm_nt(rows, w_ref[cols, :]), f1_ref, low_ref, streams.rows
     )
     finish_all(
         scatter(
@@ -731,11 +809,12 @@
     da_ref, w_hbm, factors_ref, f2_ref, out_low_ref, attn_ref, down_low_ref, down_dlow_ref,
     ffn_low_ref, ffn_dlow_ref, dm_hbm, act_hbm, grad_hbm, h_hbm,
     heads_ref, cols_ref, rows_ref,
-    all_ref, low_ref, w_ref, dm_ref, act_ref, grad_ref, h_ref, raise_ref, lower_ref, send_sem, recv_sem, local_sem,
+    all_ref, w_ref, dm_ref, act_ref, grad_ref, h_ref, raise_ref, lower_ref, send_sem, recv_sem, local_sem,
 ):
     links = Links(send_sem, recv_sem, local_sem)
     load = start_all(sum(load_out(links, w_hbm, w_ref), []))
-    all_ref[links.row] = da_ref[...]
+    all_ref[links.row, :, :D] = da_ref[...]
+    w_ref[:, D:] = f2_ref[...]
     links.greet()
     loads = []
 
@@ -749,21 +828,21 @@
 
     def after():
         wait_all(loads)
-        down_raise = mm_tn(down_low_ref[...], dm_ref[...])
+        down_raise = mm_tn(down_low_ref[:, DOWN_B], dm_ref[...])
         cols_ref[3 * RANK : 4 * RANK] = down_raise.astype(bf16)
-        cols_ref[RANK : 3 * RANK] = mm_tn(ffn_dlow_ref[...], h_ref[...]).astype(bf16)
-        both = mm_tn(ffn_low_ref[...], grad_ref[...]).astype(bf16)
-        rows_ref[:, heads : heads + half] = both[:RANK, :half]
-        rows_ref[:, heads + half : heads + 2 * half] = both[RANK:, half:]
-        rows_ref[:, heads + 2 * half :] = mm_tn(down_dlow_ref[...], act_ref[...]).astype(bf16)
+        cols_ref[RANK : 3 * RANK] = mm_tn(ffn_dlow_ref[:, FFN_A], h_ref[...]).astype(bf16)
+        for p in range(2):
+            low = ffn_low_ref[:, (4 + p) * RANK : (5 + p) * RANK]
+            raised = mm_tn(low, grad_ref[:, p * half : (p + 1) * half])
+            rows_ref[:, heads + p * half : heads + (p + 1) * half] = raised.astype(bf16)
+        rows_ref[:, heads + 2 * half :] = mm_tn(down_dlow_ref[:, DOWN_B], act_ref[...]).astype(bf16)
 
     def work(owner):
-        lowered = lower(all_ref[owner], factors_ref[OUT_B])
-        low_ref[owner] = lowered
-        value = mm_nt(all_ref[owner], w_ref[...]) + mm(lowered, f2_ref[...])
-        heads_ref[owner] = value.astype(bf16)
-        raise_ref[...] += mm_tn(out_low_ref[owner], all_ref[owner])
-        lower_ref[...] += mm_tn(low_ref[owner], attn_ref[owner])
+        lowered = lower(all_ref[owner, :, :D], factors_ref[...])
+        all_ref[owner, :, D:] = lowered
+        heads_ref[owner] = mm_nt(all_ref[owner], w_ref[...]).astype(bf16)
+        raise_ref[...] += mm_tn(out_low_ref[owner, :, OUT_B], all_ref[owner, :, :D])
+        lower_ref[...] += mm_tn(lowered[:, OUT_B], attn_ref[owner])
 
     raise_ref[...] = jnp.zeros_like(raise_ref)
     lower_ref[...] = jnp.zeros_like(lower_ref)
@@ -774,7 +853,7 @@
 
 def prepare_kernel(
     wq_hbm, wk_hbm, dv_ref, lin_hbm, inv_ref, inner_ref, f1_ref, low_ref, early_ref,
-    grad_ref, dlow_ref, rows_ref,
+    grad_ref, rows_ref,
     wq_ref, wk_ref, lin_ref, total_ref, stat_ref, send_sem, recv_sem, local_sem,
 ):
     links = Links(send_sem, recv_sem, local_sem)
@@ -799,9 +878,9 @@
             one = slice(index, index + 1)
             value = inverse[:, one] * source[rows] - lin_ref[rows, cols] * factor[:, one]
             grad_ref[rows, cols] = value.astype(bf16)
-        grad_ref[rows, 2 * third :] = dv_ref[rows]
-
-    dlow_ref[...] = lower(grad_ref[...], f1_ref[...])
+        grad_ref[rows, 2 * third : 3 * third] = dv_ref[rows]
+
+    grad_ref[:, 3 * third :] = lower(grad_ref[:, : 3 * third], f1_ref[...])
     for index in range(3):
         cols = slice(index * third, (index + 1) * third)
         low = low_ref[:, index * RANK : (index + 1) * RANK]
@@ -810,9 +889,9 @@
 
 
 def back_qkv_kernel(
-    grad_ref, dlow_ref, w_hbm, factors_ref, hidden_hbm, x_hbm, early_ref, chosen_ref,
-    final_ref, sums_ref,
-    w_ref, hidden_ref, x_ref, sum_ref, own_ref, middle_ref, turn_buf, parts_ref, got_ref, total_ref, groups_ref,
+    grad_ref, w_hbm, factors_t_ref, hidden_hbm, x_hbm, early_ref, chosen_ref,
+    turn_buf, sums_ref,
+    w_ref, hidden_ref, x_ref, sum_ref, own_ref, middle_ref, parts_ref, got_ref, total_ref, groups_ref,
     placed_ref, out_buf, relay_buf, final_buf, send_sem, recv_sem, local_sem,
 ):
     links = Links(send_sem, recv_sem, local_sem)
@@ -823,7 +902,9 @@
         load_qkv(links, w_hbm, w_ref, [links.col ^ step for step in steps]),
         [(hidden_hbm, hidden_ref)],
     )
-    x_load = links.fetch((x_hbm, x_ref))
+    x_load = links.plan((x_hbm, x_ref))
+    depth = w_ref.shape[1] - 128
+    w_ref[:, depth:] = factors_t_ref[...]
     links.greet(rows=3, columns=True, twin=True)
     width = own_ref.shape[2]
     count = grad_ref.shape[1]
@@ -842,7 +923,7 @@
         wait_all(x_load)
         late = 0.0
         for owner in range(4):
-            late = late + mm_tn(dlow_ref[owner], x_ref[owner])
+            late = late + mm_tn(grad_ref[owner, :, depth : depth + 3 * RANK], x_ref[owner])
         late = late.astype(bf16)
         parts_ref[0] = late[0 : 2 * RANK]
         parts_ref[1, :RANK] = late[2 * RANK :]
@@ -879,8 +960,7 @@
         spread.start()
 
     def product(owner, k, cols):
-        value = mm_nt(grad_ref[owner], w_ref[cols, :])
-        return value + mm(dlow_ref[owner], factors_ref[QKV_A, cols])
+        return mm_nt(grad_ref[owner], w_ref[cols, :])
 
     z_base, row_base = links.take(3), links.take(4)
     near = links.local(middle_ref.at[links.row], token_rows(turn_buf, count)(links.row))
@@ -932,36 +1012,39 @@
         def _():
             to_row(step).start()
 
+    def first(columns, finish):
+        start_all(x_load)
+
     def second(columns, finish):
+        lower_grad()
+
+    def third(columns, finish):
         add_rows()
-
-    def third(columns, finish):
-        share()
         wait_all(streams.late)
         leave_col(0, columns, finish)
 
     def fourth(columns, finish):
-        place_groups()
+        share()
         leave_col(1, columns, finish)
 
     columns, finish, sent = scatter(
         links, product, sum_ref, out_buf, relay_buf, final_buf,
         block=lambda k: links.col ^ steps[k],
         ready=streams.ready,
-        hooks=[lambda columns, finish: lower_grad(), second, third, fourth],
+        hooks=[first, second, third, fourth],
     )
     leave_row(0)
+    place_groups()
     leave_col(2, columns, finish)
-    leave_row(1)
     leave_col(3, columns, finish)
     leave_row(3)
     leave_row(2)
+    leave_row(1)
     near.wait()
     for step in range(1, 4):
         landed = token_rows(turn_buf, count)(links.row ^ step)
         at = row_base + step
         links.copy(landed, landed, at, at, links.row ^ step).wait_recv()
-    widen(turn_buf, final_ref)
     spread.arrived()
     for step in range(1, 4):
         to_row(step).wait_send()
@@ -1353,7 +1436,11 @@
         part = ff_width if p > 3 else head_width
         row_grads.append(place(adapter_ids[:, p], every[:, :, at : at + part]))
         at += part
-    return layer_out, grad_in, col_grads, row_grads
+    return (
+        layer_out, grad_in,
+        jnp.stack(col_grads[0:3]), col_grads[3], jnp.stack(col_grads[4:6]), col_grads[6],
+        jnp.stack(row_grads[0:3]), row_grads[3], jnp.stack(row_grads[4:6]), row_grads[6],
+    )
 
 
 def flat(values):
@@ -1378,9 +1465,6 @@
     own = ((count, D), bf16)
     wide = ((count, D), f32)
 
-    def low_rows(size):
-        return ((4, count, size), bf16)
-
     def gather_halves(local, axis):
         half = local.shape[axis] // 2
         return lax.dynamic_slice_in_dim(local, lax.axis_index("tok") * half, half, axis)
@@ -1396,21 +1480,26 @@
     ffn_full = gathered(gather_halves(ffn_weight, 1))
     down_full = gathered(gather_halves(down_weight, 0))
 
-    x_own, cot_mid, factors, qkv_b, out_a, ffn_b, down_a = linked(
+    (
+        x_own, cot_mid, factors, factors_t, qkv_b, out_a, out_at, ffn_b, down_a, down_at
+    ) = linked(
         intake_kernel, 1,
         [(cube(layer_in),), (cube(cotangent),), adapter_ids]
         + [jnp.pad(post_gain, ((0, RANK - 2), (0, 0)))]
         + adapters,
-        [own, (piece, bf16), ((128, D), bf16), ((48, width), bf16), ((16, head_width), bf16)]
-        + [((32, 2 * ff_width), bf16), ((16, ff_width), bf16)],
+        [own, (piece, bf16), ((128, D), bf16), ((D, 128), bf16), ((128, width), bf16)]
+        + [((128, head_width), bf16), ((head_width, 128), bf16), ((128, 2 * ff_width), bf16)]
+        + [((128, ff_width), bf16), ((ff_width, 128), bf16)],
         [(piece, bf16), ((4, 128, piece[2]), bf16)],
         per * 128,
     )
+    low = ((4, count, 128), bf16)
+    tall = ((4, count, D + 128), bf16)
     x_all, qkv_low, qkv_lin, inverses = linked(
         enter_qkv_kernel, 2,
-        [x_own, (attn_full,), factors, qkv_b],
-        [tokens + (ANY,), low_rows(48), ((4, count, width), f32, ANY), ((SLAB, 8), f32)],
-        [tokens, ((4, count, width), f32), ((D, width), bf16), ((2, SLAB, 128), f32)]
+        [x_own, (attn_full,), factors, (qkv_b,)],
+        [tokens + (ANY,), low, ((4, count, width), f32, ANY), ((SLAB, 8), f32)],
+        [tall, ((4, count, width), f32), ((D + 128, width), bf16), ((2, SLAB, 128), f32)]
         + [((4, 8, SLAB), f32)],
         per * width,
     )
@@ -1418,9 +1507,9 @@
     q_low, k_low, v_low, attn_low, log_sums = attend(qkv_lin, inverses, head_gain, *tables)
     attn_lin, out_low, hidden, h_all = linked(
         leave_out_kernel, 3,
-        [cube(attn_low), (attn_full,), out_a, factors, x_own],
-        [wide, low_rows(16), wide, tokens],
-        [((head_width, D), bf16)] + buffers,
+        [(cube(attn_low),), (attn_full,), out_a, factors, x_own],
+        [wide, low, wide, tokens],
+        [((4, count, head_width + 128), bf16), ((head_width + 128, D), bf16)] + buffers,
         per * head_width,
     )
     h_all = flat(h_all)
@@ -1428,34 +1517,35 @@
     down_low, own_out, grad_mlp, own_cot = linked(
         leave_down_kernel, 4,
         [(cube(act_low),), (down_full,), down_a, factors, (hidden,), cot_mid],
-        [low_rows(16), own, own, own],
-        [((4, count, ff_width), bf16), ((ff_width, D), bf16), wide, wide] + buffers,
+        [low, own, own, own],
+        [((4, count, ff_width + 128), bf16), ((ff_width + 128, D), bf16), wide, wide] + buffers,
         per * ff_width,
     )
     dm_all, down_dlow, grad_ffn, out_mid = linked(
         back_down_kernel, 5,
-        [grad_mlp, (down_full,), factors, down_a, (cube(gate_lin),), (cube(up_lin),), own_out],
-        [tokens + (ANY,), low_rows(16), ((4, count, 2 * ff_width), bf16, ANY), (piece, bf16)],
-        [tokens, ((ff_width, D), bf16)]
+        [grad_mlp, (down_full,), factors, down_at, (cube(gate_lin),), (cube(up_lin),), own_out],
+        [tokens + (ANY,), low, ((4, count, 2 * ff_width), bf16, ANY), (piece, bf16)],
+        [tall, ((ff_width, D + 128), bf16)]
         + [((4, count, ff_width), bf16)] * 2
         + [((4, count, 2 * ff_width), bf16)],
         per * ff_width,
     )
     ffn_dlow, grad_hidden, grad_attn = linked(
         back_ffn_kernel, 6,
-        [(grad_ffn,), (ffn_full,), ffn_b, factors, (own_cot,), (attn_lin,)],
-        [low_rows(32), wide, own],
-        [((4, count, 2 * ff_width), bf16), ((D, 2 * ff_width), bf16), own, wide, wide] + buffers,
+        [(grad_ffn,), (ffn_full,), ffn_b, factors, factors_t, (own_cot,), (attn_lin,)],
+        [low, wide, own],
+        [((4, count, 2 * ff_width + 128), bf16), ((D, 2 * ff_width + 128), bf16), own, wide, wide]
+        + buffers,
         per * 2 * ff_width,
     )
     grad_heads, early_cols, early_rows = linked(
         back_out_kernel, 7,
-        [grad_attn, (attn_full,), factors, out_a, out_low, cube(attn_low), flat(down_low)]
+        [grad_attn, (attn_full,), factors, out_at, out_low, cube(attn_low), flat(down_low)]
         + [flat(down_dlow), ffn_low, flat(ffn_dlow), (flat(dm_all),), (act_low,)]
         + [(flat(grad_ffn),), (h_all,)],
         [((4, count, head_width), bf16), ((64, D), bf16)]
         + [((16, head_width + 3 * ff_width), bf16)],
-        [tokens, low_rows(16), ((head_width, D), bf16), ((SLAB, D), bf16)]
+        [tall, ((head_width, D + 128), bf16), ((SLAB, D), bf16)]
         + [((SLAB, ff_width), bf16), ((SLAB, 2 * ff_width), bf16), ((SLAB, D), bf16)]
         + [((16, D), f32), ((16, head_width), f32)],
         per * head_width,
@@ -1464,11 +1554,11 @@
         q_low, k_low, v_low, attn_low, flat(grad_heads), log_sums, qkv_lin, head_gain, *tables,
         out_mid,
     )
-    grad_qkv, qkv_dlow, own_rows = linked(
+    grad_qkv, own_rows = linked(
         prepare_kernel, 8,
         [(weighted_q,), (weighted_k,), grad_v, (qkv_lin,), inverses, inner, qkv_b, flat(qkv_low)]
         + [early_rows],
-        [((SLAB, width), bf16), ((SLAB, 48), bf16)]
+        [((SLAB, width + 128), bf16)]
         + [((16, width + head_width + 3 * ff_width), bf16)],
         [((SLAB, head_width), f32)] * 2
         + [((SLAB, 2 * head_width), f32), ((SLAB, 8), f32), ((4, 8, SLAB), f32)],
@@ -1480,27 +1570,17 @@
     chosen = jnp.pad(chosen, ((0, 1), (0, 0)))
     grad_in, col_parts = linked(
         back_qkv_kernel, 9,
-        [cube(grad_qkv), cube(qkv_dlow), (attn_full,), factors, (grad_hidden,), (x_all,)]
+        [cube(grad_qkv), (attn_full,), factors_t, (grad_hidden,), (x_all,)]
         + [early_cols, chosen],
-        [(layer_in.shape, f32), ((4, ADAPTERS, 32, piece[2]), bf16)],
-        [((D, width), bf16), wide, tokens, wide, (piece, bf16), (piece, bf16)]
-        + [(layer_in.shape, bf16)]
+        [(layer_in.shape, bf16), ((4, ADAPTERS, 32, piece[2]), bf16)],
+        [((D, width + 128), bf16), wide, tokens, wide, (piece, bf16), (piece, bf16)]
         + [((4, 32, D), bf16)] * 2
         + [((4, 32, piece[2]), bf16), ((8, 32, piece[2]), bf16)]
         + [((ADAPTERS, 32, piece[2]), bf16)]
         + buffers,
         per * width,
     )
-    col_grads = []
-    for p in range(7):
-        rows = slice(p % 2 * RANK, (p % 2 + 1) * RANK)
-        col_grads.append(col_parts[p // 2, :, rows].astype(f32))
-    row_grads, at = [], 0
-    for p in range(7):
-        size = ff_width if p > 3 else head_width
-        row_grads.append(place(adapter_ids[:, p], every[:, :, at : at + size]))
-        at += size
-    return layer_out.astype(f32), grad_in, col_grads, row_grads
+    return finish(chosen, layer_out, grad_in, col_parts, every, head_width, ff_width)
 
 
 def diagonal(values, count):
@@ -1548,21 +1628,24 @@
         qkv_lower.swapaxes(2, 3), out_raise, ffn_lower.swapaxes(2, 3), down_raise,
         qkv_raise, out_lower.swapaxes(1, 2), ffn_raise, down_lower.swapaxes(1, 2),
     ]
-    layer_out, grad_in, col_grads, row_grads = layer(
+    (
+        layer_out, grad_in, qkv_lower_grad, out_raise_grad, ffn_lower_grad, down_raise_grad,
+        qkv_raise_grad, out_lower_grad, ffn_raise_grad, down_lower_grad,
+    ) = layer(
         layer_in, cotangent, qkv_weight, out_weight, ffn_weight, down_weight, qk_gain.astype(f32),
         post_gain, adapters, adapter_ids, (cosine, sine, bias),
     )
     return (
         layer_out,
         grad_in,
-        jnp.stack(col_grads[0:3]).swapaxes(2, 3),
-        jnp.stack(row_grads[0:3]),
-        row_grads[3].swapaxes(1, 2),
-        col_grads[3],
-        jnp.stack(col_grads[4:6]).swapaxes(2, 3),
-        jnp.stack(row_grads[4:6]),
-        row_grads[6].swapaxes(1, 2),
-        col_grads[6],
+        qkv_lower_grad.swapaxes(2, 3),
+        qkv_raise_grad,
+        out_lower_grad.swapaxes(1, 2),
+        out_raise_grad,
+        ffn_lower_grad.swapaxes(2, 3),
+        ffn_raise_grad,
+        down_lower_grad.swapaxes(1, 2),
+        down_raise_grad,
     )
 
 

time: 732 us -> 717 us (0.980)
  other arithmetic: 21.6 us -> 5.54 us
    pallas_call x9, Pallas kernels: 524 us -> 515 us  [linked(): pl.pallas_call(kernel, in_specs=specs, out_specs=[ANY if len(out) == 3 el...]
    pallas_call x0 -> x1, Pallas kernels: none -> 7.98 us  [finish(): pl.pallas_call(finish_kernel, in_specs=[SMEM] + [VMEM] * 4, out_specs=[VM...]
  transfers between devices with their start and end apart: 4 -> 4, of which waited for: 2 -> 2; matrix products, arithmetic and copies ran while one was open for 2% -> 1% of each run, Pallas kernels for 47% -> 47%
where the time goes in v5:
time: 717 us; the launch traced here: 708 us
  Pallas kernels  584 us (81%)
  waiting for transfers between devices  83.4 us (12%)
  local copies, waits for them, and re-layouts  20.3 us (3%)
  between operations  14.5 us (2%)
    pallas_call x9, Pallas kernels, linked(): pl.pallas_call(kernel, in_specs=specs, out_specs=[ANY if len(out) == 3 el...  515 us
    all_gather x3, waiting for transfers between devices, gathered(): return lax.all_gather(local, ('col', 'tok'), axis=0)  83.3 us
    pallas_call x1, Pallas kernels, ffn(): pl.pallas_call(ffn_kernel, grid=(tiles,), in_specs=[whole(h_all), part(0)...  29.9 us
    pallas_call x1, Pallas kernels, attend_back(): pl.pallas_call(attend_back_kernel, grid=(heads,), in_specs=[col(0)] * 5 +...  17.7 us
  transfers between devices with their start and end apart: 4, of which 2 were waited for; matrix products, arithmetic and copies ran while one was open for 1% of the time, Pallas kernels for 47%

profile of v5, /device:TPU:0, one launch (start us, length us, event | category | flops | bytes accessed | tf_op | source)
XLA Modules:
  0.0 707.5 jit_solution(1384267387383833991)
XLA Ops:
  7.2 1.3 constant_dynamic-slice_fusion.3
  8.6 1.0 constant_dynamic-slice_fusion.2
  9.6 1.0 pad_maximum_fusion
  10.7 3.2 constant_dynamic-slice_fusion.1
  14.0 1.1 constant_dynamic-slice_fusion
  16.3 72.6 %intake_kernel.1 = (bf16[288,2048]{1,0:T(8,128)(2,1)}, bf16[4,288,512]{2,1,0:T(8,128)(2,1)}, bf16[128,2048]{1,0:T(8,128)(2,1)}, bf16[2048,128]{1,0:T(8,128)(2,1)...) custom-call(bf16[4,288,512]{2,1,0:T(8,128)(2,1)} %bitcast.50, ...), custom_call_target="tpu_custom_call" | custom-call | flops 603979776 | bytes 1509949 | tf_op jit(solution)/shard_map/intake_kernel/pallas_call | solution.py:1071
  89.6 0.7 fusion.1.bias_ref
  90.3 2.1 fusion.2
  92.8 37.9 %all-gather.9.cloned.1.call-done = bf16[8192,512]{1,0:T(8,128)(2,1)} async-done(((bf16[1024,512]{1,0:T(8,128)(2,1)}), bf16[8192,512]{1,0:T(8,128)(2,1)}) %all-gather.9.cloned.1.call-update) | async-done | bytes 8388624 | tf_op jit(solution)/shard_map/all_gather | solution.py:1473
  130.8 52.2 %enter_qkv_kernel.1 = (bf16[4,288,2048]{2,1,0:T(8,128)(2,1)}, bf16[4,288,128]{2,1,0:T(8,128)(2,1)}, f32[4,288,1536]{2,1,0:T(8,128)}, f32[1152,8]{1,0:T(8,128)}) custom-call(bf16[288,2048]{1,0:T(8,128)(2,1)} %get-tuple-element.70.x_ref, bf16[8,1024,512]{2,1,0:T(8,128)(2,1)} %bitcast.38, bf16[128,2048]{1,0:T(8,128)(2,1)} %get-tuple-element.71.factors_ref, ...), custom_call_target="tpu_custom_call" | custom-call | flops 7247757312 | bytes 18119392 | tf_op jit(solution)/shard_map/enter_qkv_kernel/pallas_call | solution.py:1071
  183.0 1.1 copy-done.2
  184.0 13.3 %attend.1 = (bf16[1152,512]{1,0:T(8,128)(2,1)S(1)}, bf16[1152,512]{1,0:T(8,128)(2,1)S(1)}, bf16[1152,512]{1,0:T(8,128)(2,1)S(1)}, bf16[1152,512]{1,0:T(8,128)(2,1)}, f32[4,1,1152]{2,1,0:T(1,128)S(1)}) custom-call(f32[1152,1536]{1,0:T(8,128)} %bitcast.32, f32[1152,1536]{1,0:T(8,128)} %bitcast.33, f32[1152,1536]{1,0:T(8,128)} %bitcast.34, ...), custom_call_target="tpu_custom_call" | custom-call | flops 2717908992 | bytes 11796480 | tf_op jit(solution)/shard_map/attend/pallas_call | solution.py:1200
  197.3 1.0 copy-done.11
  198.3 1.0 copy-done.12
  199.3 1.0 copy-done.13
  200.3 87.4 %leave_out_kernel.1 = (f32[288,2048]{1,0:T(8,128)}, bf16[4,288,128]{2,1,0:T(8,128)(2,1)}, f32[288,2048]{1,0:T(8,128)}, bf16[4,288,2048]{2,1,0:T(8,128)(2,1)}) custom-call(bf16[4,288,512]{2,1,0:T(8,128)(2,1)} %bitcast.47, bf16[8,1024,512]{2,1,0:T(8,128)(2,1)} %bitcast.39, bf16[128,512]{1,0:T(8,128)(2,1)} %get-tuple-element.79.f1_ref, ...), custom_call_target="tpu_custom_call" | custom-call | flops 2415919104 | bytes 6039797 | tf_op jit(solution)/shard_map/leave_out_kernel/pallas_call | solution.py:1071
  287.9 1.2 copy-done.14
  289.1 29.9 %ffn.1 = (bf16[1152,128]{1,0:T(8,128)(2,1)S(1)}, bf16[1152,2048]{1,0:T(8,128)(2,1)}, bf16[1152,2048]{1,0:T(8,128)(2,1)}, bf16[1152,2048]{1,0:T(8,128)(2,1)}) custom-call(bf16[1152,2048]{1,0:T(8,128)(2,1)} %bitcast.43, bf16[8,2,256,2048]{3,2,1,0:T(8,128)(2,1)} %bitcast.61, bf16[8,2,256,2048]{3,2,1,0:T(8,128)(2,1)} %bitcast.62, ...), custom_call_target="tpu_custom_call" | custom-call | flops 19327352832 | bytes 40370176 | tf_op jit(solution)/shard_map/ffn/pallas_call | solution.py:601
  319.7 45.4 %all-gather.13.cloned.1.call-done = bf16[8192,512]{1,0:T(8,128)(2,1)} async-done(((bf16[1024,512]{1,0:T(8,128)(2,1)}), bf16[8192,512]{1,0:T(8,128)(2,1)}) %all-gather.13.cloned.1.call-update) | async-done | bytes 8388624 | tf_op jit(solution)/shard_map/all_gather | solution.py:1473
  365.1 61.0 %leave_down_kernel.1 = (bf16[4,288,128]{2,1,0:T(8,128)(2,1)}, bf16[288,2048]{1,0:T(8,128)(2,1)}, bf16[288,2048]{1,0:T(8,128)(2,1)}, bf16[288,2048]{1,0:T(8,128)(2,1)}) custom-call(bf16[4,288,2048]{2,1,0:T(8,128)(2,1)} %bitcast.45, bf16[8,1024,512]{2,1,0:T(8,128)(2,1)} %bitcast.64, bf16[128,2048]{1,0:T(8,128)(2,1)} %get-tuple-element.83.f1_ref, ...), custom_call_target="tpu_custom_call" | custom-call | flops 9663676416 | bytes 24159192 | tf_op jit(solution)/shard_map/leave_down_kernel/pallas_call | solution.py:1071
  426.2 53.2 %back_down_kernel.1 = (bf16[4,288,2048]{2,1,0:T(8,128)(2,1)}, bf16[4,288,128]{2,1,0:T(8,128)(2,1)}, bf16[4,288,4096]{2,1,0:T(8,128)(2,1)}, bf16[4,288,512]{2,1,0:T(8,128)(2,1)}) custom-call(bf16[288,2048]{1,0:T(8,128)(2,1)} %get-tuple-element.86.dm_ref, bf16[8,1024,512]{2,1,0:T(8,128)(2,1)} %bitcast.65, bf16[128,2048]{1,0:T(8,128)(2,1)} %get-tuple-element.71.factors_ref, ...), custom_call_target="tpu_custom_call" | custom-call | flops 9663676416 | bytes 24159192 | tf_op jit(solution)/shard_map/back_down_kernel/pallas_call | solution.py:1071
  479.4 53.1 %back_ffn_kernel.1 = (bf16[4,288,128]{2,1,0:T(8,128)(2,1)}, f32[288,2048]{1,0:T(8,128)}, bf16[288,2048]{1,0:T(8,128)(2,1)}) custom-call(bf16[4,288,4096]{2,1,0:T(8,128)(2,1)} %get-tuple-element.91.y_hbm, bf16[8,2,256,2048]{3,2,1,0:T(8,128)(2,1)} %bitcast.63, bf16[128,4096]{1,0:T(8,128)(2,1)} %get-tuple-element.81.fg_ref.fu_ref.f1_ref, ...), custom_call_target="tpu_custom_call" | custom-call | flops 19327352832 | bytes 48318384 | tf_op jit(solution)/shard_map/back_ffn_kernel/pallas_call | solution.py:1071
  532.5 45.2 %back_out_kernel.1 = (bf16[4,288,512]{2,1,0:T(8,128)(2,1)}, bf16[64,2048]{1,0:T(8,128)(2,1)}, bf16[16,6656]{1,0:T(8,128)(2,1)}) custom-call(bf16[288,2048]{1,0:T(8,128)(2,1)} %get-tuple-element.95.da_ref, bf16[8,1024,512]{2,1,0:T(8,128)(2,1)} %bitcast.40, bf16[128,2048]{1,0:T(8,128)(2,1)} %get-tuple-element.71.factors_ref, ...), custom_call_target="tpu_custom_call" | custom-call | flops 2415919104 | bytes 6039797 | tf_op jit(solution)/shard_map/back_out_kernel/pallas_call | solution.py:1071
  577.7 17.7 %attend_back.1 = (f32[1152,512]{1,0:T(8,128)}, f32[1152,512]{1,0:T(8,128)}, bf16[1152,512]{1,0:T(8,128)(2,1)S(1)}, f32[2,1152,128]{2,1,0:T(8,128)S(1)}, bf16[1152,512]{1,0:T(8,128)(2,1)S(1)}) custom-call(bf16[1152,512]{1,0:T(8,128)(2,1)} %copy-done.11, bf16[1152,512]{1,0:T(8,128)(2,1)} %copy-done.12, bf16[1152,512]{1,0:T(8,128)(2,1)} %copy-done.13, ...), custom_call_target="tpu_custom_call" | custom-call | flops 6794772480 | bytes 17694720 | tf_op jit(solution)/shard_map/attend_back/pallas_call | solution.py:1223
  595.4 1.0 copy-done.5
  596.4 1.0 copy-done.6
  597.4 13.8 %prepare_kernel.1 = (bf16[1152,1664]{1,0:T(8,128)(2,1)}, bf16[16,8192]{1,0:T(8,128)(2,1)}) custom-call(f32[1152,512]{1,0:T(8,128)} %get-tuple-element.107.wq_hbm, f32[1152,512]{1,0:T(8,128)} %get-tuple-element.108.wk_hbm, bf16[1152,512]{1,0:T(8,128)(2,1)} %copy-done.5, f32[1152,1536]{1,0:T(8,128)} %bitcast.37, f32[1152,8]{1,0:T(8,128)} %get-tuple-element.74.inv_ref, ...), custom_call_target="tpu_custom_call" | custom-call | flops 603979776 | bytes 1509949 | tf_op jit(solution)/shard_map/prepare_kernel/pallas_call | solution.py:1071
  612.2 76.2 %back_qkv_kernel.1 = (bf16[1152,512]{1,0:T(8,128)(2,1)}, bf16[4,8,32,512]{3,2,1,0:T(8,128)(2,1)}) custom-call(bf16[4,288,1664]{2,1,0:T(8,128)(2,1)} %bitcast.66, bf16[8,1024,512]{2,1,0:T(8,128)(2,1)} %bitcast.41, bf16[2048,128]{1,0:T(8,128)(2,1)} %get-tuple-element.92.factors_t_ref, f32[288,2048]{1,0:T(8,128)} %get-tuple-element.114.hidden_hbm, ...), custom_call_target="tpu_custom_call" | custom-call | flops 7247757312 | bytes 18119392 | tf_op jit(solution)/shard_map/back_qkv_kernel/pallas_call | solution.py:1071
  688.4 1.7 copy-done.3
  690.1 1.3 copy-done.7
  691.4 1.2 copy-done.8
  692.6 8.0 %finish.1 = (f32[1152,512]{1,0:T(8,128)}, f32[1152,512]{1,0:T(8,128)}, f32[3,8,16,512]{3,2,1,0:T(8,128)}, f32[8,16,512]{2,1,0:T(8,128)}, f32[2,8,16,512]{3,2,1,0...) custom-call(f32[8,64]{1,0:T(8,128)S(1)} %copy-done.10, ...), custom_call_target="tpu_custom_call" | custom-call | flops 100000000 | bytes 16777216 | tf_op jit(solution)/shard_map/finish/pallas_call | solution.py:699
  (51 shorter events, 4.2 us)
Async XLA Ops:
  7.2 6.8 copy-start
  7.2 123.6 %all-gather.9.cloned.1.call-start = ((), (), s32[]{:S(2)}) async-start(), calls=%async_computation | async-start | bytes 9437184 | tf_op jit(solution)/shard_map/all_gather | solution.py:1473
  10.6 277.2 %all-gather.11.cloned.1.call-start = ((), (), s32[]{:S(2)}) async-start(), calls=%async_computation.1 | async-start | bytes 18874368 | tf_op jit(solution)/shard_map/all_gather | solution.py:1473
  13.9 1.2 copy-start.16
  13.9 1.3 copy-start.17
  13.9 1.9 copy-start.18
  13.9 351.2 %all-gather.13.cloned.1.call-start = ((), (), s32[]{:S(2)}) async-start(), calls=%async_computation.2 | async-start | bytes 9437184 | tf_op jit(solution)/shard_map/all_gather | solution.py:1473
  15.0 673.3 %all-gather.15.cloned.1.call-start = ((), (), s32[]{:S(2)}) async-start(), calls=%async_computation.3 | async-start | bytes 2359296 | tf_op jit(solution)/shard_map/all_gather | solution.py:1567
  183.0 1.1 copy-start.2
  197.3 1.0 copy-start.11
  198.3 1.0 copy-start.12
  199.3 1.0 copy-start.13
  200.3 87.5 %copy-start.4 = (bf16[128,2048]{1,0:T(8,128)(2,1)S(1)}, bf16[128,2048]{1,0:T(8,128)(2,1)}, u32[]{:S(2)}) copy-start(bf16[128,2048]{1,0:T(8,128)(2,1)} %get-tuple-element.71.factors_ref) | copy-start | bytes 1572868
  287.8 1.2 copy-start.14
  319.0 0.7 copy-start.9
  595.4 1.0 copy-start.5
  596.4 1.0 copy-start.6
  597.4 13.8 %copy-start.15 = (s32[8,7]{1,0:T(8,128)S(1)}, s32[8,7]{1,0:T(8,128)}, u32[]{:S(2)}) copy-start(s32[8,7]{1,0:T(8,128)} %ids_ref.1) | copy-start | bytes 676
  612.2 76.2 %copy-start.10 = (f32[8,64]{1,0:T(8,128)S(1)}, f32[8,64]{1,0:T(8,128)}, u32[]{:S(2)}) copy-start(f32[8,64]{1,0:T(8,128)} %pad_convert_fusion.chosen_ref) | copy-start | bytes 6148
  688.4 12.2 %copy-start.1 = (bf16[2048,512]{1,0:T(8,128)(2,1)S(1)}, bf16[2048,512]{1,0:T(8,128)(2,1)}, u32[]{:S(2)}) copy-start(bf16[2048,512]{1,0:T(8,128)(2,1)} %param.23) | copy-start | bytes 6291460
  688.4 1.7 copy-start.3
  690.1 1.3 copy-start.7
  691.4 1.2 copy-start.8
Sparse Core Ops, SparseCore 0:
  10.7 119.9 all-gather.8
  132.9 150.2 all-gather.10
  284.8 80.2 all-gather.12
  611.4 27.1 all-gather.14

commit v6 on v5

--- a/solution.py
+++ b/solution.py
@@ -626,15 +626,19 @@
     )
     links.greet(columns=True)
     turned = Exchange(links, "col", slot(cot_ref), features(own_cot_ref, cot_ref.shape[2]))
-    turned.start()
     w_ref[f1_ref.shape[1] :] = factors_ref[...]
     product = leave_product(
         y_ref, lambda rows, cols: mm(rows, w_ref[:, cols]), f1_ref, low_ref, streams.rows
     )
+    def ready(k):
+        if k == 2:
+            turned.start()
+        streams.ready(k)
+
     finish_all(
         scatter(
             links, product, lin_ref, out_buf, relay_buf, final_buf,
-            ready=streams.ready,
+            ready=ready,
         )
     )
     turned.arrived()
@@ -733,7 +737,6 @@
     stores = []
 
     def before():
-        turned.start()
         wait_all(loads)
         for gate in gates[1:]:
             start_all(gate)
@@ -760,7 +763,7 @@
             )
         )
 
-    gather(links, all_ref, work, before)
+    gather(links, all_ref, work, before, turned.start)
     turned.arrived()
     turned.sent()
     wait_all(stores)

time: 717 us -> 709 us (0.989)
  waiting for transfers between devices: 83.4 us -> 73.3 us
    all_gather x3, waiting for transfers between devices: 83.3 us -> 73.2 us  [gathered(): return lax.all_gather(local, ('col', 'tok'), axis=0)]
    pallas_call x1, Pallas kernels: 29.9 us -> 40 us  [ffn(): pl.pallas_call(ffn_kernel, grid=(tiles,), in_specs=[whole(h_all), part(0)...]
    pallas_call x9, Pallas kernels: 515 us -> 506 us  [linked(): pl.pallas_call(kernel, in_specs=specs, out_specs=[ANY if len(out) == 3 el...]
  transfers between devices with their start and end apart: 4 -> 4, of which waited for: 2 -> 2; matrix products, arithmetic and copies ran while one was open for 1% -> 1% of each run, Pallas kernels for 47% -> 49%
where the time goes in v6:
time: 709 us; the launch traced here: 699 us
  Pallas kernels  585 us (83%)
  waiting for transfers between devices  73.3 us (10%)
  local copies, waits for them, and re-layouts  20.3 us (3%)
  between operations  14.5 us (2%)
    pallas_call x9, Pallas kernels, linked(): pl.pallas_call(kernel, in_specs=specs, out_specs=[ANY if len(out) == 3 el...  506 us
    all_gather x3, waiting for transfers between devices, gathered(): return lax.all_gather(local, ('col', 'tok'), axis=0)  73.2 us
    pallas_call x1, Pallas kernels, ffn(): pl.pallas_call(ffn_kernel, grid=(tiles,), in_specs=[whole(h_all), part(0)...  40 us
    pallas_call x1, Pallas kernels, attend_back(): pl.pallas_call(attend_back_kernel, grid=(heads,), in_specs=[col(0)] * 5 +...  17.7 us
  transfers between devices with their start and end apart: 4, of which 2 were waited for; matrix products, arithmetic and copies ran while one was open for 1% of the time, Pallas kernels for 49%

profile of v6, /device:TPU:0, one launch (start us, length us, event | category | flops | bytes accessed | tf_op | source)
XLA Modules:
  0.0 698.9 jit_solution(14118571382917252776)
XLA Ops:
  7.2 1.3 constant_dynamic-slice_fusion.3
  8.6 1.0 constant_dynamic-slice_fusion.2
  9.6 1.0 pad_maximum_fusion
  10.7 3.2 constant_dynamic-slice_fusion.1
  14.0 1.1 constant_dynamic-slice_fusion
  16.3 72.6 %intake_kernel.1 = (bf16[288,2048]{1,0:T(8,128)(2,1)}, bf16[4,288,512]{2,1,0:T(8,128)(2,1)}, bf16[128,2048]{1,0:T(8,128)(2,1)}, bf16[2048,128]{1,0:T(8,128)(2,1)...) custom-call(bf16[4,288,512]{2,1,0:T(8,128)(2,1)} %bitcast.50, ...), custom_call_target="tpu_custom_call" | custom-call | flops 603979776 | bytes 1509949 | tf_op jit(solution)/shard_map/intake_kernel/pallas_call | solution.py:1074
  89.6 0.7 fusion.1.bias_ref
  90.3 2.1 fusion.2
  92.8 37.9 %all-gather.9.cloned.1.call-done = bf16[8192,512]{1,0:T(8,128)(2,1)} async-done(((bf16[1024,512]{1,0:T(8,128)(2,1)}), bf16[8192,512]{1,0:T(8,128)(2,1)}) %all-gather.9.cloned.1.call-update) | async-done | bytes 8388624 | tf_op jit(solution)/shard_map/all_gather | solution.py:1476
  130.8 52.2 %enter_qkv_kernel.1 = (bf16[4,288,2048]{2,1,0:T(8,128)(2,1)}, bf16[4,288,128]{2,1,0:T(8,128)(2,1)}, f32[4,288,1536]{2,1,0:T(8,128)}, f32[1152,8]{1,0:T(8,128)}) custom-call(bf16[288,2048]{1,0:T(8,128)(2,1)} %get-tuple-element.70.x_ref, bf16[8,1024,512]{2,1,0:T(8,128)(2,1)} %bitcast.38, bf16[128,2048]{1,0:T(8,128)(2,1)} %get-tuple-element.71.factors_ref, ...), custom_call_target="tpu_custom_call" | custom-call | flops 7247757312 | bytes 18119392 | tf_op jit(solution)/shard_map/enter_qkv_kernel/pallas_call | solution.py:1074
  183.0 1.1 copy-done.2
  184.0 13.3 %attend.1 = (bf16[1152,512]{1,0:T(8,128)(2,1)S(1)}, bf16[1152,512]{1,0:T(8,128)(2,1)S(1)}, bf16[1152,512]{1,0:T(8,128)(2,1)S(1)}, bf16[1152,512]{1,0:T(8,128)(2,1)}, f32[4,1,1152]{2,1,0:T(1,128)S(1)}) custom-call(f32[1152,1536]{1,0:T(8,128)} %bitcast.32, f32[1152,1536]{1,0:T(8,128)} %bitcast.33, f32[1152,1536]{1,0:T(8,128)} %bitcast.34, ...), custom_call_target="tpu_custom_call" | custom-call | flops 2717908992 | bytes 11796480 | tf_op jit(solution)/shard_map/attend/pallas_call | solution.py:1203
  197.3 1.0 copy-done.11
  198.3 1.0 copy-done.12
  199.3 1.0 copy-done.13
  200.3 87.4 %leave_out_kernel.1 = (f32[288,2048]{1,0:T(8,128)}, bf16[4,288,128]{2,1,0:T(8,128)(2,1)}, f32[288,2048]{1,0:T(8,128)}, bf16[4,288,2048]{2,1,0:T(8,128)(2,1)}) custom-call(bf16[4,288,512]{2,1,0:T(8,128)(2,1)} %bitcast.47, bf16[8,1024,512]{2,1,0:T(8,128)(2,1)} %bitcast.39, bf16[128,512]{1,0:T(8,128)(2,1)} %get-tuple-element.79.f1_ref, ...), custom_call_target="tpu_custom_call" | custom-call | flops 2415919104 | bytes 6039797 | tf_op jit(solution)/shard_map/leave_out_kernel/pallas_call | solution.py:1074
  287.9 1.2 copy-done.14
  289.1 40.0 %ffn.1 = (bf16[1152,128]{1,0:T(8,128)(2,1)S(1)}, bf16[1152,2048]{1,0:T(8,128)(2,1)}, bf16[1152,2048]{1,0:T(8,128)(2,1)}, bf16[1152,2048]{1,0:T(8,128)(2,1)}) custom-call(bf16[1152,2048]{1,0:T(8,128)(2,1)} %bitcast.43, bf16[8,2,256,2048]{3,2,1,0:T(8,128)(2,1)} %bitcast.61, bf16[8,2,256,2048]{3,2,1,0:T(8,128)(2,1)} %bitcast.62, ...), custom_call_target="tpu_custom_call" | custom-call | flops 19327352832 | bytes 40370176 | tf_op jit(solution)/shard_map/ffn/pallas_call | solution.py:601
  329.8 35.3 %all-gather.13.cloned.1.call-done = bf16[8192,512]{1,0:T(8,128)(2,1)} async-done(((bf16[1024,512]{1,0:T(8,128)(2,1)}), bf16[8192,512]{1,0:T(8,128)(2,1)}) %all-gather.13.cloned.1.call-update) | async-done | bytes 8388624 | tf_op jit(solution)/shard_map/all_gather | solution.py:1476
  365.1 51.4 %leave_down_kernel.1 = (bf16[4,288,128]{2,1,0:T(8,128)(2,1)}, bf16[288,2048]{1,0:T(8,128)(2,1)}, bf16[288,2048]{1,0:T(8,128)(2,1)}, bf16[288,2048]{1,0:T(8,128)(2,1)}) custom-call(bf16[4,288,2048]{2,1,0:T(8,128)(2,1)} %bitcast.45, bf16[8,1024,512]{2,1,0:T(8,128)(2,1)} %bitcast.64, bf16[128,2048]{1,0:T(8,128)(2,1)} %get-tuple-element.83.f1_ref, ...), custom_call_target="tpu_custom_call" | custom-call | flops 9663676416 | bytes 24159192 | tf_op jit(solution)/shard_map/leave_down_kernel/pallas_call | solution.py:1074
  416.6 52.5 %back_down_kernel.1 = (bf16[4,288,2048]{2,1,0:T(8,128)(2,1)}, bf16[4,288,128]{2,1,0:T(8,128)(2,1)}, bf16[4,288,4096]{2,1,0:T(8,128)(2,1)}, bf16[4,288,512]{2,1,0:T(8,128)(2,1)}) custom-call(bf16[288,2048]{1,0:T(8,128)(2,1)} %get-tuple-element.86.dm_ref, bf16[8,1024,512]{2,1,0:T(8,128)(2,1)} %bitcast.65, bf16[128,2048]{1,0:T(8,128)(2,1)} %get-tuple-element.71.factors_ref, ...), custom_call_target="tpu_custom_call" | custom-call | flops 9663676416 | bytes 24159192 | tf_op jit(solution)/shard_map/back_down_kernel/pallas_call | solution.py:1074
  469.1 53.1 %back_ffn_kernel.1 = (bf16[4,288,128]{2,1,0:T(8,128)(2,1)}, f32[288,2048]{1,0:T(8,128)}, bf16[288,2048]{1,0:T(8,128)(2,1)}) custom-call(bf16[4,288,4096]{2,1,0:T(8,128)(2,1)} %get-tuple-element.91.y_hbm, bf16[8,2,256,2048]{3,2,1,0:T(8,128)(2,1)} %bitcast.63, bf16[128,4096]{1,0:T(8,128)(2,1)} %get-tuple-element.81.fg_ref.fu_ref.f1_ref, ...), custom_call_target="tpu_custom_call" | custom-call | flops 19327352832 | bytes 48318384 | tf_op jit(solution)/shard_map/back_ffn_kernel/pallas_call | solution.py:1074
  522.2 45.2 %back_out_kernel.1 = (bf16[4,288,512]{2,1,0:T(8,128)(2,1)}, bf16[64,2048]{1,0:T(8,128)(2,1)}, bf16[16,6656]{1,0:T(8,128)(2,1)}) custom-call(bf16[288,2048]{1,0:T(8,128)(2,1)} %get-tuple-element.95.da_ref, bf16[8,1024,512]{2,1,0:T(8,128)(2,1)} %bitcast.40, bf16[128,2048]{1,0:T(8,128)(2,1)} %get-tuple-element.71.factors_ref, ...), custom_call_target="tpu_custom_call" | custom-call | flops 2415919104 | bytes 6039797 | tf_op jit(solution)/shard_map/back_out_kernel/pallas_call | solution.py:1074
  567.4 17.7 %attend_back.1 = (f32[1152,512]{1,0:T(8,128)}, f32[1152,512]{1,0:T(8,128)}, bf16[1152,512]{1,0:T(8,128)(2,1)S(1)}, f32[2,1152,128]{2,1,0:T(8,128)S(1)}, bf16[1152,512]{1,0:T(8,128)(2,1)S(1)}) custom-call(bf16[1152,512]{1,0:T(8,128)(2,1)} %copy-done.11, bf16[1152,512]{1,0:T(8,128)(2,1)} %copy-done.12, bf16[1152,512]{1,0:T(8,128)(2,1)} %copy-done.13, ...), custom_call_target="tpu_custom_call" | custom-call | flops 6794772480 | bytes 17694720 | tf_op jit(solution)/shard_map/attend_back/pallas_call | solution.py:1226
  585.1 1.0 copy-done.5
  586.1 1.0 copy-done.6
  587.1 13.8 %prepare_kernel.1 = (bf16[1152,1664]{1,0:T(8,128)(2,1)}, bf16[16,8192]{1,0:T(8,128)(2,1)}) custom-call(f32[1152,512]{1,0:T(8,128)} %get-tuple-element.107.wq_hbm, f32[1152,512]{1,0:T(8,128)} %get-tuple-element.108.wk_hbm, bf16[1152,512]{1,0:T(8,128)(2,1)} %copy-done.5, f32[1152,1536]{1,0:T(8,128)} %bitcast.37, f32[1152,8]{1,0:T(8,128)} %get-tuple-element.74.inv_ref, ...), custom_call_target="tpu_custom_call" | custom-call | flops 603979776 | bytes 1509949 | tf_op jit(solution)/shard_map/prepare_kernel/pallas_call | solution.py:1074
  601.9 77.8 %back_qkv_kernel.1 = (bf16[1152,512]{1,0:T(8,128)(2,1)}, bf16[4,8,32,512]{3,2,1,0:T(8,128)(2,1)}) custom-call(bf16[4,288,1664]{2,1,0:T(8,128)(2,1)} %bitcast.66, bf16[8,1024,512]{2,1,0:T(8,128)(2,1)} %bitcast.41, bf16[2048,128]{1,0:T(8,128)(2,1)} %get-tuple-element.92.factors_t_ref, f32[288,2048]{1,0:T(8,128)} %get-tuple-element.114.hidden_hbm, ...), custom_call_target="tpu_custom_call" | custom-call | flops 7247757312 | bytes 18119392 | tf_op jit(solution)/shard_map/back_qkv_kernel/pallas_call | solution.py:1074
  679.8 1.7 copy-done.3
  681.5 1.3 copy-done.7
  682.8 1.2 copy-done.8
  684.0 8.0 %finish.1 = (f32[1152,512]{1,0:T(8,128)}, f32[1152,512]{1,0:T(8,128)}, f32[3,8,16,512]{3,2,1,0:T(8,128)}, f32[8,16,512]{2,1,0:T(8,128)}, f32[2,8,16,512]{3,2,1,0...) custom-call(f32[8,64]{1,0:T(8,128)S(1)} %copy-done.10, ...), custom_call_target="tpu_custom_call" | custom-call | flops 100000000 | bytes 16777216 | tf_op jit(solution)/shard_map/finish/pallas_call | solution.py:703
  (51 shorter events, 4.1 us)
Async XLA Ops:
  7.2 6.8 copy-start
  7.2 123.6 %all-gather.9.cloned.1.call-start = ((), (), s32[]{:S(2)}) async-start(), calls=%async_computation | async-start | bytes 9437184 | tf_op jit(solution)/shard_map/all_gather | solution.py:1476
  10.6 277.2 %all-gather.11.cloned.1.call-start = ((), (), s32[]{:S(2)}) async-start(), calls=%async_computation.1 | async-start | bytes 18874368 | tf_op jit(solution)/shard_map/all_gather | solution.py:1476
  13.9 1.2 copy-start.16
  13.9 1.3 copy-start.17
  13.9 1.9 copy-start.18
  13.9 351.2 %all-gather.13.cloned.1.call-start = ((), (), s32[]{:S(2)}) async-start(), calls=%async_computation.2 | async-start | bytes 9437184 | tf_op jit(solution)/shard_map/all_gather | solution.py:1476
  15.0 664.7 %all-gather.15.cloned.1.call-start = ((), (), s32[]{:S(2)}) async-start(), calls=%async_computation.3 | async-start | bytes 2359296 | tf_op jit(solution)/shard_map/all_gather | solution.py:1570
  183.0 1.1 copy-start.2
  197.3 1.0 copy-start.11
  198.3 1.0 copy-start.12
  199.3 1.0 copy-start.13
  200.3 87.5 %copy-start.4 = (bf16[128,2048]{1,0:T(8,128)(2,1)S(1)}, bf16[128,2048]{1,0:T(8,128)(2,1)}, u32[]{:S(2)}) copy-start(bf16[128,2048]{1,0:T(8,128)(2,1)} %get-tuple-element.71.factors_ref) | copy-start | bytes 1572868
  287.8 1.2 copy-start.14
  329.1 0.7 copy-start.9
  585.1 1.0 copy-start.5
  586.1 1.0 copy-start.6
  587.1 13.8 %copy-start.15 = (s32[8,7]{1,0:T(8,128)S(1)}, s32[8,7]{1,0:T(8,128)}, u32[]{:S(2)}) copy-start(s32[8,7]{1,0:T(8,128)} %ids_ref.1) | copy-start | bytes 676
  601.9 77.9 %copy-start.10 = (f32[8,64]{1,0:T(8,128)S(1)}, f32[8,64]{1,0:T(8,128)}, u32[]{:S(2)}) copy-start(f32[8,64]{1,0:T(8,128)} %pad_convert_fusion.chosen_ref) | copy-start | bytes 6148
  679.7 12.2 %copy-start.1 = (bf16[2048,512]{1,0:T(8,128)(2,1)S(1)}, bf16[2048,512]{1,0:T(8,128)(2,1)}, u32[]{:S(2)}) copy-start(bf16[2048,512]{1,0:T(8,128)(2,1)} %param.23) | copy-start | bytes 6291460
  679.8 1.7 copy-start.3
  681.5 1.3 copy-start.7
  682.8 1.2 copy-start.8
Sparse Core Ops, SparseCore 0:
  10.7 119.9 all-gather.8
  132.9 150.2 all-gather.10
  284.8 80.2 all-gather.12
  601.1 28.3 all-gather.14

commit v7 on v6

--- a/solution.py
+++ b/solution.py
@@ -920,7 +920,17 @@
     mine, theirs = groups_ref.at[pl.ds(base, 4)], groups_ref.at[pl.ds(4 - base, 4)]
     to_twin = links.copy(mine, mine, index, index, links.row, tok=links.tok ^ 1)
     from_twin = links.copy(theirs, theirs, index, index, links.row, tok=links.tok ^ 1)
-    spread = Exchange(links, "row", lambda key: placed_ref, slot(sums_ref))
+    mine_half, their_half = (pl.ds(tok * RANK, RANK) for tok in (links.tok, 1 - links.tok))
+    spread = Exchange(
+        links,
+        "row",
+        lambda key: placed_ref.at[:, mine_half],
+        lambda key: sums_ref.at[key, :, mine_half],
+    )
+    index = links.take(1)
+    sent_half, got_half = sums_ref.at[:, :, mine_half], sums_ref.at[:, :, their_half]
+    half_out = links.copy(sent_half, sent_half, index, index, links.row, tok=links.tok ^ 1)
+    half_in = links.copy(got_half, got_half, index, index, links.row, tok=links.tok ^ 1)
 
     def lower_grad():
         wait_all(x_load)
@@ -1022,12 +1032,11 @@
         lower_grad()
 
     def third(columns, finish):
-        add_rows()
         wait_all(streams.late)
         leave_col(0, columns, finish)
 
     def fourth(columns, finish):
-        share()
+        add_rows()
         leave_col(1, columns, finish)
 
     columns, finish, sent = scatter(
@@ -1037,20 +1046,24 @@
         hooks=[first, second, third, fourth],
     )
     leave_row(0)
-    place_groups()
+    share()
     leave_col(2, columns, finish)
     leave_col(3, columns, finish)
     leave_row(3)
+    place_groups()
     leave_row(2)
     leave_row(1)
+    spread.arrived()
+    half_out.start()
     near.wait()
     for step in range(1, 4):
         landed = token_rows(turn_buf, count)(links.row ^ step)
         at = row_base + step
         links.copy(landed, landed, at, at, links.row ^ step).wait_recv()
-    spread.arrived()
+    half_in.wait_recv()
     for step in range(1, 4):
         to_row(step).wait_send()
+    half_out.wait_send()
     for copy in z_copies:
         copy.wait_send()
     to_twin.wait_send()

time: 709 us -> 703 us (level)
  no operation moved by 1% of the time
where the time goes in v7:
time: 703 us; the launch traced here: 693 us
  Pallas kernels  580 us (83%)
  waiting for transfers between devices  73.3 us (10%)
  local copies, waits for them, and re-layouts  20.3 us (3%)
  between operations  14.5 us (2%)
    pallas_call x9, Pallas kernels, linked(): pl.pallas_call(kernel, in_specs=specs, out_specs=[ANY if len(out) == 3 el...  501 us
    all_gather x3, waiting for transfers between devices, gathered(): return lax.all_gather(local, ('col', 'tok'), axis=0)  73.2 us
    pallas_call x1, Pallas kernels, ffn(): pl.pallas_call(ffn_kernel, grid=(tiles,), in_specs=[whole(h_all), part(0)...  40 us
    pallas_call x1, Pallas kernels, attend_back(): pl.pallas_call(attend_back_kernel, grid=(heads,), in_specs=[col(0)] * 5 +...  17.7 us
  transfers between devices with their start and end apart: 4, of which 2 were waited for; matrix products, arithmetic and copies ran while one was open for 1% of the time, Pallas kernels for 49%

profile of v7, /device:TPU:0, one launch (start us, length us, event | category | flops | bytes accessed | tf_op | source)
XLA Modules:
  0.0 693.5 jit_solution(10205433102889194339)
XLA Ops:
  7.2 1.3 constant_dynamic-slice_fusion.3
  8.6 1.0 constant_dynamic-slice_fusion.2
  9.6 1.0 pad_maximum_fusion
  10.7 3.2 constant_dynamic-slice_fusion.1
  14.0 1.1 constant_dynamic-slice_fusion
  16.3 72.6 %intake_kernel.1 = (bf16[288,2048]{1,0:T(8,128)(2,1)}, bf16[4,288,512]{2,1,0:T(8,128)(2,1)}, bf16[128,2048]{1,0:T(8,128)(2,1)}, bf16[2048,128]{1,0:T(8,128)(2,1)...) custom-call(bf16[4,288,512]{2,1,0:T(8,128)(2,1)} %bitcast.50, ...), custom_call_target="tpu_custom_call" | custom-call | flops 603979776 | bytes 1509949 | tf_op jit(solution)/shard_map/intake_kernel/pallas_call | solution.py:1087
  89.6 0.7 fusion.1.bias_ref
  90.3 2.1 fusion.2
  92.8 37.9 %all-gather.9.cloned.1.call-done = bf16[8192,512]{1,0:T(8,128)(2,1)} async-done(((bf16[1024,512]{1,0:T(8,128)(2,1)}), bf16[8192,512]{1,0:T(8,128)(2,1)}) %all-gather.9.cloned.1.call-update) | async-done | bytes 8388624 | tf_op jit(solution)/shard_map/all_gather | solution.py:1489
  130.8 52.2 %enter_qkv_kernel.1 = (bf16[4,288,2048]{2,1,0:T(8,128)(2,1)}, bf16[4,288,128]{2,1,0:T(8,128)(2,1)}, f32[4,288,1536]{2,1,0:T(8,128)}, f32[1152,8]{1,0:T(8,128)}) custom-call(bf16[288,2048]{1,0:T(8,128)(2,1)} %get-tuple-element.70.x_ref, bf16[8,1024,512]{2,1,0:T(8,128)(2,1)} %bitcast.38, bf16[128,2048]{1,0:T(8,128)(2,1)} %get-tuple-element.71.factors_ref, ...), custom_call_target="tpu_custom_call" | custom-call | flops 7247757312 | bytes 18119392 | tf_op jit(solution)/shard_map/enter_qkv_kernel/pallas_call | solution.py:1087
  183.0 1.1 copy-done.2
  184.0 13.3 %attend.1 = (bf16[1152,512]{1,0:T(8,128)(2,1)S(1)}, bf16[1152,512]{1,0:T(8,128)(2,1)S(1)}, bf16[1152,512]{1,0:T(8,128)(2,1)S(1)}, bf16[1152,512]{1,0:T(8,128)(2,1)}, f32[4,1,1152]{2,1,0:T(1,128)S(1)}) custom-call(f32[1152,1536]{1,0:T(8,128)} %bitcast.32, f32[1152,1536]{1,0:T(8,128)} %bitcast.33, f32[1152,1536]{1,0:T(8,128)} %bitcast.34, ...), custom_call_target="tpu_custom_call" | custom-call | flops 2717908992 | bytes 11796480 | tf_op jit(solution)/shard_map/attend/pallas_call | solution.py:1216
  197.3 1.0 copy-done.11
  198.3 1.0 copy-done.12
  199.3 1.0 copy-done.13
  200.3 87.4 %leave_out_kernel.1 = (f32[288,2048]{1,0:T(8,128)}, bf16[4,288,128]{2,1,0:T(8,128)(2,1)}, f32[288,2048]{1,0:T(8,128)}, bf16[4,288,2048]{2,1,0:T(8,128)(2,1)}) custom-call(bf16[4,288,512]{2,1,0:T(8,128)(2,1)} %bitcast.47, bf16[8,1024,512]{2,1,0:T(8,128)(2,1)} %bitcast.39, bf16[128,512]{1,0:T(8,128)(2,1)} %get-tuple-element.79.f1_ref, ...), custom_call_target="tpu_custom_call" | custom-call | flops 2415919104 | bytes 6039797 | tf_op jit(solution)/shard_map/leave_out_kernel/pallas_call | solution.py:1087
  287.9 1.2 copy-done.14
  289.1 40.0 %ffn.1 = (bf16[1152,128]{1,0:T(8,128)(2,1)S(1)}, bf16[1152,2048]{1,0:T(8,128)(2,1)}, bf16[1152,2048]{1,0:T(8,128)(2,1)}, bf16[1152,2048]{1,0:T(8,128)(2,1)}) custom-call(bf16[1152,2048]{1,0:T(8,128)(2,1)} %bitcast.43, bf16[8,2,256,2048]{3,2,1,0:T(8,128)(2,1)} %bitcast.61, bf16[8,2,256,2048]{3,2,1,0:T(8,128)(2,1)} %bitcast.62, ...), custom_call_target="tpu_custom_call" | custom-call | flops 19327352832 | bytes 40370176 | tf_op jit(solution)/shard_map/ffn/pallas_call | solution.py:601
  329.8 35.3 %all-gather.13.cloned.1.call-done = bf16[8192,512]{1,0:T(8,128)(2,1)} async-done(((bf16[1024,512]{1,0:T(8,128)(2,1)}), bf16[8192,512]{1,0:T(8,128)(2,1)}) %all-gather.13.cloned.1.call-update) | async-done | bytes 8388624 | tf_op jit(solution)/shard_map/all_gather | solution.py:1489
  365.1 51.4 %leave_down_kernel.1 = (bf16[4,288,128]{2,1,0:T(8,128)(2,1)}, bf16[288,2048]{1,0:T(8,128)(2,1)}, bf16[288,2048]{1,0:T(8,128)(2,1)}, bf16[288,2048]{1,0:T(8,128)(2,1)}) custom-call(bf16[4,288,2048]{2,1,0:T(8,128)(2,1)} %bitcast.45, bf16[8,1024,512]{2,1,0:T(8,128)(2,1)} %bitcast.64, bf16[128,2048]{1,0:T(8,128)(2,1)} %get-tuple-element.83.f1_ref, ...), custom_call_target="tpu_custom_call" | custom-call | flops 9663676416 | bytes 24159192 | tf_op jit(solution)/shard_map/leave_down_kernel/pallas_call | solution.py:1087
  416.6 52.5 %back_down_kernel.1 = (bf16[4,288,2048]{2,1,0:T(8,128)(2,1)}, bf16[4,288,128]{2,1,0:T(8,128)(2,1)}, bf16[4,288,4096]{2,1,0:T(8,128)(2,1)}, bf16[4,288,512]{2,1,0:T(8,128)(2,1)}) custom-call(bf16[288,2048]{1,0:T(8,128)(2,1)} %get-tuple-element.86.dm_ref, bf16[8,1024,512]{2,1,0:T(8,128)(2,1)} %bitcast.65, bf16[128,2048]{1,0:T(8,128)(2,1)} %get-tuple-element.71.factors_ref, ...), custom_call_target="tpu_custom_call" | custom-call | flops 9663676416 | bytes 24159192 | tf_op jit(solution)/shard_map/back_down_kernel/pallas_call | solution.py:1087
  469.1 53.1 %back_ffn_kernel.1 = (bf16[4,288,128]{2,1,0:T(8,128)(2,1)}, f32[288,2048]{1,0:T(8,128)}, bf16[288,2048]{1,0:T(8,128)(2,1)}) custom-call(bf16[4,288,4096]{2,1,0:T(8,128)(2,1)} %get-tuple-element.91.y_hbm, bf16[8,2,256,2048]{3,2,1,0:T(8,128)(2,1)} %bitcast.63, bf16[128,4096]{1,0:T(8,128)(2,1)} %get-tuple-element.81.fg_ref.fu_ref.f1_ref, ...), custom_call_target="tpu_custom_call" | custom-call | flops 19327352832 | bytes 48318384 | tf_op jit(solution)/shard_map/back_ffn_kernel/pallas_call | solution.py:1087
  522.2 45.2 %back_out_kernel.1 = (bf16[4,288,512]{2,1,0:T(8,128)(2,1)}, bf16[64,2048]{1,0:T(8,128)(2,1)}, bf16[16,6656]{1,0:T(8,128)(2,1)}) custom-call(bf16[288,2048]{1,0:T(8,128)(2,1)} %get-tuple-element.95.da_ref, bf16[8,1024,512]{2,1,0:T(8,128)(2,1)} %bitcast.40, bf16[128,2048]{1,0:T(8,128)(2,1)} %get-tuple-element.71.factors_ref, ...), custom_call_target="tpu_custom_call" | custom-call | flops 2415919104 | bytes 6039797 | tf_op jit(solution)/shard_map/back_out_kernel/pallas_call | solution.py:1087
  567.4 17.7 %attend_back.1 = (f32[1152,512]{1,0:T(8,128)}, f32[1152,512]{1,0:T(8,128)}, bf16[1152,512]{1,0:T(8,128)(2,1)S(1)}, f32[2,1152,128]{2,1,0:T(8,128)S(1)}, bf16[1152,512]{1,0:T(8,128)(2,1)S(1)}) custom-call(bf16[1152,512]{1,0:T(8,128)(2,1)} %copy-done.11, bf16[1152,512]{1,0:T(8,128)(2,1)} %copy-done.12, bf16[1152,512]{1,0:T(8,128)(2,1)} %copy-done.13, ...), custom_call_target="tpu_custom_call" | custom-call | flops 6794772480 | bytes 17694720 | tf_op jit(solution)/shard_map/attend_back/pallas_call | solution.py:1239
  585.1 1.0 copy-done.5
  586.1 1.0 copy-done.6
  587.1 13.8 %prepare_kernel.1 = (bf16[1152,1664]{1,0:T(8,128)(2,1)}, bf16[16,8192]{1,0:T(8,128)(2,1)}) custom-call(f32[1152,512]{1,0:T(8,128)} %get-tuple-element.107.wq_hbm, f32[1152,512]{1,0:T(8,128)} %get-tuple-element.108.wk_hbm, bf16[1152,512]{1,0:T(8,128)(2,1)} %copy-done.5, f32[1152,1536]{1,0:T(8,128)} %bitcast.37, f32[1152,8]{1,0:T(8,128)} %get-tuple-element.74.inv_ref, ...), custom_call_target="tpu_custom_call" | custom-call | flops 603979776 | bytes 1509949 | tf_op jit(solution)/shard_map/prepare_kernel/pallas_call | solution.py:1087
  601.9 72.4 %back_qkv_kernel.1 = (bf16[1152,512]{1,0:T(8,128)(2,1)}, bf16[4,8,32,512]{3,2,1,0:T(8,128)(2,1)}) custom-call(bf16[4,288,1664]{2,1,0:T(8,128)(2,1)} %bitcast.66, bf16[8,1024,512]{2,1,0:T(8,128)(2,1)} %bitcast.41, bf16[2048,128]{1,0:T(8,128)(2,1)} %get-tuple-element.92.factors_t_ref, f32[288,2048]{1,0:T(8,128)} %get-tuple-element.114.hidden_hbm, ...), custom_call_target="tpu_custom_call" | custom-call | flops 7247757312 | bytes 18119392 | tf_op jit(solution)/shard_map/back_qkv_kernel/pallas_call | solution.py:1087
  674.3 1.7 copy-done.3
  676.1 1.3 copy-done.7
  677.4 1.2 copy-done.8
  678.6 8.0 %finish.1 = (f32[1152,512]{1,0:T(8,128)}, f32[1152,512]{1,0:T(8,128)}, f32[3,8,16,512]{3,2,1,0:T(8,128)}, f32[8,16,512]{2,1,0:T(8,128)}, f32[2,8,16,512]{3,2,1,0...) custom-call(f32[8,64]{1,0:T(8,128)S(1)} %copy-done.10, ...), custom_call_target="tpu_custom_call" | custom-call | flops 100000000 | bytes 16777216 | tf_op jit(solution)/shard_map/finish/pallas_call | solution.py:703
  (51 shorter events, 4.1 us)
Async XLA Ops:
  7.2 6.8 copy-start
  7.2 123.6 %all-gather.9.cloned.1.call-start = ((), (), s32[]{:S(2)}) async-start(), calls=%async_computation | async-start | bytes 9437184 | tf_op jit(solution)/shard_map/all_gather | solution.py:1489
  10.6 277.2 %all-gather.11.cloned.1.call-start = ((), (), s32[]{:S(2)}) async-start(), calls=%async_computation.1 | async-start | bytes 18874368 | tf_op jit(solution)/shard_map/all_gather | solution.py:1489
  13.9 1.2 copy-start.16
  13.9 1.3 copy-start.17
  13.9 1.9 copy-start.18
  13.9 351.2 %all-gather.13.cloned.1.call-start = ((), (), s32[]{:S(2)}) async-start(), calls=%async_computation.2 | async-start | bytes 9437184 | tf_op jit(solution)/shard_map/all_gather | solution.py:1489
  15.0 659.3 %all-gather.15.cloned.1.call-start = ((), (), s32[]{:S(2)}) async-start(), calls=%async_computation.3 | async-start | bytes 2359296 | tf_op jit(solution)/shard_map/all_gather | solution.py:1583
  183.0 1.1 copy-start.2
  197.3 1.0 copy-start.11
  198.3 1.0 copy-start.12
  199.3 1.0 copy-start.13
  200.3 87.5 %copy-start.4 = (bf16[128,2048]{1,0:T(8,128)(2,1)S(1)}, bf16[128,2048]{1,0:T(8,128)(2,1)}, u32[]{:S(2)}) copy-start(bf16[128,2048]{1,0:T(8,128)(2,1)} %get-tuple-element.71.factors_ref) | copy-start | bytes 1572868
  287.8 1.2 copy-start.14
  329.1 0.7 copy-start.9
  585.1 1.0 copy-start.5
  586.1 1.0 copy-start.6
  587.1 13.8 %copy-start.15 = (s32[8,7]{1,0:T(8,128)S(1)}, s32[8,7]{1,0:T(8,128)}, u32[]{:S(2)}) copy-start(s32[8,7]{1,0:T(8,128)} %ids_ref.1) | copy-start | bytes 676
  601.9 72.5 %copy-start.10 = (f32[8,64]{1,0:T(8,128)S(1)}, f32[8,64]{1,0:T(8,128)}, u32[]{:S(2)}) copy-start(f32[8,64]{1,0:T(8,128)} %pad_convert_fusion.chosen_ref) | copy-start | bytes 6148
  674.3 12.2 %copy-start.1 = (bf16[2048,512]{1,0:T(8,128)(2,1)S(1)}, bf16[2048,512]{1,0:T(8,128)(2,1)}, u32[]{:S(2)}) copy-start(bf16[2048,512]{1,0:T(8,128)(2,1)} %param.23) | copy-start | bytes 6291460
  674.3 1.7 copy-start.3
  676.1 1.3 copy-start.7
  677.3 1.2 copy-start.8
Sparse Core Ops, SparseCore 0:
  10.7 119.9 all-gather.8
  132.9 150.2 all-gather.10
  284.8 80.2 all-gather.12
  601.1 37.2 all-gather.14

commit v8 on v7

--- a/solution.py
+++ b/solution.py
@@ -556,9 +556,9 @@
     )
     gain = factors_ref[GAIN0].astype(f32)
 
-    @pl.loop(0, lin_ref.shape[0] // 16)
+    @pl.loop(0, lin_ref.shape[0] // 32)
     def _(tile):
-        rows = pl.ds(pl.multiple_of(tile * 16, 16), 16)
+        rows = pl.ds(pl.multiple_of(tile * 32, 32), 32)
         value = summed(lin_ref, final_buf, rows)
         lin_ref[rows] = value
         hidden = x_ref[rows].astype(f32) + value * inverse_of(value) * gain
@@ -645,9 +645,9 @@
     wait_all(streams.late)
     gain = factors_ref[GAIN1].astype(f32)
 
-    @pl.loop(0, lin_ref.shape[0] // 16)
+    @pl.loop(0, lin_ref.shape[0] // 32)
     def _(tile):
-        rows = pl.ds(pl.multiple_of(tile * 16, 16), 16)
+        rows = pl.ds(pl.multiple_of(tile * 32, 32), 32)
         value = summed(lin_ref, final_buf, rows)
         out_ref[rows] = (hidden_ref[rows] + value * inverse_of(value) * gain).astype(bf16)
         dm_ref[rows] = norm_back(value, own_cot_ref[rows].astype(f32) * gain).astype(bf16)
@@ -796,9 +796,9 @@
     wait_all(streams.late)
     gain = factors_ref[GAIN0].astype(f32)
 
-    @pl.loop(0, lin_ref.shape[0] // 16)
+    @pl.loop(0, lin_ref.shape[0] // 32)
     def _(tile):
-        rows = pl.ds(pl.multiple_of(tile * 16, 16), 16)
+        rows = pl.ds(pl.multiple_of(tile * 32, 32), 32)
         value = summed(lin_ref, final_buf, rows) + cot_ref[rows].astype(f32)
         hidden_ref[rows] = value
         da_ref[rows] = norm_back(attn_ref[rows], value * gain).astype(bf16)

time: 703 us -> 701 us (level)
  no operation moved by 1% of the time
where the time goes in v8:
time: 701 us; the launch traced here: 692 us
  Pallas kernels  577 us (82%)
  waiting for transfers between devices  74.2 us (11%)
  local copies, waits for them, and re-layouts  20.3 us (3%)
  between operations  14.5 us (2%)
    pallas_call x9, Pallas kernels, linked(): pl.pallas_call(kernel, in_specs=specs, out_specs=[ANY if len(out) == 3 el...  498 us
    all_gather x3, waiting for transfers between devices, gathered(): return lax.all_gather(local, ('col', 'tok'), axis=0)  74.1 us
    pallas_call x1, Pallas kernels, ffn(): pl.pallas_call(ffn_kernel, grid=(tiles,), in_specs=[whole(h_all), part(0)...  40.1 us
    pallas_call x1, Pallas kernels, attend_back(): pl.pallas_call(attend_back_kernel, grid=(heads,), in_specs=[col(0)] * 5 +...  17.7 us
  transfers between devices with their start and end apart: 4, of which 2 were waited for; matrix products, arithmetic and copies ran while one was open for 1% of the time, Pallas kernels for 49%

profile of v8, /device:TPU:0, one launch (start us, length us, event | category | flops | bytes accessed | tf_op | source)
XLA Modules:
  0.0 691.6 jit_solution(9599796562080759366)
XLA Ops:
  7.2 1.3 constant_dynamic-slice_fusion.3
  8.6 1.0 constant_dynamic-slice_fusion.2
  9.6 1.0 pad_maximum_fusion
  10.7 3.2 constant_dynamic-slice_fusion.1
  14.0 1.1 constant_dynamic-slice_fusion
  16.3 72.6 %intake_kernel.1 = (bf16[288,2048]{1,0:T(8,128)(2,1)}, bf16[4,288,512]{2,1,0:T(8,128)(2,1)}, bf16[128,2048]{1,0:T(8,128)(2,1)}, bf16[2048,128]{1,0:T(8,128)(2,1)...) custom-call(bf16[4,288,512]{2,1,0:T(8,128)(2,1)} %bitcast.50, ...), custom_call_target="tpu_custom_call" | custom-call | flops 603979776 | bytes 1509949 | tf_op jit(solution)/shard_map/intake_kernel/pallas_call | solution.py:1087
  89.6 0.7 fusion.1.bias_ref
  90.3 2.1 fusion.2
  92.8 37.9 %all-gather.9.cloned.1.call-done = bf16[8192,512]{1,0:T(8,128)(2,1)} async-done(((bf16[1024,512]{1,0:T(8,128)(2,1)}), bf16[8192,512]{1,0:T(8,128)(2,1)}) %all-gather.9.cloned.1.call-update) | async-done | bytes 8388624 | tf_op jit(solution)/shard_map/all_gather | solution.py:1489
  130.8 52.2 %enter_qkv_kernel.1 = (bf16[4,288,2048]{2,1,0:T(8,128)(2,1)}, bf16[4,288,128]{2,1,0:T(8,128)(2,1)}, f32[4,288,1536]{2,1,0:T(8,128)}, f32[1152,8]{1,0:T(8,128)}) custom-call(bf16[288,2048]{1,0:T(8,128)(2,1)} %get-tuple-element.70.x_ref, bf16[8,1024,512]{2,1,0:T(8,128)(2,1)} %bitcast.38, bf16[128,2048]{1,0:T(8,128)(2,1)} %get-tuple-element.71.factors_ref, ...), custom_call_target="tpu_custom_call" | custom-call | flops 7247757312 | bytes 18119392 | tf_op jit(solution)/shard_map/enter_qkv_kernel/pallas_call | solution.py:1087
  183.0 1.1 copy-done.2
  184.0 13.3 %attend.1 = (bf16[1152,512]{1,0:T(8,128)(2,1)S(1)}, bf16[1152,512]{1,0:T(8,128)(2,1)S(1)}, bf16[1152,512]{1,0:T(8,128)(2,1)S(1)}, bf16[1152,512]{1,0:T(8,128)(2,1)}, f32[4,1,1152]{2,1,0:T(1,128)S(1)}) custom-call(f32[1152,1536]{1,0:T(8,128)} %bitcast.32, f32[1152,1536]{1,0:T(8,128)} %bitcast.33, f32[1152,1536]{1,0:T(8,128)} %bitcast.34, ...), custom_call_target="tpu_custom_call" | custom-call | flops 2717908992 | bytes 11796480 | tf_op jit(solution)/shard_map/attend/pallas_call | solution.py:1216
  197.3 1.0 copy-done.11
  198.3 1.0 copy-done.12
  199.3 1.0 copy-done.13
  200.3 86.5 %leave_out_kernel.1 = (f32[288,2048]{1,0:T(8,128)}, bf16[4,288,128]{2,1,0:T(8,128)(2,1)}, f32[288,2048]{1,0:T(8,128)}, bf16[4,288,2048]{2,1,0:T(8,128)(2,1)}) custom-call(bf16[4,288,512]{2,1,0:T(8,128)(2,1)} %bitcast.47, bf16[8,1024,512]{2,1,0:T(8,128)(2,1)} %bitcast.39, bf16[128,512]{1,0:T(8,128)(2,1)} %get-tuple-element.79.f1_ref, ...), custom_call_target="tpu_custom_call" | custom-call | flops 2415919104 | bytes 6039797 | tf_op jit(solution)/shard_map/leave_out_kernel/pallas_call | solution.py:1087
  286.9 1.2 copy-done.14
  288.1 40.1 %ffn.1 = (bf16[1152,128]{1,0:T(8,128)(2,1)S(1)}, bf16[1152,2048]{1,0:T(8,128)(2,1)}, bf16[1152,2048]{1,0:T(8,128)(2,1)}, bf16[1152,2048]{1,0:T(8,128)(2,1)}) custom-call(bf16[1152,2048]{1,0:T(8,128)(2,1)} %bitcast.43, bf16[8,2,256,2048]{3,2,1,0:T(8,128)(2,1)} %bitcast.61, bf16[8,2,256,2048]{3,2,1,0:T(8,128)(2,1)} %bitcast.62, ...), custom_call_target="tpu_custom_call" | custom-call | flops 19327352832 | bytes 40370176 | tf_op jit(solution)/shard_map/ffn/pallas_call | solution.py:601
  328.9 36.2 %all-gather.13.cloned.1.call-done = bf16[8192,512]{1,0:T(8,128)(2,1)} async-done(((bf16[1024,512]{1,0:T(8,128)(2,1)}), bf16[8192,512]{1,0:T(8,128)(2,1)}) %all-gather.13.cloned.1.call-update) | async-done | bytes 8388624 | tf_op jit(solution)/shard_map/all_gather | solution.py:1489
  365.1 50.5 %leave_down_kernel.1 = (bf16[4,288,128]{2,1,0:T(8,128)(2,1)}, bf16[288,2048]{1,0:T(8,128)(2,1)}, bf16[288,2048]{1,0:T(8,128)(2,1)}, bf16[288,2048]{1,0:T(8,128)(2,1)}) custom-call(bf16[4,288,2048]{2,1,0:T(8,128)(2,1)} %bitcast.45, bf16[8,1024,512]{2,1,0:T(8,128)(2,1)} %bitcast.64, bf16[128,2048]{1,0:T(8,128)(2,1)} %get-tuple-element.83.f1_ref, ...), custom_call_target="tpu_custom_call" | custom-call | flops 9663676416 | bytes 24159192 | tf_op jit(solution)/shard_map/leave_down_kernel/pallas_call | solution.py:1087
  415.6 52.5 %back_down_kernel.1 = (bf16[4,288,2048]{2,1,0:T(8,128)(2,1)}, bf16[4,288,128]{2,1,0:T(8,128)(2,1)}, bf16[4,288,4096]{2,1,0:T(8,128)(2,1)}, bf16[4,288,512]{2,1,0:T(8,128)(2,1)}) custom-call(bf16[288,2048]{1,0:T(8,128)(2,1)} %get-tuple-element.86.dm_ref, bf16[8,1024,512]{2,1,0:T(8,128)(2,1)} %bitcast.65, bf16[128,2048]{1,0:T(8,128)(2,1)} %get-tuple-element.71.factors_ref, ...), custom_call_target="tpu_custom_call" | custom-call | flops 9663676416 | bytes 24159192 | tf_op jit(solution)/shard_map/back_down_kernel/pallas_call | solution.py:1087
  468.1 52.2 %back_ffn_kernel.1 = (bf16[4,288,128]{2,1,0:T(8,128)(2,1)}, f32[288,2048]{1,0:T(8,128)}, bf16[288,2048]{1,0:T(8,128)(2,1)}) custom-call(bf16[4,288,4096]{2,1,0:T(8,128)(2,1)} %get-tuple-element.91.y_hbm, bf16[8,2,256,2048]{3,2,1,0:T(8,128)(2,1)} %bitcast.63, bf16[128,4096]{1,0:T(8,128)(2,1)} %get-tuple-element.81.fg_ref.fu_ref.f1_ref, ...), custom_call_target="tpu_custom_call" | custom-call | flops 19327352832 | bytes 48318384 | tf_op jit(solution)/shard_map/back_ffn_kernel/pallas_call | solution.py:1087
  520.3 45.2 %back_out_kernel.1 = (bf16[4,288,512]{2,1,0:T(8,128)(2,1)}, bf16[64,2048]{1,0:T(8,128)(2,1)}, bf16[16,6656]{1,0:T(8,128)(2,1)}) custom-call(bf16[288,2048]{1,0:T(8,128)(2,1)} %get-tuple-element.95.da_ref, bf16[8,1024,512]{2,1,0:T(8,128)(2,1)} %bitcast.40, bf16[128,2048]{1,0:T(8,128)(2,1)} %get-tuple-element.71.factors_ref, ...), custom_call_target="tpu_custom_call" | custom-call | flops 2415919104 | bytes 6039797 | tf_op jit(solution)/shard_map/back_out_kernel/pallas_call | solution.py:1087
  565.6 17.7 %attend_back.1 = (f32[1152,512]{1,0:T(8,128)}, f32[1152,512]{1,0:T(8,128)}, bf16[1152,512]{1,0:T(8,128)(2,1)S(1)}, f32[2,1152,128]{2,1,0:T(8,128)S(1)}, bf16[1152,512]{1,0:T(8,128)(2,1)S(1)}) custom-call(bf16[1152,512]{1,0:T(8,128)(2,1)} %copy-done.11, bf16[1152,512]{1,0:T(8,128)(2,1)} %copy-done.12, bf16[1152,512]{1,0:T(8,128)(2,1)} %copy-done.13, ...), custom_call_target="tpu_custom_call" | custom-call | flops 6794772480 | bytes 17694720 | tf_op jit(solution)/shard_map/attend_back/pallas_call | solution.py:1239
  583.3 1.0 copy-done.5
  584.3 1.0 copy-done.6
  585.3 13.8 %prepare_kernel.1 = (bf16[1152,1664]{1,0:T(8,128)(2,1)}, bf16[16,8192]{1,0:T(8,128)(2,1)}) custom-call(f32[1152,512]{1,0:T(8,128)} %get-tuple-element.107.wq_hbm, f32[1152,512]{1,0:T(8,128)} %get-tuple-element.108.wk_hbm, bf16[1152,512]{1,0:T(8,128)(2,1)} %copy-done.5, f32[1152,1536]{1,0:T(8,128)} %bitcast.37, f32[1152,8]{1,0:T(8,128)} %get-tuple-element.74.inv_ref, ...), custom_call_target="tpu_custom_call" | custom-call | flops 603979776 | bytes 1509949 | tf_op jit(solution)/shard_map/prepare_kernel/pallas_call | solution.py:1087
  600.0 72.4 %back_qkv_kernel.1 = (bf16[1152,512]{1,0:T(8,128)(2,1)}, bf16[4,8,32,512]{3,2,1,0:T(8,128)(2,1)}) custom-call(bf16[4,288,1664]{2,1,0:T(8,128)(2,1)} %bitcast.66, bf16[8,1024,512]{2,1,0:T(8,128)(2,1)} %bitcast.41, bf16[2048,128]{1,0:T(8,128)(2,1)} %get-tuple-element.92.factors_t_ref, f32[288,2048]{1,0:T(8,128)} %get-tuple-element.114.hidden_hbm, ...), custom_call_target="tpu_custom_call" | custom-call | flops 7247757312 | bytes 18119392 | tf_op jit(solution)/shard_map/back_qkv_kernel/pallas_call | solution.py:1087
  672.5 1.7 copy-done.3
  674.2 1.3 copy-done.7
  675.5 1.2 copy-done.8
  676.7 8.0 %finish.1 = (f32[1152,512]{1,0:T(8,128)}, f32[1152,512]{1,0:T(8,128)}, f32[3,8,16,512]{3,2,1,0:T(8,128)}, f32[8,16,512]{2,1,0:T(8,128)}, f32[2,8,16,512]{3,2,1,0...) custom-call(f32[8,64]{1,0:T(8,128)S(1)} %copy-done.10, ...), custom_call_target="tpu_custom_call" | custom-call | flops 100000000 | bytes 16777216 | tf_op jit(solution)/shard_map/finish/pallas_call | solution.py:703
  (51 shorter events, 4.1 us)
Async XLA Ops:
  7.2 6.8 copy-start
  7.2 123.6 %all-gather.9.cloned.1.call-start = ((), (), s32[]{:S(2)}) async-start(), calls=%async_computation | async-start | bytes 9437184 | tf_op jit(solution)/shard_map/all_gather | solution.py:1489
  10.6 276.3 %all-gather.11.cloned.1.call-start = ((), (), s32[]{:S(2)}) async-start(), calls=%async_computation.1 | async-start | bytes 18874368 | tf_op jit(solution)/shard_map/all_gather | solution.py:1489
  13.9 1.2 copy-start.16
  13.9 1.3 copy-start.17
  13.9 1.9 copy-start.18
  13.9 351.2 %all-gather.13.cloned.1.call-start = ((), (), s32[]{:S(2)}) async-start(), calls=%async_computation.2 | async-start | bytes 9437184 | tf_op jit(solution)/shard_map/all_gather | solution.py:1489
  15.0 657.4 %all-gather.15.cloned.1.call-start = ((), (), s32[]{:S(2)}) async-start(), calls=%async_computation.3 | async-start | bytes 2359296 | tf_op jit(solution)/shard_map/all_gather | solution.py:1583
  183.0 1.1 copy-start.2
  197.3 1.0 copy-start.11
  198.3 1.0 copy-start.12
  199.3 1.0 copy-start.13
  200.3 86.6 %copy-start.4 = (bf16[128,2048]{1,0:T(8,128)(2,1)S(1)}, bf16[128,2048]{1,0:T(8,128)(2,1)}, u32[]{:S(2)}) copy-start(bf16[128,2048]{1,0:T(8,128)(2,1)} %get-tuple-element.71.factors_ref) | copy-start | bytes 1572868
  286.9 1.2 copy-start.14
  328.2 0.7 copy-start.9
  583.2 1.0 copy-start.5
  584.3 1.0 copy-start.6
  585.3 13.8 %copy-start.15 = (s32[8,7]{1,0:T(8,128)S(1)}, s32[8,7]{1,0:T(8,128)}, u32[]{:S(2)}) copy-start(s32[8,7]{1,0:T(8,128)} %ids_ref.1) | copy-start | bytes 676
  600.0 72.5 %copy-start.10 = (f32[8,64]{1,0:T(8,128)S(1)}, f32[8,64]{1,0:T(8,128)}, u32[]{:S(2)}) copy-start(f32[8,64]{1,0:T(8,128)} %pad_convert_fusion.chosen_ref) | copy-start | bytes 6148
  672.4 12.2 %copy-start.1 = (bf16[2048,512]{1,0:T(8,128)(2,1)S(1)}, bf16[2048,512]{1,0:T(8,128)(2,1)}, u32[]{:S(2)}) copy-start(bf16[2048,512]{1,0:T(8,128)(2,1)} %param.23) | copy-start | bytes 6291460
  672.5 1.7 copy-start.3
  674.2 1.3 copy-start.7
  675.5 1.2 copy-start.8
Sparse Core Ops, SparseCore 0:
  10.7 119.9 all-gather.8
  132.9 150.2 all-gather.10
  284.8 80.2 all-gather.12
  599.2 37.2 all-gather.14
